TPU v7x, 32 devices: a whole 2x2x4 slice. The times are simulated.
32 devices in a mesh: sp: 2 (over core), dp: 16 (over z, y, x).
Axes of the slice: x: 2, y: 2, z: 4, core: 2. Of those that a mesh axis runs over, the one named last changes fastest.
Arguments:
- hidden: bfloat16 [16, 256, 2048], P('dp', 'sp'), may hold values from -6 to 6
- cotangent: bfloat16 [16, 256, 2048], P('dp', 'sp'), may hold values from -6 to 6
- exit_layers: int32 [16, 2], P('dp'), may hold values from 4 to 24, as said below
- qkv_weight: bfloat16 [2048, 6144], P('sp'), may hold values from -0.125 to 0.125
- out_weight: bfloat16 [2048, 2048], P('sp'), may hold values from -3 to 3
- up_weight: bfloat16 [2048, 8192], P('sp'), may hold values from -0.125 to 0.125
- down_weight: bfloat16 [8192, 2048], P('sp'), may hold values from -0.0625 to 0.0625
- query_bias: float32 [2048], replicated, may hold values from -2 to 2
- value_bias: float32 [2048], replicated, may hold values from -2 to 2
- out_bias: float32 [2048], replicated, may hold values from -2 to 2
- up_bias: float32 [8192], replicated, may hold values from -2 to 2
- down_bias: float32 [2048], replicated, may hold values from -2 to 2
- attn_gain: float32 [2048], replicated, may hold values from 0.5 to 1.5
- attn_shift: float32 [2048], replicated, may hold values from -2 to 2
- ffn_gain: float32 [2048], replicated, may hold values from 0.5 to 1.5
- ffn_shift: float32 [2048], replicated, may hold values from -2 to 2
Outputs:
- mixed: bfloat16 [16, 256, 2048], P('dp', 'sp')
- input_grad: bfloat16 [16, 256, 2048], P('dp', 'sp')
- qkv_grad: float32 [2048, 6144], P('sp')
- out_grad: float32 [2048, 2048], P('sp')
- up_grad: float32 [2048, 8192], P('sp')
- down_grad: float32 [8192, 2048], P('sp')
- query_bias_grad: float32 [2048], replicated
- value_bias_grad: float32 [2048], replicated
- out_bias_grad: float32 [2048], replicated
- up_bias_grad: float32 [8192], replicated
- down_bias_grad: float32 [2048], replicated
- attn_gain_grad: float32 [2048], replicated
- attn_shift_grad: float32 [2048], replicated
- ffn_gain_grad: float32 [2048], replicated
- ffn_shift_grad: float32 [2048], replicated
Inputs may be any that keep to these rules, and one draw needn't show every extreme that they name: `exit_layers`: row s holds sequence s's smallest exit layer, then its largest; the smallest is at most 11 and the largest at least 13, and some row holds 4, some row 24.
All inputs are finite; a program needn't handle non-finite values.
Results may differ from a plain program's by a relative error of at most 0.02.
Values may be sent and summed in bfloat16 or wider, within the bound.
No kernel may reach another device: no remote copies, remote signals or barrier semaphores. Data moves between devices by JAX's collectives and lax.ppermute only.
A program may use at most 704 MiB of HBM per device.

v0:
```python
import jax
import jax.numpy as jnp
from jax import lax
from jax.sharding import PartitionSpec as P

HEAD_DIM = 64
TILE = 128
LAYER = 12


def layer_norm(values, gain, shift):
    center = jnp.mean(values, axis=-1, keepdims=True)
    centered = values - center
    variance = jnp.mean(centered * centered, axis=-1, keepdims=True)
    return centered * lax.rsqrt(variance + 1e-05) * gain + shift


def active_rows(bounds, first_row, row_count, sequence_length):
    position = first_row + jnp.arange(row_count, dtype=jnp.int32)
    tile_start = position // TILE * TILE
    exit_layer = bounds[1] - (bounds[1] - bounds[0]) * tile_start // sequence_length
    return (exit_layer > LAYER).astype(jnp.float32)[:, None]


def project(left_side, weight):
    return jnp.dot(
        left_side,
        lax.all_gather(weight, "sp", axis=0, tiled=True),
        preferred_element_type=jnp.float32,
    )


def project_back(gradient, weight):
    return lax.dot_general(
        gradient,
        lax.all_gather(weight, "sp", axis=0, tiled=True),
        (((1,), (1,)), ((), ())),
        preferred_element_type=jnp.float32,
    )


def weight_term(left_side, gradient):
    return lax.psum_scatter(
        lax.dot_general(
            left_side, gradient, (((0,), (0,)), ((), ())), preferred_element_type=jnp.float32
        ).astype(jnp.bfloat16),
        "sp",
        scatter_dimension=0,
        tiled=True,
    ).astype(jnp.float32)


def masked_scores(query_part, key_rows, first_row, score_scale):
    block_rows = query_part.shape[0]
    scores = (
        jnp.einsum("qhd,khd->hqk", query_part, key_rows, preferred_element_type=jnp.float32)
        * score_scale
    )
    key_place = jnp.arange(key_rows.shape[0], dtype=jnp.int32)
    query_place = first_row + jnp.arange(block_rows, dtype=jnp.int32)
    allowed = key_place[None, :] <= query_place[:, None]
    return jnp.where(allowed[None], scores, -1e30)


def attend_forward(queries, key_rows, value_rows, block_rows, score_scale):
    sequence_length = queries.shape[0]

    def query_block(block_index):
        first_row = block_index * block_rows
        scores = masked_scores(queries, key_rows, first_row, score_scale)
        row_peak = jnp.max(scores, axis=-1, keepdims=True)
        raised = jnp.exp(scores - row_peak)
        row_total = jnp.sum(raised, axis=-1, keepdims=True)
        chances = (raised / row_total).astype(jnp.bfloat16)
        result = jnp.einsum("hqk,khd->qhd", chances, value_rows, preferred_element_type=jnp.float32)
        return (
            result.astype(jnp.bfloat16).reshape(block_rows, -1),
            (row_peak + jnp.log(row_total))[..., 0],
        )

    results, log_totals = lax.map(
        query_block, jnp.arange(sequence_length // block_rows, dtype=jnp.int32)
    )
    return (results.reshape(sequence_length, -1), log_totals)


def attend_backward(
    queries, key_rows, value_rows, result_grads, log_totals, block_rows, score_scale
):
    sequence_length = queries.shape[0]
    zeros_acc = jnp.zeros(key_rows.shape, jnp.float32)

    def query_block(running, block_index):
        key_acc, value_acc = running
        first_row = block_index * block_rows
        scores = masked_scores(queries, key_rows, first_row, score_scale)
        chances = jnp.exp(scores - log_totals[block_index][..., None])
        chances_low = chances.astype(jnp.bfloat16)
        value_acc = value_acc + jnp.einsum(
            "hqk,qhd->khd", chances_low, result_grads, preferred_element_type=jnp.float32
        )
        chance_grad = jnp.einsum(
            "qhd,khd->hqk", result_grads, value_rows, preferred_element_type=jnp.float32
        )
        inner_sum = jnp.sum(chances * chance_grad, axis=-1, keepdims=True)
        score_grad = (chances * (chance_grad - inner_sum)).astype(jnp.bfloat16)
        query_grad = (
            jnp.einsum("hqk,khd->qhd", score_grad, key_rows, preferred_element_type=jnp.float32)
            * score_scale
        )
        key_acc = (
            key_acc
            + jnp.einsum("hqk,qhd->khd", score_grad, queries, preferred_element_type=jnp.float32)
            * score_scale
        )
        return ((key_acc, value_acc), query_grad.astype(jnp.bfloat16))

    (key_acc, value_acc), query_grads = lax.scan(
        query_block,
        (zeros_acc, zeros_acc),
        jnp.arange(sequence_length // block_rows, dtype=jnp.int32),
    )
    query_grads = query_grads.reshape(sequence_length, -1)
    return (
        query_grads,
        key_acc.astype(jnp.bfloat16).reshape(sequence_length, -1),
        value_acc.astype(jnp.bfloat16).reshape(sequence_length, -1),
    )


def per_device(
    hidden,
    cotangent,
    exit_layers,
    qkv_weight,
    out_weight,
    up_weight,
    down_weight,
    query_bias,
    value_bias,
    out_bias,
    up_bias,
    down_bias,
    attn_gain,
    attn_shift,
    ffn_gain,
    ffn_shift,
):
    groups = lax.axis_size("sp")
    row_count = hidden.shape[1]
    model_width = hidden.shape[2]
    sequence_length = row_count * groups
    block_rows = min(512, sequence_length)
    score_scale = HEAD_DIM ** (-0.5)
    inputs = hidden[0].astype(jnp.float32)
    active = active_rows(
        exit_layers[0], lax.axis_index("sp") * row_count, row_count, sequence_length
    )
    normed_one, norm_one_back = jax.vjp(layer_norm, inputs, attn_gain, attn_shift)
    normed_one_low = normed_one.astype(jnp.bfloat16)
    bias_cat = jnp.concatenate([query_bias, jnp.zeros_like(query_bias), value_bias])
    qkv = project(normed_one_low, qkv_weight) + bias_cat
    qkv_low = qkv.astype(jnp.bfloat16).reshape(row_count, 3, model_width)
    head_rows = lax.all_to_all(qkv_low, "sp", split_axis=2, concat_axis=0, tiled=True)
    queries = head_rows[:, 0].reshape(sequence_length, -1, HEAD_DIM)
    key_rows = head_rows[:, 1].reshape(sequence_length, -1, HEAD_DIM)
    value_rows = head_rows[:, 2].reshape(sequence_length, -1, HEAD_DIM)
    attended_heads, log_totals = attend_forward(
        queries, key_rows, value_rows, block_rows, score_scale
    )
    attended = lax.all_to_all(attended_heads, "sp", split_axis=0, concat_axis=1, tiled=True)
    attn_out = project(attended, out_weight) + out_bias
    middle = inputs + active * attn_out
    normed_two, norm_two_back = jax.vjp(layer_norm, middle, ffn_gain, ffn_shift)
    normed_two_low = normed_two.astype(jnp.bfloat16)
    up_rows = project(normed_two_low, up_weight) + up_bias
    inner_act, gelu_back = jax.vjp(jax.nn.gelu, up_rows)
    inner_low = inner_act.astype(jnp.bfloat16)
    down_rows = project(inner_low, down_weight) + down_bias
    output = middle + active * down_rows
    grad_output = cotangent[0].astype(jnp.float32)
    down_grad_low = (active * grad_output).astype(jnp.bfloat16)
    down_term = weight_term(inner_low, down_grad_low)
    inner_grad = project_back(down_grad_low, down_weight)
    up_grad_low = gelu_back(inner_grad)[0].astype(jnp.bfloat16)
    up_term = weight_term(normed_two_low, up_grad_low)
    normed_two_grad = project_back(up_grad_low, up_weight)
    middle_part, gain_two_grad, shift_two_grad = norm_two_back(normed_two_grad)
    middle_grad = grad_output + middle_part
    attn_grad_low = (active * middle_grad).astype(jnp.bfloat16)
    out_term = weight_term(attended, attn_grad_low)
    attended_grad = project_back(attn_grad_low, out_weight).astype(jnp.bfloat16)
    head_grads = lax.all_to_all(attended_grad, "sp", split_axis=1, concat_axis=0, tiled=True)
    head_grads = head_grads.reshape(sequence_length, -1, HEAD_DIM)
    query_grads, key_grads, value_grads = attend_backward(
        queries, key_rows, value_rows, head_grads, log_totals, block_rows, score_scale
    )
    stacked_grads = jnp.stack([query_grads, key_grads, value_grads], axis=1)
    qkv_grad_low = lax.all_to_all(
        stacked_grads, "sp", split_axis=0, concat_axis=2, tiled=True
    ).reshape(row_count, 3 * model_width)
    qkv_term = weight_term(normed_one_low, qkv_grad_low)
    normed_one_grad = project_back(qkv_grad_low, qkv_weight)
    input_part, gain_one_grad, shift_one_grad = norm_one_back(normed_one_grad)
    input_grad = (middle_grad + input_part).astype(jnp.bfloat16)
    qkv_columns = jnp.sum(qkv_grad_low.astype(jnp.float32), axis=0).reshape(3, model_width)
    small_grads = lax.psum(
        (
            qkv_columns[0],
            qkv_columns[2],
            jnp.sum(attn_grad_low.astype(jnp.float32), axis=0),
            jnp.sum(up_grad_low.astype(jnp.float32), axis=0),
            jnp.sum(down_grad_low.astype(jnp.float32), axis=0),
            gain_one_grad,
            shift_one_grad,
            gain_two_grad,
            shift_two_grad,
        ),
        ("sp", "dp"),
    )
    shares = (
        lax.psum_scatter(qkv_term, "dp", scatter_dimension=0, tiled=True),
        lax.psum_scatter(out_term, "dp", scatter_dimension=0, tiled=True),
        lax.psum_scatter(up_term, "dp", scatter_dimension=0, tiled=True),
        lax.psum_scatter(down_term, "dp", scatter_dimension=0, tiled=True),
    )
    summed = (
        lax.all_gather(shares[0].astype(jnp.bfloat16), "dp", axis=0, tiled=True).astype(
            jnp.float32
        ),
        lax.all_gather(shares[1].astype(jnp.bfloat16), "dp", axis=0, tiled=True).astype(
            jnp.float32
        ),
        lax.all_gather(shares[2].astype(jnp.bfloat16), "dp", axis=0, tiled=True).astype(
            jnp.float32
        ),
        lax.all_gather(shares[3].astype(jnp.bfloat16), "dp", axis=0, tiled=True).astype(
            jnp.float32
        ),
    )
    return (
        output.astype(jnp.bfloat16)[None],
        input_grad[None],
        summed[0],
        summed[1],
        summed[2],
        summed[3],
        small_grads[0],
        small_grads[1],
        small_grads[2],
        small_grads[3],
        small_grads[4],
        small_grads[5],
        small_grads[6],
        small_grads[7],
        small_grads[8],
    )


def solution(mesh):
    return jax.shard_map(
        per_device,
        mesh=mesh,
        in_specs=(
            P("dp", "sp", None),
            P("dp", "sp", None),
            P("dp", None),
            P("sp", None),
            P("sp", None),
            P("sp", None),
            P("sp", None),
            P(),
            P(),
            P(),
            P(),
            P(),
            P(),
            P(),
            P(),
            P(),
        ),
        out_specs=(
            P("dp", "sp", None),
            P("dp", "sp", None),
            P("sp", None),
            P("sp", None),
            P("sp", None),
            P("sp", None),
            P(),
            P(),
            P(),
            P(),
            P(),
            P(),
            P(),
            P(),
            P(),
        ),
        check_vma=False,
    )
```

profile of v0, /device:TPU:0, one launch (start us, length us, event | category | flops | bytes accessed | tf_op | source)
XLA Modules:
  0.0 2228.4 jit_solution(8153960267773995833)
XLA Ops:
  13.2 39.4 %all-gather.9.cloned.1.call-done = bf16[2048,6144]{1,0:T(8,128)(2,1)} async-done(((bf16[1024,6144]{1,0:T(8,128)(2,1)}), bf16[2048,6144]{1,0:T(8,128)(2,1)}) %all-gather.9.cloned.1.call-update) | async-done | bytes 25165840 | tf_op jit(solution)/shard_map/all_gather | solution.py:28
  100.4 30.3 %all-gather.13.cloned.1.call-done = bf16[2048,8192]{1,0:T(8,128)(2,1)} async-done(((bf16[1024,8192]{1,0:T(8,128)(2,1)}), bf16[2048,8192]{1,0:T(8,128)(2,1)}) %all-gather.13.cloned.1.call-update) | async-done | bytes 33554448 | tf_op jit(solution)/shard_map/all_gather | solution.py:28
  130.7 20.2 convolution_add_fusion
  150.9 33.6 %all-gather.15.cloned.1.call-done = bf16[8192,2048]{1,0:T(8,128)(2,1)} async-done(((bf16[4096,2048]{1,0:T(8,128)(2,1)}), bf16[8192,2048]{1,0:T(8,128)(2,1)}) %all-gather.15.cloned.1.call-update) | async-done | bytes 33554448 | tf_op jit(solution)/shard_map/all_gather | solution.py:28
  184.5 19.9 convert_reduce_fusion
  204.4 19.7 multiply_reduce_fusion.1
  241.7 15.8 all_to_all.69
  309.2 23.7 %convolution_convert_fusion.1 = bf16[8192,2048]{1,0:T(8,128)(2,1)} fusion(bf16[1,128,2048]{2,1,0:T(8,128)(2,1)} %param.17, f32[128]{0:T(128)S(1)} %compare_convert_fusion, f32[128,8192]{1,0:T(8,128)} %convolution_add_fusion), kind=kOutput, calls=%fused_computation.1 | convolution fusion | flops 4321968128 | bytes 38273536 | tf_op jit(solution)/shard_map/dot_general | solution.py:44
  333.0 18.5 convolution_convert_fusion
  352.9 42.5 %reduce-scatter.22.cloned.1.call-done = bf16[4096,2048]{1,0:T(8,128)(2,1)} async-done(((bf16[8192,2048]{1,0:T(8,128)(2,1)}), bf16[4096,2048]{1,0:T(8,128)(2,1)}) %reduce-scatter.22.cloned.1.call-update) | async-done | bytes 16777232 | tf_op jit(solution)/shard_map/reduce_scatter | solution.py:43
  395.5 49.3 %reduce-scatter.18.cloned.1.call-done = bf16[1024,8192]{1,0:T(8,128)(2,1)} async-done(((bf16[2048,8192]{1,0:T(8,128)(2,1)}), bf16[1024,8192]{1,0:T(8,128)(2,1)}) %reduce-scatter.18.cloned.1.call-update) | async-done | bytes 16777232 | tf_op jit(solution)/shard_map/reduce_scatter | solution.py:43
  444.8 98.7 %reduce-scatter.16.cloned.1.call-done = bf16[64,2048]{1,0:T(8,128)(2,1)} async-done(((bf16[1024,2048]{1,0:T(8,128)(2,1)}), bf16[64,2048]{1,0:T(8,128)(2,1)}) %reduce-scatter.16.cloned.1.call-update) | async-done | bytes 262160 | tf_op jit(solution)/shard_map/reduce_scatter | solution.py:223
  543.6 210.0 %reduce-scatter.12.cloned.1.call-done = bf16[64,6144]{1,0:T(8,128)(2,1)} async-done(((bf16[1024,6144]{1,0:T(8,128)(2,1)}), bf16[64,6144]{1,0:T(8,128)(2,1)}) %reduce-scatter.12.cloned.1.call-update) | async-done | bytes 786448 | tf_op jit(solution)/shard_map/reduce_scatter | solution.py:222
  753.7 348.2 %reduce-scatter.24.cloned.1.call-done = bf16[256,2048]{1,0:T(8,128)(2,1)} async-done(((bf16[4096,2048]{1,0:T(8,128)(2,1)}), bf16[256,2048]{1,0:T(8,128)(2,1)}) %reduce-scatter.24.cloned.1.call-update) | async-done | bytes 1048592 | tf_op jit(solution)/shard_map/reduce_scatter | solution.py:225
  1102.0 354.1 %reduce-scatter.20.cloned.1.call-done = bf16[64,8192]{1,0:T(8,128)(2,1)} async-done(((bf16[1024,8192]{1,0:T(8,128)(2,1)}), bf16[64,8192]{1,0:T(8,128)(2,1)}) %reduce-scatter.20.cloned.1.call-update) | async-done | bytes 1048592 | tf_op jit(solution)/shard_map/reduce_scatter | solution.py:224
  1456.2 15.3 fusion.64
  1474.6 17.9 fusion.15
  1493.9 46.8 %all-gather.19.cloned.1.call-done = bf16[1024,2048]{1,0:T(8,128)(2,1)} async-done(((bf16[64,2048]{1,0:T(8,128)(2,1)}), bf16[1024,2048]{1,0:T(8,128)(2,1)}) %all-gather.19.cloned.1.call-update) | async-done | bytes 4194320 | tf_op jit(solution)/shard_map/all_gather | solution.py:231
  1547.3 146.6 %all-gather.17.cloned.1.call-done = bf16[1024,6144]{1,0:T(8,128)(2,1)} async-done(((bf16[64,6144]{1,0:T(8,128)(2,1)}), bf16[1024,6144]{1,0:T(8,128)(2,1)}) %all-gather.17.cloned.1.call-update) | async-done | bytes 12582928 | tf_op jit(solution)/shard_map/all_gather | solution.py:228
  1708.6 177.8 %all-gather.23.cloned.1.call-done = bf16[4096,2048]{1,0:T(8,128)(2,1)} async-done(((bf16[256,2048]{1,0:T(8,128)(2,1)}), bf16[4096,2048]{1,0:T(8,128)(2,1)}) %all-gather.23.cloned.1.call-update) | async-done | bytes 16777232 | tf_op jit(solution)/shard_map/all_gather | solution.py:237
  1886.4 19.0 convert_element_type.197
  1905.4 173.4 %all-gather.21.cloned.1.call-done = bf16[1024,8192]{1,0:T(8,128)(2,1)} async-done(((bf16[64,8192]{1,0:T(8,128)(2,1)}), bf16[1024,8192]{1,0:T(8,128)(2,1)}) %all-gather.21.cloned.1.call-update) | async-done | bytes 16777232 | tf_op jit(solution)/shard_map/all_gather | solution.py:234
  2078.8 18.6 convert_element_type.193
  2097.5 112.3 %all-reduce.4.cloned.1.call-done = (f32[2048]{0:T(1024)}, f32[2048]{0:T(1024)}, f32[2048]{0:T(1024)}, f32[8192]{0:T(1024)}, f32[2048]{0:T(1024)}, /*index=5*/f32...) async-done(((f32[2048]{0:T(1024)}, f32[2048]{0:T(1024)}, f32[2048]{0:T(1024)}, f32[8192]{0:T(1024)}, f32[2048]{0:T(1024)}, /*index=5*/f32[2048]{0:T(1024)}, ...) | async-done | bytes 98320 | tf_op jit(solution)/shard_map/psum | solution.py:207
  (161 shorter events, 160.6 us)
Async XLA Ops:
  7.2 45.4 %all-gather.9.cloned.1.call-start = ((), (), s32[]{:S(2)}) async-start(), calls=%async_computation.12 | async-start | bytes 37748736 | tf_op jit(solution)/shard_map/all_gather | solution.py:28
  7.9 82.7 %all-gather.11.cloned.1.call-start = ((), (), s32[]{:S(2)}) async-start(), calls=%async_computation.13 | async-start | bytes 12582912 | tf_op jit(solution)/shard_map/all_gather | solution.py:28
  8.7 122.0 %all-gather.13.cloned.1.call-start = ((), (), s32[]{:S(2)}) async-start(), calls=%async_computation.14 | async-start | bytes 50331648 | tf_op jit(solution)/shard_map/all_gather | solution.py:28
  9.4 43.1 %copy-start.15 = (f32[2048]{0:T(1024)S(1)}, f32[2048]{0:T(1024)}, u32[]{:S(2)}) copy-start(f32[2048]{0:T(1024)} %param.28) | copy-start | bytes 24580
  9.4 43.1 %copy-start.17 = (f32[2048]{0:T(1024)S(1)}, f32[2048]{0:T(1024)}, u32[]{:S(2)}) copy-start(f32[2048]{0:T(1024)} %param.29) | copy-start | bytes 24580
  9.5 175.1 %all-gather.15.cloned.1.call-start = ((), (), s32[]{:S(2)}) async-start(), calls=%async_computation.15 | async-start | bytes 50331648 | tf_op jit(solution)/shard_map/all_gather | solution.py:28
  13.1 51.2 %copy-start.24 = (f32[128]{0:T(128)}, f32[128]{0:T(128)S(1)}, u32[]{:S(2)}) copy-start(f32[128]{0:T(128)S(1)} %fusion.38) | copy-start | bytes 1540
  86.8 5.3 all-to-all-start.1
  90.4 261.2 %reduce-scatter.14.cloned.1.call-start = ((), (), s32[]{:S(2)}) async-start(), calls=%async_computation.18 | async-start | bytes 12582912 | tf_op jit(solution)/shard_map/reduce_scatter | solution.py:43
  92.1 38.6 %copy-start.18 = (f32[2048]{0:T(1024)S(1)}, f32[2048]{0:T(1024)}, u32[]{:S(2)}) copy-start(f32[2048]{0:T(1024)} %param.31) | copy-start | bytes 24580
  92.1 38.6 %copy-start.19 = (f32[8192]{0:T(1024)S(1)}, f32[8192]{0:T(1024)}, u32[]{:S(2)}) copy-start(f32[8192]{0:T(1024)} %param.26) | copy-start | bytes 98308
  100.3 84.2 %copy-start.7 = (bf16[1,128,2048]{2,1,0:T(8,128)(2,1)S(1)}, bf16[1,128,2048]{2,1,0:T(8,128)(2,1)}, u32[]{:S(2)}) copy-start(bf16[1,128,2048]{2,1,0:T(8,128)(2,1)} %param.17) | copy-start | bytes 1572868
  234.3 118.0 %reduce-scatter.26.cloned.1.call-start = ((), (), s32[]{:S(2)}) async-start(), calls=%async_computation.27 | async-start | bytes 37748736
  309.2 86.2 %reduce-scatter.22.cloned.1.call-start = ((), (), s32[]{:S(2)}) async-start(), calls=%async_computation.24 | async-start | bytes 50331648 | tf_op jit(solution)/shard_map/reduce_scatter | solution.py:43
  332.9 111.8 %reduce-scatter.18.cloned.1.call-start = ((), (), s32[]{:S(2)}) async-start(), calls=%async_computation.21 | async-start | bytes 50331648 | tf_op jit(solution)/shard_map/reduce_scatter | solution.py:43
  351.5 192.0 %reduce-scatter.16.cloned.1.call-start = ((), (), s32[]{:S(2)}) async-start(), calls=%async_computation.19 | async-start | bytes 4456448 | tf_op jit(solution)/shard_map/reduce_scatter | solution.py:223
  352.3 401.3 %reduce-scatter.12.cloned.1.call-start = ((), (), s32[]{:S(2)}) async-start(), calls=%async_computation.16 | async-start | bytes 13369344 | tf_op jit(solution)/shard_map/reduce_scatter | solution.py:222
  352.9 749.0 %reduce-scatter.24.cloned.1.call-start = ((), (), s32[]{:S(2)}) async-start(), calls=%async_computation.25 | async-start | bytes 17825792 | tf_op jit(solution)/shard_map/reduce_scatter | solution.py:225
  395.4 1060.7 %reduce-scatter.20.cloned.1.call-start = ((), (), s32[]{:S(2)}) async-start(), calls=%async_computation.22 | async-start | bytes 17825792 | tf_op jit(solution)/shard_map/reduce_scatter | solution.py:224
  444.8 1095.9 %all-gather.19.cloned.1.call-start = ((), (), s32[]{:S(2)}) async-start(), calls=%async_computation.20 | async-start | bytes 4456448 | tf_op jit(solution)/shard_map/all_gather | solution.py:231
  543.5 1150.4 %all-gather.17.cloned.1.call-start = ((), (), s32[]{:S(2)}) async-start(), calls=%async_computation.17 | async-start | bytes 13369344 | tf_op jit(solution)/shard_map/all_gather | solution.py:228
  753.6 1132.7 %all-gather.23.cloned.1.call-start = ((), (), s32[]{:S(2)}) async-start(), calls=%async_computation.26 | async-start | bytes 17825792 | tf_op jit(solution)/shard_map/all_gather | solution.py:237
  1101.9 976.9 %all-gather.21.cloned.1.call-start = ((), (), s32[]{:S(2)}) async-start(), calls=%async_computation.23 | async-start | bytes 17825792 | tf_op jit(solution)/shard_map/all_gather | solution.py:234
  1456.2 753.5 %all-reduce.4.cloned.1.call-start = ((), (), s32[]{:S(2)}) async-start(), calls=%async_computation.28 | async-start | bytes 196608 | tf_op jit(solution)/shard_map/psum | solution.py:207
  (21 other events, 170.3 us)
Sparse Core Ops, SparseCore 0:
  9.6 42.9 all-gather.8
  54.1 22.5 all-gather.10
  78.2 52.3 all-gather.12
  132.1 52.3 all-gather.14
  234.5 17.9 reduce-scatter.13
  309.3 36.6 reduce-scatter.25
  349.0 46.3 reduce-scatter.21
  398.4 46.3 reduce-scatter.17
  447.2 96.2 reduce-scatter.15
  549.9 203.6 reduce-scatter.11
  755.9 345.9 reduce-scatter.23
  1104.1 352.0 reduce-scatter.19
  1458.9 81.7 all-gather.18
  1543.3 150.6 all-gather.16
  1696.5 189.7 all-gather.22
  1889.0 189.7 all-gather.20
  2086.3 123.4 all-reduce.3
where the time goes:
time: 2240 us; the launch traced here: 2230 us
  waiting for transfers between devices  1870 us (83%)
  matrix products  192 us (9%)
  other arithmetic  75.2 us (3%)
  local copies, waits for them, and re-layouts  43.9 us (2%)
  blocking collectives  28.1 us (1%)
    reduce_scatter x1, waiting for transfers between devices, per_device(): lax.psum_scatter(up_term, 'dp', scatter_dimension=0, tiled=True)  354 us
    reduce_scatter x1, waiting for transfers between devices, per_device(): lax.psum_scatter(down_term, 'dp', scatter_dimension=0, tiled=True)  348 us
    reduce_scatter x1, waiting for transfers between devices, per_device(): lax.psum_scatter(qkv_term, 'dp', scatter_dimension=0, tiled=True)  210 us
    all_gather x1, waiting for transfers between devices, per_device(): lax.all_gather(shares[3].astype(jnp.bfloat16), 'dp', axis=0, tiled=True)  178 us
    all_gather x1, waiting for transfers between devices, per_device(): lax.all_gather(shares[2].astype(jnp.bfloat16), 'dp', axis=0, tiled=True)  173 us
    all_gather x1, waiting for transfers between devices, per_device(): lax.all_gather(shares[0].astype(jnp.bfloat16), 'dp', axis=0, tiled=True)  147 us
    psum x1, waiting for transfers between devices, per_device(): lax.psum((qkv_columns[0], qkv_columns[2], jnp.sum(attn_grad_low.astype(jn...  112 us
    all_gather x4, waiting for transfers between devices, project(): lax.all_gather(weight, 'sp', axis=0, tiled=True)  103 us
  transfers between devices with their start and end apart: 18, of which 15 were waited for; matrix products, arithmetic and copies ran while one was open for 11% of the time, Pallas kernels for 0%

commit v1 on v0

v1 whole, which is shorter than its diff:
```python
import functools

import jax
import jax.numpy as jnp
from jax import lax
from jax.experimental import pallas as pl
from jax.experimental.pallas import tpu as pltpu
from jax.sharding import PartitionSpec as P

HEAD_DIM = 64
TILE = 128
LAYER = 12
LINE = 4
GROUP = 4
F32 = jnp.float32
LOW = jnp.bfloat16


def layer_norm(values, gain, shift):
    center = jnp.mean(values, axis=-1, keepdims=True)
    centered = values - center
    variance = jnp.mean(centered * centered, axis=-1, keepdims=True)
    return centered * lax.rsqrt(variance + 1e-05) * gain + shift


def active_rows(bounds, first_row, row_count, sequence_length):
    position = first_row + jnp.arange(row_count, dtype=jnp.int32)
    tile_start = position // TILE * TILE
    exit_layer = bounds[1] - (bounds[1] - bounds[0]) * tile_start // sequence_length
    return (exit_layer > LAYER).astype(F32)[:, None]


def gelu_and_slope(values):
    scale = (2.0 / jnp.pi) ** 0.5
    square = values * values
    bend = jnp.tanh(scale * values * (1.0 + 0.044715 * square))
    rise = 0.5 * (1.0 + bend)
    slope = rise + 0.5 * values * (1.0 - bend * bend) * scale * (1.0 + 0.134145 * square)
    return values * rise, slope


def dot(left, right, left_dim, right_dim):
    return lax.dot_general(
        left, right, (((left_dim,), (right_dim,)), ((), ())), preferred_element_type=F32
    )


def roll_rows(value):
    rows = value.shape[0] // 2
    return jnp.concatenate([value[rows:], value[:rows]])


def estimate(flops, *arrays):
    return pl.CostEstimate(
        flops=flops,
        bytes_accessed=sum(a.size * a.dtype.itemsize for a in arrays),
        transcendentals=0,
    )


def far(value):
    return pltpu.with_memory_space_constraint(value, pltpu.HBM)


def limit(mebibytes):
    return pltpu.CompilerParams(vmem_limit_bytes=mebibytes << 20)


def halves(core_ref, values, mine_ref, theirs_ref):
    width = mine_ref.shape[1]
    first = core_ref[0] == 0
    low, high = values[:, :width], values[:, width:]
    mine_ref[...] = jnp.where(first, low, high).astype(LOW)
    theirs_ref[...] = jnp.where(first, high, low).astype(LOW)


def norm_one_kernel(core_ref, x_ref, gain_ref, shift_ref, mine_ref, theirs_ref):
    normed = layer_norm(x_ref[...].astype(F32), gain_ref[...], shift_ref[...])
    halves(core_ref, normed, mine_ref, theirs_ref)


def norm_two_kernel(
    core_ref, x_ref, active_ref, part_ref, theirs_part_ref, bias_ref, gain_ref, shift_ref,
    middle_ref, mine_ref, theirs_ref,
):
    rows = x_ref.shape[0]
    attn = part_ref[:rows] + theirs_part_ref[...] + bias_ref[...]
    middle = x_ref[...].astype(F32) + active_ref[...] * attn
    middle_ref[...] = middle
    halves(core_ref, layer_norm(middle, gain_ref[...], shift_ref[...]), mine_ref, theirs_ref)


def norm(kernel, core, rows, width, whole, *operands):
    half = jax.ShapeDtypeStruct((rows, width // 2), LOW)
    outs = [jax.ShapeDtypeStruct((rows, width), F32)] * whole + [half, half]
    vmem = pl.BlockSpec(memory_space=pltpu.VMEM)
    return pl.pallas_call(
        kernel,
        in_specs=[pl.BlockSpec(memory_space=pltpu.SMEM)] + [vmem] * len(operands),
        out_specs=[vmem] * len(outs),
        out_shape=outs,
        compiler_params=limit(24),
        cost_estimate=estimate(20 * rows * width, *operands),
    )(core, *operands)


def columns_kernel(table_ref, left_ref, weight_ref, out_ref):
    out_ref[...] = dot(left_ref[...], weight_ref[...], 1, 0)


def times_columns(left, weight, table, block):
    rows, depth = left.shape
    steps = table.shape[0]
    return pl.pallas_call(
        columns_kernel,
        grid_spec=pltpu.PrefetchScalarGridSpec(
            num_scalar_prefetch=1,
            grid=(steps,),
            in_specs=[
                pl.BlockSpec((rows, depth), lambda i, t: (0, 0)),
                pl.BlockSpec((depth, block), lambda i, t: (0, t[i])),
            ],
            out_specs=pl.BlockSpec((rows, block), lambda i, t: (0, i)),
        ),
        out_shape=jax.ShapeDtypeStruct((rows, steps * block), F32),
        compiler_params=limit(24),
        cost_estimate=pl.CostEstimate(
            flops=2 * rows * depth * steps * block,
            bytes_accessed=2 * depth * (rows + steps * block) + 4 * rows * steps * block,
            transcendentals=0,
        ),
    )(table, left, far(weight))


def back_kernel(turned, table_ref, left_ref, weight_ref, *rest):
    out_ref = rest[-1]
    left = left_ref[...]
    if turned:
        left = roll_rows(left)
    part = dot(left, weight_ref[...], 1, 1)

    @pl.when(pl.program_id(1) == 0)
    def _():
        out_ref[...] = part + rest[0][...] if len(rest) > 1 else part

    @pl.when(pl.program_id(1) > 0)
    def _():
        out_ref[...] += part


def times_back(left, weight, table, block, deep, start=None, turned=False):
    rows = left.shape[0]
    depth = weight.shape[0]
    steps = table.shape[0]
    out_spec = pl.BlockSpec((rows, deep), lambda k, i, t: (0, k))
    in_specs = [
        pl.BlockSpec((rows, block), lambda k, i, t: (0, i)),
        pl.BlockSpec((deep, block), lambda k, i, t: (k, t[i])),
    ]
    operands = [table, left, far(weight)]
    if start is not None:
        in_specs.append(out_spec)
        operands.append(start)
    return pl.pallas_call(
        functools.partial(back_kernel, turned),
        grid_spec=pltpu.PrefetchScalarGridSpec(
            num_scalar_prefetch=1,
            grid=(depth // deep, steps),
            in_specs=in_specs,
            out_specs=out_spec,
        ),
        out_shape=jax.ShapeDtypeStruct((rows, depth), F32),
        compiler_params=limit(32),
        cost_estimate=pl.CostEstimate(
            flops=2 * rows * depth * steps * block,
            bytes_accessed=2 * steps * block * (rows + depth) + 8 * rows * depth,
            transcendentals=0,
        ),
    )(*operands)


def inner_kernel(grad_ref, weight_ref, mine_ref, theirs_ref, bias_ref, act_ref, out_ref, sum_ref):
    act, slope = gelu_and_slope(mine_ref[...] + roll_rows(theirs_ref[...]) + bias_ref[...])
    act_ref[...] = act.astype(LOW)
    grad = (dot(grad_ref[...], weight_ref[...], 1, 1) * slope).astype(LOW)
    out_ref[...] = grad
    sum_ref[...] = jnp.sum(grad.astype(F32), axis=0, keepdims=True)


def inner_layer(grads, weight, mine, theirs, bias, block):
    rows, width = grads.shape
    hidden = weight.shape[0]
    part = pl.BlockSpec((rows, block), lambda i: (0, i))
    line = pl.BlockSpec((1, block), lambda i: (0, i))
    return pl.pallas_call(
        inner_kernel,
        grid=(hidden // block,),
        in_specs=[
            pl.BlockSpec((rows, width), lambda i: (0, 0)),
            pl.BlockSpec((block, width), lambda i: (i, 0)),
            part,
            part,
            line,
        ],
        out_specs=[part, part, line],
        out_shape=[
            jax.ShapeDtypeStruct((rows, hidden), LOW),
            jax.ShapeDtypeStruct((rows, hidden), LOW),
            jax.ShapeDtypeStruct((1, hidden), F32),
        ],
        compiler_params=limit(32),
        cost_estimate=pl.CostEstimate(
            flops=2 * rows * width * hidden,
            bytes_accessed=2 * width * (rows + hidden) + 12 * rows * hidden,
            transcendentals=rows * hidden,
        ),
    )(grads, far(weight), mine, theirs, bias)


def head_chances(queries, keys, lanes_of_head, allowed):
    keys_of_head = jnp.where(lanes_of_head, keys, jnp.zeros_like(keys))
    scores = dot(queries, keys_of_head, 1, 1) * (HEAD_DIM**-0.5)
    scores = jnp.where(allowed, scores, -1e30)
    raised = jnp.exp(scores - jnp.max(scores, axis=-1, keepdims=True))
    return raised / jnp.sum(raised, axis=-1, keepdims=True)


def attend_masks(first, length, lanes):
    lane = lax.broadcasted_iota(jnp.int32, (length, lanes), 1)
    row = lax.broadcasted_iota(jnp.int32, (length, length), 0) + first
    column = lax.broadcasted_iota(jnp.int32, (length, length), 1) + first
    row = jnp.where(row >= length, row - length, row)
    column = jnp.where(column >= length, column - length, column)
    return lane, column <= row


def attend_forward_kernel(first_ref, *refs):
    mine, theirs, biases, lows, o_ref = refs[:3], refs[3:6], refs[6:9], refs[9:12], refs[12]
    sums = [
        (m[...] + roll_rows(t[...]) + b[...]).astype(LOW)
        for m, t, b in zip(mine, theirs, biases)
    ]
    for low, value in zip(lows, sums):
        low[...] = value
    queries, keys, values = sums
    lane, allowed = attend_masks(first_ref[0], *queries.shape)
    total = jnp.zeros(queries.shape, F32)
    for head in range(queries.shape[1] // HEAD_DIM):
        own = lane // HEAD_DIM == head
        chances = head_chances(queries, keys, own, allowed).astype(LOW)
        total += dot(chances, jnp.where(own, values, jnp.zeros_like(values)), 1, 0)
    o_ref[...] = total.astype(LOW)


def attend_forward(first, mine, theirs, bias):
    length, width = mine.shape
    width //= 3
    steps = width // 128
    parts = [
        pl.BlockSpec((length, 128), functools.partial(lambda p, i, t: (0, p * steps + i), p))
        for p in range(3)
    ]
    lines = [
        pl.BlockSpec((1, 128), functools.partial(lambda p, i, t: (0, p * steps + i), p))
        for p in range(3)
    ]
    return pl.pallas_call(
        attend_forward_kernel,
        grid_spec=pltpu.PrefetchScalarGridSpec(
            num_scalar_prefetch=1,
            grid=(steps,),
            in_specs=parts + parts + lines,
            out_specs=[parts[0]] * 4,
        ),
        out_shape=[jax.ShapeDtypeStruct((length, width), LOW)] * 4,
        compiler_params=limit(16),
        cost_estimate=pl.CostEstimate(
            flops=4 * length * length * width,
            bytes_accessed=32 * length * width,
            transcendentals=length * length * width // HEAD_DIM,
        ),
    )(first, mine, mine, mine, theirs, theirs, theirs, bias, bias, bias)


def attend_backward_kernel(first_ref, q_ref, k_ref, v_ref, g_ref, out_ref):
    queries, keys, values, grads = q_ref[...], k_ref[...], v_ref[...], g_ref[...]
    lane, allowed = attend_masks(first_ref[0], *queries.shape)
    dq = jnp.zeros(queries.shape, F32)
    dk = jnp.zeros(queries.shape, F32)
    dv = jnp.zeros(queries.shape, F32)
    for head in range(queries.shape[1] // HEAD_DIM):
        own = lane // HEAD_DIM == head
        chances = head_chances(queries, keys, own, allowed)
        head_grads = jnp.where(own, grads, jnp.zeros_like(grads))
        dv += dot(chances.astype(LOW), head_grads, 0, 0)
        chance_grads = dot(head_grads, values, 1, 1)
        inner = jnp.sum(chances * chance_grads, axis=-1, keepdims=True)
        score_grads = (chances * (chance_grads - inner)).astype(LOW)
        dq += dot(score_grads, jnp.where(own, keys, jnp.zeros_like(keys)), 1, 0)
        dk += dot(score_grads, jnp.where(own, queries, jnp.zeros_like(queries)), 0, 0)
    scale = HEAD_DIM**-0.5
    out_ref[0] = (dq * scale).astype(LOW)
    out_ref[1] = (dk * scale).astype(LOW)
    out_ref[2] = dv.astype(LOW)


def attend_backward(first, *operands):
    length, width = operands[0].shape
    block = pl.BlockSpec((length, 128), lambda i, t: (0, i))
    return pl.pallas_call(
        attend_backward_kernel,
        grid_spec=pltpu.PrefetchScalarGridSpec(
            num_scalar_prefetch=1,
            grid=(width // 128,),
            in_specs=[block] * 4,
            out_specs=pl.BlockSpec((3, length, 128), lambda i, t: (0, 0, i)),
        ),
        out_shape=jax.ShapeDtypeStruct((3, length, width), LOW),
        compiler_params=limit(16),
        cost_estimate=pl.CostEstimate(
            flops=10 * length * length * width,
            bytes_accessed=14 * length * width,
            transcendentals=length * length * width // HEAD_DIM,
        ),
    )(first, *operands)


def place_kernel(high, table_ref, *refs):
    count = len(refs) - 4
    pieces, out_ref, held, sems = refs[:count], refs[-3], refs[-2], refs[-1]
    slots, broad = held.shape[0], held.shape[2]

    def copy(step):
        row = pl.multiple_of(table_ref[2 * step] * high, high)
        column = pl.multiple_of(table_ref[2 * step + 1] * broad, broad)
        return pltpu.make_async_copy(
            held.at[step % slots],
            out_ref.at[pl.ds(row, high), pl.ds(column, broad)],
            sems.at[step % slots],
        )

    step = 0
    for piece in pieces:
        for i in range(piece.shape[0] // high):
            for j in range(piece.shape[1] // broad):
                if step >= slots:
                    copy(step - slots).wait()
                part = piece[i * high : (i + 1) * high, j * broad : (j + 1) * broad]
                held[step % slots] = part.astype(F32)
                copy(step).start()
                step += 1
    for waited in range(max(step - slots, 0), step):
        copy(waited).wait()


def place(pieces, whole, places, high, broad):
    slots = 4
    vmem = pl.BlockSpec(memory_space=pltpu.VMEM)
    return pl.pallas_call(
        functools.partial(place_kernel, high),
        in_specs=[pl.BlockSpec(memory_space=pltpu.SMEM)]
        + [vmem] * len(pieces)
        + [pl.BlockSpec(memory_space=pl.ANY)],
        out_specs=pl.BlockSpec(memory_space=pl.ANY),
        out_shape=jax.ShapeDtypeStruct(whole.shape, F32),
        scratch_shapes=[
            pltpu.VMEM((slots, high, broad), F32),
            pltpu.SemaphoreType.DMA((slots,)),
        ],
        input_output_aliases={len(pieces) + 1: 0},
        compiler_params=limit(32),
        cost_estimate=pl.CostEstimate(
            flops=0, bytes_accessed=sum(6 * p.size for p in pieces), transcendentals=0
        ),
    )(jnp.stack(places).astype(jnp.int32), *pieces, whole)


def blank_kernel(out_ref):
    pass


def blank(shape):
    return pl.pallas_call(
        blank_kernel,
        out_specs=pl.BlockSpec(memory_space=pl.ANY),
        out_shape=jax.ShapeDtypeStruct(shape, F32),
    )()


class Lane:
    def __init__(self):
        self.last = None

    def send(self, sends, after=()):
        if self.last is not None:
            held = lax.optimization_barrier(([v for v, _ in sends], self.last, after))
            sends = [(v, m) for v, (_, m) in zip(held[0], sends)]
        results = [lax.ppermute(v, "dp", m) for v, m in sends]
        self.last = results
        return results


def per_device(
    hidden,
    cotangent,
    exit_layers,
    qkv_weight,
    out_weight,
    up_weight,
    down_weight,
    query_bias,
    value_bias,
    out_bias,
    up_bias,
    down_bias,
    attn_gain,
    attn_shift,
    ffn_gain,
    ffn_shift,
):
    core = lax.axis_index("sp")
    other = 1 - core
    chips = lax.axis_size("dp")
    plane = chips // LINE
    chip = lax.axis_index("dp")
    spot = chip % GROUP
    level = chip // plane
    rows = hidden.shape[1]
    width = hidden.shape[2]
    length = 2 * rows
    half = width // 2
    inner = up_weight.shape[1]
    inner_half = inner // 2
    across, first_hop, middle_hop, last_hop = Lane(), Lane(), Lane(), Lane()

    def swap(value):
        return lax.ppermute(value, "sp", [(0, 1), (1, 0)])

    def in_plane(distance):
        return [(i, i // plane * plane + ((i % plane) ^ distance)) for i in range(chips)]

    def along(*moves):
        return [(a * plane + i, b * plane + i) for a, b in moves for i in range(plane)]

    inward, middle_moves, outward = (
        along((0, 1), (3, 2)),
        along((1, 2), (2, 1)),
        along((1, 0), (2, 3)),
    )

    def split(value, axis, size):
        return (
            lax.dynamic_slice_in_dim(value, core * size, size, axis),
            lax.dynamic_slice_in_dim(value, other * size, size, axis),
        )

    def in_order(mine, theirs, axis):
        return jnp.where(
            core == 0,
            jnp.concatenate([mine, theirs], axis),
            jnp.concatenate([theirs, mine], axis),
        )

    def gather_group(value):
        return [value] + across.send([(value, in_plane(d)) for d in range(1, GROUP)])

    def scatter_group(value, axis, size):
        blocks = [
            lax.dynamic_slice_in_dim(value, (spot ^ d) * size, size, axis) for d in range(GROUP)
        ]
        return blocks[:1] + across.send([(blocks[d], in_plane(d)) for d in range(1, GROUP)])

    def both(mine):
        mine = jnp.concatenate(mine)
        theirs = swap(mine)
        pair = [v.reshape(GROUP, 1, rows, -1) for v in (mine, theirs)]
        return jnp.concatenate(pair, 1).reshape(GROUP * length, -1)

    def turn(value):
        return value.reshape(-1, 2, rows, value.shape[-1])[:, ::-1].reshape(value.shape)

    end = (level == 0) | (level == LINE - 1)

    def line_sum(value):
        value = value + first_hop.send([(value, inward)])[0]
        value = value + middle_hop.send([(value, middle_moves)])[0]
        value = jnp.where(end, last_hop.send([(value, outward)])[0], value)
        distance = GROUP
        while distance < plane:
            value = value + lax.ppermute(value, "dp", in_plane(distance))
            distance *= 2
        return value

    def spread(value, after):
        size = value.shape[0] // 2
        first, second = across.send([(value, in_plane(1)), (value, in_plane(2))], after)
        upper, lower = across.send([(first[:size], in_plane(2)), (second[size:], in_plane(1))])
        return [value, first, second, upper, lower]

    def table(size, start, count=None):
        return jnp.arange(size if count is None else count, dtype=jnp.int32) + start

    inputs = hidden[0].astype(F32)
    active = active_rows(exit_layers[0], core * rows, rows, length)
    first_row = (core * rows).astype(jnp.int32)[None]
    grad_output = cotangent[0].astype(F32)
    down_grad = (active * grad_output).astype(LOW)
    down_grad_all = jnp.concatenate([down_grad, swap(down_grad)])

    core_number = core.astype(jnp.int32)[None]
    mine, theirs = norm(
        norm_one_kernel, core_number, rows, width, 0,
        hidden[0], attn_gain[None], attn_shift[None],
    )
    normed_one_half = jnp.concatenate([mine, swap(theirs)])
    down_mine = gather_group(down_grad)
    qkv_left = gather_group(normed_one_half)
    block = min(512, half)
    count = half // block

    def qkv_table(c):
        return jnp.concatenate([table(count, (2 * p + c) * count) for p in range(3)])

    theirs = times_columns(normed_one_half, qkv_weight, qkv_table(other), block)
    theirs = swap(theirs)
    mine = times_columns(normed_one_half, qkv_weight, qkv_table(core), block)
    bias = jnp.stack([query_bias, jnp.zeros_like(query_bias), value_bias])
    bias = lax.dynamic_slice_in_dim(bias, core * half, half, 1).reshape(1, -1)
    queries, keys, values, attended = attend_forward(first_row, mine, theirs, bias)
    attended, down_mine = lax.optimization_barrier((attended, down_mine))
    out_part = dot(attended, out_weight, 1, 0)
    middle, mine, theirs = norm(
        norm_two_kernel, core_number, rows, width, 1,
        hidden[0], active, out_part, swap(out_part[rows:]),
        out_bias[None], ffn_gain[None], ffn_shift[None],
    )
    normed_two_half = jnp.concatenate([mine, swap(theirs)])
    count = inner_half // block
    theirs = times_columns(normed_two_half, up_weight, table(count, other * count), block)
    theirs = swap(theirs)
    mine = times_columns(normed_two_half, up_weight, table(count, core * count), block)
    bias = lax.dynamic_slice_in_dim(up_bias, core * inner_half, inner_half).reshape(1, -1)
    mine, qkv_left = lax.optimization_barrier((mine, qkv_left))
    inner_low, up_grad, up_sums = inner_layer(
        down_grad_all, down_weight, mine, theirs, bias, block
    )
    down_left = scatter_group(inner_low, 1, inner_half // GROUP)
    up_right = scatter_group(up_grad, 1, inner_half // GROUP)
    up_left = gather_group(normed_two_half)
    out_left = gather_group(attended)
    block = min(1024, inner_half)
    count = inner_half // block
    up_grad_theirs = swap(up_grad)
    part = times_back(up_grad, up_weight, table(count, core * count), block, 512)
    part = times_back(
        up_grad_theirs, up_weight, table(count, other * count), block, 512, part, True
    )
    normed_two_grad = in_order(part[:rows], swap(part[rows:]), 1)
    _, norm_two_back = jax.vjp(layer_norm, middle, ffn_gain, ffn_shift)
    middle_part, gain_two_grad, shift_two_grad = norm_two_back(normed_two_grad)
    middle_grad = grad_output + middle_part
    attn_grad = (active * middle_grad).astype(LOW)
    attn_grad_all = jnp.concatenate([attn_grad, swap(attn_grad)])
    out_right = scatter_group(attn_grad, 1, width // GROUP)
    head_grads = dot(attn_grad_all, out_weight, 1, 1).astype(LOW)
    qkv_grad = attend_backward(first_row, queries, keys, values, head_grads)
    qkv_right = scatter_group(qkv_grad, 2, half // GROUP)
    flat = jnp.concatenate([qkv_grad[0], qkv_grad[1], qkv_grad[2]], 1)
    flat_theirs = swap(flat)
    block = min(1024, half)
    count = half // block

    def qkv_table(c):
        return jnp.concatenate([table(count, (2 * p + c) * count) for p in range(3)])

    inner_low, flat_theirs = lax.optimization_barrier((inner_low, flat_theirs))
    down_part = dot(inner_low, down_weight, 1, 0)
    output = middle + active * (down_part[:rows] + swap(down_part[rows:]) + down_bias)
    part = times_back(flat, qkv_weight, qkv_table(core), block, 512)
    part = times_back(flat_theirs, qkv_weight, qkv_table(other), block, 512, part, True)
    normed_one_grad = in_order(part[:rows], swap(part[rows:]), 1)
    _, norm_one_back = jax.vjp(layer_norm, inputs, attn_gain, attn_shift)
    input_part, gain_one_grad, shift_one_grad = norm_one_back(normed_one_grad)
    input_grad = (middle_grad + input_part).astype(LOW)

    chunks = []
    down_right = both(down_mine)
    down_left = jnp.concatenate(down_left)
    size = inner_half // GROUP
    first = 0
    for cut in (width // 4, width // 4, width // 2):
        chunks.append(("down", down_left, down_right[:, first : first + cut], first // cut))
        first += cut
    up_left = jnp.concatenate(up_left)
    up_right = jnp.concatenate(up_right)
    chunks.append(("up", up_left, up_right, core))
    chunks.append(("up", up_left, turn(swap(up_right)), other))
    chunks.append(("out", jnp.concatenate(out_left), both(out_right), 0))
    qkv_left = jnp.concatenate(qkv_left)
    qkv_right = jnp.concatenate(
        [jnp.concatenate([r[0], r[1], r[2]], 1) for r in qkv_right]
    )
    chunks.append(("qkv", qkv_left, qkv_right, core))
    chunks.append(("qkv", qkv_left, turn(swap(qkv_right)), other))

    shapes = {
        "down": (inner_half, width),
        "up": (half, inner),
        "out": (half, width),
        "qkv": (half, 3 * width),
    }
    wholes = {name: blank(shape) for name, shape in shapes.items()}
    sums = [line_sum(dot(left, right, 0, 0).astype(LOW)) for _, left, right, _ in chunks]
    done = [()] * 2
    for (name, _, _, where), total in zip(chunks, sums):
        pieces = spread(total, done[-2])
        tall, wide = total.shape
        high = min(256, tall)
        broad = wide // 3 if name == "qkv" else wide
        places = []
        for d in range(GROUP):
            owner = spot ^ d
            for i in range(tall // high):
                row = jnp.int32(i)
                if name == "down":
                    row, columns = owner * (tall // high) + i, [jnp.int32(where)]
                elif name == "up":
                    columns = [where * GROUP + owner]
                elif name == "out":
                    columns = [owner]
                else:
                    columns = [(2 * p + where) * GROUP + owner for p in range(3)]
                for column in columns:
                    places += [row, column]
        wholes[name] = place(pieces, wholes[name], places, high, broad)
        done.append(wholes[name])

    def widen(value):
        return in_order(value, jnp.zeros_like(value), 0)

    qkv_sums = jnp.sum(qkv_grad.astype(F32), axis=1)
    small = jnp.concatenate(
        [
            widen(qkv_sums[0]),
            widen(qkv_sums[2]),
            jnp.sum(attn_grad.astype(F32), axis=0),
            widen(up_sums[0]),
            jnp.sum(down_grad.astype(F32), axis=0),
            gain_one_grad,
            shift_one_grad,
            gain_two_grad,
            shift_two_grad,
        ]
    ).reshape(-1, 128)
    small = small + swap(small)
    distance = 1
    while distance < plane:
        small = small + lax.ppermute(small, "dp", in_plane(distance))
        distance *= 2
    small = small + lax.ppermute(small, "dp", inward)
    small = small + lax.ppermute(small, "dp", middle_moves)
    small = jnp.where(end, lax.ppermute(small, "dp", outward), small).reshape(-1)
    small_grads = []
    first = 0
    for size in (width, width, width, inner, width, width, width, width, width):
        small_grads.append(small[first : first + size])
        first += size

    return (
        output.astype(LOW)[None],
        input_grad[None],
        wholes["qkv"],
        wholes["out"],
        wholes["up"],
        wholes["down"],
        *small_grads,
    )


def solution(mesh):
    return jax.shard_map(
        per_device,
        mesh=mesh,
        in_specs=(
            P("dp", "sp", None),
            P("dp", "sp", None),
            P("dp", None),
            P("sp", None),
            P("sp", None),
            P("sp", None),
            P("sp", None),
            P(),
            P(),
            P(),
            P(),
            P(),
            P(),
            P(),
            P(),
            P(),
        ),
        out_specs=(
            P("dp", "sp", None),
            P("dp", "sp", None),
            P("sp", None),
            P("sp", None),
            P("sp", None),
            P("sp", None),
            P(),
            P(),
            P(),
            P(),
            P(),
            P(),
            P(),
            P(),
            P(),
        ),
        check_vma=False,
    )
```

time: 2240 us -> 771 us (0.34)
  waiting for transfers between devices: 1870 us -> 293 us
  matrix products: 192 us -> 39.3 us
  Pallas kernels: 0 us -> 150 us
  starting transfers between devices: 4.46 us -> 142 us
  blocking collectives: 28.1 us -> 0 us
    reduce_scatter x7 -> x0, waiting for transfers between devices: 1100 us -> none  [the longest x1 354 us: per_device(): lax.psum_scatter(up_term, 'dp', scatter_dimension=0, tiled=True)]
    all_gather x8 -> x0, waiting for transfers between devices: 648 us -> none  [the longest x1 178 us: per_device(): lax.all_gather(shares[3].astype(jnp.bfloat16), 'dp', axis=0, tiled=True)]
    ppermute x0 -> x102, waiting for transfers between devices: none -> 293 us  [the longest x80 242 us: send(): results = [lax.ppermute(v, 'dp', m) for v, m in sends]]
    dot_general x18 -> x11, matrix products: 192 us -> 39.3 us  [dot(): lax.dot_general(left, right, (((left_dim,), (right_dim,)), ((), ())), pre...]
    pallas_call x0 -> x25, Pallas kernels: none -> 150 us  [the longest x8 56.7 us: place(): pl.pallas_call(functools.partial(place_kernel, high), in_specs=[pl.BlockS...]
    ppermute x0 -> x102, starting transfers between devices: none -> 142 us  [the longest x80 130 us: send(): results = [lax.ppermute(v, 'dp', m) for v, m in sends]]
    psum x1 -> x0, waiting for transfers between devices: 112 us -> none  [per_device(): lax.psum((qkv_columns[0], qkv_columns[2], jnp.sum(attn_grad_low.astype(jn...]
    convert_element_type x6 -> x2, other arithmetic: 60.7 us -> 1.41 us  [active_rows(): return (exit_layer > LAYER).astype(F32)[:, None]]
  transfers between devices with their start and end apart: 18 -> 102, of which waited for: 15 -> 40; matrix products, arithmetic and copies ran while one was open for 11% -> 19% of each run, Pallas kernels for 0% -> 16%
where the time goes in v1:
time: 771 us; the launch traced here: 760 us
  waiting for transfers between devices  293 us (38%)
  Pallas kernels  150 us (19%)
  starting transfers between devices  142 us (18%)
  other arithmetic  74.5 us (10%)
  local copies, waits for them, and re-layouts  57 us (7%)
  matrix products  39.3 us (5%)
    ppermute x80, waiting for transfers between devices, send(): results = [lax.ppermute(v, 'dp', m) for v, m in sends]  242 us
    ppermute x80, starting transfers between devices, send(): results = [lax.ppermute(v, 'dp', m) for v, m in sends]  130 us
    pallas_call x8, Pallas kernels, place(): pl.pallas_call(functools.partial(place_kernel, high), in_specs=[pl.BlockS...  56.7 us
    dot_general x11, matrix products, dot(): lax.dot_general(left, right, (((left_dim,), (right_dim,)), ((), ())), pre...  39.3 us
    ppermute x2, waiting for transfers between devices, per_device(): small = small + lax.ppermute(small, 'dp', in_plane(distance))  37 us
    pallas_call x4, Pallas kernels, times_back(): pl.pallas_call(functools.partial(back_kernel, turned), grid_spec=pltpu.Pr...  32.6 us
    unnamed x259, local copies, waits for them, and re-layouts  31.9 us
    pallas_call x4, Pallas kernels, times_columns(): pl.pallas_call(columns_kernel, grid_spec=pltpu.PrefetchScalarGridSpec(num...  31.5 us
  transfers between devices with their start and end apart: 102, of which 40 were waited for; matrix products, arithmetic and copies ran while one was open for 19% of the time, Pallas kernels for 16%

profile of v1, /device:TPU:0, one launch (start us, length us, event | category | flops | bytes accessed | tf_op | source)
XLA Modules:
  0.0 760.4 jit_solution(154781023619353319)
XLA Ops:
  36.3 10.2 %collective-permute-done.3 = bf16[128,2048]{1,0:T(8,128)(2,1)} collective-permute-done((bf16[128,2048]{1,0:T(8,128)(2,1)}, bf16[128,2048]{1,0:T(8,128)(2,1)}, u32[]{:S(2)}, u32[]{:S(2)}) %collective-permute-start.3) | collective-permute-done | bytes 524320 | tf_op jit(solution)/shard_map/ppermute | solution.py:398
  53.6 9.5 %shard_map.277 = f32[256,4096]{1,0:T(8,128)} custom-call(s32[8]{0:T(128)S(1)} %iota_add_fusion.3.table_ref, bf16[256,1024]{1,0:T(8,128)(2,1)S(1)} %get-tuple-element.143.left_ref, bf16[1024,8192]{1,0:T(8,128)(2,1)} %weight_ref.15), custom_call_target="tpu_custom_call" | custom-call | flops 2147483648 | bytes 13107200 | tf_op jit(solution)/shard_map/pallas_call | solution.py:114
  87.0 9.1 %collective-permute-done.9 = bf16[256,1024]{1,0:T(8,128)(2,1)S(1)} collective-permute-done((bf16[256,1024]{1,0:T(8,128)(2,1)S(1)}, bf16[256,1024]{1,0:T(8,128)(2,1)S(1)}, u32[]{:S(2)}, u32[]{:S(2)}) %collective-permute-start.9) | collective-permute-done | bytes 524320 | tf_op jit(solution)/shard_map/ppermute | solution.py:398
  98.5 12.4 %shard_map.278 = (bf16[256,4096]{1,0:T(8,128)(2,1)S(1)}, bf16[256,4096]{1,0:T(8,128)(2,1)S(1)}, f32[1,4096]{1,0:T(1,128)S(1)}) custom-call(bf16[256,2048]{1,0:T(8,128)(2,1)S(1)} %pad_maximum_fusion.4.grad_ref, bf16[4096,2048]{1,0:T(8,128)(2,1)} %weight_ref.13, f32[256,4096]{1,0:T(8,128)S(1)} %shard_map.276.mine_ref, ...), custom_call_target="tpu_custom_call" | custom-call | flops 4294967296 | bytes 30408704 | tf_op jit(solution)/shard_map/pallas_call | solution.py:195
  127.1 10.1 %collective-permute-done.19 = bf16[256,1024]{1,0:T(8,128)(2,1)S(1)} collective-permute-done((bf16[256,1024]{1,0:T(8,128)(2,1)S(1)}, bf16[256,1024]{1,0:T(8,128)(2,1)S(1)}, u32[]{:S(2)}, u32[]{:S(2)}) %collective-permute-start.19) | collective-permute-done | bytes 524320 | tf_op jit(solution)/shard_map/ppermute | solution.py:398
  152.3 11.4 %collective-permute-done.40 = bf16[1024,512]{1,0:T(8,128)(2,1)} collective-permute-done((bf16[1024,512]{1,0:T(8,128)(2,1)}, bf16[1024,512]{1,0:T(8,128)(2,1)}, u32[]{:S(2)}, u32[]{:S(2)}) %collective-permute-start.40) | collective-permute-done | bytes 1048608 | tf_op jit(solution)/shard_map/ppermute | solution.py:398
  169.5 9.0 %shard_map.279.rest_0_ = f32[256,1024]{1,0:T(8,128)S(1)} custom-call(s32[4]{0:T(128)S(1)} %iota_add_fusion.1.table_ref, bf16[256,4096]{1,0:T(8,128)(2,1)S(1)} %get-tuple-element.128.left_ref, bf16[1024,8192]{1,0:T(8,128)(2,1)} %weight_ref.15), custom_call_target="tpu_custom_call" | custom-call | flops 2147483648 | bytes 12582912 | tf_op jit(solution)/shard_map/pallas_call | solution.py:164
  187.2 9.3 %shard_map.280 = f32[256,1024]{1,0:T(8,128)S(1)} custom-call(s32[4]{0:T(128)S(1)} %iota_add_fusion.2.table_ref, bf16[256,4096]{1,0:T(8,128)(2,1)} %collective-permute-done.12.left_ref, bf16[1024,8192]{1,0:T(8,128)(2,1)} %weight_ref.15, f32[256,1024]{1,0:T(8,128)S(1)} %shard_map.279.rest_0_), custom_call_target="tpu_custom_call" | custom-call | flops 2147483648 | bytes 12582912 | tf_op jit(solution)/shard_map/pallas_call | solution.py:164
  214.3 27.2 %collective-permute-done.42 = bf16[1024,1024]{1,0:T(8,128)(2,1)S(1)} collective-permute-done((bf16[1024,1024]{1,0:T(8,128)(2,1)S(1)}, bf16[1024,1024]{1,0:T(8,128)(2,1)S(1)}, u32[]{:S(2)}, u32[]{:S(2)}) %collective-permute-start.42) | collective-permute-done | bytes 2097184 | tf_op jit(solution)/shard_map/ppermute | solution.py:398
  255.8 9.8 %shard_map.281 = bf16[3,256,1024]{2,1,0:T(8,128)(2,1)S(1)} custom-call(s32[1]{0:T(128)} %bitcast.4.first_ref, bf16[256,1024]{1,0:T(8,128)(2,1)S(1)} %copy-done.40, bf16[256,1024]{1,0:T(8,128)(2,1)S(1)} %copy-done.42, bf16[256,1024]{1,0:T(8,128)(2,1)S(1)} %copy-done.44, bf16[256,1024]{1,0:T(8,128)(2,1)S(1)} %convolution_convert_fusion.6.g_ref), custom_call_target="tpu_custom_call" | custom-call | flops 671088640 | bytes 3670016 | tf_op jit(solution)/shard_map/pallas_call | solution.py:310
  291.7 11.9 %collective-permute-done.57 = bf16[1024,512]{1,0:T(8,128)(2,1)S(1)} collective-permute-done((bf16[1024,512]{1,0:T(8,128)(2,1)S(1)}, bf16[1024,512]{1,0:T(8,128)(2,1)S(1)}, u32[]{:S(2)}, u32[]{:S(2)}) %collective-permute-start.57) | collective-permute-done | bytes 1048608 | tf_op jit(solution)/shard_map/ppermute | solution.py:398
  316.5 10.2 %collective-permute-done.66.refs_3_ = bf16[512,512]{1,0:T(8,128)(2,1)S(1)} collective-permute-done((bf16[512,512]{1,0:T(8,128)(2,1)S(1)}, bf16[512,512]{1,0:T(8,128)(2,1)S(1)}, u32[]{:S(2)}, u32[]{:S(2)}) %collective-permute-start.66) | collective-permute-done | bytes 524320 | tf_op jit(solution)/shard_map/ppermute | solution.py:398
  345.3 12.6 %collective-permute-start.44 = (bf16[1024,1024]{1,0:T(8,128)(2,1)}, bf16[1024,1024]{1,0:T(8,128)(2,1)}, u32[]{:S(2)}, u32[]{:S(2)}) collective-permute-start(bf16[1024,1024]{1,0:T(8,128)(2,1)} %convolution_convert_fusion.1), channel_id=1, source_target_pairs={{0,4},{1,5},{2,6},{3,7},{12,8},{13,9},{14,10},{15,11},{16,20},{17,... | collective-permute-start | bytes 6291464 | tf_op jit(solution)/shard_map/ppermute | solution.py:398
  383.7 14.7 %collective-permute-done.44 = bf16[1024,1024]{1,0:T(8,128)(2,1)} collective-permute-done((bf16[1024,1024]{1,0:T(8,128)(2,1)}, bf16[1024,1024]{1,0:T(8,128)(2,1)}, u32[]{:S(2)}, u32[]{:S(2)}) %collective-permute-start.44) | collective-permute-done | bytes 2097184 | tf_op jit(solution)/shard_map/ppermute | solution.py:398
  405.1 15.5 %collective-permute-done.72.refs_1_ = bf16[1024,1024]{1,0:T(8,128)(2,1)S(1)} collective-permute-done((bf16[1024,1024]{1,0:T(8,128)(2,1)S(1)}, bf16[1024,1024]{1,0:T(8,128)(2,1)S(1)}, u32[]{:S(2)}, u32[]{:S(2)}) %collective-permute-start.72) | collective-permute-done | bytes 2097184 | tf_op jit(solution)/shard_map/ppermute | solution.py:398
  463.1 10.9 %maximum_maximum_fusion = bf16[1024,768]{1,0:T(8,128)(2,1)S(1)} fusion(bf16[256,256]{1,0:T(8,128)(2,1)S(1)} %get-tuple-element.257, bf16[256,256]{1,0:T(8,128)(2,1)S(1)} %get-tuple-element.258, bf16[256,256]{1,0:T(8,128)(2,1)S(1)} %get-tuple-element.256, bf16[256,256]{1,0:T(8,128)(2,1)S(1)} %get-tuple-element.254, ...), kind=kLoop, calls=%fused_computation.23 | loop fusion | flops 18874368 | bytes 3145728 | tf_op jit(solution)/shard_map/concatenate | solution.py:600
  474.0 16.5 %collective-permute-done.76.refs_1_ = bf16[1024,1024]{1,0:T(8,128)(2,1)S(1)} collective-permute-done((bf16[1024,1024]{1,0:T(8,128)(2,1)S(1)}, bf16[1024,1024]{1,0:T(8,128)(2,1)S(1)}, u32[]{:S(2)}, u32[]{:S(2)}) %collective-permute-start.76) | collective-permute-done | bytes 2097184 | tf_op jit(solution)/shard_map/ppermute | solution.py:398
  545.3 10.8 %collective-permute-done.80.refs_1_ = bf16[1024,1024]{1,0:T(8,128)(2,1)} collective-permute-done((bf16[1024,1024]{1,0:T(8,128)(2,1)}, bf16[1024,1024]{1,0:T(8,128)(2,1)}, u32[]{:S(2)}, u32[]{:S(2)}) %collective-permute-start.80) | collective-permute-done | bytes 2097184 | tf_op jit(solution)/shard_map/ppermute | solution.py:398
  613.8 9.5 %shard_map.290 = f32[1024,8192]{1,0:T(8,128)} custom-call(s32[32]{0:T(128)S(1)} %stack.147.table_ref, bf16[1024,1024]{1,0:T(8,128)(2,1)} %broadcast_select_fusion.2.refs_0_, bf16[1024,1024]{1,0:T(8,128)(2,1)} %collective-permute-done.80.refs_1_, bf16[1024,1024]{1,0:T(8,128)(2,1)} %collective-permute-done.81.refs_2_, ...), custom_call_target="tpu_custom_call", output_to_operand_aliasing={{}: (6, {})} | custom-call | bytes 25165824 | tf_op jit(solution)/shard_map/pallas_call | solution.py:359
  634.2 23.8 %collective-permute-done.88.refs_1_ = bf16[1024,768]{1,0:T(8,128)(2,1)S(1)} collective-permute-done((bf16[1024,768]{1,0:T(8,128)(2,1)S(1)}, bf16[1024,768]{1,0:T(8,128)(2,1)S(1)}, u32[]{:S(2)}, u32[]{:S(2)}) %collective-permute-start.88) | collective-permute-done | bytes 1572896 | tf_op jit(solution)/shard_map/ppermute | solution.py:398
  665.9 11.3 %collective-permute-done.90.refs_3_ = bf16[512,768]{1,0:T(8,128)(2,1)S(1)} collective-permute-done((bf16[512,768]{1,0:T(8,128)(2,1)S(1)}, bf16[512,768]{1,0:T(8,128)(2,1)S(1)}, u32[]{:S(2)}, u32[]{:S(2)}) %collective-permute-start.90) | collective-permute-done | bytes 786464 | tf_op jit(solution)/shard_map/ppermute | solution.py:398
  681.2 33.4 %collective-permute-done.97 = f32[192,128]{1,0:T(8,128)S(1)} collective-permute-done((f32[192,128]{1,0:T(8,128)S(1)}, f32[192,128]{1,0:T(8,128)S(1)}, u32[]{:S(2)}, u32[]{:S(2)}) %collective-permute-start.97) | collective-permute-done | bytes 98336 | tf_op jit(solution)/shard_map/ppermute | solution.py:658
  741.0 9.5 %shard_map.294.refs_5_ = f32[1024,6144]{1,0:T(8,128)} custom-call(s32[96]{0:T(128)S(1)} %stack.161.table_ref, bf16[1024,768]{1,0:T(8,128)(2,1)S(1)} %broadcast_select_fusion.3.refs_0_, bf16[1024,768]{1,0:T(8,128)(2,1)S(1)} %collective-permute-done.88.refs_1_, bf16[1024,768]{1,0:T(8,128)(2,1)S(1)} %collective-permute-done.89.refs_2_, ...), custom_call_target="tpu_custom_call", output_to_operand_aliasing={{}: (6, {})} | custom-call | bytes 18874368 | tf_op jit(solution)/shard_map/pallas_call | solution.py:359
  750.5 9.5 %shard_map.295 = f32[1024,6144]{1,0:T(8,128)} custom-call(s32[96]{0:T(128)S(1)} %stack.123.table_ref, bf16[1024,768]{1,0:T(8,128)(2,1)S(1)} %broadcast_select_fusion.4.refs_0_, bf16[1024,768]{1,0:T(8,128)(2,1)S(1)} %collective-permute-done.92.refs_1_, bf16[1024,768]{1,0:T(8,128)(2,1)S(1)} %collective-permute-done.93.refs_2_, ...), custom_call_target="tpu_custom_call", output_to_operand_aliasing={{}: (6, {})} | custom-call | bytes 18874368 | tf_op jit(solution)/shard_map/pallas_call | solution.py:359
  (600 shorter events, 437.9 us)
Async XLA Ops:
  70.8 45.0 %collective-permute-start.39 = (bf16[512,2048]{1,0:T(8,128)(2,1)}, bf16[512,2048]{1,0:T(8,128)(2,1)}, u32[]{:S(2)}, u32[]{:S(2)}) collective-permute-start(bf16[512,2048]{1,0:T(8,128)(2,1)} %constant_dynamic-update-slice_fusion.13), channel_id=1, source_target_pairs={{0,16},{16,0},{1,17},{17,1},{2,18},{18,2},{3,19},{19,3},{4,20},{20... | collective-permute-start | bytes 6291464 | tf_op jit(solution)/shard_map/ppermute | solution.py:437
  118.4 68.1 %collective-permute-start.12 = (bf16[256,4096]{1,0:T(8,128)(2,1)S(1)}, bf16[256,4096]{1,0:T(8,128)(2,1)}, u32[]{:S(2)}, u32[]{:S(2)}) collective-permute-start(bf16[256,4096]{1,0:T(8,128)(2,1)S(1)} %get-tuple-element.128.left_ref), channel_id=1, source_target_pairs={{0,16},{16,0},{1,17},{17,1},{2,18},{18,2},{3,19},{19,3},{4,20},{20... | collective-permute-start | bytes 6291464 | tf_op jit(solution)/shard_map/ppermute | solution.py:437
  196.5 44.9 %collective-permute-start.42 = (bf16[1024,1024]{1,0:T(8,128)(2,1)S(1)}, bf16[1024,1024]{1,0:T(8,128)(2,1)S(1)}, u32[]{:S(2)}, u32[]{:S(2)}) collective-permute-start(bf16[1024,1024]{1,0:T(8,128)(2,1)S(1)} %fusion.10), channel_id=1, source_target_pairs={{0,4},{1,5},{2,6},{3,7},{12,8},{13,9},{14,10},{15,11},{16,20},{17,... | collective-permute-start | bytes 6291464 | tf_op jit(solution)/shard_map/ppermute | solution.py:398
  203.8 44.3 %collective-permute-start.27 = (bf16[256,1024]{1,0:T(8,128)(2,1)S(1)}, bf16[256,1024]{1,0:T(8,128)(2,1)}, u32[]{:S(2)}, u32[]{:S(2)}) collective-permute-start(bf16[256,1024]{1,0:T(8,128)(2,1)S(1)} %copy-done.52), channel_id=1, source_target_pairs={{0,1},{1,0},{2,3},{3,2},{4,5},{5,4},{6,7},{7,6},{8,9},{9,8},{10,11... | collective-permute-start | bytes 1572872 | tf_op jit(solution)/shard_map/ppermute | solution.py:398
  205.5 44.3 %collective-permute-start.28 = (bf16[256,1024]{1,0:T(8,128)(2,1)S(1)}, bf16[256,1024]{1,0:T(8,128)(2,1)}, u32[]{:S(2)}, u32[]{:S(2)}) collective-permute-start(bf16[256,1024]{1,0:T(8,128)(2,1)S(1)} %copy-done.52), channel_id=1, source_target_pairs={{0,2},{1,3},{2,0},{3,1},{4,6},{5,7},{6,4},{7,5},{8,10},{9,11},{10,... | collective-permute-start | bytes 1572872 | tf_op jit(solution)/shard_map/ppermute | solution.py:398
  246.2 41.7 %collective-permute-start.50 = (bf16[1024,1024]{1,0:T(8,128)(2,1)S(1)}, bf16[1024,1024]{1,0:T(8,128)(2,1)S(1)}, u32[]{:S(2)}, u32[]{:S(2)}) collective-permute-start(bf16[1024,1024]{1,0:T(8,128)(2,1)S(1)} %add.669), channel_id=1, source_target_pairs={{4,8},{5,9},{6,10},{7,11},{8,4},{9,5},{10,6},{11,7},{20,24},{21,25... | collective-permute-start | bytes 6291464 | tf_op jit(solution)/shard_map/ppermute | solution.py:398
  279.7 51.0 %collective-permute-start.43 = (bf16[1024,1024]{1,0:T(8,128)(2,1)S(1)}, bf16[1024,1024]{1,0:T(8,128)(2,1)S(1)}, u32[]{:S(2)}, u32[]{:S(2)}) collective-permute-start(bf16[1024,1024]{1,0:T(8,128)(2,1)S(1)} %convolution_convert_fusion), channel_id=1, source_target_pairs={{0,4},{1,5},{2,6},{3,7},{12,8},{13,9},{14,10},{15,11},{16,20},{17,... | collective-permute-start | bytes 6291464 | tf_op jit(solution)/shard_map/ppermute | solution.py:398
  287.0 47.9 %collective-permute-start.38 = (bf16[1024,1024]{1,0:T(8,128)(2,1)S(1)}, bf16[1024,1024]{1,0:T(8,128)(2,1)S(1)}, u32[]{:S(2)}, u32[]{:S(2)}) collective-permute-start(bf16[1024,1024]{1,0:T(8,128)(2,1)S(1)} %pad_maximum_fusion.1), channel_id=1, source_target_pairs={{0,16},{16,0},{1,17},{17,1},{2,18},{18,2},{3,19},{19,3},{4,20},{20... | collective-permute-start | bytes 6291464 | tf_op jit(solution)/shard_map/ppermute | solution.py:437
  303.6 71.5 %collective-permute-start.58 = (bf16[1024,1024]{1,0:T(8,128)(2,1)}, bf16[1024,1024]{1,0:T(8,128)(2,1)}, u32[]{:S(2)}, u32[]{:S(2)}) collective-permute-start(bf16[1024,1024]{1,0:T(8,128)(2,1)} %add.677), channel_id=1, source_target_pairs={{4,0},{5,1},{6,2},{7,3},{8,12},{9,13},{10,14},{11,15},{20,16},{21,... | collective-permute-start | bytes 6291464 | tf_op jit(solution)/shard_map/ppermute | solution.py:398
  333.0 45.0 %collective-permute-start.51 = (bf16[1024,1024]{1,0:T(8,128)(2,1)}, bf16[1024,1024]{1,0:T(8,128)(2,1)}, u32[]{:S(2)}, u32[]{:S(2)}) collective-permute-start(bf16[1024,1024]{1,0:T(8,128)(2,1)} %add.668), channel_id=1, source_target_pairs={{4,8},{5,9},{6,10},{7,11},{8,4},{9,5},{10,6},{11,7},{20,24},{21,25... | collective-permute-start | bytes 6291464 | tf_op jit(solution)/shard_map/ppermute | solution.py:398
  345.3 53.1 %collective-permute-start.44 = (bf16[1024,1024]{1,0:T(8,128)(2,1)}, bf16[1024,1024]{1,0:T(8,128)(2,1)}, u32[]{:S(2)}, u32[]{:S(2)}) collective-permute-start(bf16[1024,1024]{1,0:T(8,128)(2,1)} %convolution_convert_fusion.1), channel_id=1, source_target_pairs={{0,4},{1,5},{2,6},{3,7},{12,8},{13,9},{14,10},{15,11},{16,20},{17,... | collective-permute-start | bytes 6291464 | tf_op jit(solution)/shard_map/ppermute | solution.py:398
  377.0 43.5 %collective-permute-start.72 = (bf16[1024,1024]{1,0:T(8,128)(2,1)S(1)}, bf16[1024,1024]{1,0:T(8,128)(2,1)S(1)}, u32[]{:S(2)}, u32[]{:S(2)}) collective-permute-start(bf16[1024,1024]{1,0:T(8,128)(2,1)S(1)} %broadcast_select_fusion.refs_0_), channel_id=1, source_target_pairs={{0,1},{1,0},{2,3},{3,2},{4,5},{5,4},{6,7},{7,6},{8,9},{9,8},{10,11... | collective-permute-start | bytes 6291464 | tf_op jit(solution)/shard_map/ppermute | solution.py:398
  377.4 44.3 %collective-permute-start.73 = (bf16[1024,1024]{1,0:T(8,128)(2,1)S(1)}, bf16[1024,1024]{1,0:T(8,128)(2,1)S(1)}, u32[]{:S(2)}, u32[]{:S(2)}) collective-permute-start(bf16[1024,1024]{1,0:T(8,128)(2,1)S(1)} %broadcast_select_fusion.refs_0_), channel_id=1, source_target_pairs={{0,2},{1,3},{2,0},{3,1},{4,6},{5,7},{6,4},{7,5},{8,10},{9,11},{10,... | collective-permute-start | bytes 6291464 | tf_op jit(solution)/shard_map/ppermute | solution.py:398
  382.5 54.1 %collective-permute-start.59 = (bf16[1024,1024]{1,0:T(8,128)(2,1)}, bf16[1024,1024]{1,0:T(8,128)(2,1)}, u32[]{:S(2)}, u32[]{:S(2)}) collective-permute-start(bf16[1024,1024]{1,0:T(8,128)(2,1)} %add.676), channel_id=1, source_target_pairs={{4,0},{5,1},{6,2},{7,3},{8,12},{9,13},{10,14},{11,15},{20,16},{21,... | collective-permute-start | bytes 6291464 | tf_op jit(solution)/shard_map/ppermute | solution.py:398
  402.9 45.9 %collective-permute-start.52 = (bf16[1024,1024]{1,0:T(8,128)(2,1)}, bf16[1024,1024]{1,0:T(8,128)(2,1)}, u32[]{:S(2)}, u32[]{:S(2)}) collective-permute-start(bf16[1024,1024]{1,0:T(8,128)(2,1)} %add.667), channel_id=1, source_target_pairs={{4,8},{5,9},{6,10},{7,11},{8,4},{9,5},{10,6},{11,7},{20,24},{21,25... | collective-permute-start | bytes 6291464 | tf_op jit(solution)/shard_map/ppermute | solution.py:398
  447.0 43.6 %collective-permute-start.76 = (bf16[1024,1024]{1,0:T(8,128)(2,1)S(1)}, bf16[1024,1024]{1,0:T(8,128)(2,1)S(1)}, u32[]{:S(2)}, u32[]{:S(2)}) collective-permute-start(bf16[1024,1024]{1,0:T(8,128)(2,1)S(1)} %broadcast_select_fusion.1.refs_0_), channel_id=1, source_target_pairs={{0,1},{1,0},{2,3},{3,2},{4,5},{5,4},{6,7},{7,6},{8,9},{9,8},{10,11... | collective-permute-start | bytes 6291464 | tf_op jit(solution)/shard_map/ppermute | solution.py:398
  447.4 43.2 %collective-permute-start.77 = (bf16[1024,1024]{1,0:T(8,128)(2,1)S(1)}, bf16[1024,1024]{1,0:T(8,128)(2,1)S(1)}, u32[]{:S(2)}, u32[]{:S(2)}) collective-permute-start(bf16[1024,1024]{1,0:T(8,128)(2,1)S(1)} %broadcast_select_fusion.1.refs_0_), channel_id=1, source_target_pairs={{0,2},{1,3},{2,0},{3,1},{4,6},{5,7},{6,4},{7,5},{8,10},{9,11},{10,... | collective-permute-start | bytes 6291464 | tf_op jit(solution)/shard_map/ppermute | solution.py:398
  452.6 57.6 %collective-permute-start.60 = (bf16[1024,1024]{1,0:T(8,128)(2,1)S(1)}, bf16[1024,1024]{1,0:T(8,128)(2,1)S(1)}, u32[]{:S(2)}, u32[]{:S(2)}) collective-permute-start(bf16[1024,1024]{1,0:T(8,128)(2,1)S(1)} %add.675), channel_id=1, source_target_pairs={{4,0},{5,1},{6,2},{7,3},{8,12},{9,13},{10,14},{11,15},{20,16},{21,... | collective-permute-start | bytes 6291464 | tf_op jit(solution)/shard_map/ppermute | solution.py:398
  474.0 46.2 %collective-permute-start.36 = (bf16[1024,768]{1,0:T(8,128)(2,1)S(1)}, bf16[1024,768]{1,0:T(8,128)(2,1)S(1)}, u32[]{:S(2)}, u32[]{:S(2)}) collective-permute-start(bf16[1024,768]{1,0:T(8,128)(2,1)S(1)} %maximum_maximum_fusion), channel_id=1, source_target_pairs={{0,16},{16,0},{1,17},{17,1},{2,18},{18,2},{3,19},{19,3},{4,20},{20... | collective-permute-start | bytes 4718600 | tf_op jit(solution)/shard_map/ppermute | solution.py:437
  516.4 42.1 %collective-permute-start.81 = (bf16[1024,1024]{1,0:T(8,128)(2,1)}, bf16[1024,1024]{1,0:T(8,128)(2,1)}, u32[]{:S(2)}, u32[]{:S(2)}) collective-permute-start(bf16[1024,1024]{1,0:T(8,128)(2,1)} %broadcast_select_fusion.2.refs_0_), channel_id=1, source_target_pairs={{0,2},{1,3},{2,0},{3,1},{4,6},{5,7},{6,4},{7,5},{8,10},{9,11},{10,... | collective-permute-start | bytes 6291464 | tf_op jit(solution)/shard_map/ppermute | solution.py:398
  612.1 49.2 %collective-permute-start.63 = (bf16[1024,768]{1,0:T(8,128)(2,1)S(1)}, bf16[1024,768]{1,0:T(8,128)(2,1)S(1)}, u32[]{:S(2)}, u32[]{:S(2)}) collective-permute-start(bf16[1024,768]{1,0:T(8,128)(2,1)S(1)} %add.672), channel_id=1, source_target_pairs={{4,0},{5,1},{6,2},{7,3},{8,12},{9,13},{10,14},{11,15},{20,16},{21,... | collective-permute-start | bytes 4718600 | tf_op jit(solution)/shard_map/ppermute | solution.py:398
  633.1 99.8 %collective-permute-start.16 = (f32[128,2048]{1,0:T(8,128)S(1)}, f32[128,2048]{1,0:T(8,128)S(1)}, u32[]{:S(2)}, u32[]{:S(2)}) collective-permute-start(f32[128,2048]{1,0:T(8,128)S(1)} %slice.262), channel_id=1, source_target_pairs={{0,16},{16,0},{1,17},{17,1},{2,18},{18,2},{3,19},{19,3},{4,20},{20... | collective-permute-start | bytes 3145736 | tf_op jit(solution)/shard_map/ppermute | solution.py:437
  678.7 51.6 %collective-permute-start.92 = (bf16[1024,768]{1,0:T(8,128)(2,1)S(1)}, bf16[1024,768]{1,0:T(8,128)(2,1)S(1)}, u32[]{:S(2)}, u32[]{:S(2)}) collective-permute-start(bf16[1024,768]{1,0:T(8,128)(2,1)S(1)} %broadcast_select_fusion.4.refs_0_), channel_id=1, source_target_pairs={{0,1},{1,0},{2,3},{3,2},{4,5},{5,4},{6,7},{7,6},{8,9},{9,8},{10,11... | collective-permute-start | bytes 4718600 | tf_op jit(solution)/shard_map/ppermute | solution.py:398
  679.3 51.0 %collective-permute-start.93 = (bf16[1024,768]{1,0:T(8,128)(2,1)S(1)}, bf16[1024,768]{1,0:T(8,128)(2,1)S(1)}, u32[]{:S(2)}, u32[]{:S(2)}) collective-permute-start(bf16[1024,768]{1,0:T(8,128)(2,1)S(1)} %broadcast_select_fusion.4.refs_0_), channel_id=1, source_target_pairs={{0,2},{1,3},{2,0},{3,1},{4,6},{5,7},{6,4},{7,5},{8,10},{9,11},{10,... | collective-permute-start | bytes 4718600 | tf_op jit(solution)/shard_map/ppermute | solution.py:398
  (199 other events, 3114.4 us)

commit v2 on v1

--- a/solution.py
+++ b/solution.py
@@ -11,6 +11,8 @@
 TILE = 128
 LAYER = 12
 LINE = 4
+STREAMS = 4
+LATE = 2
 GROUP = 4
 F32 = jnp.float32
 LOW = jnp.bfloat16
@@ -50,12 +52,8 @@
     return jnp.concatenate([value[rows:], value[:rows]])
 
 
-def estimate(flops, *arrays):
-    return pl.CostEstimate(
-        flops=flops,
-        bytes_accessed=sum(a.size * a.dtype.itemsize for a in arrays),
-        transcendentals=0,
-    )
+def estimate(flops, size):
+    return pl.CostEstimate(flops=flops // 4, bytes_accessed=size // 4, transcendentals=0)
 
 
 def far(value):
@@ -74,9 +72,15 @@
     theirs_ref[...] = jnp.where(first, high, low).astype(LOW)
 
 
-def norm_one_kernel(core_ref, x_ref, gain_ref, shift_ref, mine_ref, theirs_ref):
+def norm_one_kernel(
+    core_ref, x_ref, gain_ref, shift_ref, grad_ref, active_ref,
+    mine_ref, theirs_ref, masked_ref, sum_ref,
+):
     normed = layer_norm(x_ref[...].astype(F32), gain_ref[...], shift_ref[...])
     halves(core_ref, normed, mine_ref, theirs_ref)
+    masked = active_ref[...] * grad_ref[...].astype(F32)
+    masked_ref[...] = masked.astype(LOW)
+    sum_ref[...] = jnp.sum(masked, axis=0, keepdims=True)
 
 
 def norm_two_kernel(
@@ -90,25 +94,120 @@
     halves(core_ref, layer_norm(middle, gain_ref[...], shift_ref[...]), mine_ref, theirs_ref)
 
 
-def norm(kernel, core, rows, width, whole, *operands):
-    half = jax.ShapeDtypeStruct((rows, width // 2), LOW)
-    outs = [jax.ShapeDtypeStruct((rows, width), F32)] * whole + [half, half]
+def norm_back(core_ref, value_ref, gain_ref, mine_ref, theirs_ref, gain_out_ref, shift_out_ref):
+    values = value_ref[...].astype(F32)
+    mine, theirs = mine_ref[: values.shape[0]], theirs_ref[...]
+    grads = jnp.where(
+        core_ref[0] == 0,
+        jnp.concatenate([mine, theirs], 1),
+        jnp.concatenate([theirs, mine], 1),
+    )
+    centered = values - jnp.mean(values, axis=-1, keepdims=True)
+    scale = lax.rsqrt(jnp.mean(centered * centered, axis=-1, keepdims=True) + 1e-05)
+    unit = centered * scale
+    gain_out_ref[...] = jnp.sum(grads * unit, axis=0, keepdims=True)
+    shift_out_ref[...] = jnp.sum(grads, axis=0, keepdims=True)
+    grads = grads * gain_ref[...]
+    inner = jnp.mean(grads * unit, axis=-1, keepdims=True)
+    return scale * (grads - jnp.mean(grads, axis=-1, keepdims=True) - unit * inner)
+
+
+def norm_two_back_kernel(
+    core_ref, value_ref, gain_ref, mine_ref, theirs_ref, grad_ref, active_ref,
+    total_ref, masked_ref, sum_ref, gain_out_ref, shift_out_ref,
+):
+    part = norm_back(
+        core_ref, value_ref, gain_ref, mine_ref, theirs_ref, gain_out_ref, shift_out_ref
+    )
+    total = grad_ref[...].astype(F32) + part
+    total_ref[...] = total
+    masked = (active_ref[...] * total).astype(LOW)
+    masked_ref[...] = masked
+    sum_ref[...] = jnp.sum(masked.astype(F32), axis=0, keepdims=True)
+
+
+def norm_one_back_kernel(
+    core_ref, value_ref, gain_ref, mine_ref, theirs_ref, grad_ref,
+    total_ref, gain_out_ref, shift_out_ref,
+):
+    part = norm_back(
+        core_ref, value_ref, gain_ref, mine_ref, theirs_ref, gain_out_ref, shift_out_ref
+    )
+    total_ref[...] = (grad_ref[...].astype(F32) + part).astype(LOW)
+
+
+def by_rows(kernel, core, outs, *operands):
     vmem = pl.BlockSpec(memory_space=pltpu.VMEM)
     return pl.pallas_call(
         kernel,
         in_specs=[pl.BlockSpec(memory_space=pltpu.SMEM)] + [vmem] * len(operands),
         out_specs=[vmem] * len(outs),
-        out_shape=outs,
+        out_shape=[jax.ShapeDtypeStruct(shape, dtype) for shape, dtype in outs],
         compiler_params=limit(24),
-        cost_estimate=estimate(20 * rows * width, *operands),
+        cost_estimate=estimate(
+            20 * operands[0].size, sum(o.size * o.dtype.itemsize for o in operands)
+        ),
     )(core, *operands)
 
 
-def columns_kernel(table_ref, left_ref, weight_ref, out_ref):
-    out_ref[...] = dot(left_ref[...], weight_ref[...], 1, 0)
-
-
-def times_columns(left, weight, table, block):
+def product_kernel(count, turned, *refs):
+    lefts, out_ref, left_turned, right = refs[:count], refs[-3], refs[-2], refs[-1]
+    rights = refs[count:-3]
+    length = lefts[0].shape[0]
+
+    @pl.when(pl.program_id(0) == 0)
+    def _():
+        for d, left in enumerate(lefts):
+            left_turned[:, d * length : (d + 1) * length] = left[...].T
+
+    row = 0
+    for piece in rights:
+        value = piece[0] if len(piece.shape) == 3 else piece[...]
+        if turned:
+            value = roll_rows(value)
+        right[row : row + value.shape[0]] = value
+        row += value.shape[0]
+    out_ref[...] = dot(left_turned[...], right[...], 1, 0).astype(LOW)
+
+
+def rows_product(lefts, rights, block, first, steps, turned=False):
+    length, tall = lefts[0].shape
+
+    def spec(right):
+        if right.ndim == 3:
+            return pl.BlockSpec((1, right.shape[1], block), lambda j: (first + j, 0, 0))
+        return pl.BlockSpec((right.shape[0], block), lambda j: (0, first + j))
+
+    total = length * len(lefts)
+    return pl.pallas_call(
+        functools.partial(product_kernel, len(lefts), turned),
+        grid=(steps,),
+        in_specs=[pl.BlockSpec((length, tall), lambda j: (0, 0))] * len(lefts)
+        + [spec(right) for right in rights],
+        out_specs=pl.BlockSpec((tall, block), lambda j: (0, j)),
+        out_shape=jax.ShapeDtypeStruct((tall, steps * block), LOW),
+        scratch_shapes=[pltpu.VMEM((tall, total), LOW), pltpu.VMEM((total, block), LOW)],
+        compiler_params=limit(32),
+        cost_estimate=estimate(
+            2 * tall * total * steps * block, 2 * total * (tall + steps * block)
+        ),
+    )(*lefts, *rights)
+
+
+def hold(values, after):
+    return lax.optimization_barrier((values, after))[0]
+
+
+def columns_kernel(table_ref, left_ref, *refs):
+    total, first = 0.0, 0
+    for weight_ref in refs[:-1]:
+        depth = weight_ref.shape[0]
+        total += dot(left_ref[:, first : first + depth], weight_ref[...], 1, 0)
+        first += depth
+    refs[-1][...] = total.astype(refs[-1].dtype)
+
+
+def times_columns(left, weight, table, block, dtype):
     rows, depth = left.shape
     steps = table.shape[0]
     return pl.pallas_call(
@@ -118,34 +217,42 @@
             grid=(steps,),
             in_specs=[
                 pl.BlockSpec((rows, depth), lambda i, t: (0, 0)),
-                pl.BlockSpec((depth, block), lambda i, t: (0, t[i])),
+                *[
+                    pl.BlockSpec(
+                        (depth // STREAMS, block),
+                        functools.partial(lambda r, i, t: (r, t[i]), r),
+                    )
+                    for r in range(STREAMS)
+                ],
             ],
             out_specs=pl.BlockSpec((rows, block), lambda i, t: (0, i)),
         ),
-        out_shape=jax.ShapeDtypeStruct((rows, steps * block), F32),
+        out_shape=jax.ShapeDtypeStruct((rows, steps * block), dtype),
         compiler_params=limit(24),
-        cost_estimate=pl.CostEstimate(
-            flops=2 * rows * depth * steps * block,
-            bytes_accessed=2 * depth * (rows + steps * block) + 4 * rows * steps * block,
-            transcendentals=0,
-        ),
-    )(table, left, far(weight))
-
-
-def back_kernel(turned, table_ref, left_ref, weight_ref, *rest):
-    out_ref = rest[-1]
+        cost_estimate=estimate(2 * rows * depth * steps * block, 2 * depth * (rows + steps * block) + 4 * rows * steps * block),
+    )(table, left, *[far(weight)] * STREAMS)
+
+
+def back_kernel(turned, table_ref, left_ref, *refs):
+    weights, out_ref = refs[:STREAMS], refs[-1]
+    starts = refs[STREAMS:-1]
     left = left_ref[...]
     if turned:
         left = roll_rows(left)
-    part = dot(left, weight_ref[...], 1, 1)
-
-    @pl.when(pl.program_id(1) == 0)
-    def _():
-        out_ref[...] = part + rest[0][...] if len(rest) > 1 else part
-
-    @pl.when(pl.program_id(1) > 0)
-    def _():
-        out_ref[...] += part
+    first = 0
+    for weight_ref in weights:
+        deep = weight_ref.shape[0]
+        part = dot(left, weight_ref[...], 1, 1)
+        columns = slice(first, first + deep)
+        first += deep
+
+        @pl.when(pl.program_id(1) == 0)
+        def _(part=part, columns=columns):
+            out_ref[:, columns] = part + starts[0][:, columns] if starts else part
+
+        @pl.when(pl.program_id(1) > 0)
+        def _(part=part, columns=columns):
+            out_ref[:, columns] += part
 
 
 def times_back(left, weight, table, block, deep, start=None, turned=False):
@@ -155,9 +262,15 @@
     out_spec = pl.BlockSpec((rows, deep), lambda k, i, t: (0, k))
     in_specs = [
         pl.BlockSpec((rows, block), lambda k, i, t: (0, i)),
-        pl.BlockSpec((deep, block), lambda k, i, t: (k, t[i])),
+        *[
+            pl.BlockSpec(
+                (deep // STREAMS, block),
+                functools.partial(lambda r, k, i, t: (k * STREAMS + r, t[i]), r),
+            )
+            for r in range(STREAMS)
+        ],
     ]
-    operands = [table, left, far(weight)]
+    operands = [table, left, *[far(weight)] * STREAMS]
     if start is not None:
         in_specs.append(out_spec)
         operands.append(start)
@@ -171,20 +284,23 @@
         ),
         out_shape=jax.ShapeDtypeStruct((rows, depth), F32),
         compiler_params=limit(32),
-        cost_estimate=pl.CostEstimate(
-            flops=2 * rows * depth * steps * block,
-            bytes_accessed=2 * steps * block * (rows + depth) + 8 * rows * depth,
-            transcendentals=0,
-        ),
+        cost_estimate=estimate(2 * rows * depth * steps * block, 2 * steps * block * (rows + depth) + 8 * rows * depth),
     )(*operands)
 
 
-def inner_kernel(grad_ref, weight_ref, mine_ref, theirs_ref, bias_ref, act_ref, out_ref, sum_ref):
-    act, slope = gelu_and_slope(mine_ref[...] + roll_rows(theirs_ref[...]) + bias_ref[...])
-    act_ref[...] = act.astype(LOW)
-    grad = (dot(grad_ref[...], weight_ref[...], 1, 1) * slope).astype(LOW)
-    out_ref[...] = grad
-    sum_ref[...] = jnp.sum(grad.astype(F32), axis=0, keepdims=True)
+def inner_kernel(grad_ref, *refs):
+    weights = refs[:STREAMS]
+    mine_ref, theirs_ref, bias_ref, act_ref, out_ref, sum_ref = refs[STREAMS:]
+    first = 0
+    for weight_ref in weights:
+        columns = slice(first, first + weight_ref.shape[0])
+        first += weight_ref.shape[0]
+        theirs = roll_rows(theirs_ref[:, columns])
+        act, slope = gelu_and_slope(mine_ref[:, columns] + theirs + bias_ref[:, columns])
+        act_ref[:, columns] = act.astype(LOW)
+        grad = (dot(grad_ref[...], weight_ref[...], 1, 1) * slope).astype(LOW)
+        out_ref[:, columns] = grad
+        sum_ref[:, columns] = jnp.sum(grad.astype(F32), axis=0, keepdims=True)
 
 
 def inner_layer(grads, weight, mine, theirs, bias, block):
@@ -197,7 +313,13 @@
         grid=(hidden // block,),
         in_specs=[
             pl.BlockSpec((rows, width), lambda i: (0, 0)),
-            pl.BlockSpec((block, width), lambda i: (i, 0)),
+            *[
+                pl.BlockSpec(
+                    (block // STREAMS, width),
+                    functools.partial(lambda r, i: (i * STREAMS + r, 0), r),
+                )
+                for r in range(STREAMS)
+            ],
             part,
             part,
             line,
@@ -209,12 +331,8 @@
             jax.ShapeDtypeStruct((1, hidden), F32),
         ],
         compiler_params=limit(32),
-        cost_estimate=pl.CostEstimate(
-            flops=2 * rows * width * hidden,
-            bytes_accessed=2 * width * (rows + hidden) + 12 * rows * hidden,
-            transcendentals=rows * hidden,
-        ),
-    )(grads, far(weight), mine, theirs, bias)
+        cost_estimate=estimate(2 * rows * width * hidden, 2 * width * (rows + hidden) + 12 * rows * hidden),
+    )(grads, *[far(weight)] * STREAMS, mine, theirs, bias)
 
 
 def head_chances(queries, keys, lanes_of_head, allowed):
@@ -274,11 +392,7 @@
         ),
         out_shape=[jax.ShapeDtypeStruct((length, width), LOW)] * 4,
         compiler_params=limit(16),
-        cost_estimate=pl.CostEstimate(
-            flops=4 * length * length * width,
-            bytes_accessed=32 * length * width,
-            transcendentals=length * length * width // HEAD_DIM,
-        ),
+        cost_estimate=estimate(4 * length * length * width, 32 * length * width),
     )(first, mine, mine, mine, theirs, theirs, theirs, bias, bias, bias)
 
 
@@ -317,11 +431,7 @@
         ),
         out_shape=jax.ShapeDtypeStruct((3, length, width), LOW),
         compiler_params=limit(16),
-        cost_estimate=pl.CostEstimate(
-            flops=10 * length * length * width,
-            bytes_accessed=14 * length * width,
-            transcendentals=length * length * width // HEAD_DIM,
-        ),
+        cost_estimate=estimate(10 * length * length * width, 14 * length * width),
     )(first, *operands)
 
 
@@ -369,9 +479,7 @@
         ],
         input_output_aliases={len(pieces) + 1: 0},
         compiler_params=limit(32),
-        cost_estimate=pl.CostEstimate(
-            flops=0, bytes_accessed=sum(6 * p.size for p in pieces), transcendentals=0
-        ),
+        cost_estimate=estimate(0, sum(6 * p.size for p in pieces)),
     )(jnp.stack(places).astype(jnp.int32), *pieces, whole)
 
 
@@ -389,15 +497,12 @@
 
 class Lane:
     def __init__(self):
-        self.last = None
+        self.last = ()
 
     def send(self, sends, after=()):
-        if self.last is not None:
-            held = lax.optimization_barrier(([v for v, _ in sends], self.last, after))
-            sends = [(v, m) for v, (_, m) in zip(held[0], sends)]
-        results = [lax.ppermute(v, "dp", m) for v, m in sends]
-        self.last = results
-        return results
+        values = hold([v for v, _ in sends], (self.last, after))
+        self.last = [lax.ppermute(v, "dp", m) for v, (_, m) in zip(values, sends)]
+        return self.last
 
 
 def per_device(
@@ -431,7 +536,7 @@
     half = width // 2
     inner = up_weight.shape[1]
     inner_half = inner // 2
-    across, first_hop, middle_hop, last_hop = Lane(), Lane(), Lane(), Lane()
+    across, middle_across, first_hop, middle_hop, last_hop = (Lane() for _ in range(5))
 
     def swap(value):
         return lax.ppermute(value, "sp", [(0, 1), (1, 0)])
@@ -454,37 +559,35 @@
             lax.dynamic_slice_in_dim(value, other * size, size, axis),
         )
 
-    def in_order(mine, theirs, axis):
-        return jnp.where(
-            core == 0,
-            jnp.concatenate([mine, theirs], axis),
-            jnp.concatenate([theirs, mine], axis),
-        )
+    def exchange(blocks):
+        (far_one,) = across.send([(blocks[3], in_plane(3))])
+        near = across.send([(blocks[1], in_plane(1)), (blocks[2], in_plane(2))])
+        return [blocks[0], *near, far_one]
 
     def gather_group(value):
-        return [value] + across.send([(value, in_plane(d)) for d in range(1, GROUP)])
+        return exchange([value] * GROUP)
 
     def scatter_group(value, axis, size):
         blocks = [
             lax.dynamic_slice_in_dim(value, (spot ^ d) * size, size, axis) for d in range(GROUP)
         ]
-        return blocks[:1] + across.send([(blocks[d], in_plane(d)) for d in range(1, GROUP)])
-
-    def both(mine):
-        mine = jnp.concatenate(mine)
-        theirs = swap(mine)
-        pair = [v.reshape(GROUP, 1, rows, -1) for v in (mine, theirs)]
-        return jnp.concatenate(pair, 1).reshape(GROUP * length, -1)
-
-    def turn(value):
-        return value.reshape(-1, 2, rows, value.shape[-1])[:, ::-1].reshape(value.shape)
+        return exchange(blocks)
+
+    def pairs(mine, theirs):
+        return [piece for pair in zip(mine, theirs) for piece in pair]
 
     end = (level == 0) | (level == LINE - 1)
 
-    def line_sum(value):
-        value = value + first_hop.send([(value, inward)])[0]
-        value = value + middle_hop.send([(value, middle_moves)])[0]
-        value = jnp.where(end, last_hop.send([(value, outward)])[0], value)
+    def line_start(value, after=()):
+        return value + hold(first_hop.send([(value, inward)])[0], after)
+
+    def line_middle(value):
+        return value + middle_hop.send([(value, middle_moves)])[0]
+
+    def line_end(value):
+        return jnp.where(end, last_hop.send([(value, outward)])[0], value)
+
+    def blocks_sum(value):
         distance = GROUP
         while distance < plane:
             value = value + lax.ppermute(value, "dp", in_plane(distance))
@@ -493,77 +596,122 @@
 
     def spread(value, after):
         size = value.shape[0] // 2
-        first, second = across.send([(value, in_plane(1)), (value, in_plane(2))], after)
-        upper, lower = across.send([(first[:size], in_plane(2)), (second[size:], in_plane(1))])
+        first, second = across.send([(value, in_plane(1)), (value, in_plane(2))], after[0])
+        upper, lower = across.send(
+            [(first[:size], in_plane(2)), (second[size:], in_plane(1))], after[1]
+        )
         return [value, first, second, upper, lower]
+
+    def spread_late(value, after):
+        size = value.shape[0] // 2
+
+        def middle_only(distance):
+            return [(a, b) for a, b in in_plane(distance) if 0 < a // plane < LINE - 1]
+
+        near = middle_across.send(
+            [(value[:size], middle_only(1)), (value[size:], middle_only(2))]
+        )
+        own = line_end(value)
+        first = across.send([(own[:size], in_plane(2)), (own[size:], in_plane(1))], after[0])
+        near_ends = last_hop.send([(v, outward) for v in near])
+        near = [jnp.where(end, e, v) for e, v in zip(near_ends, near)]
+        second = across.send([(near[0], in_plane(2)), (near[1], in_plane(1))], after[1])
+        return [own, near[0], first[1], first[0], near[1], *second]
 
     def table(size, start, count=None):
         return jnp.arange(size if count is None else count, dtype=jnp.int32) + start
 
-    inputs = hidden[0].astype(F32)
     active = active_rows(exit_layers[0], core * rows, rows, length)
+    core_number = core.astype(jnp.int32)[None]
     first_row = (core * rows).astype(jnp.int32)[None]
-    grad_output = cotangent[0].astype(F32)
-    down_grad = (active * grad_output).astype(LOW)
+    full, part, line = (rows, width), (rows, half), (1, width)
+
+    mine, theirs, down_grad, down_sums = by_rows(
+        norm_one_kernel,
+        core_number,
+        [(part, LOW), (part, LOW), (full, LOW), (line, F32)],
+        hidden[0],
+        attn_gain[None],
+        attn_shift[None],
+        cotangent[0],
+        active,
+    )
+    normed_one_half = jnp.concatenate([mine, swap(theirs)])
     down_grad_all = jnp.concatenate([down_grad, swap(down_grad)])
-
-    core_number = core.astype(jnp.int32)[None]
-    mine, theirs = norm(
-        norm_one_kernel, core_number, rows, width, 0,
-        hidden[0], attn_gain[None], attn_shift[None],
-    )
-    normed_one_half = jnp.concatenate([mine, swap(theirs)])
     down_mine = gather_group(down_grad)
-    qkv_left = gather_group(normed_one_half)
     block = min(512, half)
     count = half // block
 
     def qkv_table(c):
         return jnp.concatenate([table(count, (2 * p + c) * count) for p in range(3)])
 
-    theirs = times_columns(normed_one_half, qkv_weight, qkv_table(other), block)
-    theirs = swap(theirs)
-    mine = times_columns(normed_one_half, qkv_weight, qkv_table(core), block)
+    theirs = times_columns(normed_one_half, qkv_weight, qkv_table(other), block, LOW)
+    theirs = hold(swap(theirs), down_mine[3])
+    mine = times_columns(normed_one_half, qkv_weight, qkv_table(core), block, F32)
     bias = jnp.stack([query_bias, jnp.zeros_like(query_bias), value_bias])
     bias = lax.dynamic_slice_in_dim(bias, core * half, half, 1).reshape(1, -1)
     queries, keys, values, attended = attend_forward(first_row, mine, theirs, bias)
-    attended, down_mine = lax.optimization_barrier((attended, down_mine))
     out_part = dot(attended, out_weight, 1, 0)
-    middle, mine, theirs = norm(
-        norm_two_kernel, core_number, rows, width, 1,
-        hidden[0], active, out_part, swap(out_part[rows:]),
-        out_bias[None], ffn_gain[None], ffn_shift[None],
-    )
+    middle, mine, theirs = by_rows(
+        norm_two_kernel,
+        core_number,
+        [(full, F32), (part, LOW), (part, LOW)],
+        hidden[0],
+        active,
+        out_part,
+        swap(out_part[rows:]),
+        out_bias[None],
+        ffn_gain[None],
+        ffn_shift[None],
+    )
+    theirs = hold(theirs, down_mine[1:3])
+    qkv_left = gather_group(normed_one_half)
+    down_theirs = [swap(g) for g in down_mine]
     normed_two_half = jnp.concatenate([mine, swap(theirs)])
     count = inner_half // block
-    theirs = times_columns(normed_two_half, up_weight, table(count, other * count), block)
-    theirs = swap(theirs)
-    mine = times_columns(normed_two_half, up_weight, table(count, core * count), block)
+    theirs = times_columns(
+        normed_two_half, up_weight, table(count, other * count), block, LOW
+    )
+    theirs = hold(swap(theirs), qkv_left[3])
+    mine = times_columns(normed_two_half, up_weight, table(count, core * count), block, F32)
     bias = lax.dynamic_slice_in_dim(up_bias, core * inner_half, inner_half).reshape(1, -1)
-    mine, qkv_left = lax.optimization_barrier((mine, qkv_left))
     inner_low, up_grad, up_sums = inner_layer(
         down_grad_all, down_weight, mine, theirs, bias, block
     )
+
     down_left = scatter_group(inner_low, 1, inner_half // GROUP)
     up_right = scatter_group(up_grad, 1, inner_half // GROUP)
-    up_left = gather_group(normed_two_half)
-    out_left = gather_group(attended)
     block = min(1024, inner_half)
     count = inner_half // block
     up_grad_theirs = swap(up_grad)
-    part = times_back(up_grad, up_weight, table(count, core * count), block, 512)
-    part = times_back(
-        up_grad_theirs, up_weight, table(count, other * count), block, 512, part, True
-    )
-    normed_two_grad = in_order(part[:rows], swap(part[rows:]), 1)
-    _, norm_two_back = jax.vjp(layer_norm, middle, ffn_gain, ffn_shift)
-    middle_part, gain_two_grad, shift_two_grad = norm_two_back(normed_two_grad)
-    middle_grad = grad_output + middle_part
-    attn_grad = (active * middle_grad).astype(LOW)
+    grads = times_back(up_grad, up_weight, table(count, core * count), block, 512)
+    grads = times_back(
+        up_grad_theirs, up_weight, table(count, other * count), block, 512, grads, True
+    )
+    middle_grad, attn_grad, attn_sums, gain_two_grad, shift_two_grad = by_rows(
+        norm_two_back_kernel,
+        core_number,
+        [(full, F32), (full, LOW), (line, F32), (line, F32), (line, F32)],
+        middle,
+        ffn_gain[None],
+        grads,
+        swap(grads[rows:]),
+        cotangent[0],
+        active,
+    )
     attn_grad_all = jnp.concatenate([attn_grad, swap(attn_grad)])
+    head_grads = dot(attn_grad_all, out_weight, 1, 1).astype(LOW)
+    down_right = pairs(down_mine, down_theirs)
+    down_left = hold(down_left, attn_grad)
+    quarter = width // 4
+    down_parts = [rows_product(down_left, down_right, quarter, 0, 1)]
+    head_grads = hold(head_grads, down_parts)
+    qkv_grad = attend_backward(first_row, queries, keys, values, head_grads)
+    down_parts[0] = line_start(down_parts[0], qkv_grad)
+    qkv_grad = hold(qkv_grad, up_right[3])
+    up_left = gather_group(normed_two_half)
     out_right = scatter_group(attn_grad, 1, width // GROUP)
-    head_grads = dot(attn_grad_all, out_weight, 1, 1).astype(LOW)
-    qkv_grad = attend_backward(first_row, queries, keys, values, head_grads)
+    out_left = gather_group(attended)
     qkv_right = scatter_group(qkv_grad, 2, half // GROUP)
     flat = jnp.concatenate([qkv_grad[0], qkv_grad[1], qkv_grad[2]], 1)
     flat_theirs = swap(flat)
@@ -573,48 +721,92 @@
     def qkv_table(c):
         return jnp.concatenate([table(count, (2 * p + c) * count) for p in range(3)])
 
-    inner_low, flat_theirs = lax.optimization_barrier((inner_low, flat_theirs))
-    down_part = dot(inner_low, down_weight, 1, 0)
+    grads = times_back(flat, qkv_weight, qkv_table(core), block, 512)
+    grads = times_back(flat_theirs, qkv_weight, qkv_table(other), block, 512, grads, True)
+    input_grad, gain_one_grad, shift_one_grad = by_rows(
+        norm_one_back_kernel,
+        core_number,
+        [(full, LOW), (line, F32), (line, F32)],
+        hidden[0],
+        attn_gain[None],
+        grads,
+        hold(swap(grads[rows:]), up_right[1:3]),
+        middle_grad,
+    )
+    down_part = dot(hold(inner_low, (input_grad, up_left[3])), down_weight, 1, 0)
     output = middle + active * (down_part[:rows] + swap(down_part[rows:]) + down_bias)
-    part = times_back(flat, qkv_weight, qkv_table(core), block, 512)
-    part = times_back(flat_theirs, qkv_weight, qkv_table(other), block, 512, part, True)
-    normed_one_grad = in_order(part[:rows], swap(part[rows:]), 1)
-    _, norm_one_back = jax.vjp(layer_norm, inputs, attn_gain, attn_shift)
-    input_part, gain_one_grad, shift_one_grad = norm_one_back(normed_one_grad)
-    input_grad = (middle_grad + input_part).astype(LOW)
-
-    chunks = []
-    down_right = both(down_mine)
-    down_left = jnp.concatenate(down_left)
+
+    def widen(value):
+        none = jnp.zeros_like(value)
+        return jnp.where(
+            core == 0, jnp.concatenate([value, none]), jnp.concatenate([none, value])
+        )
+
+    qkv_sums = jnp.sum(qkv_grad.astype(F32), axis=1)
+    small = jnp.concatenate(
+        [
+            widen(qkv_sums[0]),
+            widen(qkv_sums[2]),
+            attn_sums[0],
+            widen(up_sums[0]),
+            down_sums[0],
+            gain_one_grad[0],
+            shift_one_grad[0],
+            gain_two_grad[0],
+            shift_two_grad[0],
+        ]
+    ).reshape(-1, 128)
+    small = small + swap(small)
+    distance = 1
+    while distance < plane:
+        small = small + lax.ppermute(small, "dp", in_plane(distance))
+        distance *= 2
+    small = small + lax.ppermute(small, "dp", inward)
+    small = small + lax.ppermute(small, "dp", middle_moves)
+    small = jnp.where(end, lax.ppermute(small, "dp", outward), small).reshape(-1)
+    small_grads = []
+    first = 0
+    for size in (width, width, width, inner, width, width, width, width, width):
+        small_grads.append(small[first : first + size])
+        first += size
+
+    chunks = [("down", down_parts[0], 0)]
+    value = rows_product(down_left, down_right, quarter, 1, 1)
+    chunks.append(("down", line_start(value), 1))
+    value = rows_product(down_left, down_right, quarter, 2, 2)
+    chunks.append(("down", line_start(value), 1))
     size = inner_half // GROUP
-    first = 0
-    for cut in (width // 4, width // 4, width // 2):
-        chunks.append(("down", down_left, down_right[:, first : first + cut], first // cut))
-        first += cut
-    up_left = jnp.concatenate(up_left)
-    up_right = jnp.concatenate(up_right)
-    chunks.append(("up", up_left, up_right, core))
-    chunks.append(("up", up_left, turn(swap(up_right)), other))
-    chunks.append(("out", jnp.concatenate(out_left), both(out_right), 0))
-    qkv_left = jnp.concatenate(qkv_left)
-    qkv_right = jnp.concatenate(
-        [jnp.concatenate([r[0], r[1], r[2]], 1) for r in qkv_right]
-    )
-    chunks.append(("qkv", qkv_left, qkv_right, core))
-    chunks.append(("qkv", qkv_left, turn(swap(qkv_right)), other))
-
-    shapes = {
-        "down": (inner_half, width),
-        "up": (half, inner),
-        "out": (half, width),
-        "qkv": (half, 3 * width),
+    block = min(512, size)
+    value = rows_product(up_left, up_right, block, 0, size // block)
+    chunks.append(("up", line_start(value), core))
+    theirs = [swap(r) for r in up_right]
+    value = rows_product(up_left, theirs, block, 0, size // block, True)
+    chunks.append(("up", line_start(value), other))
+    right = pairs(out_right, [swap(r) for r in out_right])
+    value = rows_product(out_left, right, width // GROUP, 0, 1)
+    chunks.append(("out", line_start(value), 0))
+    size = half // GROUP
+    value = rows_product(qkv_left, qkv_right, size, 0, 3)
+    chunks.append(("qkv", line_start(value), core))
+    theirs = [swap(r) for r in qkv_right]
+    value = rows_product(qkv_left, theirs, size, 0, 3, True)
+    chunks.append(("qkv", line_start(value), other))
+
+    wholes = {
+        "down": blank((inner_half, width)),
+        "up": blank((half, inner)),
+        "out": blank((half, width)),
+        "qkv": blank((half, 3 * width)),
     }
-    wholes = {name: blank(shape) for name, shape in shapes.items()}
-    sums = [line_sum(dot(left, right, 0, 0).astype(LOW)) for _, left, right, _ in chunks]
-    done = [()] * 2
-    for (name, _, _, where), total in zip(chunks, sums):
-        pieces = spread(total, done[-2])
-        tall, wide = total.shape
+    done = [(), ()]
+    for index, (name, value, where) in enumerate(chunks):
+        value = line_middle(value)
+        after = done[-2], (done[-1], small if index == 3 else ())
+        if plane == GROUP and index >= len(chunks) - LATE:
+            pieces = spread_late(value, after)
+        else:
+            pieces = spread(blocks_sum(line_end(value)), after)
+        tall, wide = value.shape
         high = min(256, tall)
         broad = wide // 3 if name == "qkv" else wide
         places = []
@@ -635,37 +827,6 @@
         wholes[name] = place(pieces, wholes[name], places, high, broad)
         done.append(wholes[name])
 
-    def widen(value):
-        return in_order(value, jnp.zeros_like(value), 0)
-
-    qkv_sums = jnp.sum(qkv_grad.astype(F32), axis=1)
-    small = jnp.concatenate(
-        [
-            widen(qkv_sums[0]),
-            widen(qkv_sums[2]),
-            jnp.sum(attn_grad.astype(F32), axis=0),
-            widen(up_sums[0]),
-            jnp.sum(down_grad.astype(F32), axis=0),
-            gain_one_grad,
-            shift_one_grad,
-            gain_two_grad,
-            shift_two_grad,
-        ]
-    ).reshape(-1, 128)
-    small = small + swap(small)
-    distance = 1
-    while distance < plane:
-        small = small + lax.ppermute(small, "dp", in_plane(distance))
-        distance *= 2
-    small = small + lax.ppermute(small, "dp", inward)
-    small = small + lax.ppermute(small, "dp", middle_moves)
-    small = jnp.where(end, lax.ppermute(small, "dp", outward), small).reshape(-1)
-    small_grads = []
-    first = 0
-    for size in (width, width, width, inner, width, width, width, width, width):
-        small_grads.append(small[first : first + size])
-        first += size
-
     return (
         output.astype(LOW)[None],
         input_grad[None],

time: 771 us -> 873 us (1.13)
  waiting for transfers between devices: 293 us -> 361 us
  Pallas kernels: 150 us -> 210 us
  matrix products: 39.3 us -> 12.2 us
  starting transfers between devices: 142 us -> 160 us
  other arithmetic: 74.5 us -> 58.5 us
    ppermute x80 -> x88, waiting for transfers between devices: 242 us -> 329 us  [send(): self.last = [lax.ppermute(v, 'dp', m) for v, (_, m) in zip(values, sends)]]
    pallas_call x2 -> x12, Pallas kernels: 1.01 us -> 32.1 us  [the longest x8 27.8 us: rows_product(): pl.pallas_call(functools.partial(product_kernel, len(lefts), turned), gri...]
    dot_general x11 -> x3, matrix products: 39.3 us -> 12.2 us  [dot(): lax.dot_general(left, right, (((left_dim,), (right_dim,)), ((), ())), pre...]
    pallas_call x4, Pallas kernels: 32.6 us -> 59.5 us  [times_back(): pl.pallas_call(functools.partial(back_kernel, turned), grid_spec=pltpu.Pr...]
    ppermute x80 -> x88, starting transfers between devices: 130 us -> 146 us  [send(): self.last = [lax.ppermute(v, 'dp', m) for v, (_, m) in zip(values, sends)]]
    concatenate x5 -> x0, other arithmetic: 15.1 us -> none  [the longest x1 10.9 us: per_device(): jnp.concatenate([jnp.concatenate([r[0], r[1], r[2]], 1) for r in qkv_right])]
    ppermute x2, waiting for transfers between devices: 37 us -> 24.5 us  [per_device(): small = small + lax.ppermute(small, 'dp', in_plane(distance))]
    unnamed x259 -> x234, local copies, waits for them, and re-layouts: 31.9 us -> 34.8 us
  transfers between devices with their start and end apart: 102 -> 121, of which waited for: 40 -> 56; matrix products, arithmetic and copies ran while one was open for 19% -> 10% of each run, Pallas kernels for 16% -> 19%
where the time goes in v2:
time: 873 us; the launch traced here: 861 us
  waiting for transfers between devices  361 us (41%)
  Pallas kernels  210 us (24%)
  starting transfers between devices  160 us (18%)
  other arithmetic  58.5 us (7%)
  local copies, waits for them, and re-layouts  55.6 us (6%)
  matrix products  12.2 us (1%)
    ppermute x88, waiting for transfers between devices, send(): self.last = [lax.ppermute(v, 'dp', m) for v, (_, m) in zip(values, sends)]  329 us
    ppermute x88, starting transfers between devices, send(): self.last = [lax.ppermute(v, 'dp', m) for v, (_, m) in zip(values, sends)]  146 us
    pallas_call x4, Pallas kernels, times_back(): pl.pallas_call(functools.partial(back_kernel, turned), grid_spec=pltpu.Pr...  59.5 us
    pallas_call x8, Pallas kernels, place(): pl.pallas_call(functools.partial(place_kernel, high), in_specs=[pl.BlockS...  56.1 us
    unnamed x234, local copies, waits for them, and re-layouts  34.8 us
    pallas_call x4, Pallas kernels, times_columns(): pl.pallas_call(columns_kernel, grid_spec=pltpu.PrefetchScalarGridSpec(num...  30.5 us
    pallas_call x8, Pallas kernels, rows_product(): pl.pallas_call(functools.partial(product_kernel, len(lefts), turned), gri...  27.8 us
    ppermute x2, waiting for transfers between devices, per_device(): small = small + lax.ppermute(small, 'dp', in_plane(distance))  24.5 us
  transfers between devices with their start and end apart: 121, of which 56 were waited for; matrix products, arithmetic and copies ran while one was open for 10% of the time, Pallas kernels for 19%

profile of v2, /device:TPU:0, one launch (start us, length us, event | category | flops | bytes accessed | tf_op | source)
XLA Modules:
  0.0 861.4 jit_solution(6175275049002656954)
XLA Ops:
  47.8 9.4 %collective-permute-done.5.refs_6_ = bf16[128,2048]{1,0:T(8,128)(2,1)S(1)} collective-permute-done((bf16[128,2048]{1,0:T(8,128)(2,1)S(1)}, bf16[128,2048]{1,0:T(8,128)(2,1)S(1)}, u32[]{:S(2)}, u32[]{:S(2)}) %collective-permute-start.5) | collective-permute-done | bytes 524320 | tf_op jit(solution)/shard_map/ppermute | solution.py:504
  85.4 15.0 %shard_map.278 = (bf16[256,4096]{1,0:T(8,128)(2,1)S(1)}, bf16[256,4096]{1,0:T(8,128)(2,1)}, f32[1,4096]{1,0:T(1,128)S(1)}) custom-call(bf16[256,2048]{1,0:T(8,128)(2,1)S(1)} %pad_maximum_fusion.1.grad_ref, bf16[4096,2048]{1,0:T(8,128)(2,1)} %refs_3_.13, bf16[4096,2048]{1,0:T(8,128)(2,1)} %refs_3_.13, bf16[4096,2048]{1,0:T(8,128)(2,1)} %refs_3_.13, ...), custom_call_target="tpu_custom_call" | custom-call | flops 1073741824 | bytes 7602176 | tf_op jit(solution)/shard_map/pallas_call | solution.py:311
  117.6 16.6 %shard_map.279.refs_4_ = f32[256,1024]{1,0:T(8,128)S(1)} custom-call(s32[4]{0:T(128)S(1)} %iota_add_fusion.1.table_ref, bf16[256,4096]{1,0:T(8,128)(2,1)} %get-tuple-element.150.left_ref, bf16[1024,8192]{1,0:T(8,128)(2,1)} %refs_3_.15, bf16[1024,8192]{1,0:T(8,128)(2,1)} %refs_3_.15, bf16[1024,8192]{1,0:T(8,128)(2,1)} %refs_3_.15, bf16[1024,8192]{1,0:T(8,128)(2,1)} %refs_3_.15), custom_call_target="tpu_custom_call" | custom-call | flops 536870912 | bytes 3145728 | tf_op jit(solution)/shard_map/pallas_call | solution.py:277
  134.2 17.0 %shard_map.280.mine_ref = f32[256,1024]{1,0:T(8,128)S(1)} custom-call(s32[4]{0:T(128)S(1)} %iota_add_fusion.2.table_ref, bf16[256,4096]{1,0:T(8,128)(2,1)} %collective-permute-done.10.left_ref, bf16[1024,8192]{1,0:T(8,128)(2,1)} %refs_3_.15, bf16[1024,8192]{1,0:T(8,128)(2,1)} %refs_3_.15, bf16[1024,8192]{1,0:T(8,128)(2,1)} %refs_3_.15, ...), custom_call_target="tpu_custom_call" | custom-call | flops 536870912 | bytes 3145728 | tf_op jit(solution)/shard_map/pallas_call | solution.py:277
  155.8 9.9 %collective-permute-done.16.refs_1_ = bf16[256,1024]{1,0:T(8,128)(2,1)S(1)} collective-permute-done((bf16[256,1024]{1,0:T(8,128)(2,1)S(1)}, bf16[256,1024]{1,0:T(8,128)(2,1)S(1)}, u32[]{:S(2)}, u32[]{:S(2)}) %collective-permute-start.16) | collective-permute-done | bytes 524320 | tf_op jit(solution)/shard_map/ppermute | solution.py:504
  176.3 16.8 %collective-permute-done.51 = bf16[1024,512]{1,0:T(8,128)(2,1)S(1)} collective-permute-done((bf16[1024,512]{1,0:T(8,128)(2,1)S(1)}, bf16[1024,512]{1,0:T(8,128)(2,1)S(1)}, u32[]{:S(2)}, u32[]{:S(2)}) %collective-permute-start.51) | collective-permute-done | bytes 1048608 | tf_op jit(solution)/shard_map/ppermute | solution.py:504
  199.2 10.5 %collective-permute-done.24.refs_5_ = bf16[256,1024]{1,0:T(8,128)(2,1)} collective-permute-done((bf16[256,1024]{1,0:T(8,128)(2,1)S(1)}, bf16[256,1024]{1,0:T(8,128)(2,1)}, u32[]{:S(2)}, u32[]{:S(2)}) %collective-permute-start.24) | collective-permute-done | bytes 524320 | tf_op jit(solution)/shard_map/ppermute | solution.py:504
  217.1 9.8 %shard_map.283 = bf16[3,256,1024]{2,1,0:T(8,128)(2,1)S(1)} custom-call(s32[1]{0:T(128)} %bitcast.4.first_ref, bf16[256,1024]{1,0:T(8,128)(2,1)S(1)} %copy-done.67, bf16[256,1024]{1,0:T(8,128)(2,1)S(1)} %copy-done.69, bf16[256,1024]{1,0:T(8,128)(2,1)S(1)} %copy-done.71, bf16[256,1024]{1,0:T(8,128)(2,1)S(1)} %convolution_convert_fusion.g_ref), custom_call_target="tpu_custom_call" | custom-call | flops 167772160 | bytes 917504 | tf_op jit(solution)/shard_map/pallas_call | solution.py:424
  407.2 32.4 %collective-permute-done.55 = bf16[1024,1024]{1,0:T(8,128)(2,1)S(1)} collective-permute-done((bf16[1024,1024]{1,0:T(8,128)(2,1)S(1)}, bf16[1024,1024]{1,0:T(8,128)(2,1)S(1)}, u32[]{:S(2)}, u32[]{:S(2)}) %collective-permute-start.55) | collective-permute-done | bytes 2097184 | tf_op jit(solution)/shard_map/ppermute | solution.py:504
  460.9 19.9 %collective-permute-done.92.refs_3_ = bf16[512,1024]{1,0:T(8,128)(2,1)S(1)} collective-permute-done((bf16[512,1024]{1,0:T(8,128)(2,1)S(1)}, bf16[512,1024]{1,0:T(8,128)(2,1)S(1)}, u32[]{:S(2)}, u32[]{:S(2)}) %collective-permute-start.92) | collective-permute-done | bytes 1048608 | tf_op jit(solution)/shard_map/ppermute | solution.py:504
  493.8 12.4 %collective-permute-start.56 = (bf16[1024,512]{1,0:T(8,128)(2,1)S(1)}, bf16[1024,512]{1,0:T(8,128)(2,1)S(1)}, u32[]{:S(2)}, u32[]{:S(2)}) collective-permute-start(bf16[1024,512]{1,0:T(8,128)(2,1)S(1)} %shard_map.289), channel_id=1, source_target_pairs={{0,4},{1,5},{2,6},{3,7},{12,8},{13,9},{14,10},{15,11},{16,20},{17,... | collective-permute-start | bytes 3145736 | tf_op jit(solution)/shard_map/ppermute | solution.py:504
  515.2 11.2 %collective-permute-done.94.refs_1_ = bf16[1024,1024]{1,0:T(8,128)(2,1)S(1)} collective-permute-done((bf16[1024,1024]{1,0:T(8,128)(2,1)S(1)}, bf16[1024,1024]{1,0:T(8,128)(2,1)S(1)}, u32[]{:S(2)}, u32[]{:S(2)}) %collective-permute-start.94) | collective-permute-done | bytes 2097184 | tf_op jit(solution)/shard_map/ppermute | solution.py:504
  559.4 16.3 %collective-permute-done.57 = bf16[1024,768]{1,0:T(8,128)(2,1)S(1)} collective-permute-done((bf16[1024,768]{1,0:T(8,128)(2,1)S(1)}, bf16[1024,768]{1,0:T(8,128)(2,1)S(1)}, u32[]{:S(2)}, u32[]{:S(2)}) %collective-permute-start.57) | collective-permute-done | bytes 1572896 | tf_op jit(solution)/shard_map/ppermute | solution.py:504
  585.7 12.9 %shard_map.284.refs_4_ = f32[256,1024]{1,0:T(8,128)S(1)} custom-call(s32[3]{0:T(128)S(1)} %pad_add_fusion.3.table_ref, bf16[256,3072]{1,0:T(8,128)(2,1)} %pad_maximum_fusion.left_ref, bf16[1024,6144]{1,0:T(8,128)(2,1)} %refs_3_.17, bf16[1024,6144]{1,0:T(8,128)(2,1)} %refs_3_.17, bf16[1024,6144]{1,0:T(8,128)(2,1)} %refs_3_.17, bf16[1024,6144]{1,0:T(8,128)(2,1)} %refs_3_.17), custom_call_target="tpu_custom_call" | custom-call | flops 402653184 | bytes 2490368 | tf_op jit(solution)/shard_map/pallas_call | solution.py:277
  599.0 13.0 %shard_map.285.mine_ref = f32[256,1024]{1,0:T(8,128)S(1)} custom-call(s32[3]{0:T(128)S(1)} %pad_add_fusion.2.table_ref, bf16[256,3072]{1,0:T(8,128)(2,1)} %collective-permute-done.22.left_ref, bf16[1024,6144]{1,0:T(8,128)(2,1)} %refs_3_.17, bf16[1024,6144]{1,0:T(8,128)(2,1)} %refs_3_.17, bf16[1024,6144]{1,0:T(8,128)(2,1)} %refs_3_.17, ...), custom_call_target="tpu_custom_call" | custom-call | flops 402653184 | bytes 2490368 | tf_op jit(solution)/shard_map/pallas_call | solution.py:277
  646.3 20.4 %collective-permute-done.116 = f32[192,128]{1,0:T(8,128)S(1)} collective-permute-done((f32[192,128]{1,0:T(8,128)S(1)}, f32[192,128]{1,0:T(8,128)S(1)}, u32[]{:S(2)}, u32[]{:S(2)}) %collective-permute-start.116) | collective-permute-done | bytes 98336 | tf_op jit(solution)/shard_map/ppermute | solution.py:762
  719.1 24.8 %collective-permute-done.76 = bf16[512,768]{1,0:T(8,128)(2,1)S(1)} collective-permute-done((bf16[512,768]{1,0:T(8,128)(2,1)}, bf16[512,768]{1,0:T(8,128)(2,1)S(1)}, u32[]{:S(2)}, u32[]{:S(2)}) %collective-permute-start.76) | collective-permute-done | bytes 786464 | tf_op jit(solution)/shard_map/ppermute | solution.py:504
  744.7 12.4 %collective-permute-done.77 = bf16[512,768]{1,0:T(8,128)(2,1)S(1)} collective-permute-done((bf16[512,768]{1,0:T(8,128)(2,1)}, bf16[512,768]{1,0:T(8,128)(2,1)S(1)}, u32[]{:S(2)}, u32[]{:S(2)}) %collective-permute-start.77) | collective-permute-done | bytes 786464 | tf_op jit(solution)/shard_map/ppermute | solution.py:504
  775.2 18.6 %collective-permute-done.78 = bf16[1024,768]{1,0:T(8,128)(2,1)S(1)} collective-permute-done((bf16[1024,768]{1,0:T(8,128)(2,1)S(1)}, bf16[1024,768]{1,0:T(8,128)(2,1)S(1)}, u32[]{:S(2)}, u32[]{:S(2)}) %collective-permute-start.78) | collective-permute-done | bytes 1572896 | tf_op jit(solution)/shard_map/ppermute | solution.py:504
  798.8 17.3 %collective-permute-done.81 = bf16[512,768]{1,0:T(8,128)(2,1)S(1)} collective-permute-done((bf16[512,768]{1,0:T(8,128)(2,1)S(1)}, bf16[512,768]{1,0:T(8,128)(2,1)S(1)}, u32[]{:S(2)}, u32[]{:S(2)}) %collective-permute-start.81) | collective-permute-done | bytes 786464 | tf_op jit(solution)/shard_map/ppermute | solution.py:504
  816.2 11.3 %collective-permute-done.112 = bf16[512,768]{1,0:T(8,128)(2,1)S(1)} collective-permute-done((bf16[512,768]{1,0:T(8,128)(2,1)S(1)}, bf16[512,768]{1,0:T(8,128)(2,1)S(1)}, u32[]{:S(2)}, u32[]{:S(2)}) %collective-permute-start.112) | collective-permute-done | bytes 786464 | tf_op jit(solution)/shard_map/ppermute | solution.py:504
  827.6 9.5 %shard_map.304.refs_7_ = f32[1024,6144]{1,0:T(8,128)} custom-call(s32[96]{0:T(128)S(1)} %stack.161.table_ref, bf16[1024,768]{1,0:T(8,128)(2,1)S(1)} %broadcast_select_fusion.3.refs_0_, bf16[512,768]{1,0:T(8,128)(2,1)S(1)} %broadcast_select_fusion.10.refs_1_, bf16[512,768]{1,0:T(8,128)(2,1)S(1)} %collective-permute-done.107.refs_2_, ...), custom_call_target="tpu_custom_call", output_to_operand_aliasing={{}: (8, {})} | custom-call | bytes 4718592 | tf_op jit(solution)/shard_map/pallas_call | solution.py:469
  841.2 10.0 %collective-permute-done.113.refs_5_ = bf16[512,768]{1,0:T(8,128)(2,1)S(1)} collective-permute-done((bf16[512,768]{1,0:T(8,128)(2,1)S(1)}, bf16[512,768]{1,0:T(8,128)(2,1)S(1)}, u32[]{:S(2)}, u32[]{:S(2)}) %collective-permute-start.113) | collective-permute-done | bytes 786464 | tf_op jit(solution)/shard_map/ppermute | solution.py:504
  851.5 9.5 %shard_map.305 = f32[1024,6144]{1,0:T(8,128)} custom-call(s32[96]{0:T(128)S(1)} %stack.123.table_ref, bf16[1024,768]{1,0:T(8,128)(2,1)S(1)} %broadcast_select_fusion.4.refs_0_, bf16[512,768]{1,0:T(8,128)(2,1)S(1)} %broadcast_select_fusion.11.refs_1_, bf16[512,768]{1,0:T(8,128)(2,1)S(1)} %collective-permute-done.110.refs_2_, ...), custom_call_target="tpu_custom_call", output_to_operand_aliasing={{}: (8, {})} | custom-call | bytes 4718592 | tf_op jit(solution)/shard_map/pallas_call | solution.py:469
  (587 shorter events, 500.0 us)
Async XLA Ops:
  229.8 53.4 %collective-permute-start.53 = (bf16[1024,1024]{1,0:T(8,128)(2,1)}, bf16[1024,1024]{1,0:T(8,128)(2,1)}, u32[]{:S(2)}, u32[]{:S(2)}) collective-permute-start(bf16[1024,1024]{1,0:T(8,128)(2,1)} %shard_map.292), channel_id=1, source_target_pairs={{0,4},{1,5},{2,6},{3,7},{12,8},{13,9},{14,10},{15,11},{16,20},{17,... | collective-permute-start | bytes 6291464 | tf_op jit(solution)/shard_map/ppermute | solution.py:504
  287.7 54.1 %collective-permute-start.61 = (bf16[1024,1024]{1,0:T(8,128)(2,1)}, bf16[1024,1024]{1,0:T(8,128)(2,1)}, u32[]{:S(2)}, u32[]{:S(2)}) collective-permute-start(bf16[1024,1024]{1,0:T(8,128)(2,1)} %add.639), channel_id=1, source_target_pairs={{4,8},{5,9},{6,10},{7,11},{8,4},{9,5},{10,6},{11,7},{20,24},{21,25... | collective-permute-start | bytes 6291464 | tf_op jit(solution)/shard_map/ppermute | solution.py:504
  346.3 48.5 %collective-permute-start.71 = (bf16[1024,1024]{1,0:T(8,128)(2,1)}, bf16[1024,1024]{1,0:T(8,128)(2,1)}, u32[]{:S(2)}, u32[]{:S(2)}) collective-permute-start(bf16[1024,1024]{1,0:T(8,128)(2,1)} %add.647), channel_id=1, source_target_pairs={{4,0},{5,1},{6,2},{7,3},{8,12},{9,13},{10,14},{11,15},{20,16},{21,... | collective-permute-start | bytes 6291464 | tf_op jit(solution)/shard_map/ppermute | solution.py:504
  391.1 48.5 %collective-permute-start.55 = (bf16[1024,1024]{1,0:T(8,128)(2,1)S(1)}, bf16[1024,1024]{1,0:T(8,128)(2,1)S(1)}, u32[]{:S(2)}, u32[]{:S(2)}) collective-permute-start(bf16[1024,1024]{1,0:T(8,128)(2,1)S(1)} %shard_map.290), channel_id=1, source_target_pairs={{0,4},{1,5},{2,6},{3,7},{12,8},{13,9},{14,10},{15,11},{16,20},{17,... | collective-permute-start | bytes 6291464 | tf_op jit(solution)/shard_map/ppermute | solution.py:504
  399.5 54.6 %collective-permute-start.90 = (bf16[1024,1024]{1,0:T(8,128)(2,1)}, bf16[1024,1024]{1,0:T(8,128)(2,1)}, u32[]{:S(2)}, u32[]{:S(2)}) collective-permute-start(bf16[1024,1024]{1,0:T(8,128)(2,1)} %broadcast_select_fusion.refs_0_), channel_id=1, source_target_pairs={{0,1},{1,0},{2,3},{3,2},{4,5},{5,4},{6,7},{7,6},{8,9},{9,8},{10,11... | collective-permute-start | bytes 6291464 | tf_op jit(solution)/shard_map/ppermute | solution.py:504
  400.5 54.9 %collective-permute-start.91 = (bf16[1024,1024]{1,0:T(8,128)(2,1)}, bf16[1024,1024]{1,0:T(8,128)(2,1)}, u32[]{:S(2)}, u32[]{:S(2)}) collective-permute-start(bf16[1024,1024]{1,0:T(8,128)(2,1)} %broadcast_select_fusion.refs_0_), channel_id=1, source_target_pairs={{0,2},{1,3},{2,0},{3,1},{4,6},{5,7},{6,4},{7,5},{8,10},{9,11},{10,... | collective-permute-start | bytes 6291464 | tf_op jit(solution)/shard_map/ppermute | solution.py:504
  405.8 53.2 %collective-permute-start.72 = (bf16[1024,1024]{1,0:T(8,128)(2,1)}, bf16[1024,1024]{1,0:T(8,128)(2,1)}, u32[]{:S(2)}, u32[]{:S(2)}) collective-permute-start(bf16[1024,1024]{1,0:T(8,128)(2,1)} %add.646), channel_id=1, source_target_pairs={{4,0},{5,1},{6,2},{7,3},{8,12},{9,13},{10,14},{11,15},{20,16},{21,... | collective-permute-start | bytes 6291464 | tf_op jit(solution)/shard_map/ppermute | solution.py:504
  441.8 41.8 %collective-permute-start.63 = (bf16[1024,1024]{1,0:T(8,128)(2,1)}, bf16[1024,1024]{1,0:T(8,128)(2,1)}, u32[]{:S(2)}, u32[]{:S(2)}) collective-permute-start(bf16[1024,1024]{1,0:T(8,128)(2,1)} %add.637), channel_id=1, source_target_pairs={{4,8},{5,9},{6,10},{7,11},{8,4},{9,5},{10,6},{11,7},{20,24},{21,25... | collective-permute-start | bytes 6291464 | tf_op jit(solution)/shard_map/ppermute | solution.py:504
  481.3 45.1 %collective-permute-start.94 = (bf16[1024,1024]{1,0:T(8,128)(2,1)S(1)}, bf16[1024,1024]{1,0:T(8,128)(2,1)S(1)}, u32[]{:S(2)}, u32[]{:S(2)}) collective-permute-start(bf16[1024,1024]{1,0:T(8,128)(2,1)S(1)} %broadcast_select_fusion.1.refs_0_), channel_id=1, source_target_pairs={{0,1},{1,0},{2,3},{3,2},{4,5},{5,4},{6,7},{7,6},{8,9},{9,8},{10,11... | collective-permute-start | bytes 6291464 | tf_op jit(solution)/shard_map/ppermute | solution.py:504
  482.3 45.2 %collective-permute-start.95 = (bf16[1024,1024]{1,0:T(8,128)(2,1)S(1)}, bf16[1024,1024]{1,0:T(8,128)(2,1)S(1)}, u32[]{:S(2)}, u32[]{:S(2)}) collective-permute-start(bf16[1024,1024]{1,0:T(8,128)(2,1)S(1)} %broadcast_select_fusion.1.refs_0_), channel_id=1, source_target_pairs={{0,2},{1,3},{2,0},{3,1},{4,6},{5,7},{6,4},{7,5},{8,10},{9,11},{10,... | collective-permute-start | bytes 6291464 | tf_op jit(solution)/shard_map/ppermute | solution.py:504
  486.9 56.5 %collective-permute-start.73 = (bf16[1024,1024]{1,0:T(8,128)(2,1)S(1)}, bf16[1024,1024]{1,0:T(8,128)(2,1)S(1)}, u32[]{:S(2)}, u32[]{:S(2)}) collective-permute-start(bf16[1024,1024]{1,0:T(8,128)(2,1)S(1)} %add.645), channel_id=1, source_target_pairs={{4,0},{5,1},{6,2},{7,3},{8,12},{9,13},{10,14},{11,15},{20,16},{21,... | collective-permute-start | bytes 6291464 | tf_op jit(solution)/shard_map/ppermute | solution.py:504
  542.9 56.1 %collective-permute-start.22 = (bf16[256,3072]{1,0:T(8,128)(2,1)}, bf16[256,3072]{1,0:T(8,128)(2,1)}, u32[]{:S(2)}, u32[]{:S(2)}) collective-permute-start(bf16[256,3072]{1,0:T(8,128)(2,1)} %pad_maximum_fusion.left_ref), channel_id=1, source_target_pairs={{0,16},{16,0},{1,17},{17,1},{2,18},{18,2},{3,19},{19,3},{4,20},{20... | collective-permute-start | bytes 4718600 | tf_op jit(solution)/shard_map/ppermute | solution.py:542
  552.6 82.8 %collective-permute-start.98 = (bf16[1024,1024]{1,0:T(8,128)(2,1)}, bf16[1024,1024]{1,0:T(8,128)(2,1)}, u32[]{:S(2)}, u32[]{:S(2)}) collective-permute-start(bf16[1024,1024]{1,0:T(8,128)(2,1)} %broadcast_select_fusion.2.refs_0_), channel_id=1, source_target_pairs={{0,1},{1,0},{2,3},{3,2},{4,5},{5,4},{6,7},{7,6},{8,9},{9,8},{10,11... | collective-permute-start | bytes 6291464 | tf_op jit(solution)/shard_map/ppermute | solution.py:504
  553.9 82.8 %collective-permute-start.99 = (bf16[1024,1024]{1,0:T(8,128)(2,1)}, bf16[1024,1024]{1,0:T(8,128)(2,1)}, u32[]{:S(2)}, u32[]{:S(2)}) collective-permute-start(bf16[1024,1024]{1,0:T(8,128)(2,1)} %broadcast_select_fusion.2.refs_0_), channel_id=1, source_target_pairs={{0,2},{1,3},{2,0},{3,1},{4,6},{5,7},{6,4},{7,5},{8,10},{9,11},{10,... | collective-permute-start | bytes 6291464 | tf_op jit(solution)/shard_map/ppermute | solution.py:504
  575.7 41.6 %collective-permute-start.58 = (bf16[1024,768]{1,0:T(8,128)(2,1)}, bf16[1024,768]{1,0:T(8,128)(2,1)}, u32[]{:S(2)}, u32[]{:S(2)}) collective-permute-start(bf16[1024,768]{1,0:T(8,128)(2,1)} %shard_map.287), channel_id=1, source_target_pairs={{0,4},{1,5},{2,6},{3,7},{12,8},{13,9},{14,10},{15,11},{16,20},{17,... | collective-permute-start | bytes 4718600 | tf_op jit(solution)/shard_map/ppermute | solution.py:504
  620.7 66.3 %collective-permute-start.66 = (bf16[1024,768]{1,0:T(8,128)(2,1)}, bf16[1024,768]{1,0:T(8,128)(2,1)}, u32[]{:S(2)}, u32[]{:S(2)}) collective-permute-start(bf16[1024,768]{1,0:T(8,128)(2,1)} %add.634), channel_id=1, source_target_pairs={{4,8},{5,9},{6,10},{7,11},{8,4},{9,5},{10,6},{11,7},{20,24},{21,25... | collective-permute-start | bytes 4718600 | tf_op jit(solution)/shard_map/ppermute | solution.py:504
  638.0 41.0 %collective-permute-start.100 = (bf16[512,1024]{1,0:T(8,128)(2,1)S(1)}, bf16[512,1024]{1,0:T(8,128)(2,1)S(1)}, u32[]{:S(2)}, u32[]{:S(2)}) collective-permute-start(bf16[512,1024]{1,0:T(8,128)(2,1)S(1)} %slice.224), channel_id=1, source_target_pairs={{0,2},{1,3},{2,0},{3,1},{4,6},{5,7},{6,4},{7,5},{8,10},{9,11},{10,... | collective-permute-start | bytes 3145736 | tf_op jit(solution)/shard_map/ppermute | solution.py:504
  645.0 47.9 %collective-permute-start.75 = (bf16[1024,768]{1,0:T(8,128)(2,1)}, bf16[1024,768]{1,0:T(8,128)(2,1)}, u32[]{:S(2)}, u32[]{:S(2)}) collective-permute-start(bf16[1024,768]{1,0:T(8,128)(2,1)} %add.643), channel_id=1, source_target_pairs={{4,0},{5,1},{6,2},{7,3},{8,12},{9,13},{10,14},{11,15},{20,16},{21,... | collective-permute-start | bytes 4718600 | tf_op jit(solution)/shard_map/ppermute | solution.py:504
  692.3 72.1 %collective-permute-start.119 = (f32[192,128]{1,0:T(8,128)S(1)}, f32[192,128]{1,0:T(8,128)S(1)}, u32[]{:S(2)}, u32[]{:S(2)}) collective-permute-start(f32[192,128]{1,0:T(8,128)S(1)} %add.677), channel_id=1, source_target_pairs={{4,8},{5,9},{6,10},{7,11},{8,4},{9,5},{10,6},{11,7},{20,24},{21,25... | collective-permute-start | bytes 294920 | tf_op jit(solution)/shard_map/ppermute | solution.py:765
  693.0 51.0 %collective-permute-start.76 = (bf16[512,768]{1,0:T(8,128)(2,1)}, bf16[512,768]{1,0:T(8,128)(2,1)S(1)}, u32[]{:S(2)}, u32[]{:S(2)}) collective-permute-start(bf16[512,768]{1,0:T(8,128)(2,1)} %collective-permute-done.67), channel_id=1, source_target_pairs={{4,0},{5,1},{6,2},{7,3},{8,12},{9,13},{10,14},{11,15},{20,16},{21,... | collective-permute-start | bytes 2359304 | tf_op jit(solution)/shard_map/ppermute | solution.py:504
  694.3 62.8 %collective-permute-start.77 = (bf16[512,768]{1,0:T(8,128)(2,1)}, bf16[512,768]{1,0:T(8,128)(2,1)S(1)}, u32[]{:S(2)}, u32[]{:S(2)}) collective-permute-start(bf16[512,768]{1,0:T(8,128)(2,1)} %collective-permute-done.68), channel_id=1, source_target_pairs={{4,0},{5,1},{6,2},{7,3},{8,12},{9,13},{10,14},{11,15},{20,16},{21,... | collective-permute-start | bytes 2359304 | tf_op jit(solution)/shard_map/ppermute | solution.py:504
  717.7 45.3 %collective-permute-start.106 = (bf16[512,768]{1,0:T(8,128)(2,1)S(1)}, bf16[512,768]{1,0:T(8,128)(2,1)S(1)}, u32[]{:S(2)}, u32[]{:S(2)}) collective-permute-start(bf16[512,768]{1,0:T(8,128)(2,1)S(1)} %get-tuple-element.235), channel_id=1, source_target_pairs={{0,2},{1,3},{2,0},{3,1},{4,6},{5,7},{6,4},{7,5},{8,10},{9,11},{10,... | collective-permute-start | bytes 2359304 | tf_op jit(solution)/shard_map/ppermute | solution.py:504
  718.0 45.8 %collective-permute-start.107 = (bf16[512,768]{1,0:T(8,128)(2,1)S(1)}, bf16[512,768]{1,0:T(8,128)(2,1)S(1)}, u32[]{:S(2)}, u32[]{:S(2)}) collective-permute-start(bf16[512,768]{1,0:T(8,128)(2,1)S(1)} %get-tuple-element.236), channel_id=1, source_target_pairs={{0,1},{1,0},{2,3},{3,2},{4,5},{5,4},{6,7},{7,6},{8,9},{9,8},{10,11... | collective-permute-start | bytes 2359304 | tf_op jit(solution)/shard_map/ppermute | solution.py:504
  796.9 43.2 %collective-permute-start.27 = (f32[128,2048]{1,0:T(8,128)S(1)}, f32[128,2048]{1,0:T(8,128)S(1)}, u32[]{:S(2)}, u32[]{:S(2)}) collective-permute-start(f32[128,2048]{1,0:T(8,128)S(1)} %slice.207), channel_id=1, source_target_pairs={{0,16},{16,0},{1,17},{17,1},{2,18},{18,2},{3,19},{19,3},{4,20},{20... | collective-permute-start | bytes 3145736 | tf_op jit(solution)/shard_map/ppermute | solution.py:542
  (210 other events, 2755.4 us)

commit v3 on v2

--- a/solution.py
+++ b/solution.py
@@ -11,8 +11,8 @@
 TILE = 128
 LAYER = 12
 LINE = 4
-STREAMS = 4
-LATE = 2
+STREAMS = 1
+LATE = ("up",)
 GROUP = 4
 F32 = jnp.float32
 LOW = jnp.bfloat16
@@ -174,6 +174,9 @@
     length, tall = lefts[0].shape
 
     def spec(right):
+        if isinstance(right, tuple):
+            _, index, count = right
+            return pl.BlockSpec((count, block), lambda j: (index, first + j))
         if right.ndim == 3:
             return pl.BlockSpec((1, right.shape[1], block), lambda j: (first + j, 0, 0))
         return pl.BlockSpec((right.shape[0], block), lambda j: (0, first + j))
@@ -191,7 +194,7 @@
         cost_estimate=estimate(
             2 * tall * total * steps * block, 2 * total * (tall + steps * block)
         ),
-    )(*lefts, *rights)
+    )(*lefts, *[r[0] if isinstance(r, tuple) else r for r in rights])
 
 
 def hold(values, after):
@@ -487,11 +490,11 @@
     pass
 
 
-def blank(shape):
+def blank(shape, dtype=F32):
     return pl.pallas_call(
         blank_kernel,
         out_specs=pl.BlockSpec(memory_space=pl.ANY),
-        out_shape=jax.ShapeDtypeStruct(shape, F32),
+        out_shape=jax.ShapeDtypeStruct(shape, dtype),
     )()
 
 
@@ -560,9 +563,7 @@
         )
 
     def exchange(blocks):
-        (far_one,) = across.send([(blocks[3], in_plane(3))])
-        near = across.send([(blocks[1], in_plane(1)), (blocks[2], in_plane(2))])
-        return [blocks[0], *near, far_one]
+        return blocks[:1] + across.send([(blocks[d], in_plane(d)) for d in range(1, GROUP)])
 
     def gather_group(value):
         return exchange([value] * GROUP)
@@ -626,6 +627,14 @@
     first_row = (core * rows).astype(jnp.int32)[None]
     full, part, line = (rows, width), (rows, half), (1, width)
 
+    always = exit_layers[0, 1] > 0
+
+    def segment(steps, *operands):
+        def skip(*_):
+            return [blank(shape.shape, shape.dtype) for shape in jax.eval_shape(steps, *operands)]
+
+        return lax.cond(always, lambda *o: list(steps(*o)), skip, *operands)
+
     mine, theirs, down_grad, down_sums = by_rows(
         norm_one_kernel,
         core_number,
@@ -636,105 +645,150 @@
         cotangent[0],
         active,
     )
-    normed_one_half = jnp.concatenate([mine, swap(theirs)])
-    down_grad_all = jnp.concatenate([down_grad, swap(down_grad)])
     down_mine = gather_group(down_grad)
-    block = min(512, half)
-    count = half // block
-
-    def qkv_table(c):
-        return jnp.concatenate([table(count, (2 * p + c) * count) for p in range(3)])
-
-    theirs = times_columns(normed_one_half, qkv_weight, qkv_table(other), block, LOW)
-    theirs = hold(swap(theirs), down_mine[3])
-    mine = times_columns(normed_one_half, qkv_weight, qkv_table(core), block, F32)
+    qkv_block = min(1024, half)
+    qkv_count = half // qkv_block
     bias = jnp.stack([query_bias, jnp.zeros_like(query_bias), value_bias])
     bias = lax.dynamic_slice_in_dim(bias, core * half, half, 1).reshape(1, -1)
-    queries, keys, values, attended = attend_forward(first_row, mine, theirs, bias)
-    out_part = dot(attended, out_weight, 1, 0)
-    middle, mine, theirs = by_rows(
-        norm_two_kernel,
-        core_number,
-        [(full, F32), (part, LOW), (part, LOW)],
-        hidden[0],
-        active,
-        out_part,
-        swap(out_part[rows:]),
-        out_bias[None],
-        ffn_gain[None],
-        ffn_shift[None],
-    )
-    theirs = hold(theirs, down_mine[1:3])
+
+    def qkv_table(c):
+        return jnp.concatenate(
+            [table(qkv_count, (2 * p + c) * qkv_count) for p in range(3)]
+        )
+
+    def to_attended(mine, theirs, down_grad, qkv_weight, bias, my_table, their_table, first_row):
+        normed = jnp.concatenate([mine, swap(theirs)])
+        theirs = times_columns(normed, qkv_weight, their_table, qkv_block, LOW)
+        theirs = swap(theirs)
+        mine = times_columns(normed, qkv_weight, my_table, qkv_block, F32)
+        results = attend_forward(first_row, mine, theirs, bias)
+        return [normed, *results, swap(down_grad)]
+
+    normed_one_half, queries, keys, values, attended, down_grad_theirs = segment(
+        to_attended, mine, theirs, down_grad, qkv_weight, bias,
+        qkv_table(core), qkv_table(other), first_row,
+    )
+    attended, down_mine = lax.optimization_barrier((attended, down_mine))
     qkv_left = gather_group(normed_one_half)
-    down_theirs = [swap(g) for g in down_mine]
-    normed_two_half = jnp.concatenate([mine, swap(theirs)])
-    count = inner_half // block
-    theirs = times_columns(
-        normed_two_half, up_weight, table(count, other * count), block, LOW
-    )
-    theirs = hold(swap(theirs), qkv_left[3])
-    mine = times_columns(normed_two_half, up_weight, table(count, core * count), block, F32)
-    bias = lax.dynamic_slice_in_dim(up_bias, core * inner_half, inner_half).reshape(1, -1)
-    inner_low, up_grad, up_sums = inner_layer(
-        down_grad_all, down_weight, mine, theirs, bias, block
-    )
-
-    down_left = scatter_group(inner_low, 1, inner_half // GROUP)
-    up_right = scatter_group(up_grad, 1, inner_half // GROUP)
     block = min(1024, inner_half)
     count = inner_half // block
-    up_grad_theirs = swap(up_grad)
-    grads = times_back(up_grad, up_weight, table(count, core * count), block, 512)
-    grads = times_back(
-        up_grad_theirs, up_weight, table(count, other * count), block, 512, grads, True
-    )
-    middle_grad, attn_grad, attn_sums, gain_two_grad, shift_two_grad = by_rows(
-        norm_two_back_kernel,
-        core_number,
-        [(full, F32), (full, LOW), (line, F32), (line, F32), (line, F32)],
-        middle,
-        ffn_gain[None],
-        grads,
-        swap(grads[rows:]),
-        cotangent[0],
-        active,
-    )
-    attn_grad_all = jnp.concatenate([attn_grad, swap(attn_grad)])
-    head_grads = dot(attn_grad_all, out_weight, 1, 1).astype(LOW)
+
+    def to_inner(
+        hidden, active, attended, out_weight, lines, up_weight, tables, core_number,
+        grads, down_weight,
+    ):
+        out_part = dot(attended, out_weight, 1, 0)
+        middle, mine, theirs = by_rows(
+            norm_two_kernel,
+            core_number,
+            [(full, F32), (part, LOW), (part, LOW)],
+            hidden,
+            active,
+            out_part,
+            swap(out_part[rows:]),
+            *lines[:3],
+        )
+        normed = jnp.concatenate([mine, swap(theirs)])
+        theirs = times_columns(normed, up_weight, tables[1], block, LOW)
+        theirs = swap(theirs)
+        mine = times_columns(normed, up_weight, tables[0], block, F32)
+        results = inner_layer(
+            grads, down_weight, mine, theirs, lines[3], min(512, inner_half)
+        )
+        return [middle, normed, *results]
+
+    bias = lax.dynamic_slice_in_dim(up_bias, core * inner_half, inner_half).reshape(1, -1)
+    middle, normed_two_half, inner_low, up_grad, up_sums = segment(
+        to_inner, hidden[0], active, attended, out_weight,
+        (out_bias[None], ffn_gain[None], ffn_shift[None], bias), up_weight,
+        (table(count, core * count), table(count, other * count)), core_number,
+        jnp.concatenate([down_grad, down_grad_theirs]), down_weight,
+    )
+    (inner_low, up_grad), qkv_left = lax.optimization_barrier(((inner_low, up_grad), qkv_left))
+
+    down_left = scatter_group(inner_low, 1, inner_half // GROUP)
+
+    def to_middle(
+        up_grad, up_weight, middle, gain, cotangent, active, core_number, down_mine, tables
+    ):
+        theirs = swap(up_grad)
+        grads = times_back(up_grad, up_weight, tables[0], inner_half, 256)
+        grads = times_back(theirs, up_weight, tables[1], inner_half, 256, grads, True)
+        results = by_rows(
+            norm_two_back_kernel,
+            core_number,
+            [(full, F32), (full, LOW), (line, F32), (line, F32), (line, F32)],
+            middle,
+            gain,
+            grads,
+            swap(grads[rows:]),
+            cotangent,
+            active,
+        )
+        return [*results, swap(jnp.concatenate(down_mine[1:]))]
+
+    middle_grad, attn_grad, attn_sums, gain_two_grad, shift_two_grad, down_theirs = segment(
+        to_middle, up_grad, up_weight, middle, ffn_gain[None], cotangent[0], active,
+        core_number, down_mine, (table(1, core), table(1, other)),
+    )
+    down_theirs = [down_grad_theirs] + [(down_theirs, d, rows) for d in range(GROUP - 1)]
     down_right = pairs(down_mine, down_theirs)
-    down_left = hold(down_left, attn_grad)
     quarter = width // 4
-    down_parts = [rows_product(down_left, down_right, quarter, 0, 1)]
-    head_grads = hold(head_grads, down_parts)
-    qkv_grad = attend_backward(first_row, queries, keys, values, head_grads)
-    down_parts[0] = line_start(down_parts[0], qkv_grad)
-    qkv_grad = hold(qkv_grad, up_right[3])
+    down_left, attn_grad = lax.optimization_barrier((down_left, attn_grad))
+    up_right = scatter_group(up_grad, 1, inner_half // GROUP)
+    sums = [rows_product(down_left, down_right, quarter, 0, 1)]
+    (come,) = first_hop.send([(sums[0], inward)])
+    attn_grad, sums[0] = lax.optimization_barrier((attn_grad, sums[0]))
+
+    def to_qkv(attn_grad, out_weight, first_row, *operands):
+        grads = jnp.concatenate([attn_grad, swap(attn_grad)])
+        grads = dot(grads, out_weight, 1, 1).astype(LOW)
+        qkv_grad = attend_backward(first_row, *operands, grads)
+        flat = jnp.concatenate([qkv_grad[0], qkv_grad[1], qkv_grad[2]], 1)
+        return [qkv_grad, flat, swap(flat)]
+
+    qkv_grad, flat, flat_theirs = segment(to_qkv, attn_grad, out_weight, first_row, queries, keys, values)
+    qkv_grad, up_right, come, sums = lax.optimization_barrier((qkv_grad, up_right, come, sums))
+    sums[0] += come
+    (passed,) = middle_hop.send([(sums[0], middle_moves)])
     up_left = gather_group(normed_two_half)
+
+    def to_input(flat, theirs, qkv_weight, tables):
+        grads = times_back(flat, qkv_weight, tables[0], qkv_block, 512)
+        return [times_back(theirs, qkv_weight, tables[1], qkv_block, 512, grads, True)]
+
+    (grads,) = segment(
+        to_input, hold(flat, qkv_grad), flat_theirs, qkv_weight,
+        (qkv_table(core), qkv_table(other)),
+    )
+    grads, up_left, passed = lax.optimization_barrier((grads, up_left, passed))
+    sums[0] = line_end(sums[0] + passed)
+    for part_index in range(1, 4):
+        value = rows_product(down_left, down_right, quarter, part_index, 1)
+        sums.append(line_start(hold(value, grads)))
     out_right = scatter_group(attn_grad, 1, width // GROUP)
     out_left = gather_group(attended)
     qkv_right = scatter_group(qkv_grad, 2, half // GROUP)
-    flat = jnp.concatenate([qkv_grad[0], qkv_grad[1], qkv_grad[2]], 1)
-    flat_theirs = swap(flat)
-    block = min(1024, half)
-    count = half // block
-
-    def qkv_table(c):
-        return jnp.concatenate([table(count, (2 * p + c) * count) for p in range(3)])
-
-    grads = times_back(flat, qkv_weight, qkv_table(core), block, 512)
-    grads = times_back(flat_theirs, qkv_weight, qkv_table(other), block, 512, grads, True)
-    input_grad, gain_one_grad, shift_one_grad = by_rows(
-        norm_one_back_kernel,
-        core_number,
-        [(full, LOW), (line, F32), (line, F32)],
-        hidden[0],
-        attn_gain[None],
-        grads,
-        hold(swap(grads[rows:]), up_right[1:3]),
-        middle_grad,
-    )
-    down_part = dot(hold(inner_low, (input_grad, up_left[3])), down_weight, 1, 0)
-    output = middle + active * (down_part[:rows] + swap(down_part[rows:]) + down_bias)
+
+    def to_ends(grads, hidden, gain, middle_grad, core_number, inner_low, down_weight):
+        results = by_rows(
+            norm_one_back_kernel,
+            core_number,
+            [(full, LOW), (line, F32), (line, F32)],
+            hidden,
+            gain,
+            grads,
+            swap(grads[rows:]),
+            middle_grad,
+        )
+        down_part = dot(inner_low, down_weight, 1, 0)
+        return [*results, down_part[:rows], swap(down_part[rows:])]
+
+    input_grad, gain_one_grad, shift_one_grad, mine, theirs = segment(
+        to_ends, hold(grads, sums[0]), hidden[0], attn_gain[None], middle_grad, core_number,
+        inner_low, down_weight,
+    )
+    output = middle + active * (mine + theirs + down_bias)
 
     def widen(value):
         none = jnp.zeros_like(value)
@@ -770,11 +824,7 @@
         small_grads.append(small[first : first + size])
         first += size
 
-    chunks = [("down", down_parts[0], 0)]
-    value = rows_product(down_left, down_right, quarter, 1, 1)
-    chunks.append(("down", line_start(value), 1))
-    value = rows_product(down_left, down_right, quarter, 2, 2)
-    chunks.append(("down", line_start(value), 1))
+    chunks = [("down", value, index) for index, value in enumerate(sums)]
     size = inner_half // GROUP
     block = min(512, size)
     value = rows_product(up_left, up_right, block, 0, size // block)
@@ -782,15 +832,15 @@
     theirs = [swap(r) for r in up_right]
     value = rows_product(up_left, theirs, block, 0, size // block, True)
     chunks.append(("up", line_start(value), other))
-    right = pairs(out_right, [swap(r) for r in out_right])
-    value = rows_product(out_left, right, width // GROUP, 0, 1)
-    chunks.append(("out", line_start(value), 0))
     size = half // GROUP
     value = rows_product(qkv_left, qkv_right, size, 0, 3)
     chunks.append(("qkv", line_start(value), core))
     theirs = [swap(r) for r in qkv_right]
     value = rows_product(qkv_left, theirs, size, 0, 3, True)
     chunks.append(("qkv", line_start(value), other))
+    right = pairs(out_right, [swap(r) for r in out_right])
+    value = rows_product(out_left, right, width // GROUP, 0, 1)
+    chunks.append(("out", line_start(value), 0))
 
     wholes = {
         "down": blank((inner_half, width)),
@@ -800,12 +850,13 @@
     }
     done = [(), ()]
     for index, (name, value, where) in enumerate(chunks):
-        value = line_middle(value)
-        after = done[-2], (done[-1], small if index == 3 else ())
-        if plane == GROUP and index >= len(chunks) - LATE:
-            pieces = spread_late(value, after)
+        after = done[-2], small if index == 3 else ()
+        if index == 0:
+            pieces = spread(blocks_sum(value), after)
+        elif plane == GROUP and name in LATE:
+            pieces = spread_late(line_middle(value), after)
         else:
-            pieces = spread(blocks_sum(line_end(value)), after)
+            pieces = spread(blocks_sum(line_end(line_middle(value))), after)
         tall, wide = value.shape
         high = min(256, tall)
         broad = wide // 3 if name == "qkv" else wide

time: 873 us -> 807 us (0.924)
  waiting for transfers between devices: 361 us -> 252 us
  starting transfers between devices: 160 us -> 191 us
  Pallas kernels: 210 us -> 185 us
  other arithmetic: 58.5 us -> 74.7 us
  local copies, waits for them, and re-layouts: 55.6 us -> 67.4 us
    ppermute x88 -> x95, waiting for transfers between devices: 329 us -> 205 us  [send(): self.last = [lax.ppermute(v, 'dp', m) for v, (_, m) in zip(values, sends)]]
    pallas_call x4, Pallas kernels: 59.5 us -> 26.7 us  [times_back(): pl.pallas_call(functools.partial(back_kernel, turned), grid_spec=pltpu.Pr...]
    ppermute x88 -> x95, starting transfers between devices: 146 us -> 177 us  [send(): self.last = [lax.ppermute(v, 'dp', m) for v, (_, m) in zip(values, sends)]]
    ppermute x28 -> x26, waiting for transfers between devices: 7.59 us -> 19.3 us  [swap(): return lax.ppermute(value, 'sp', [(0, 1), (1, 0)])]
    pallas_call x8 -> x9, Pallas kernels: 27.8 us -> 33.6 us  [rows_product(): pl.pallas_call(functools.partial(product_kernel, len(lefts), turned), gri...]
    pallas_call x8 -> x9, Pallas kernels: 56.1 us -> 61.8 us  [place(): pl.pallas_call(functools.partial(place_kernel, high), in_specs=[pl.BlockS...]
    unnamed x234 -> x195, local copies, waits for them, and re-layouts: 34.8 us -> 29.7 us
  transfers between devices with their start and end apart: 121 -> 126, of which waited for: 56 -> 47; matrix products, arithmetic and copies ran while one was open for 10% -> 15% of each run, Pallas kernels for 19% -> 22%
where the time goes in v3:
time: 807 us; the launch traced here: 792 us
  waiting for transfers between devices  252 us (31%)
  starting transfers between devices  191 us (24%)
  Pallas kernels  185 us (23%)
  other arithmetic  74.7 us (9%)
  local copies, waits for them, and re-layouts  67.4 us (8%)
  matrix products  16 us (2%)
    ppermute x95, waiting for transfers between devices, send(): self.last = [lax.ppermute(v, 'dp', m) for v, (_, m) in zip(values, sends)]  205 us
    ppermute x95, starting transfers between devices, send(): self.last = [lax.ppermute(v, 'dp', m) for v, (_, m) in zip(values, sends)]  177 us
    pallas_call x9, Pallas kernels, place(): pl.pallas_call(functools.partial(place_kernel, high), in_specs=[pl.BlockS...  61.8 us
    pallas_call x9, Pallas kernels, rows_product(): pl.pallas_call(functools.partial(product_kernel, len(lefts), turned), gri...  33.6 us
    unnamed x195, local copies, waits for them, and re-layouts  29.7 us
    pallas_call x4, Pallas kernels, times_back(): pl.pallas_call(functools.partial(back_kernel, turned), grid_spec=pltpu.Pr...  26.7 us
    pallas_call x4, Pallas kernels, times_columns(): pl.pallas_call(columns_kernel, grid_spec=pltpu.PrefetchScalarGridSpec(num...  24.2 us
    ppermute x2, waiting for transfers between devices, per_device(): small = small + lax.ppermute(small, 'dp', in_plane(distance))  23.5 us
  transfers between devices with their start and end apart: 126, of which 47 were waited for; matrix products, arithmetic and copies ran while one was open for 15% of the time, Pallas kernels for 22%

profile of v3, /device:TPU:0, one launch (start us, length us, event | category | flops | bytes accessed | tf_op | source)
XLA Modules:
  0.0 792.2 jit_solution(2949229927379526894)
XLA Ops:
  13.4 20.0 %conditional.6 = (bf16[256,1024]{1,0:T(8,128)(2,1)}, bf16[256,1024]{1,0:T(8,128)(2,1)}, bf16[256,1024]{1,0:T(8,128)(2,1)}, bf16[256,1024]{1,0:T(8,128)(2,1)}, bf...) conditional(s32[]{:T(128)} %convert_element_type.30, () %tuple.141, (bf16[128,1024]{1,0:T(8,128)(2,1)S(1)}, ...), branch_computations={%region_0.1_spmd, %region_1.2_spmd} | conditional | flops 872415232 | bytes 17613018 | solution.py:636
  41.0 37.7 %conditional.7 = (f32[128,2048]{1,0:T(8,128)}, bf16[256,1024]{1,0:T(8,128)(2,1)}, bf16[256,4096]{1,0:T(8,128)(2,1)}, bf16[256,4096]{1,0:T(8,128)(2,1)}, f32[4096...) conditional(s32[]{:T(128)} %convert_element_type.30, () %tuple.140, (bf16[256,1024]{1,0:T(8,128)(2,1)}, ...), branch_computations={%region_2.3_spmd, %region_3.4_spmd} | conditional | flops 3222536192 | bytes 43063800 | solution.py:636
  64.6 13.4 %branch_1_fun.20 = (bf16[256,4096]{1,0:T(8,128)(2,1)}, bf16[256,4096]{1,0:T(8,128)(2,1)}, f32[1,4096]{1,0:T(1,128)}) custom-call(bf16[256,2048]{1,0:T(8,128)(2,1)S(1)} %copy-done.84, bf16[4096,2048]{1,0:T(8,128)(2,1)} %get-tuple-element.185.refs_0_, f32[256,4096]{1,0:T(8,128)S(1)} %branch_1_fun.18.refs_1_, ...), custom_call_target="tpu_custom_call" | custom-call | flops 1073741824 | bytes 7602176 | tf_op jit(solution)/shard_map/cond/branch_1_fun/pallas_call | solution.py:314
  85.4 19.5 %conditional.8 = (f32[128,2048]{1,0:T(8,128)}, bf16[128,2048]{1,0:T(8,128)(2,1)}, bf16[384,2048]{1,0:T(8,128)(2,1)}, f32[2048]{0:T(1024)}, f32[2048]{0:T(1024)}, /*index=5*/f32[2048]{0:T(1024)}) conditional(s32[]{:T(128)} %convert_element_type.30, () %tuple.152, (bf16[256,4096]{1,0:T(8,128)(2,1)}, s32[1]{0:T(128)}, bf16[1024,8192]{1,0:T(8,128)(2,1)}, ...), branch_computations={%region_4.5_spmd, %region_5.6_spmd} | conditional | flops 1079771136 | bytes 30148932 | solution.py:636
  122.1 21.0 %conditional.9 = (bf16[3,256,1024]{2,1,0:T(8,128)(2,1)}, bf16[256,3072]{1,0:T(8,128)(2,1)}, bf16[256,3072]{1,0:T(8,128)(2,1)}) conditional(s32[]{:T(128)} %convert_element_type.30, () %tuple.150, (bf16[128,2048]{1,0:T(8,128)(2,1)}, bf16[1024,2048]{1,0:T(8,128)(2,1)}, s32[1]{0:T(128)}, bf16[256,1024]{1,0:T(8,128)(2,1)}, bf16[256,1024]{1,0:T(8,128)(2,1)}, ...), branch_computations={%region_6.7_spmd, %region_7.8_spmd} | conditional | flops 1248591872 | bytes 40239292 | solution.py:636
  127.8 10.3 %branch_1_fun.24 = bf16[3,256,1024]{2,1,0:T(8,128)(2,1)S(1)} custom-call(s32[1]{0:T(128)} %get-tuple-element.212.first_ref, bf16[256,1024]{1,0:T(8,128)(2,1)} %get-tuple-element.213.q_ref, bf16[256,1024]{1,0:T(8,128)(2,1)} %get-tuple-element.214.k_ref, bf16[256,1024]{1,0:T(8,128)(2,1)} %get-tuple-element.215.v_ref, ...), custom_call_target="tpu_custom_call" | custom-call | flops 167772160 | bytes 917504 | tf_op jit(solution)/shard_map/cond/branch_1_fun/pallas_call | solution.py:427
  154.8 14.8 %conditional.10 = (f32[256,1024]{1,0:T(8,128)}) conditional(s32[]{:T(128)} %convert_element_type.30, () %tuple.149, (s32[3]{0:T(128)S(1)}, bf16[256,3072]{1,0:T(8,128)(2,1)}, bf16[1024,6144]{1,0:T(8,128)(2,1)}, s32[3]{0:T(128)S(1)}, bf16[256,3072]{1,0:T(8,128)(2,1)}) %tuple.160), branch_computations={%region_8.9_spmd, %region_9.10_spmd} | conditional | flops 805306368 | bytes 11272228 | solution.py:636
  179.4 16.5 %collective-permute-done.48 = bf16[1024,512]{1,0:T(8,128)(2,1)} collective-permute-done((bf16[1024,512]{1,0:T(8,128)(2,1)}, bf16[1024,512]{1,0:T(8,128)(2,1)}, u32[]{:S(2)}, u32[]{:S(2)}) %collective-permute-start.48) | collective-permute-done | bytes 1048608 | tf_op jit(solution)/shard_map/ppermute | solution.py:507
  240.3 14.7 %collective-permute-done.36.refs_2_ = bf16[256,1024]{1,0:T(8,128)(2,1)S(1)} collective-permute-done((bf16[256,1024]{1,0:T(8,128)(2,1)}, bf16[256,1024]{1,0:T(8,128)(2,1)S(1)}, u32[]{:S(2)}, u32[]{:S(2)}) %collective-permute-start.36) | collective-permute-done | bytes 524320 | tf_op jit(solution)/shard_map/ppermute | solution.py:507
  284.0 13.7 %collective-permute-done.77.refs_1_ = bf16[1024,512]{1,0:T(8,128)(2,1)S(1)} collective-permute-done((bf16[1024,512]{1,0:T(8,128)(2,1)S(1)}, bf16[1024,512]{1,0:T(8,128)(2,1)S(1)}, u32[]{:S(2)}, u32[]{:S(2)}) %collective-permute-start.77) | collective-permute-done | bytes 1048608 | tf_op jit(solution)/shard_map/ppermute | solution.py:507
  301.7 9.1 %collective-permute-done.79.refs_3_ = bf16[512,512]{1,0:T(8,128)(2,1)S(1)} collective-permute-done((bf16[512,512]{1,0:T(8,128)(2,1)S(1)}, bf16[512,512]{1,0:T(8,128)(2,1)S(1)}, u32[]{:S(2)}, u32[]{:S(2)}) %collective-permute-start.79) | collective-permute-done | bytes 524320 | tf_op jit(solution)/shard_map/ppermute | solution.py:507
  326.8 10.3 %collective-permute-done.81.refs_1_ = bf16[1024,512]{1,0:T(8,128)(2,1)S(1)} collective-permute-done((bf16[1024,512]{1,0:T(8,128)(2,1)S(1)}, bf16[1024,512]{1,0:T(8,128)(2,1)S(1)}, u32[]{:S(2)}, u32[]{:S(2)}) %collective-permute-start.81) | collective-permute-done | bytes 1048608 | tf_op jit(solution)/shard_map/ppermute | solution.py:507
  403.6 15.3 %collective-permute-done.69 = bf16[1024,1024]{1,0:T(8,128)(2,1)} collective-permute-done((bf16[1024,1024]{1,0:T(8,128)(2,1)}, bf16[1024,1024]{1,0:T(8,128)(2,1)}, u32[]{:S(2)}, u32[]{:S(2)}) %collective-permute-start.69) | collective-permute-done | bytes 2097184 | tf_op jit(solution)/shard_map/ppermute | solution.py:507
  440.3 26.8 %collective-permute-start.53 = (bf16[1024,768]{1,0:T(8,128)(2,1)S(1)}, bf16[1024,768]{1,0:T(8,128)(2,1)S(1)}, u32[]{:S(2)}, u32[]{:S(2)}) collective-permute-start(bf16[1024,768]{1,0:T(8,128)(2,1)S(1)} %shard_map.277), channel_id=1, source_target_pairs={{0,4},{1,5},{2,6},{3,7},{12,8},{13,9},{14,10},{15,11},{16,20},{17,... | collective-permute-start | bytes 4718600 | tf_op jit(solution)/shard_map/ppermute | solution.py:507
  476.6 16.0 %collective-permute-done.93.refs_3_ = bf16[512,1024]{1,0:T(8,128)(2,1)S(1)} collective-permute-done((bf16[512,1024]{1,0:T(8,128)(2,1)S(1)}, bf16[512,1024]{1,0:T(8,128)(2,1)S(1)}, u32[]{:S(2)}, u32[]{:S(2)}) %collective-permute-start.93) | collective-permute-done | bytes 1048608 | tf_op jit(solution)/shard_map/ppermute | solution.py:507
  510.3 11.8 %collective-permute-start.54 = (bf16[1024,768]{1,0:T(8,128)(2,1)}, bf16[1024,768]{1,0:T(8,128)(2,1)}, u32[]{:S(2)}, u32[]{:S(2)}) collective-permute-start(bf16[1024,768]{1,0:T(8,128)(2,1)} %shard_map.276), channel_id=1, source_target_pairs={{0,4},{1,5},{2,6},{3,7},{12,8},{13,9},{14,10},{15,11},{16,20},{17,... | collective-permute-start | bytes 4718600 | tf_op jit(solution)/shard_map/ppermute | solution.py:507
  551.7 20.6 %collective-permute-done.74 = bf16[512,1024]{1,0:T(8,128)(2,1)} collective-permute-done((bf16[512,1024]{1,0:T(8,128)(2,1)}, bf16[512,1024]{1,0:T(8,128)(2,1)}, u32[]{:S(2)}, u32[]{:S(2)}) %collective-permute-start.74) | collective-permute-done | bytes 1048608 | tf_op jit(solution)/shard_map/ppermute | solution.py:507
  599.9 9.2 %collective-permute-done.75 = bf16[1024,768]{1,0:T(8,128)(2,1)} collective-permute-done((bf16[1024,768]{1,0:T(8,128)(2,1)}, bf16[1024,768]{1,0:T(8,128)(2,1)}, u32[]{:S(2)}, u32[]{:S(2)}) %collective-permute-start.75) | collective-permute-done | bytes 1572896 | tf_op jit(solution)/shard_map/ppermute | solution.py:507
  631.8 12.8 %collective-permute-done.101.refs_1_ = bf16[1024,768]{1,0:T(8,128)(2,1)S(1)} collective-permute-done((bf16[1024,768]{1,0:T(8,128)(2,1)S(1)}, bf16[1024,768]{1,0:T(8,128)(2,1)S(1)}, u32[]{:S(2)}, u32[]{:S(2)}) %collective-permute-start.101) | collective-permute-done | bytes 1572896 | tf_op jit(solution)/shard_map/ppermute | solution.py:507
  675.3 16.4 %conditional.11 = (f32[128,2048]{1,0:T(8,128)}, f32[128,2048]{1,0:T(8,128)}, bf16[1,128,2048]{2,1,0:T(8,128)(2,1)}, f32[2048]{0:T(1024)S(1)}, f32[2048]{0:T(1024)S(1)}) conditional(s32[]{:T(128)} %convert_element_type.30, () %tuple.146, (bf16[256,4096]{1,0:T(8,128)(2,1)}, bf16[4096,2048]{1,0:T(8,128)(2,1)}, f32[256,1024]{1,0:T(8,128)}, ...), branch_computations={%region_10.11_spmd, %region_11.12_spmd} | conditional | flops 4296278016 | bytes 47974632 | solution.py:636
  691.7 11.8 %collective-permute-done.105.refs_1_ = bf16[1024,768]{1,0:T(8,128)(2,1)S(1)} collective-permute-done((bf16[1024,768]{1,0:T(8,128)(2,1)S(1)}, bf16[1024,768]{1,0:T(8,128)(2,1)S(1)}, u32[]{:S(2)}, u32[]{:S(2)}) %collective-permute-start.105) | collective-permute-done | bytes 1572896 | tf_op jit(solution)/shard_map/ppermute | solution.py:507
  713.3 10.3 %shard_map.292.refs_5_ = f32[1024,6144]{1,0:T(8,128)} custom-call(s32[96]{0:T(128)S(1)} %stack.162.table_ref, bf16[1024,768]{1,0:T(8,128)(2,1)S(1)} %copy-done.3, bf16[1024,768]{1,0:T(8,128)(2,1)S(1)} %copy-done.15, bf16[1024,768]{1,0:T(8,128)(2,1)S(1)} %copy-done.17, ...), custom_call_target="tpu_custom_call", output_to_operand_aliasing={{}: (6, {})} | custom-call | bytes 4718592 | tf_op jit(solution)/shard_map/pallas_call | solution.py:472
  729.6 23.4 %collective-permute-done.122 = f32[192,128]{1,0:T(8,128)S(1)} collective-permute-done((f32[192,128]{1,0:T(8,128)S(1)}, f32[192,128]{1,0:T(8,128)S(1)}, u32[]{:S(2)}, u32[]{:S(2)}) %collective-permute-start.122) | collective-permute-done | bytes 98336 | tf_op jit(solution)/shard_map/ppermute | solution.py:816
  775.5 10.8 %shard_map.293 = f32[1024,6144]{1,0:T(8,128)} custom-call(s32[96]{0:T(128)S(1)} %stack.127.table_ref, bf16[1024,768]{1,0:T(8,128)(2,1)S(1)} %broadcast_select_fusion.3.refs_0_, bf16[1024,768]{1,0:T(8,128)(2,1)S(1)} %copy-done.13, bf16[1024,768]{1,0:T(8,128)(2,1)} %collective-permute-done.106.refs_2_, ...), custom_call_target="tpu_custom_call", output_to_operand_aliasing={{}: (6, {})} | custom-call | bytes 4718592 | tf_op jit(solution)/shard_map/pallas_call | solution.py:472
  (593 shorter events, 530.3 us)
Async XLA Ops:
  35.2 43.5 %collective-permute-start.16 = (bf16[256,1024]{1,0:T(8,128)(2,1)}, bf16[256,1024]{1,0:T(8,128)(2,1)S(1)}, u32[]{:S(2)}, u32[]{:S(2)}) collective-permute-start(bf16[256,1024]{1,0:T(8,128)(2,1)} %get-tuple-element.464.refs_0_), channel_id=1, source_target_pairs={{0,1},{1,0},{2,3},{3,2},{4,5},{5,4},{6,7},{7,6},{8,9},{9,8},{10,11... | collective-permute-start | bytes 1572872 | tf_op jit(solution)/shard_map/ppermute | solution.py:507
  36.4 42.3 %collective-permute-start.17 = (bf16[256,1024]{1,0:T(8,128)(2,1)}, bf16[256,1024]{1,0:T(8,128)(2,1)S(1)}, u32[]{:S(2)}, u32[]{:S(2)}) collective-permute-start(bf16[256,1024]{1,0:T(8,128)(2,1)} %get-tuple-element.464.refs_0_), channel_id=1, source_target_pairs={{0,2},{1,3},{2,0},{3,1},{4,6},{5,7},{6,4},{7,5},{8,10},{9,11},{10,... | collective-permute-start | bytes 1572872 | tf_op jit(solution)/shard_map/ppermute | solution.py:507
  37.2 41.5 %collective-permute-start.18 = (bf16[256,1024]{1,0:T(8,128)(2,1)}, bf16[256,1024]{1,0:T(8,128)(2,1)}, u32[]{:S(2)}, u32[]{:S(2)}) collective-permute-start(bf16[256,1024]{1,0:T(8,128)(2,1)} %get-tuple-element.464.refs_0_), channel_id=1, source_target_pairs={{0,3},{1,2},{2,1},{3,0},{4,7},{5,6},{6,5},{7,4},{8,11},{9,10},{10,... | collective-permute-start | bytes 1572872 | tf_op jit(solution)/shard_map/ppermute | solution.py:507
  216.0 43.4 %collective-permute-start.30 = (bf16[1024,512]{1,0:T(8,128)(2,1)}, bf16[1024,512]{1,0:T(8,128)(2,1)}, u32[]{:S(2)}, u32[]{:S(2)}) collective-permute-start(bf16[1024,512]{1,0:T(8,128)(2,1)} %add.258), channel_id=1, source_target_pairs={{4,0},{5,1},{6,2},{7,3},{8,12},{9,13},{10,14},{11,15},{20,16},{21,... | collective-permute-start | bytes 3145736 | tf_op jit(solution)/shard_map/ppermute | solution.py:507
  223.6 43.7 %collective-permute-start.55 = (bf16[1024,512]{1,0:T(8,128)(2,1)}, bf16[1024,512]{1,0:T(8,128)(2,1)}, u32[]{:S(2)}, u32[]{:S(2)}) collective-permute-start(bf16[1024,512]{1,0:T(8,128)(2,1)} %add.288), channel_id=1, source_target_pairs={{4,8},{5,9},{6,10},{7,11},{8,4},{9,5},{10,6},{11,7},{20,24},{21,25... | collective-permute-start | bytes 3145736 | tf_op jit(solution)/shard_map/ppermute | solution.py:507
  225.4 42.6 %collective-permute-start.50 = (bf16[1024,512]{1,0:T(8,128)(2,1)}, bf16[1024,512]{1,0:T(8,128)(2,1)}, u32[]{:S(2)}, u32[]{:S(2)}) collective-permute-start(bf16[1024,512]{1,0:T(8,128)(2,1)} %shard_map.280), channel_id=1, source_target_pairs={{0,4},{1,5},{2,6},{3,7},{12,8},{13,9},{14,10},{15,11},{16,20},{17,... | collective-permute-start | bytes 3145736 | tf_op jit(solution)/shard_map/ppermute | solution.py:507
  268.1 44.6 %collective-permute-start.51 = (bf16[1024,1024]{1,0:T(8,128)(2,1)S(1)}, bf16[1024,1024]{1,0:T(8,128)(2,1)S(1)}, u32[]{:S(2)}, u32[]{:S(2)}) collective-permute-start(bf16[1024,1024]{1,0:T(8,128)(2,1)S(1)} %shard_map.279), channel_id=1, source_target_pairs={{0,4},{1,5},{2,6},{3,7},{12,8},{13,9},{14,10},{15,11},{16,20},{17,... | collective-permute-start | bytes 6291464 | tf_op jit(solution)/shard_map/ppermute | solution.py:507
  318.1 40.3 %collective-permute-start.58 = (bf16[1024,1024]{1,0:T(8,128)(2,1)}, bf16[1024,1024]{1,0:T(8,128)(2,1)}, u32[]{:S(2)}, u32[]{:S(2)}) collective-permute-start(bf16[1024,1024]{1,0:T(8,128)(2,1)} %add.285), channel_id=1, source_target_pairs={{4,8},{5,9},{6,10},{7,11},{8,4},{9,5},{10,6},{11,7},{20,24},{21,25... | collective-permute-start | bytes 6291464 | tf_op jit(solution)/shard_map/ppermute | solution.py:507
  342.6 50.1 %collective-permute-start.52 = (bf16[1024,1024]{1,0:T(8,128)(2,1)S(1)}, bf16[1024,1024]{1,0:T(8,128)(2,1)}, u32[]{:S(2)}, u32[]{:S(2)}) collective-permute-start(bf16[1024,1024]{1,0:T(8,128)(2,1)S(1)} %shard_map.278), channel_id=1, source_target_pairs={{0,4},{1,5},{2,6},{3,7},{12,8},{13,9},{14,10},{15,11},{16,20},{17,... | collective-permute-start | bytes 6291464 | tf_op jit(solution)/shard_map/ppermute | solution.py:507
  371.8 47.1 %collective-permute-start.69 = (bf16[1024,1024]{1,0:T(8,128)(2,1)}, bf16[1024,1024]{1,0:T(8,128)(2,1)}, u32[]{:S(2)}, u32[]{:S(2)}) collective-permute-start(bf16[1024,1024]{1,0:T(8,128)(2,1)} %add.292), channel_id=1, source_target_pairs={{4,0},{5,1},{6,2},{7,3},{8,12},{9,13},{10,14},{11,15},{20,16},{21,... | collective-permute-start | bytes 6291464 | tf_op jit(solution)/shard_map/ppermute | solution.py:507
  396.7 70.6 %collective-permute-start.59 = (bf16[1024,1024]{1,0:T(8,128)(2,1)}, bf16[1024,1024]{1,0:T(8,128)(2,1)}, u32[]{:S(2)}, u32[]{:S(2)}) collective-permute-start(bf16[1024,1024]{1,0:T(8,128)(2,1)} %add.284), channel_id=1, source_target_pairs={{4,8},{5,9},{6,10},{7,11},{8,4},{9,5},{10,6},{11,7},{20,24},{21,25... | collective-permute-start | bytes 6291464 | tf_op jit(solution)/shard_map/ppermute | solution.py:507
  418.9 49.0 %collective-permute-start.70 = (bf16[512,1024]{1,0:T(8,128)(2,1)}, bf16[512,1024]{1,0:T(8,128)(2,1)}, u32[]{:S(2)}, u32[]{:S(2)}) collective-permute-start(bf16[512,1024]{1,0:T(8,128)(2,1)} %collective-permute-done.62), channel_id=1, source_target_pairs={{4,0},{5,1},{6,2},{7,3},{8,12},{9,13},{10,14},{11,15},{20,16},{21,... | collective-permute-start | bytes 3145736 | tf_op jit(solution)/shard_map/ppermute | solution.py:507
  420.2 49.4 %collective-permute-start.71 = (bf16[512,1024]{1,0:T(8,128)(2,1)}, bf16[512,1024]{1,0:T(8,128)(2,1)}, u32[]{:S(2)}, u32[]{:S(2)}) collective-permute-start(bf16[512,1024]{1,0:T(8,128)(2,1)} %collective-permute-done.63), channel_id=1, source_target_pairs={{4,0},{5,1},{6,2},{7,3},{8,12},{9,13},{10,14},{11,15},{20,16},{21,... | collective-permute-start | bytes 3145736 | tf_op jit(solution)/shard_map/ppermute | solution.py:507
  440.3 61.0 %collective-permute-start.53 = (bf16[1024,768]{1,0:T(8,128)(2,1)S(1)}, bf16[1024,768]{1,0:T(8,128)(2,1)S(1)}, u32[]{:S(2)}, u32[]{:S(2)}) collective-permute-start(bf16[1024,768]{1,0:T(8,128)(2,1)S(1)} %shard_map.277), channel_id=1, source_target_pairs={{0,4},{1,5},{2,6},{3,7},{12,8},{13,9},{14,10},{15,11},{16,20},{17,... | collective-permute-start | bytes 4718600 | tf_op jit(solution)/shard_map/ppermute | solution.py:507
  472.8 50.4 %collective-permute-start.72 = (bf16[1024,1024]{1,0:T(8,128)(2,1)S(1)}, bf16[1024,1024]{1,0:T(8,128)(2,1)S(1)}, u32[]{:S(2)}, u32[]{:S(2)}) collective-permute-start(bf16[1024,1024]{1,0:T(8,128)(2,1)S(1)} %add.291), channel_id=1, source_target_pairs={{4,0},{5,1},{6,2},{7,3},{8,12},{9,13},{10,14},{11,15},{20,16},{21,... | collective-permute-start | bytes 6291464 | tf_op jit(solution)/shard_map/ppermute | solution.py:507
  503.5 43.0 %collective-permute-start.60 = (bf16[1024,768]{1,0:T(8,128)(2,1)}, bf16[1024,768]{1,0:T(8,128)(2,1)}, u32[]{:S(2)}, u32[]{:S(2)}) collective-permute-start(bf16[1024,768]{1,0:T(8,128)(2,1)} %add.283), channel_id=1, source_target_pairs={{4,8},{5,9},{6,10},{7,11},{8,4},{9,5},{10,6},{11,7},{20,24},{21,25... | collective-permute-start | bytes 4718600 | tf_op jit(solution)/shard_map/ppermute | solution.py:507
  510.3 63.2 %collective-permute-start.54 = (bf16[1024,768]{1,0:T(8,128)(2,1)}, bf16[1024,768]{1,0:T(8,128)(2,1)}, u32[]{:S(2)}, u32[]{:S(2)}) collective-permute-start(bf16[1024,768]{1,0:T(8,128)(2,1)} %shard_map.276), channel_id=1, source_target_pairs={{0,4},{1,5},{2,6},{3,7},{12,8},{13,9},{14,10},{15,11},{16,20},{17,... | collective-permute-start | bytes 4718600 | tf_op jit(solution)/shard_map/ppermute | solution.py:507
  527.0 45.2 %collective-permute-start.74 = (bf16[512,1024]{1,0:T(8,128)(2,1)}, bf16[512,1024]{1,0:T(8,128)(2,1)}, u32[]{:S(2)}, u32[]{:S(2)}) collective-permute-start(bf16[512,1024]{1,0:T(8,128)(2,1)} %collective-permute-done.65), channel_id=1, source_target_pairs={{4,0},{5,1},{6,2},{7,3},{8,12},{9,13},{10,14},{11,15},{20,16},{21,... | collective-permute-start | bytes 3145736 | tf_op jit(solution)/shard_map/ppermute | solution.py:507
  545.9 37.7 %collective-permute-start.97 = (bf16[512,1024]{1,0:T(8,128)(2,1)S(1)}, bf16[512,1024]{1,0:T(8,128)(2,1)S(1)}, u32[]{:S(2)}, u32[]{:S(2)}) collective-permute-start(bf16[512,1024]{1,0:T(8,128)(2,1)S(1)} %get-tuple-element.537), channel_id=1, source_target_pairs={{0,2},{1,3},{2,0},{3,1},{4,6},{5,7},{6,4},{7,5},{8,10},{9,11},{10,... | collective-permute-start | bytes 3145736 | tf_op jit(solution)/shard_map/ppermute | solution.py:507
  546.6 38.1 %collective-permute-start.98 = (bf16[512,1024]{1,0:T(8,128)(2,1)S(1)}, bf16[512,1024]{1,0:T(8,128)(2,1)S(1)}, u32[]{:S(2)}, u32[]{:S(2)}) collective-permute-start(bf16[512,1024]{1,0:T(8,128)(2,1)S(1)} %get-tuple-element.538), channel_id=1, source_target_pairs={{0,1},{1,0},{2,3},{3,2},{4,5},{5,4},{6,7},{7,6},{8,9},{9,8},{10,11... | collective-permute-start | bytes 3145736 | tf_op jit(solution)/shard_map/ppermute | solution.py:507
  616.4 49.6 %collective-permute-start.76 = (bf16[1024,768]{1,0:T(8,128)(2,1)}, bf16[1024,768]{1,0:T(8,128)(2,1)}, u32[]{:S(2)}, u32[]{:S(2)}) collective-permute-start(bf16[1024,768]{1,0:T(8,128)(2,1)} %add.289), channel_id=1, source_target_pairs={{4,0},{5,1},{6,2},{7,3},{8,12},{9,13},{10,14},{11,15},{20,16},{21,... | collective-permute-start | bytes 4718600 | tf_op jit(solution)/shard_map/ppermute | solution.py:507
  673.9 49.7 %collective-permute-start.115 = (bf16[1024,512]{1,0:T(8,128)(2,1)}, bf16[1024,512]{1,0:T(8,128)(2,1)}, u32[]{:S(2)}, u32[]{:S(2)}) collective-permute-start(bf16[1024,512]{1,0:T(8,128)(2,1)} %add.637), channel_id=1, source_target_pairs={{4,0},{5,1},{6,2},{7,3},{8,12},{9,13},{10,14},{11,15},{20,16},{21,... | collective-permute-start | bytes 3145736 | tf_op jit(solution)/shard_map/ppermute | solution.py:507
  726.1 40.9 %collective-permute-start.116 = (bf16[1024,512]{1,0:T(8,128)(2,1)S(1)}, bf16[1024,512]{1,0:T(8,128)(2,1)}, u32[]{:S(2)}, u32[]{:S(2)}) collective-permute-start(bf16[1024,512]{1,0:T(8,128)(2,1)S(1)} %broadcast_select_fusion.8.refs_0_), channel_id=1, source_target_pairs={{0,1},{1,0},{2,3},{3,2},{4,5},{5,4},{6,7},{7,6},{8,9},{9,8},{10,11... | collective-permute-start | bytes 3145736 | tf_op jit(solution)/shard_map/ppermute | solution.py:507
  727.5 40.7 %collective-permute-start.117 = (bf16[1024,512]{1,0:T(8,128)(2,1)S(1)}, bf16[1024,512]{1,0:T(8,128)(2,1)}, u32[]{:S(2)}, u32[]{:S(2)}) collective-permute-start(bf16[1024,512]{1,0:T(8,128)(2,1)S(1)} %broadcast_select_fusion.8.refs_0_), channel_id=1, source_target_pairs={{0,2},{1,3},{2,0},{3,1},{4,6},{5,7},{6,4},{7,5},{8,10},{9,11},{10,... | collective-permute-start | bytes 3145736 | tf_op jit(solution)/shard_map/ppermute | solution.py:507
  (208 other events, 2512.8 us)

commit v4 on v3

--- a/solution.py
+++ b/solution.py
@@ -12,7 +12,7 @@
 LAYER = 12
 LINE = 4
 STREAMS = 1
-LATE = ("up",)
+LATE = ()
 GROUP = 4
 F32 = jnp.float32
 LOW = jnp.bfloat16
@@ -568,11 +568,13 @@
     def gather_group(value):
         return exchange([value] * GROUP)
 
-    def scatter_group(value, axis, size):
-        blocks = [
+    def blocks_of(value, axis, size):
+        return [
             lax.dynamic_slice_in_dim(value, (spot ^ d) * size, size, axis) for d in range(GROUP)
         ]
-        return exchange(blocks)
+
+    def scatter_group(value, axis, size):
+        return exchange(blocks_of(value, axis, size))
 
     def pairs(mine, theirs):
         return [piece for pair in zip(mine, theirs) for piece in pair]
@@ -725,9 +727,12 @@
             cotangent,
             active,
         )
-        return [*results, swap(jnp.concatenate(down_mine[1:]))]
-
-    middle_grad, attn_grad, attn_sums, gain_two_grad, shift_two_grad, down_theirs = segment(
+        down_theirs = swap(jnp.concatenate(down_mine[1:]))
+        return [*results, down_theirs, *blocks_of(up_grad, 1, inner_half // GROUP)]
+
+    (
+        middle_grad, attn_grad, attn_sums, gain_two_grad, shift_two_grad, down_theirs, *up_right
+    ) = segment(
         to_middle, up_grad, up_weight, middle, ffn_gain[None], cotangent[0], active,
         core_number, down_mine, (table(1, core), table(1, other)),
     )
@@ -735,7 +740,7 @@
     down_right = pairs(down_mine, down_theirs)
     quarter = width // 4
     down_left, attn_grad = lax.optimization_barrier((down_left, attn_grad))
-    up_right = scatter_group(up_grad, 1, inner_half // GROUP)
+    up_right = exchange(up_right)
     sums = [rows_product(down_left, down_right, quarter, 0, 1)]
     (come,) = first_hop.send([(sums[0], inward)])
     attn_grad, sums[0] = lax.optimization_barrier((attn_grad, sums[0]))
@@ -745,9 +750,10 @@
         grads = dot(grads, out_weight, 1, 1).astype(LOW)
         qkv_grad = attend_backward(first_row, *operands, grads)
         flat = jnp.concatenate([qkv_grad[0], qkv_grad[1], qkv_grad[2]], 1)
-        return [qkv_grad, flat, swap(flat)]
-
-    qkv_grad, flat, flat_theirs = segment(to_qkv, attn_grad, out_weight, first_row, queries, keys, values)
+        blocks = blocks_of(qkv_grad, 2, half // GROUP)
+        return [qkv_grad, flat, swap(flat), *blocks]
+
+    qkv_grad, flat, flat_theirs, *qkv_right = segment(to_qkv, attn_grad, out_weight, first_row, queries, keys, values)
     qkv_grad, up_right, come, sums = lax.optimization_barrier((qkv_grad, up_right, come, sums))
     sums[0] += come
     (passed,) = middle_hop.send([(sums[0], middle_moves)])
@@ -762,13 +768,17 @@
         (qkv_table(core), qkv_table(other)),
     )
     grads, up_left, passed = lax.optimization_barrier((grads, up_left, passed))
-    sums[0] = line_end(sums[0] + passed)
-    for part_index in range(1, 4):
-        value = rows_product(down_left, down_right, quarter, part_index, 1)
-        sums.append(line_start(hold(value, grads)))
-    out_right = scatter_group(attn_grad, 1, width // GROUP)
-    out_left = gather_group(attended)
-    qkv_right = scatter_group(qkv_grad, 2, half // GROUP)
+    sums[0] += passed
+    qkv_right = exchange(qkv_right)
+    value = hold(rows_product(down_left, down_right, quarter, 1, 1), grads)
+    come = first_hop.send([(value, inward)])
+    passed, come, qkv_right = lax.optimization_barrier(
+        (last_hop.send([(sums[0], outward)]), come, qkv_right)
+    )
+    sums[0] = jnp.where(end, passed[0], sums[0])
+    sums.append(value + come[0])
+    for part_index in range(2, 4):
+        sums.append(line_start(rows_product(down_left, down_right, quarter, part_index, 1)))
 
     def to_ends(grads, hidden, gain, middle_grad, core_number, inner_low, down_weight):
         results = by_rows(
@@ -784,8 +794,8 @@
         down_part = dot(inner_low, down_weight, 1, 0)
         return [*results, down_part[:rows], swap(down_part[rows:])]
 
-    input_grad, gain_one_grad, shift_one_grad, mine, theirs = segment(
-        to_ends, hold(grads, sums[0]), hidden[0], attn_gain[None], middle_grad, core_number,
+    input_grad, gain_one_grad, shift_one_grad, mine, theirs = to_ends(
+        hold(grads, sums[0]), hidden[0], attn_gain[None], middle_grad, core_number,
         inner_low, down_weight,
     )
     output = middle + active * (mine + theirs + down_bias)
@@ -817,7 +827,8 @@
         distance *= 2
     small = small + lax.ppermute(small, "dp", inward)
     small = small + lax.ppermute(small, "dp", middle_moves)
-    small = jnp.where(end, lax.ppermute(small, "dp", outward), small).reshape(-1)
+    small_last = lax.ppermute(small, "dp", outward)
+    small = jnp.where(end, small_last, small).reshape(-1)
     small_grads = []
     first = 0
     for size in (width, width, width, inner, width, width, width, width, width):
@@ -838,9 +849,7 @@
     theirs = [swap(r) for r in qkv_right]
     value = rows_product(qkv_left, theirs, size, 0, 3, True)
     chunks.append(("qkv", line_start(value), other))
-    right = pairs(out_right, [swap(r) for r in out_right])
-    value = rows_product(out_left, right, width // GROUP, 0, 1)
-    chunks.append(("out", line_start(value), 0))
+    chunks.append(("out", None, 0))
 
     wholes = {
         "down": blank((inner_half, width)),
@@ -850,13 +859,20 @@
     }
     done = [(), ()]
     for index, (name, value, where) in enumerate(chunks):
-        after = done[-2], small if index == 3 else ()
-        if index == 0:
-            pieces = spread(blocks_sum(value), after)
-        elif plane == GROUP and name in LATE:
-            pieces = spread_late(line_middle(value), after)
+        if name == "out":
+            right = pairs(out_right, [swap(r) for r in out_right])
+            value = line_start(rows_product(out_left, right, width // GROUP, 0, 1))
+        after = done[-2], small_last if index == 2 else ()
+        if index > 0:
+            value = line_middle(value)
+        if plane == GROUP and name in LATE:
+            pieces = spread_late(value, after)
         else:
-            pieces = spread(blocks_sum(line_end(line_middle(value))), after)
+            value = blocks_sum(line_end(value) if index > 0 else value)
+            pieces = spread(value, after)
+        if index == 1:
+            out_right = scatter_group(attn_grad, 1, width // GROUP)
+            out_left = gather_group(attended)
         tall, wide = value.shape
         high = min(256, tall)
         broad = wide // 3 if name == "qkv" else wide

time: 807 us -> 818 us (1.014)
  waiting for transfers between devices: 252 us -> 297 us
  starting transfers between devices: 191 us -> 164 us
    ppermute x95 -> x87, waiting for transfers between devices: 205 us -> 245 us  [send(): self.last = [lax.ppermute(v, 'dp', m) for v, (_, m) in zip(values, sends)]]
    ppermute x95 -> x87, starting transfers between devices: 177 us -> 150 us  [send(): self.last = [lax.ppermute(v, 'dp', m) for v, (_, m) in zip(values, sends)]]
    ppermute x1, waiting for transfers between devices: 2.48 us -> 19.2 us  [per_device(): small_last = lax.ppermute(small, 'dp', outward)]
    ppermute x26, waiting for transfers between devices: 19.3 us -> 10.4 us  [swap(): return lax.ppermute(value, 'sp', [(0, 1), (1, 0)])]
    add x8 -> x7, other arithmetic: 20 us -> 15.7 us  [line_start(): return value + hold(first_hop.send([(value, inward)])[0], after)]
    unnamed x195 -> x227, local copies, waits for them, and re-layouts: 29.7 us -> 29.3 us
  transfers between devices with their start and end apart: 126 -> 118, of which waited for: 47 -> 49; matrix products, arithmetic and copies ran while one was open for 15% -> 15% of each run, Pallas kernels for 22% -> 22%
where the time goes in v4:
time: 818 us; the launch traced here: 807 us
  waiting for transfers between devices  297 us (36%)
  Pallas kernels  185 us (23%)
  starting transfers between devices  164 us (20%)
  other arithmetic  72.2 us (9%)
  local copies, waits for them, and re-layouts  67.6 us (8%)
  matrix products  16 us (2%)
    ppermute x87, waiting for transfers between devices, send(): self.last = [lax.ppermute(v, 'dp', m) for v, (_, m) in zip(values, sends)]  245 us
    ppermute x87, starting transfers between devices, send(): self.last = [lax.ppermute(v, 'dp', m) for v, (_, m) in zip(values, sends)]  150 us
    pallas_call x9, Pallas kernels, place(): pl.pallas_call(functools.partial(place_kernel, high), in_specs=[pl.BlockS...  60.4 us
    pallas_call x9, Pallas kernels, rows_product(): pl.pallas_call(functools.partial(product_kernel, len(lefts), turned), gri...  32.1 us
    unnamed x227, local copies, waits for them, and re-layouts  29.3 us
    pallas_call x4, Pallas kernels, times_back(): pl.pallas_call(functools.partial(back_kernel, turned), grid_spec=pltpu.Pr...  27.4 us
    pallas_call x4, Pallas kernels, times_columns(): pl.pallas_call(columns_kernel, grid_spec=pltpu.PrefetchScalarGridSpec(num...  24.5 us
    add x8, other arithmetic, line_middle(): return value + middle_hop.send([(value, middle_moves)])[0]  19.4 us
  transfers between devices with their start and end apart: 118, of which 49 were waited for; matrix products, arithmetic and copies ran while one was open for 15% of the time, Pallas kernels for 22%

profile of v4, /device:TPU:0, one launch (start us, length us, event | category | flops | bytes accessed | tf_op | source)
XLA Modules:
  0.0 807.1 jit_solution(13230810410787626991)
XLA Ops:
  14.6 20.3 %conditional.5 = (bf16[256,1024]{1,0:T(8,128)(2,1)}, bf16[256,1024]{1,0:T(8,128)(2,1)}, bf16[256,1024]{1,0:T(8,128)(2,1)}, bf16[256,1024]{1,0:T(8,128)(2,1)}, bf...) conditional(s32[]{:T(128)} %convert_element_type.29, () %tuple.121, (bf16[128,1024]{1,0:T(8,128)(2,1)S(1)}, ...), branch_computations={%region_0.1_spmd, %region_1.2_spmd} | conditional | flops 872415232 | bytes 17613018 | solution.py:638
  41.6 37.8 %conditional.6 = (f32[128,2048]{1,0:T(8,128)}, bf16[256,1024]{1,0:T(8,128)(2,1)}, bf16[256,4096]{1,0:T(8,128)(2,1)}, bf16[256,4096]{1,0:T(8,128)(2,1)}, f32[4096...) conditional(s32[]{:T(128)} %convert_element_type.29, () %tuple.120, (bf16[256,1024]{1,0:T(8,128)(2,1)}, ...), branch_computations={%region_2.3_spmd, %region_3.4_spmd} | conditional | flops 3222536192 | bytes 43063800 | solution.py:638
  65.3 13.4 %branch_1_fun.19 = (bf16[256,4096]{1,0:T(8,128)(2,1)}, bf16[256,4096]{1,0:T(8,128)(2,1)}, f32[1,4096]{1,0:T(1,128)}) custom-call(bf16[256,2048]{1,0:T(8,128)(2,1)S(1)} %copy-done.89, bf16[4096,2048]{1,0:T(8,128)(2,1)} %get-tuple-element.172.refs_0_, f32[256,4096]{1,0:T(8,128)S(1)} %branch_1_fun.17.refs_1_, ...), custom_call_target="tpu_custom_call" | custom-call | flops 1073741824 | bytes 7602176 | tf_op jit(solution)/shard_map/cond/branch_1_fun/pallas_call | solution.py:314
  86.1 23.0 %conditional.7 = (f32[128,2048]{1,0:T(8,128)}, bf16[128,2048]{1,0:T(8,128)(2,1)}, bf16[384,2048]{1,0:T(8,128)(2,1)}, bf16[256,1024]{1,0:T(8,128)(2,1)}, bf16[256...) conditional(s32[]{:T(128)} %convert_element_type.29, () %tuple.131, ...), branch_computations={%region_4.5_spmd, %region_5.6_spmd} | conditional | flops 1079771136 | bytes 34343496 | solution.py:638
  119.8 23.0 %conditional.8 = (bf16[3,256,1024]{2,1,0:T(8,128)(2,1)}, bf16[256,3072]{1,0:T(8,128)(2,1)}, bf16[256,3072]{1,0:T(8,128)(2,1)}, bf16[3,256,256]{2,1,0:T(8,128)(2,...) conditional(s32[]{:T(128)} %convert_element_type.29, () %tuple.129, ...), branch_computations={%region_6.7_spmd, %region_7.8_spmd} | conditional | flops 1248591872 | bytes 24510828 | solution.py:638
  125.5 10.8 %branch_1_fun.23 = bf16[3,256,1024]{2,1,0:T(8,128)(2,1)} custom-call(s32[1]{0:T(128)} %get-tuple-element.200.first_ref, bf16[256,1024]{1,0:T(8,128)(2,1)} %get-tuple-element.201.q_ref, bf16[256,1024]{1,0:T(8,128)(2,1)} %get-tuple-element.202.k_ref, bf16[256,1024]{1,0:T(8,128)(2,1)} %get-tuple-element.203.v_ref, ...), custom_call_target="tpu_custom_call" | custom-call | flops 167772160 | bytes 917504 | tf_op jit(solution)/shard_map/cond/branch_1_fun/pallas_call | solution.py:427
  154.2 15.4 %conditional.9 = (f32[256,1024]{1,0:T(8,128)}) conditional(s32[]{:T(128)} %convert_element_type.29, () %tuple.128, (s32[3]{0:T(128)}, bf16[256,3072]{1,0:T(8,128)(2,1)}, bf16[1024,6144]{1,0:T(8,128)(2,1)}, s32[3]{0:T(128)}, bf16[256,3072]{1,0:T(8,128)(2,1)}) %tuple.139), branch_computations={%region_8.9_spmd, %region_9.10_spmd} | conditional | flops 805306368 | bytes 4980744 | solution.py:638
  218.4 9.8 %collective-permute-done.43 = bf16[1024,512]{1,0:T(8,128)(2,1)} collective-permute-done((bf16[1024,512]{1,0:T(8,128)(2,1)S(1)}, bf16[1024,512]{1,0:T(8,128)(2,1)}, u32[]{:S(2)}, u32[]{:S(2)}) %collective-permute-start.43) | collective-permute-done | bytes 1048608 | tf_op jit(solution)/shard_map/ppermute | solution.py:507
  262.8 17.0 %collective-permute-done.67.refs_1_ = bf16[1024,512]{1,0:T(8,128)(2,1)S(1)} collective-permute-done((bf16[1024,512]{1,0:T(8,128)(2,1)S(1)}, bf16[1024,512]{1,0:T(8,128)(2,1)S(1)}, u32[]{:S(2)}, u32[]{:S(2)}) %collective-permute-start.67) | collective-permute-done | bytes 1048608 | tf_op jit(solution)/shard_map/ppermute | solution.py:507
  343.5 8.4 %collective-permute-start.46 = (bf16[1024,1024]{1,0:T(8,128)(2,1)S(1)}, bf16[1024,1024]{1,0:T(8,128)(2,1)}, u32[]{:S(2)}, u32[]{:S(2)}) collective-permute-start(bf16[1024,1024]{1,0:T(8,128)(2,1)S(1)} %shard_map.280), channel_id=1, source_target_pairs={{0,4},{1,5},{2,6},{3,7},{12,8},{13,9},{14,10},{15,11},{16,20},{17,... | collective-permute-start | bytes 6291464 | tf_op jit(solution)/shard_map/ppermute | solution.py:507
  371.4 16.9 %collective-permute-done.81 = f32[192,128]{1,0:T(8,128)S(1)} collective-permute-done((f32[192,128]{1,0:T(8,128)S(1)}, f32[192,128]{1,0:T(8,128)S(1)}, u32[]{:S(2)}, u32[]{:S(2)}) %collective-permute-start.81) | collective-permute-done | bytes 98336 | tf_op jit(solution)/shard_map/ppermute | solution.py:826
  402.5 19.2 %collective-permute-done.84 = f32[192,128]{1,0:T(8,128)S(1)} collective-permute-done((f32[192,128]{1,0:T(8,128)S(1)}, f32[192,128]{1,0:T(8,128)S(1)}, u32[]{:S(2)}, u32[]{:S(2)}) %collective-permute-start.84) | collective-permute-done | bytes 98336 | tf_op jit(solution)/shard_map/ppermute | solution.py:830
  444.6 15.0 %collective-permute-done.87.refs_1_ = bf16[1024,512]{1,0:T(8,128)(2,1)S(1)} collective-permute-done((bf16[1024,512]{1,0:T(8,128)(2,1)S(1)}, bf16[1024,512]{1,0:T(8,128)(2,1)S(1)}, u32[]{:S(2)}, u32[]{:S(2)}) %collective-permute-start.87) | collective-permute-done | bytes 1048608 | tf_op jit(solution)/shard_map/ppermute | solution.py:507
  487.6 16.6 %collective-permute-start.47 = (bf16[1024,768]{1,0:T(8,128)(2,1)S(1)}, bf16[1024,768]{1,0:T(8,128)(2,1)}, u32[]{:S(2)}, u32[]{:S(2)}) collective-permute-start(bf16[1024,768]{1,0:T(8,128)(2,1)S(1)} %shard_map.279), channel_id=1, source_target_pairs={{0,4},{1,5},{2,6},{3,7},{12,8},{13,9},{14,10},{15,11},{16,20},{17,... | collective-permute-start | bytes 4718600 | tf_op jit(solution)/shard_map/ppermute | solution.py:507
  504.1 15.2 %collective-permute-done.91.refs_1_ = bf16[1024,1024]{1,0:T(8,128)(2,1)S(1)} collective-permute-done((bf16[1024,1024]{1,0:T(8,128)(2,1)S(1)}, bf16[1024,1024]{1,0:T(8,128)(2,1)S(1)}, u32[]{:S(2)}, u32[]{:S(2)}) %collective-permute-start.91) | collective-permute-done | bytes 2097184 | tf_op jit(solution)/shard_map/ppermute | solution.py:507
  523.4 10.0 %collective-permute-done.47 = bf16[1024,768]{1,0:T(8,128)(2,1)} collective-permute-done((bf16[1024,768]{1,0:T(8,128)(2,1)S(1)}, bf16[1024,768]{1,0:T(8,128)(2,1)}, u32[]{:S(2)}, u32[]{:S(2)}) %collective-permute-start.47) | collective-permute-done | bytes 1572896 | tf_op jit(solution)/shard_map/ppermute | solution.py:507
  560.1 31.0 %collective-permute-done.48 = bf16[1024,768]{1,0:T(8,128)(2,1)S(1)} collective-permute-done((bf16[1024,768]{1,0:T(8,128)(2,1)S(1)}, bf16[1024,768]{1,0:T(8,128)(2,1)S(1)}, u32[]{:S(2)}, u32[]{:S(2)}) %collective-permute-start.48) | collective-permute-done | bytes 1572896 | tf_op jit(solution)/shard_map/ppermute | solution.py:507
  630.2 27.2 %collective-permute-done.99.refs_1_ = bf16[1024,768]{1,0:T(8,128)(2,1)S(1)} collective-permute-done((bf16[1024,768]{1,0:T(8,128)(2,1)S(1)}, bf16[1024,768]{1,0:T(8,128)(2,1)S(1)}, u32[]{:S(2)}, u32[]{:S(2)}) %collective-permute-start.99) | collective-permute-done | bytes 1572896 | tf_op jit(solution)/shard_map/ppermute | solution.py:507
  698.4 22.1 %collective-permute-done.103.refs_1_ = bf16[1024,768]{1,0:T(8,128)(2,1)S(1)} collective-permute-done((bf16[1024,768]{1,0:T(8,128)(2,1)S(1)}, bf16[1024,768]{1,0:T(8,128)(2,1)S(1)}, u32[]{:S(2)}, u32[]{:S(2)}) %collective-permute-start.103) | collective-permute-done | bytes 1572896 | tf_op jit(solution)/shard_map/ppermute | solution.py:507
  725.4 8.7 %fusion.21 = f32[256,2048]{1,0:T(8,128)S(1)} fusion(bf16[256,4096]{1,0:T(8,128)(2,1)} %get-tuple-element.403, bf16[4096,2048]{1,0:T(8,128)(2,1)} %param.32), kind=kOutput, calls=%fused_computation.105 | convolution fusion | flops 4294967296 | bytes 20971520 | tf_op jit(solution)/shard_map/dot_general | solution.py:45
  736.0 12.4 %collective-permute-done.113 = bf16[1024,512]{1,0:T(8,128)(2,1)} collective-permute-done((bf16[1024,512]{1,0:T(8,128)(2,1)S(1)}, bf16[1024,512]{1,0:T(8,128)(2,1)}, u32[]{:S(2)}, u32[]{:S(2)}) %collective-permute-start.113) | collective-permute-done | bytes 1048608 | tf_op jit(solution)/shard_map/ppermute | solution.py:507
  752.6 10.3 %shard_map.293.refs_5_ = f32[1024,6144]{1,0:T(8,128)} custom-call(s32[96]{0:T(128)S(1)} %stack.162.table_ref, bf16[1024,768]{1,0:T(8,128)(2,1)S(1)} %copy-done.5, bf16[1024,768]{1,0:T(8,128)(2,1)S(1)} %copy-done.21, bf16[1024,768]{1,0:T(8,128)(2,1)S(1)} %copy-done.25, ...), custom_call_target="tpu_custom_call", output_to_operand_aliasing={{}: (6, {})} | custom-call | bytes 4718592 | tf_op jit(solution)/shard_map/pallas_call | solution.py:472
  769.0 17.0 %collective-permute-done.114.refs_1_ = bf16[1024,512]{1,0:T(8,128)(2,1)S(1)} collective-permute-done((bf16[1024,512]{1,0:T(8,128)(2,1)S(1)}, bf16[1024,512]{1,0:T(8,128)(2,1)S(1)}, u32[]{:S(2)}, u32[]{:S(2)}) %collective-permute-start.114) | collective-permute-done | bytes 1048608 | tf_op jit(solution)/shard_map/ppermute | solution.py:507
  791.4 10.1 %shard_map.294 = f32[1024,6144]{1,0:T(8,128)} custom-call(s32[96]{0:T(128)S(1)} %stack.127.table_ref, bf16[1024,768]{1,0:T(8,128)(2,1)S(1)} %copy-done.3, bf16[1024,768]{1,0:T(8,128)(2,1)S(1)} %copy-done.23, bf16[1024,768]{1,0:T(8,128)(2,1)S(1)} %copy-done.27, bf16[512,768]{1,0:T(8,128)(2,1)S(1)} %collective-permute-done.105.refs_3_, ...), custom_call_target="tpu_custom_call", output_to_operand_aliasing={{}: (6, {})} | custom-call | bytes 4718592 | tf_op jit(solution)/shard_map/pallas_call | solution.py:472
  (588 shorter events, 510.8 us)
Async XLA Ops:
  35.8 43.6 %collective-permute-start.14 = (bf16[256,1024]{1,0:T(8,128)(2,1)}, bf16[256,1024]{1,0:T(8,128)(2,1)S(1)}, u32[]{:S(2)}, u32[]{:S(2)}) collective-permute-start(bf16[256,1024]{1,0:T(8,128)(2,1)} %get-tuple-element.457.refs_0_), channel_id=1, source_target_pairs={{0,1},{1,0},{2,3},{3,2},{4,5},{5,4},{6,7},{7,6},{8,9},{9,8},{10,11... | collective-permute-start | bytes 1572872 | tf_op jit(solution)/shard_map/ppermute | solution.py:507
  37.1 42.3 %collective-permute-start.15 = (bf16[256,1024]{1,0:T(8,128)(2,1)}, bf16[256,1024]{1,0:T(8,128)(2,1)S(1)}, u32[]{:S(2)}, u32[]{:S(2)}) collective-permute-start(bf16[256,1024]{1,0:T(8,128)(2,1)} %get-tuple-element.457.refs_0_), channel_id=1, source_target_pairs={{0,2},{1,3},{2,0},{3,1},{4,6},{5,7},{6,4},{7,5},{8,10},{9,11},{10,... | collective-permute-start | bytes 1572872 | tf_op jit(solution)/shard_map/ppermute | solution.py:507
  38.6 40.9 %collective-permute-start.16 = (bf16[256,1024]{1,0:T(8,128)(2,1)}, bf16[256,1024]{1,0:T(8,128)(2,1)}, u32[]{:S(2)}, u32[]{:S(2)}) collective-permute-start(bf16[256,1024]{1,0:T(8,128)(2,1)} %get-tuple-element.457.refs_0_), channel_id=1, source_target_pairs={{0,3},{1,2},{2,1},{3,0},{4,7},{5,6},{6,5},{7,4},{8,11},{9,10},{10,... | collective-permute-start | bytes 1572872 | tf_op jit(solution)/shard_map/ppermute | solution.py:507
  252.4 48.5 %collective-permute-start.45 = (bf16[1024,1024]{1,0:T(8,128)(2,1)S(1)}, bf16[1024,1024]{1,0:T(8,128)(2,1)}, u32[]{:S(2)}, u32[]{:S(2)}) collective-permute-start(bf16[1024,1024]{1,0:T(8,128)(2,1)S(1)} %shard_map.281), channel_id=1, source_target_pairs={{0,4},{1,5},{2,6},{3,7},{12,8},{13,9},{14,10},{15,11},{16,20},{17,... | collective-permute-start | bytes 6291464 | tf_op jit(solution)/shard_map/ppermute | solution.py:507
  261.1 39.0 %collective-permute-start.51 = (bf16[1024,512]{1,0:T(8,128)(2,1)}, bf16[1024,512]{1,0:T(8,128)(2,1)}, u32[]{:S(2)}, u32[]{:S(2)}) collective-permute-start(bf16[1024,512]{1,0:T(8,128)(2,1)} %add.295), channel_id=1, source_target_pairs={{4,8},{5,9},{6,10},{7,11},{8,4},{9,5},{10,6},{11,7},{20,24},{21,25... | collective-permute-start | bytes 3145736 | tf_op jit(solution)/shard_map/ppermute | solution.py:507
  298.8 41.2 %collective-permute-start.57 = (bf16[1024,512]{1,0:T(8,128)(2,1)}, bf16[1024,512]{1,0:T(8,128)(2,1)}, u32[]{:S(2)}, u32[]{:S(2)}) collective-permute-start(bf16[1024,512]{1,0:T(8,128)(2,1)} %add.303), channel_id=1, source_target_pairs={{4,0},{5,1},{6,2},{7,3},{8,12},{9,13},{10,14},{11,15},{20,16},{21,... | collective-permute-start | bytes 3145736 | tf_op jit(solution)/shard_map/ppermute | solution.py:507
  307.5 55.7 %collective-permute-start.52 = (bf16[1024,1024]{1,0:T(8,128)(2,1)}, bf16[1024,1024]{1,0:T(8,128)(2,1)}, u32[]{:S(2)}, u32[]{:S(2)}) collective-permute-start(bf16[1024,1024]{1,0:T(8,128)(2,1)} %add.294), channel_id=1, source_target_pairs={{4,8},{5,9},{6,10},{7,11},{8,4},{9,5},{10,6},{11,7},{20,24},{21,25... | collective-permute-start | bytes 6291464 | tf_op jit(solution)/shard_map/ppermute | solution.py:507
  343.5 95.0 %collective-permute-start.46 = (bf16[1024,1024]{1,0:T(8,128)(2,1)S(1)}, bf16[1024,1024]{1,0:T(8,128)(2,1)}, u32[]{:S(2)}, u32[]{:S(2)}) collective-permute-start(bf16[1024,1024]{1,0:T(8,128)(2,1)S(1)} %shard_map.280), channel_id=1, source_target_pairs={{0,4},{1,5},{2,6},{3,7},{12,8},{13,9},{14,10},{15,11},{16,20},{17,... | collective-permute-start | bytes 6291464 | tf_op jit(solution)/shard_map/ppermute | solution.py:507
  359.8 40.4 %collective-permute-start.77 = (bf16[1024,512]{1,0:T(8,128)(2,1)S(1)}, bf16[1024,512]{1,0:T(8,128)(2,1)S(1)}, u32[]{:S(2)}, u32[]{:S(2)}) collective-permute-start(bf16[1024,512]{1,0:T(8,128)(2,1)S(1)} %broadcast_select_fusion.6.refs_0_), channel_id=1, source_target_pairs={{0,1},{1,0},{2,3},{3,2},{4,5},{5,4},{6,7},{7,6},{8,9},{9,8},{10,11... | collective-permute-start | bytes 3145736 | tf_op jit(solution)/shard_map/ppermute | solution.py:507
  362.1 39.0 %collective-permute-start.78 = (bf16[1024,512]{1,0:T(8,128)(2,1)S(1)}, bf16[1024,512]{1,0:T(8,128)(2,1)S(1)}, u32[]{:S(2)}, u32[]{:S(2)}) collective-permute-start(bf16[1024,512]{1,0:T(8,128)(2,1)S(1)} %broadcast_select_fusion.6.refs_0_), channel_id=1, source_target_pairs={{0,2},{1,3},{2,0},{3,1},{4,6},{5,7},{6,4},{7,5},{8,10},{9,11},{10,... | collective-permute-start | bytes 3145736 | tf_op jit(solution)/shard_map/ppermute | solution.py:507
  370.1 99.4 %collective-permute-start.59 = (bf16[1024,1024]{1,0:T(8,128)(2,1)}, bf16[1024,1024]{1,0:T(8,128)(2,1)}, u32[]{:S(2)}, u32[]{:S(2)}) collective-permute-start(bf16[1024,1024]{1,0:T(8,128)(2,1)} %add.301), channel_id=1, source_target_pairs={{4,0},{5,1},{6,2},{7,3},{8,12},{9,13},{10,14},{11,15},{20,16},{21,... | collective-permute-start | bytes 6291464 | tf_op jit(solution)/shard_map/ppermute | solution.py:507
  475.6 43.7 %collective-permute-start.91 = (bf16[1024,1024]{1,0:T(8,128)(2,1)S(1)}, bf16[1024,1024]{1,0:T(8,128)(2,1)S(1)}, u32[]{:S(2)}, u32[]{:S(2)}) collective-permute-start(bf16[1024,1024]{1,0:T(8,128)(2,1)S(1)} %broadcast_select_fusion.refs_0_), channel_id=1, source_target_pairs={{0,1},{1,0},{2,3},{3,2},{4,5},{5,4},{6,7},{7,6},{8,9},{9,8},{10,11... | collective-permute-start | bytes 6291464 | tf_op jit(solution)/shard_map/ppermute | solution.py:507
  476.6 43.9 %collective-permute-start.92 = (bf16[1024,1024]{1,0:T(8,128)(2,1)S(1)}, bf16[1024,1024]{1,0:T(8,128)(2,1)S(1)}, u32[]{:S(2)}, u32[]{:S(2)}) collective-permute-start(bf16[1024,1024]{1,0:T(8,128)(2,1)S(1)} %broadcast_select_fusion.refs_0_), channel_id=1, source_target_pairs={{0,2},{1,3},{2,0},{3,1},{4,6},{5,7},{6,4},{7,5},{8,10},{9,11},{10,... | collective-permute-start | bytes 6291464 | tf_op jit(solution)/shard_map/ppermute | solution.py:507
  481.8 58.5 %collective-permute-start.60 = (bf16[1024,1024]{1,0:T(8,128)(2,1)}, bf16[1024,1024]{1,0:T(8,128)(2,1)}, u32[]{:S(2)}, u32[]{:S(2)}) collective-permute-start(bf16[1024,1024]{1,0:T(8,128)(2,1)} %add.300), channel_id=1, source_target_pairs={{4,0},{5,1},{6,2},{7,3},{8,12},{9,13},{10,14},{11,15},{20,16},{21,... | collective-permute-start | bytes 6291464 | tf_op jit(solution)/shard_map/ppermute | solution.py:507
  487.6 45.8 %collective-permute-start.47 = (bf16[1024,768]{1,0:T(8,128)(2,1)S(1)}, bf16[1024,768]{1,0:T(8,128)(2,1)}, u32[]{:S(2)}, u32[]{:S(2)}) collective-permute-start(bf16[1024,768]{1,0:T(8,128)(2,1)S(1)} %shard_map.279), channel_id=1, source_target_pairs={{0,4},{1,5},{2,6},{3,7},{12,8},{13,9},{14,10},{15,11},{16,20},{17,... | collective-permute-start | bytes 4718600 | tf_op jit(solution)/shard_map/ppermute | solution.py:507
  543.1 51.8 %collective-permute-start.95 = (bf16[1024,1024]{1,0:T(8,128)(2,1)S(1)}, bf16[1024,1024]{1,0:T(8,128)(2,1)S(1)}, u32[]{:S(2)}, u32[]{:S(2)}) collective-permute-start(bf16[1024,1024]{1,0:T(8,128)(2,1)S(1)} %broadcast_select_fusion.1.refs_0_), channel_id=1, source_target_pairs={{0,1},{1,0},{2,3},{3,2},{4,5},{5,4},{6,7},{7,6},{8,9},{9,8},{10,11... | collective-permute-start | bytes 6291464 | tf_op jit(solution)/shard_map/ppermute | solution.py:507
  544.1 51.9 %collective-permute-start.96 = (bf16[1024,1024]{1,0:T(8,128)(2,1)S(1)}, bf16[1024,1024]{1,0:T(8,128)(2,1)S(1)}, u32[]{:S(2)}, u32[]{:S(2)}) collective-permute-start(bf16[1024,1024]{1,0:T(8,128)(2,1)S(1)} %broadcast_select_fusion.1.refs_0_), channel_id=1, source_target_pairs={{0,2},{1,3},{2,0},{3,1},{4,6},{5,7},{6,4},{7,5},{8,10},{9,11},{10,... | collective-permute-start | bytes 6291464 | tf_op jit(solution)/shard_map/ppermute | solution.py:507
  551.4 39.8 %collective-permute-start.48 = (bf16[1024,768]{1,0:T(8,128)(2,1)S(1)}, bf16[1024,768]{1,0:T(8,128)(2,1)S(1)}, u32[]{:S(2)}, u32[]{:S(2)}) collective-permute-start(bf16[1024,768]{1,0:T(8,128)(2,1)S(1)} %shard_map.278), channel_id=1, source_target_pairs={{0,4},{1,5},{2,6},{3,7},{12,8},{13,9},{14,10},{15,11},{16,20},{17,... | collective-permute-start | bytes 4718600 | tf_op jit(solution)/shard_map/ppermute | solution.py:507
  558.9 60.3 %collective-permute-start.61 = (bf16[1024,768]{1,0:T(8,128)(2,1)}, bf16[1024,768]{1,0:T(8,128)(2,1)}, u32[]{:S(2)}, u32[]{:S(2)}) collective-permute-start(bf16[1024,768]{1,0:T(8,128)(2,1)} %add.299), channel_id=1, source_target_pairs={{4,0},{5,1},{6,2},{7,3},{8,12},{9,13},{10,14},{11,15},{20,16},{21,... | collective-permute-start | bytes 4718600 | tf_op jit(solution)/shard_map/ppermute | solution.py:507
  628.2 44.2 %collective-permute-start.62 = (bf16[1024,768]{1,0:T(8,128)(2,1)}, bf16[1024,768]{1,0:T(8,128)(2,1)}, u32[]{:S(2)}, u32[]{:S(2)}) collective-permute-start(bf16[1024,768]{1,0:T(8,128)(2,1)} %add.298), channel_id=1, source_target_pairs={{4,0},{5,1},{6,2},{7,3},{8,12},{9,13},{10,14},{11,15},{20,16},{21,... | collective-permute-start | bytes 4718600 | tf_op jit(solution)/shard_map/ppermute | solution.py:507
  685.1 36.4 %collective-permute-start.104 = (bf16[1024,768]{1,0:T(8,128)(2,1)S(1)}, bf16[1024,768]{1,0:T(8,128)(2,1)S(1)}, u32[]{:S(2)}, u32[]{:S(2)}) collective-permute-start(bf16[1024,768]{1,0:T(8,128)(2,1)S(1)} %broadcast_select_fusion.3.refs_0_), channel_id=1, source_target_pairs={{0,2},{1,3},{2,0},{3,1},{4,6},{5,7},{6,4},{7,5},{8,10},{9,11},{10,... | collective-permute-start | bytes 4718600 | tf_op jit(solution)/shard_map/ppermute | solution.py:507
  696.8 51.6 %collective-permute-start.113 = (bf16[1024,512]{1,0:T(8,128)(2,1)S(1)}, bf16[1024,512]{1,0:T(8,128)(2,1)}, u32[]{:S(2)}, u32[]{:S(2)}) collective-permute-start(bf16[1024,512]{1,0:T(8,128)(2,1)S(1)} %add.646), channel_id=1, source_target_pairs={{4,0},{5,1},{6,2},{7,3},{8,12},{9,13},{10,14},{11,15},{20,16},{21,... | collective-permute-start | bytes 3145736 | tf_op jit(solution)/shard_map/ppermute | solution.py:507
  723.4 39.5 %collective-permute-start.105 = (bf16[512,768]{1,0:T(8,128)(2,1)}, bf16[512,768]{1,0:T(8,128)(2,1)S(1)}, u32[]{:S(2)}, u32[]{:S(2)}) collective-permute-start(bf16[512,768]{1,0:T(8,128)(2,1)} %slice.214), channel_id=1, source_target_pairs={{0,2},{1,3},{2,0},{3,1},{4,6},{5,7},{6,4},{7,5},{8,10},{9,11},{10,... | collective-permute-start | bytes 2359304 | tf_op jit(solution)/shard_map/ppermute | solution.py:507
  724.5 38.4 %collective-permute-start.106 = (bf16[512,768]{1,0:T(8,128)(2,1)}, bf16[512,768]{1,0:T(8,128)(2,1)}, u32[]{:S(2)}, u32[]{:S(2)}) collective-permute-start(bf16[512,768]{1,0:T(8,128)(2,1)} %slice.215), channel_id=1, source_target_pairs={{0,1},{1,0},{2,3},{3,2},{4,5},{5,4},{6,7},{7,6},{8,9},{9,8},{10,11... | collective-permute-start | bytes 2359304 | tf_op jit(solution)/shard_map/ppermute | solution.py:507
  (208 other events, 2851.2 us)

commit v5 on v4

--- a/solution.py
+++ b/solution.py
@@ -170,23 +170,17 @@
     out_ref[...] = dot(left_turned[...], right[...], 1, 0).astype(LOW)
 
 
-def rows_product(lefts, rights, block, first, steps, turned=False):
-    length, tall = lefts[0].shape
-
-    def spec(right):
-        if isinstance(right, tuple):
-            _, index, count = right
-            return pl.BlockSpec((count, block), lambda j: (index, first + j))
-        if right.ndim == 3:
-            return pl.BlockSpec((1, right.shape[1], block), lambda j: (first + j, 0, 0))
-        return pl.BlockSpec((right.shape[0], block), lambda j: (0, first + j))
-
+def rows_product(lefts, rights, tall, block, steps, turned=False):
+    length = lefts[0][0].shape[0]
+    left_specs = [
+        pl.BlockSpec((length, tall), functools.partial(lambda c, j: (0, c), c)) for _, c in lefts
+    ]
+    right_specs = [pl.BlockSpec(shape, place) for _, shape, place in rights]
     total = length * len(lefts)
     return pl.pallas_call(
         functools.partial(product_kernel, len(lefts), turned),
         grid=(steps,),
-        in_specs=[pl.BlockSpec((length, tall), lambda j: (0, 0))] * len(lefts)
-        + [spec(right) for right in rights],
+        in_specs=left_specs + right_specs,
         out_specs=pl.BlockSpec((tall, block), lambda j: (0, j)),
         out_shape=jax.ShapeDtypeStruct((tall, steps * block), LOW),
         scratch_shapes=[pltpu.VMEM((tall, total), LOW), pltpu.VMEM((total, block), LOW)],
@@ -194,7 +188,11 @@
         cost_estimate=estimate(
             2 * tall * total * steps * block, 2 * total * (tall + steps * block)
         ),
-    )(*lefts, *[r[0] if isinstance(r, tuple) else r for r in rights])
+    )(*[left[0] for left in lefts], *[right[0] for right in rights])
+
+
+def columns_from(value, rows, row, first, block):
+    return value, (rows, block), lambda j: (row, first + j)
 
 
 def hold(values, after):
@@ -576,9 +574,6 @@
     def scatter_group(value, axis, size):
         return exchange(blocks_of(value, axis, size))
 
-    def pairs(mine, theirs):
-        return [piece for pair in zip(mine, theirs) for piece in pair]
-
     end = (level == 0) | (level == LINE - 1)
 
     def line_start(value, after=()):
@@ -664,14 +659,15 @@
         theirs = swap(theirs)
         mine = times_columns(normed, qkv_weight, my_table, qkv_block, F32)
         results = attend_forward(first_row, mine, theirs, bias)
-        return [normed, *results, swap(down_grad)]
-
-    normed_one_half, queries, keys, values, attended, down_grad_theirs = segment(
+        both = jnp.concatenate([normed, results[3]], 1)
+        return [*results, swap(down_grad), both]
+
+    queries, keys, values, attended, down_grad_theirs, early = segment(
         to_attended, mine, theirs, down_grad, qkv_weight, bias,
         qkv_table(core), qkv_table(other), first_row,
     )
     attended, down_mine = lax.optimization_barrier((attended, down_mine))
-    qkv_left = gather_group(normed_one_half)
+    early = gather_group(early)
     block = min(1024, inner_half)
     count = inner_half // block
 
@@ -706,7 +702,7 @@
         (table(count, core * count), table(count, other * count)), core_number,
         jnp.concatenate([down_grad, down_grad_theirs]), down_weight,
     )
-    (inner_low, up_grad), qkv_left = lax.optimization_barrier(((inner_low, up_grad), qkv_left))
+    (inner_low, up_grad), early = lax.optimization_barrier(((inner_low, up_grad), early))
 
     down_left = scatter_group(inner_low, 1, inner_half // GROUP)
 
@@ -736,12 +732,20 @@
         to_middle, up_grad, up_weight, middle, ffn_gain[None], cotangent[0], active,
         core_number, down_mine, (table(1, core), table(1, other)),
     )
-    down_theirs = [down_grad_theirs] + [(down_theirs, d, rows) for d in range(GROUP - 1)]
-    down_right = pairs(down_mine, down_theirs)
+    down_theirs = [(down_grad_theirs, 0)] + [(down_theirs, d) for d in range(GROUP - 1)]
+
+    def down_product(first, steps):
+        rights = []
+        for own, (value, row) in zip(down_mine, down_theirs):
+            rights.append(columns_from(own, rows, 0, first, quarter))
+            rights.append(columns_from(value, rows, row, first, quarter))
+        lefts = [(left, 0) for left in down_left]
+        return rows_product(lefts, rights, inner_half // GROUP, quarter, steps)
+
     quarter = width // 4
     down_left, attn_grad = lax.optimization_barrier((down_left, attn_grad))
     up_right = exchange(up_right)
-    sums = [rows_product(down_left, down_right, quarter, 0, 1)]
+    sums = [down_product(0, 1)]
     (come,) = first_hop.send([(sums[0], inward)])
     attn_grad, sums[0] = lax.optimization_barrier((attn_grad, sums[0]))
 
@@ -750,13 +754,21 @@
         grads = dot(grads, out_weight, 1, 1).astype(LOW)
         qkv_grad = attend_backward(first_row, *operands, grads)
         flat = jnp.concatenate([qkv_grad[0], qkv_grad[1], qkv_grad[2]], 1)
-        blocks = blocks_of(qkv_grad, 2, half // GROUP)
+        blocks = []
+        for wide, block in zip(
+            blocks_of(attn_grad, 1, width // GROUP), blocks_of(qkv_grad, 2, half // GROUP)
+        ):
+            narrow = wide.shape[1] // 2
+            wide = jnp.concatenate([wide[:, :narrow], wide[:, narrow:]])
+            blocks.append(jnp.concatenate([block, wide[None]]))
         return [qkv_grad, flat, swap(flat), *blocks]
 
-    qkv_grad, flat, flat_theirs, *qkv_right = segment(to_qkv, attn_grad, out_weight, first_row, queries, keys, values)
+    qkv_grad, flat, flat_theirs, *late = segment(to_qkv, attn_grad, out_weight, first_row, queries, keys, values)
+    sums.append(down_product(1, 1))
     qkv_grad, up_right, come, sums = lax.optimization_barrier((qkv_grad, up_right, come, sums))
     sums[0] += come
     (passed,) = middle_hop.send([(sums[0], middle_moves)])
+    (come,) = first_hop.send([(sums[1], inward)])
     up_left = gather_group(normed_two_half)
 
     def to_input(flat, theirs, qkv_weight, tables):
@@ -767,18 +779,18 @@
         to_input, hold(flat, qkv_grad), flat_theirs, qkv_weight,
         (qkv_table(core), qkv_table(other)),
     )
-    grads, up_left, passed = lax.optimization_barrier((grads, up_left, passed))
+    grads, up_left, passed, come = lax.optimization_barrier((grads, up_left, passed, come))
     sums[0] += passed
-    qkv_right = exchange(qkv_right)
-    value = hold(rows_product(down_left, down_right, quarter, 1, 1), grads)
+    sums[1] += come
+    late = exchange(late)
+    value = hold(down_product(2, 1), grads)
     come = first_hop.send([(value, inward)])
-    passed, come, qkv_right = lax.optimization_barrier(
-        (last_hop.send([(sums[0], outward)]), come, qkv_right)
+    passed, come, late = lax.optimization_barrier(
+        (last_hop.send([(sums[0], outward)]), come, late)
     )
     sums[0] = jnp.where(end, passed[0], sums[0])
     sums.append(value + come[0])
-    for part_index in range(2, 4):
-        sums.append(line_start(rows_product(down_left, down_right, quarter, part_index, 1)))
+    sums.append(line_start(hold(down_product(3, 1), late)))
 
     def to_ends(grads, hidden, gain, middle_grad, core_number, inner_low, down_weight):
         results = by_rows(
@@ -821,14 +833,27 @@
         ]
     ).reshape(-1, 128)
     small = small + swap(small)
-    distance = 1
+
+    def exchange_sum(value, step, count):
+        def from_chip(distance):
+            moves = []
+            for i in range(chips):
+                place = i // step % count
+                moves.append((i, i + ((place ^ distance) - place) * step))
+            return lax.ppermute(value, "dp", moves)
+
+        others = [value] + [from_chip(d) for d in range(1, count)]
+        while len(others) > 1:
+            others = [a + b for a, b in zip(others[::2], others[1::2])]
+        return others[0]
+
+    small = exchange_sum(small, 1, GROUP)
+    distance = GROUP
     while distance < plane:
         small = small + lax.ppermute(small, "dp", in_plane(distance))
         distance *= 2
-    small = small + lax.ppermute(small, "dp", inward)
-    small = small + lax.ppermute(small, "dp", middle_moves)
-    small_last = lax.ppermute(small, "dp", outward)
-    small = jnp.where(end, small_last, small).reshape(-1)
+    small_sum = exchange_sum(small, plane, LINE)
+    small = small_sum.reshape(-1)
     small_grads = []
     first = 0
     for size in (width, width, width, inner, width, width, width, width, width):
@@ -836,20 +861,46 @@
         first += size
 
     chunks = [("down", value, index) for index, value in enumerate(sums)]
-    size = inner_half // GROUP
-    block = min(512, size)
-    value = rows_product(up_left, up_right, block, 0, size // block)
-    chunks.append(("up", line_start(value), core))
-    theirs = [swap(r) for r in up_right]
-    value = rows_product(up_left, theirs, block, 0, size // block, True)
-    chunks.append(("up", line_start(value), other))
-    size = half // GROUP
-    value = rows_product(qkv_left, qkv_right, size, 0, 3)
-    chunks.append(("qkv", line_start(value), core))
-    theirs = [swap(r) for r in qkv_right]
-    value = rows_product(qkv_left, theirs, size, 0, 3, True)
-    chunks.append(("qkv", line_start(value), other))
-    chunks.append(("out", None, 0))
+    chunks += [("up", None, 2 * GROUP * core), ("up", None, 2 * GROUP * core + 1)]
+    chunks += [("up", None, GROUP * other)]
+    chunks += [("qkv", None, core), ("qkv", None, other), ("out", None, 0)]
+    up_width = inner_half // GROUP
+    up_block = min(512, up_width)
+
+    def to_up(*operands):
+        lefts = [(left, 0) for left in operands[:GROUP]]
+        mine = operands[GROUP:]
+        theirs = swap(jnp.concatenate(mine))
+        results = []
+        for first in range(inner_half // GROUP // up_block):
+            rights = [columns_from(right, length, 0, first, up_block) for right in mine]
+            results.append(rows_product(lefts, rights, half, up_block, 1))
+        rights = [columns_from(theirs, length, d, 0, up_block) for d in range(GROUP)]
+        steps = inner_half // GROUP // up_block
+        return [*results, rows_product(lefts, rights, half, up_block, steps, True)]
+
+    rest_block = half // GROUP
+
+    def to_rest(*operands):
+        early, mine = operands[:GROUP], operands[GROUP:]
+        theirs = swap(jnp.concatenate(mine))
+
+        def part(value, d):
+            return value, (1, length, rest_block), lambda j: (4 * d + j, 0, 0)
+
+        def out_part(value, d):
+            return value, (1, rows, rest_block), lambda j: (4 * d + 3, j, 0)
+
+        lefts = [(left, 0) for left in early]
+        rights = [part(right, 0) for right in mine]
+        own = rows_product(lefts, rights, half, rest_block, 3)
+        rights = [part(theirs, d) for d in range(GROUP)]
+        other_half = rows_product(lefts, rights, half, rest_block, 3, True)
+        lefts = [(left, 1) for left in early]
+        rights = []
+        for d, right in enumerate(mine):
+            rights += [out_part(right, 0), out_part(theirs, d)]
+        return [own, other_half, rows_product(lefts, rights, half, rest_block, 2)]
 
     wholes = {
         "down": blank((inner_half, width)),
@@ -857,12 +908,15 @@
         "out": blank((half, width)),
         "qkv": blank((half, 3 * width)),
     }
+    size = inner_half // GROUP
+    values = []
     done = [(), ()]
     for index, (name, value, where) in enumerate(chunks):
-        if name == "out":
-            right = pairs(out_right, [swap(r) for r in out_right])
-            value = line_start(rows_product(out_left, right, width // GROUP, 0, 1))
-        after = done[-2], small_last if index == 2 else ()
+        if value is None:
+            value = values.pop(0)
+        if index == 0:
+            values = segment(to_up, *hold(up_left, late), *up_right)
+        after = done[-2], {0: values, 4: small_sum}.get(index, ())
         if index > 0:
             value = line_middle(value)
         if plane == GROUP and name in LATE:
@@ -870,9 +924,11 @@
         else:
             value = blocks_sum(line_end(value) if index > 0 else value)
             pieces = spread(value, after)
-        if index == 1:
-            out_right = scatter_group(attn_grad, 1, width // GROUP)
-            out_left = gather_group(attended)
+        if index == 0:
+            values = [line_start(v) for v in values]
+        if index == 3:
+            rest = segment(to_rest, *hold(early, pieces[1:3]), *late)
+            values += [line_start(v) for v in rest]
         tall, wide = value.shape
         high = min(256, tall)
         broad = wide // 3 if name == "qkv" else wide
@@ -884,7 +940,7 @@
                 if name == "down":
                     row, columns = owner * (tall // high) + i, [jnp.int32(where)]
                 elif name == "up":
-                    columns = [where * GROUP + owner]
+                    columns = [where + owner * (size // wide)]
                 elif name == "out":
                     columns = [owner]
                 else:

time: 818 us -> 804 us (0.983)
  waiting for transfers between devices: 297 us -> 283 us
  Pallas kernels: 185 us -> 198 us
  starting transfers between devices: 164 us -> 152 us
  local copies, waits for them, and re-layouts: 67.6 us -> 58.2 us
  other arithmetic: 72.2 us -> 80.8 us
    ppermute x87 -> x88, waiting for transfers between devices: 245 us -> 201 us  [send(): self.last = [lax.ppermute(v, 'dp', m) for v, (_, m) in zip(values, sends)]]
    ppermute x5 -> x6, waiting for transfers between devices: 42 us -> 75.9 us  [from_chip(): return lax.ppermute(value, 'dp', moves)]
    ppermute x87 -> x88, starting transfers between devices: 150 us -> 137 us  [send(): self.last = [lax.ppermute(v, 'dp', m) for v, (_, m) in zip(values, sends)]]
    pallas_call x9 -> x10, Pallas kernels: 32.1 us -> 42.1 us  [rows_product(): pl.pallas_call(functools.partial(product_kernel, len(lefts), turned), gri...]
    concatenate x0 -> x7, other arithmetic: none -> 8.92 us  [the longest x4 3.4 us: to_qkv(): blocks.append(jnp.concatenate([block, wide[None]]))]
    unnamed x227 -> x159, local copies, waits for them, and re-layouts: 29.3 us -> 24.2 us
    pallas_call x9 -> x10, Pallas kernels: 60.4 us -> 63.1 us  [place(): pl.pallas_call(functools.partial(place_kernel, high), in_specs=[pl.BlockS...]
    add x8 -> x9, other arithmetic: 19.4 us -> 17.9 us  [line_middle(): return value + middle_hop.send([(value, middle_moves)])[0]]
  transfers between devices with their start and end apart: 118 -> 110, of which waited for: 49 -> 34; matrix products, arithmetic and copies ran while one was open for 15% -> 15% of each run, Pallas kernels for 22% -> 24%
where the time goes in v5:
time: 804 us; the launch traced here: 793 us
  waiting for transfers between devices  283 us (35%)
  Pallas kernels  198 us (25%)
  starting transfers between devices  152 us (19%)
  other arithmetic  80.8 us (10%)
  local copies, waits for them, and re-layouts  58.2 us (7%)
  matrix products  16 us (2%)
    ppermute x88, waiting for transfers between devices, send(): self.last = [lax.ppermute(v, 'dp', m) for v, (_, m) in zip(values, sends)]  201 us
    ppermute x88, starting transfers between devices, send(): self.last = [lax.ppermute(v, 'dp', m) for v, (_, m) in zip(values, sends)]  137 us
    ppermute x6, waiting for transfers between devices, from_chip(): return lax.ppermute(value, 'dp', moves)  75.9 us
    pallas_call x10, Pallas kernels, place(): pl.pallas_call(functools.partial(place_kernel, high), in_specs=[pl.BlockS...  63.1 us
    pallas_call x10, Pallas kernels, rows_product(): pl.pallas_call(functools.partial(product_kernel, len(lefts), turned), gri...  42.1 us
    pallas_call x4, Pallas kernels, times_back(): pl.pallas_call(functools.partial(back_kernel, turned), grid_spec=pltpu.Pr...  27.2 us
    pallas_call x4, Pallas kernels, times_columns(): pl.pallas_call(columns_kernel, grid_spec=pltpu.PrefetchScalarGridSpec(num...  25.2 us
    unnamed x159, local copies, waits for them, and re-layouts  24.2 us
  transfers between devices with their start and end apart: 110, of which 34 were waited for; matrix products, arithmetic and copies ran while one was open for 15% of the time, Pallas kernels for 24%

profile of v5, /device:TPU:0, one launch (start us, length us, event | category | flops | bytes accessed | tf_op | source)
XLA Modules:
  0.0 793.0 jit_solution(4450978825128786394)
XLA Ops:
  13.4 22.3 %conditional.7 = (bf16[256,1024]{1,0:T(8,128)(2,1)}, bf16[256,1024]{1,0:T(8,128)(2,1)}, bf16[256,1024]{1,0:T(8,128)(2,1)}, bf16[256,1024]{1,0:T(8,128)(2,1)}, bf...) conditional(s32[]{:T(128)} %convert_element_type.31, () %tuple.144, (bf16[128,1024]{1,0:T(8,128)(2,1)S(1)}, ...), branch_computations={%region_0.1_spmd, %region_1.2_spmd} | conditional | flops 874512384 | bytes 19710170 | solution.py:633
  41.5 37.7 %conditional.8 = (f32[128,2048]{1,0:T(8,128)}, bf16[256,1024]{1,0:T(8,128)(2,1)}, bf16[256,4096]{1,0:T(8,128)(2,1)}, bf16[256,4096]{1,0:T(8,128)(2,1)}, f32[4096...) conditional(s32[]{:T(128)} %convert_element_type.31, () %tuple.143, (bf16[256,1024]{1,0:T(8,128)(2,1)}, ...), branch_computations={%region_2.3_spmd, %region_3.4_spmd} | conditional | flops 3222536192 | bytes 42932700 | solution.py:633
  65.1 13.4 %branch_1_fun.25 = (bf16[256,4096]{1,0:T(8,128)(2,1)}, bf16[256,4096]{1,0:T(8,128)(2,1)}, f32[1,4096]{1,0:T(1,128)}) custom-call(bf16[256,2048]{1,0:T(8,128)(2,1)S(1)} %copy-done.62, bf16[4096,2048]{1,0:T(8,128)(2,1)} %get-tuple-element.204.refs_0_, f32[256,4096]{1,0:T(8,128)S(1)} %branch_1_fun.23.refs_1_, ...), custom_call_target="tpu_custom_call" | custom-call | flops 1073741824 | bytes 7602176 | tf_op jit(solution)/shard_map/cond/branch_1_fun/pallas_call | solution.py:312
  91.7 23.0 %conditional.9 = (f32[128,2048]{1,0:T(8,128)}, bf16[128,2048]{1,0:T(8,128)(2,1)}, bf16[384,2048]{1,0:T(8,128)(2,1)}, bf16[256,1024]{1,0:T(8,128)(2,1)}, bf16[256...) conditional(s32[]{:T(128)} %convert_element_type.31, () %tuple.154, ...), branch_computations={%region_4.5_spmd, %region_5.6_spmd} | conditional | flops 1079771136 | bytes 34343496 | solution.py:633
  125.2 25.4 %conditional.10 = (bf16[3,256,1024]{2,1,0:T(8,128)(2,1)}, bf16[256,3072]{1,0:T(8,128)(2,1)}, bf16[256,3072]{1,0:T(8,128)(2,1)}, bf16[4,256,256]{2,1,0:T(8,128)(2...) conditional(s32[]{:T(128)} %convert_element_type.31, () %tuple.152, ...), branch_computations={%region_6.7_spmd, %region_7.8_spmd} | conditional | flops 1250689024 | bytes 30802540 | solution.py:633
  131.0 10.8 %branch_1_fun.29 = bf16[3,256,1024]{2,1,0:T(8,128)(2,1)} custom-call(s32[1]{0:T(128)} %get-tuple-element.232.first_ref, bf16[256,1024]{1,0:T(8,128)(2,1)} %get-tuple-element.233.q_ref, bf16[256,1024]{1,0:T(8,128)(2,1)} %get-tuple-element.234.k_ref, bf16[256,1024]{1,0:T(8,128)(2,1)} %get-tuple-element.235.v_ref, ...), custom_call_target="tpu_custom_call" | custom-call | flops 167772160 | bytes 917504 | tf_op jit(solution)/shard_map/cond/branch_1_fun/pallas_call | solution.py:425
  167.9 15.3 %conditional.11 = (f32[256,1024]{1,0:T(8,128)}) conditional(s32[]{:T(128)} %convert_element_type.31, () %tuple.151, (s32[3]{0:T(128)S(1)}, bf16[256,3072]{1,0:T(8,128)(2,1)}, bf16[1024,6144]{1,0:T(8,128)(2,1)}, s32[3]{0:T(128)S(1)}, bf16[256,3072]{1,0:T(8,128)(2,1)}) %tuple.162), branch_computations={%region_8.9_spmd, %region_9.10_spmd} | conditional | flops 805306368 | bytes 4980744 | solution.py:633
  205.0 8.7 %collective-permute-done.34 = bf16[4,256,256]{2,1,0:T(8,128)(2,1)} collective-permute-done((bf16[4,256,256]{2,1,0:T(8,128)(2,1)S(1)}, bf16[4,256,256]{2,1,0:T(8,128)(2,1)}, u32[]{:S(2)}, u32[]{:S(2)}) %collective-permute-start.34) | collective-permute-done | bytes 524320 | tf_op jit(solution)/shard_map/ppermute | solution.py:505
  235.2 16.0 %conditional.12 = (bf16[1024,512]{1,0:T(8,128)(2,1)}, bf16[1024,512]{1,0:T(8,128)(2,1)}, bf16[1024,1024]{1,0:T(8,128)(2,1)}) conditional(s32[]{:T(128)} %convert_element_type.31, () %tuple.181, (bf16[256,1024]{1,0:T(8,128)(2,1)}, bf16[256,1024]{1,0:T(8,128)(2,1)}, bf16[256,1024]{1,0:T(8,128)(2,1)}, bf16[256,1024]{1,0:T(8,128)(2,1)}, ...), branch_computations={%region_10.11_spmd, %region_11.12_spmd} | conditional | flops 1082130432 | bytes 15204416 | solution.py:633
  251.9 12.9 %collective-permute-start.59 = (bf16[1024,512]{1,0:T(8,128)(2,1)}, bf16[1024,512]{1,0:T(8,128)(2,1)S(1)}, u32[]{:S(2)}, u32[]{:S(2)}) collective-permute-start(bf16[1024,512]{1,0:T(8,128)(2,1)} %get-tuple-element.578), channel_id=1, source_target_pairs={{0,4},{1,5},{2,6},{3,7},{12,8},{13,9},{14,10},{15,11},{16,20},{17,... | collective-permute-start | bytes 3145736 | tf_op jit(solution)/shard_map/ppermute | solution.py:505
  268.8 11.2 %collective-permute-done.47.refs_3_ = bf16[512,512]{1,0:T(8,128)(2,1)S(1)} collective-permute-done((bf16[512,512]{1,0:T(8,128)(2,1)S(1)}, bf16[512,512]{1,0:T(8,128)(2,1)S(1)}, u32[]{:S(2)}, u32[]{:S(2)}) %collective-permute-start.47) | collective-permute-done | bytes 524320 | tf_op jit(solution)/shard_map/ppermute | solution.py:505
  295.8 10.0 %collective-permute-done.49.refs_1_ = bf16[1024,512]{1,0:T(8,128)(2,1)S(1)} collective-permute-done((bf16[1024,512]{1,0:T(8,128)(2,1)S(1)}, bf16[1024,512]{1,0:T(8,128)(2,1)S(1)}, u32[]{:S(2)}, u32[]{:S(2)}) %collective-permute-start.49) | collective-permute-done | bytes 1048608 | tf_op jit(solution)/shard_map/ppermute | solution.py:505
  336.8 10.8 %collective-permute-done.53.refs_1_ = bf16[1024,512]{1,0:T(8,128)(2,1)S(1)} collective-permute-done((bf16[1024,512]{1,0:T(8,128)(2,1)S(1)}, bf16[1024,512]{1,0:T(8,128)(2,1)S(1)}, u32[]{:S(2)}, u32[]{:S(2)}) %collective-permute-start.53) | collective-permute-done | bytes 1048608 | tf_op jit(solution)/shard_map/ppermute | solution.py:505
  376.0 10.1 %collective-permute-done.57.refs_1_ = bf16[1024,512]{1,0:T(8,128)(2,1)S(1)} collective-permute-done((bf16[1024,512]{1,0:T(8,128)(2,1)S(1)}, bf16[1024,512]{1,0:T(8,128)(2,1)S(1)}, u32[]{:S(2)}, u32[]{:S(2)}) %collective-permute-start.57) | collective-permute-done | bytes 1048608 | tf_op jit(solution)/shard_map/ppermute | solution.py:505
  399.8 25.4 %collective-permute-done.80 = f32[192,128]{1,0:T(8,128)S(1)} collective-permute-done((f32[192,128]{1,0:T(8,128)S(1)}, f32[192,128]{1,0:T(8,128)S(1)}, u32[]{:S(2)}, u32[]{:S(2)}) %collective-permute-start.80) | collective-permute-done | bytes 98336 | tf_op jit(solution)/shard_map/ppermute | solution.py:843
  449.2 42.7 %collective-permute-done.82 = f32[192,128]{1,0:T(8,128)S(1)} collective-permute-done((f32[192,128]{1,0:T(8,128)S(1)}, f32[192,128]{1,0:T(8,128)S(1)}, u32[]{:S(2)}, u32[]{:S(2)}) %collective-permute-start.82) | collective-permute-done | bytes 98336 | tf_op jit(solution)/shard_map/ppermute | solution.py:843
  498.1 17.7 %conditional.13 = (bf16[1024,768]{1,0:T(8,128)(2,1)}, bf16[1024,768]{1,0:T(8,128)(2,1)}, bf16[1024,512]{1,0:T(8,128)(2,1)}) conditional(s32[]{:T(128)} %convert_element_type.31, () %tuple.171, (bf16[256,2048]{1,0:T(8,128)(2,1)}, bf16[256,2048]{1,0:T(8,128)(2,1)}, bf16[256,2048]{1,0:T(8,128)(2,1)}, bf16[256,2048]{1,0:T(8,128)(2,1)}, ...), branch_computations={%region_12.13_spmd, %region_13.14_spmd} | conditional | flops 1076887552 | bytes 15204416 | solution.py:633
  529.7 24.5 %collective-permute-done.87.refs_1_ = bf16[1024,512]{1,0:T(8,128)(2,1)S(1)} collective-permute-done((bf16[1024,512]{1,0:T(8,128)(2,1)S(1)}, bf16[1024,512]{1,0:T(8,128)(2,1)S(1)}, u32[]{:S(2)}, u32[]{:S(2)}) %collective-permute-start.87) | collective-permute-done | bytes 1048608 | tf_op jit(solution)/shard_map/ppermute | solution.py:505
  577.1 28.5 %collective-permute-done.63 = bf16[1024,768]{1,0:T(8,128)(2,1)S(1)} collective-permute-done((bf16[1024,768]{1,0:T(8,128)(2,1)S(1)}, bf16[1024,768]{1,0:T(8,128)(2,1)S(1)}, u32[]{:S(2)}, u32[]{:S(2)}) %collective-permute-start.63) | collective-permute-done | bytes 1572896 | tf_op jit(solution)/shard_map/ppermute | solution.py:505
  656.2 20.0 %collective-permute-done.95.refs_1_ = bf16[1024,768]{1,0:T(8,128)(2,1)S(1)} collective-permute-done((bf16[1024,768]{1,0:T(8,128)(2,1)S(1)}, bf16[1024,768]{1,0:T(8,128)(2,1)S(1)}, u32[]{:S(2)}, u32[]{:S(2)}) %collective-permute-start.95) | collective-permute-done | bytes 1572896 | tf_op jit(solution)/shard_map/ppermute | solution.py:505
  702.0 27.0 %collective-permute-done.99.refs_1_ = bf16[1024,768]{1,0:T(8,128)(2,1)S(1)} collective-permute-done((bf16[1024,768]{1,0:T(8,128)(2,1)S(1)}, bf16[1024,768]{1,0:T(8,128)(2,1)S(1)}, u32[]{:S(2)}, u32[]{:S(2)}) %collective-permute-start.99) | collective-permute-done | bytes 1572896 | tf_op jit(solution)/shard_map/ppermute | solution.py:505
  738.4 10.1 %shard_map.290.refs_5_ = f32[1024,6144]{1,0:T(8,128)} custom-call(s32[96]{0:T(128)S(1)} %stack.189.table_ref, bf16[1024,768]{1,0:T(8,128)(2,1)S(1)} %copy-done.1, bf16[1024,768]{1,0:T(8,128)(2,1)S(1)} %copy-done.11, bf16[1024,768]{1,0:T(8,128)(2,1)S(1)} %copy-done.13, bf16[512,768]{1,0:T(8,128)(2,1)S(1)} %copy-done.37, ...), custom_call_target="tpu_custom_call", output_to_operand_aliasing={{}: (6, {})} | custom-call | bytes 4718592 | tf_op jit(solution)/shard_map/pallas_call | solution.py:470
  751.2 8.7 %fusion.21 = f32[256,2048]{1,0:T(8,128)S(1)} fusion(bf16[256,4096]{1,0:T(8,128)(2,1)} %get-tuple-element.469, bf16[4096,2048]{1,0:T(8,128)(2,1)} %param.36), kind=kOutput, calls=%fused_computation.122 | convolution fusion | flops 4294967296 | bytes 20971520 | tf_op jit(solution)/shard_map/dot_general | solution.py:45
  776.7 10.3 %shard_map.291 = f32[1024,6144]{1,0:T(8,128)} custom-call(s32[96]{0:T(128)S(1)} %stack.145.table_ref, bf16[1024,768]{1,0:T(8,128)(2,1)S(1)} %broadcast_select_fusion.2.refs_0_, bf16[1024,768]{1,0:T(8,128)(2,1)S(1)} %copy-done.7, bf16[1024,768]{1,0:T(8,128)(2,1)S(1)} %copy-done.9, ...), custom_call_target="tpu_custom_call", output_to_operand_aliasing={{}: (6, {})} | custom-call | bytes 4718592 | tf_op jit(solution)/shard_map/pallas_call | solution.py:470
  (518 shorter events, 502.8 us)
Async XLA Ops:
  35.8 43.4 %collective-permute-start.16 = (bf16[256,2048]{1,0:T(8,128)(2,1)}, bf16[256,2048]{1,0:T(8,128)(2,1)}, u32[]{:S(2)}, u32[]{:S(2)}) collective-permute-start(bf16[256,2048]{1,0:T(8,128)(2,1)} %get-tuple-element.572), channel_id=1, source_target_pairs={{0,1},{1,0},{2,3},{3,2},{4,5},{5,4},{6,7},{7,6},{8,9},{9,8},{10,11... | collective-permute-start | bytes 3145736 | tf_op jit(solution)/shard_map/ppermute | solution.py:505
  37.8 47.7 %collective-permute-start.17 = (bf16[256,2048]{1,0:T(8,128)(2,1)}, bf16[256,2048]{1,0:T(8,128)(2,1)}, u32[]{:S(2)}, u32[]{:S(2)}) collective-permute-start(bf16[256,2048]{1,0:T(8,128)(2,1)} %get-tuple-element.572), channel_id=1, source_target_pairs={{0,2},{1,3},{2,0},{3,1},{4,6},{5,7},{6,4},{7,5},{8,10},{9,11},{10,... | collective-permute-start | bytes 3145736 | tf_op jit(solution)/shard_map/ppermute | solution.py:505
  39.3 46.2 %collective-permute-start.18 = (bf16[256,2048]{1,0:T(8,128)(2,1)}, bf16[256,2048]{1,0:T(8,128)(2,1)}, u32[]{:S(2)}, u32[]{:S(2)}) collective-permute-start(bf16[256,2048]{1,0:T(8,128)(2,1)} %get-tuple-element.572), channel_id=1, source_target_pairs={{0,3},{1,2},{2,1},{3,0},{4,7},{5,6},{6,5},{7,4},{8,11},{9,10},{10,... | collective-permute-start | bytes 3145736 | tf_op jit(solution)/shard_map/ppermute | solution.py:505
  117.3 37.0 %collective-permute-start.26 = (bf16[1024,512]{1,0:T(8,128)(2,1)S(1)}, bf16[1024,512]{1,0:T(8,128)(2,1)}, u32[]{:S(2)}, u32[]{:S(2)}) collective-permute-start(bf16[1024,512]{1,0:T(8,128)(2,1)S(1)} %shard_map.275), channel_id=1, source_target_pairs={{0,4},{1,5},{2,6},{3,7},{12,8},{13,9},{14,10},{15,11},{16,20},{17,... | collective-permute-start | bytes 3145736 | tf_op jit(solution)/shard_map/ppermute | solution.py:505
  226.4 38.3 %collective-permute-start.45 = (bf16[1024,512]{1,0:T(8,128)(2,1)S(1)}, bf16[1024,512]{1,0:T(8,128)(2,1)S(1)}, u32[]{:S(2)}, u32[]{:S(2)}) collective-permute-start(bf16[1024,512]{1,0:T(8,128)(2,1)S(1)} %broadcast_select_fusion.9.refs_0_), channel_id=1, source_target_pairs={{0,1},{1,0},{2,3},{3,2},{4,5},{5,4},{6,7},{7,6},{8,9},{9,8},{10,11... | collective-permute-start | bytes 3145736 | tf_op jit(solution)/shard_map/ppermute | solution.py:505
  227.9 36.9 %collective-permute-start.46 = (bf16[1024,512]{1,0:T(8,128)(2,1)S(1)}, bf16[1024,512]{1,0:T(8,128)(2,1)}, u32[]{:S(2)}, u32[]{:S(2)}) collective-permute-start(bf16[1024,512]{1,0:T(8,128)(2,1)S(1)} %broadcast_select_fusion.9.refs_0_), channel_id=1, source_target_pairs={{0,2},{1,3},{2,0},{3,1},{4,6},{5,7},{6,4},{7,5},{8,10},{9,11},{10,... | collective-permute-start | bytes 3145736 | tf_op jit(solution)/shard_map/ppermute | solution.py:505
  231.3 36.2 %collective-permute-start.42 = (bf16[1024,512]{1,0:T(8,128)(2,1)}, bf16[1024,512]{1,0:T(8,128)(2,1)}, u32[]{:S(2)}, u32[]{:S(2)}) collective-permute-start(bf16[1024,512]{1,0:T(8,128)(2,1)} %add.326), channel_id=1, source_target_pairs={{4,0},{5,1},{6,2},{7,3},{8,12},{9,13},{10,14},{11,15},{20,16},{21,... | collective-permute-start | bytes 3145736 | tf_op jit(solution)/shard_map/ppermute | solution.py:505
  251.1 34.7 %collective-permute-start.40 = (bf16[1024,512]{1,0:T(8,128)(2,1)S(1)}, bf16[1024,512]{1,0:T(8,128)(2,1)S(1)}, u32[]{:S(2)}, u32[]{:S(2)}) collective-permute-start(bf16[1024,512]{1,0:T(8,128)(2,1)S(1)} %copy-done.58), channel_id=1, source_target_pairs={{4,8},{5,9},{6,10},{7,11},{8,4},{9,5},{10,6},{11,7},{20,24},{21,25... | collective-permute-start | bytes 3145736 | tf_op jit(solution)/shard_map/ppermute | solution.py:505
  251.9 35.9 %collective-permute-start.59 = (bf16[1024,512]{1,0:T(8,128)(2,1)}, bf16[1024,512]{1,0:T(8,128)(2,1)S(1)}, u32[]{:S(2)}, u32[]{:S(2)}) collective-permute-start(bf16[1024,512]{1,0:T(8,128)(2,1)} %get-tuple-element.578), channel_id=1, source_target_pairs={{0,4},{1,5},{2,6},{3,7},{12,8},{13,9},{14,10},{15,11},{16,20},{17,... | collective-permute-start | bytes 3145736 | tf_op jit(solution)/shard_map/ppermute | solution.py:505
  319.0 49.6 %collective-permute-start.61 = (bf16[1024,1024]{1,0:T(8,128)(2,1)}, bf16[1024,1024]{1,0:T(8,128)(2,1)}, u32[]{:S(2)}, u32[]{:S(2)}) collective-permute-start(bf16[1024,1024]{1,0:T(8,128)(2,1)} %get-tuple-element.580), channel_id=1, source_target_pairs={{0,4},{1,5},{2,6},{3,7},{12,8},{13,9},{14,10},{15,11},{16,20},{17,... | collective-permute-start | bytes 6291464 | tf_op jit(solution)/shard_map/ppermute | solution.py:505
  335.1 36.8 %collective-permute-start.65 = (bf16[1024,512]{1,0:T(8,128)(2,1)}, bf16[1024,512]{1,0:T(8,128)(2,1)}, u32[]{:S(2)}, u32[]{:S(2)}) collective-permute-start(bf16[1024,512]{1,0:T(8,128)(2,1)} %add.342), channel_id=1, source_target_pairs={{4,8},{5,9},{6,10},{7,11},{8,4},{9,5},{10,6},{11,7},{20,24},{21,25... | collective-permute-start | bytes 3145736 | tf_op jit(solution)/shard_map/ppermute | solution.py:505
  371.9 66.9 %collective-permute-start.66 = (bf16[1024,1024]{1,0:T(8,128)(2,1)S(1)}, bf16[1024,1024]{1,0:T(8,128)(2,1)S(1)}, u32[]{:S(2)}, u32[]{:S(2)}) collective-permute-start(bf16[1024,1024]{1,0:T(8,128)(2,1)S(1)} %add.341), channel_id=1, source_target_pairs={{4,8},{5,9},{6,10},{7,11},{8,4},{9,5},{10,6},{11,7},{20,24},{21,25... | collective-permute-start | bytes 6291464 | tf_op jit(solution)/shard_map/ppermute | solution.py:505
  390.3 50.9 %collective-permute-start.70 = (bf16[1024,512]{1,0:T(8,128)(2,1)S(1)}, bf16[1024,512]{1,0:T(8,128)(2,1)S(1)}, u32[]{:S(2)}, u32[]{:S(2)}) collective-permute-start(bf16[1024,512]{1,0:T(8,128)(2,1)S(1)} %add.347), channel_id=1, source_target_pairs={{4,0},{5,1},{6,2},{7,3},{8,12},{9,13},{10,14},{11,15},{20,16},{21,... | collective-permute-start | bytes 3145736 | tf_op jit(solution)/shard_map/ppermute | solution.py:505
  397.3 95.2 %collective-permute-start.76 = (bf16[1024,512]{1,0:T(8,128)(2,1)S(1)}, bf16[1024,512]{1,0:T(8,128)(2,1)S(1)}, u32[]{:S(2)}, u32[]{:S(2)}) collective-permute-start(bf16[1024,512]{1,0:T(8,128)(2,1)S(1)} %broadcast_select_fusion.4.refs_0_), channel_id=1, source_target_pairs={{0,1},{1,0},{2,3},{3,2},{4,5},{5,4},{6,7},{7,6},{8,9},{9,8},{10,11... | collective-permute-start | bytes 3145736 | tf_op jit(solution)/shard_map/ppermute | solution.py:505
  397.7 95.7 %collective-permute-start.77 = (bf16[1024,512]{1,0:T(8,128)(2,1)S(1)}, bf16[1024,512]{1,0:T(8,128)(2,1)S(1)}, u32[]{:S(2)}, u32[]{:S(2)}) collective-permute-start(bf16[1024,512]{1,0:T(8,128)(2,1)S(1)} %broadcast_select_fusion.4.refs_0_), channel_id=1, source_target_pairs={{0,2},{1,3},{2,0},{3,1},{4,6},{5,7},{6,4},{7,5},{8,10},{9,11},{10,... | collective-permute-start | bytes 3145736 | tf_op jit(solution)/shard_map/ppermute | solution.py:505
  441.2 124.8 %collective-permute-start.71 = (bf16[1024,1024]{1,0:T(8,128)(2,1)}, bf16[1024,1024]{1,0:T(8,128)(2,1)}, u32[]{:S(2)}, u32[]{:S(2)}) collective-permute-start(bf16[1024,1024]{1,0:T(8,128)(2,1)} %add.346), channel_id=1, source_target_pairs={{4,0},{5,1},{6,2},{7,3},{8,12},{9,13},{10,14},{11,15},{20,16},{21,... | collective-permute-start | bytes 6291464 | tf_op jit(solution)/shard_map/ppermute | solution.py:505
  443.9 48.0 %collective-permute-start.82 = (f32[192,128]{1,0:T(8,128)S(1)}, f32[192,128]{1,0:T(8,128)S(1)}, u32[]{:S(2)}, u32[]{:S(2)}) collective-permute-start(f32[192,128]{1,0:T(8,128)S(1)} %add_add_fusion.1), channel_id=1, source_target_pairs={{0,4},{1,5},{2,6},{3,7},{4,0},{5,1},{6,2},{7,3},{8,12},{9,13},{10,... | collective-permute-start | bytes 294920 | tf_op jit(solution)/shard_map/ppermute | solution.py:843
  494.8 33.9 %collective-permute-start.85 = (bf16[512,512]{1,0:T(8,128)(2,1)}, bf16[512,512]{1,0:T(8,128)(2,1)}, u32[]{:S(2)}, u32[]{:S(2)}) collective-permute-start(bf16[512,512]{1,0:T(8,128)(2,1)} %slice.238), channel_id=1, source_target_pairs={{0,2},{1,3},{2,0},{3,1},{4,6},{5,7},{6,4},{7,5},{8,10},{9,11},{10,... | collective-permute-start | bytes 1572872 | tf_op jit(solution)/shard_map/ppermute | solution.py:505
  515.7 41.9 %collective-permute-start.62 = (bf16[1024,768]{1,0:T(8,128)(2,1)}, bf16[1024,768]{1,0:T(8,128)(2,1)}, u32[]{:S(2)}, u32[]{:S(2)}) collective-permute-start(bf16[1024,768]{1,0:T(8,128)(2,1)} %get-tuple-element.581), channel_id=1, source_target_pairs={{0,4},{1,5},{2,6},{3,7},{12,8},{13,9},{14,10},{15,11},{16,20},{17,... | collective-permute-start | bytes 4718600 | tf_op jit(solution)/shard_map/ppermute | solution.py:505
  570.3 46.0 %collective-permute-start.91 = (bf16[1024,1024]{1,0:T(8,128)(2,1)S(1)}, bf16[1024,1024]{1,0:T(8,128)(2,1)S(1)}, u32[]{:S(2)}, u32[]{:S(2)}) collective-permute-start(bf16[1024,1024]{1,0:T(8,128)(2,1)S(1)} %broadcast_select_fusion.refs_0_), channel_id=1, source_target_pairs={{0,1},{1,0},{2,3},{3,2},{4,5},{5,4},{6,7},{7,6},{8,9},{9,8},{10,11... | collective-permute-start | bytes 6291464 | tf_op jit(solution)/shard_map/ppermute | solution.py:505
  570.8 46.6 %collective-permute-start.92 = (bf16[1024,1024]{1,0:T(8,128)(2,1)S(1)}, bf16[1024,1024]{1,0:T(8,128)(2,1)S(1)}, u32[]{:S(2)}, u32[]{:S(2)}) collective-permute-start(bf16[1024,1024]{1,0:T(8,128)(2,1)S(1)} %broadcast_select_fusion.refs_0_), channel_id=1, source_target_pairs={{0,2},{1,3},{2,0},{3,1},{4,6},{5,7},{6,4},{7,5},{8,10},{9,11},{10,... | collective-permute-start | bytes 6291464 | tf_op jit(solution)/shard_map/ppermute | solution.py:505
  575.8 55.9 %collective-permute-start.72 = (bf16[1024,768]{1,0:T(8,128)(2,1)}, bf16[1024,768]{1,0:T(8,128)(2,1)}, u32[]{:S(2)}, u32[]{:S(2)}) collective-permute-start(bf16[1024,768]{1,0:T(8,128)(2,1)} %add.345), channel_id=1, source_target_pairs={{4,0},{5,1},{6,2},{7,3},{8,12},{9,13},{10,14},{11,15},{20,16},{21,... | collective-permute-start | bytes 4718600 | tf_op jit(solution)/shard_map/ppermute | solution.py:505
  607.1 37.6 %collective-permute-start.68 = (bf16[1024,768]{1,0:T(8,128)(2,1)}, bf16[1024,768]{1,0:T(8,128)(2,1)}, u32[]{:S(2)}, u32[]{:S(2)}) collective-permute-start(bf16[1024,768]{1,0:T(8,128)(2,1)} %add.339), channel_id=1, source_target_pairs={{4,8},{5,9},{6,10},{7,11},{8,4},{9,5},{10,6},{11,7},{20,24},{21,25... | collective-permute-start | bytes 4718600 | tf_op jit(solution)/shard_map/ppermute | solution.py:505
  648.2 44.3 %collective-permute-start.73 = (bf16[1024,768]{1,0:T(8,128)(2,1)}, bf16[1024,768]{1,0:T(8,128)(2,1)}, u32[]{:S(2)}, u32[]{:S(2)}) collective-permute-start(bf16[1024,768]{1,0:T(8,128)(2,1)} %add.344), channel_id=1, source_target_pairs={{4,0},{5,1},{6,2},{7,3},{8,12},{9,13},{10,14},{11,15},{20,16},{21,... | collective-permute-start | bytes 4718600 | tf_op jit(solution)/shard_map/ppermute | solution.py:505
  (165 other events, 2329.6 us)

commit v6 on v5

--- a/solution.py
+++ b/solution.py
@@ -916,7 +916,7 @@
             value = values.pop(0)
         if index == 0:
             values = segment(to_up, *hold(up_left, late), *up_right)
-        after = done[-2], {0: values, 4: small_sum}.get(index, ())
+        after = done[-2], {0: values, len(chunks) - 1: done[-1]}.get(index, ())
         if index > 0:
             value = line_middle(value)
         if plane == GROUP and name in LATE:

time: 804 us -> 770 us (0.958)
  waiting for transfers between devices: 283 us -> 244 us
    ppermute x6, waiting for transfers between devices: 75.9 us -> 25.1 us  [from_chip(): return lax.ppermute(value, 'dp', moves)]
    ppermute x88, waiting for transfers between devices: 201 us -> 212 us  [send(): self.last = [lax.ppermute(v, 'dp', m) for v, (_, m) in zip(values, sends)]]
    unnamed x159 -> x181, local copies, waits for them, and re-layouts: 24.2 us -> 26.1 us
  transfers between devices with their start and end apart: 110 -> 110, of which waited for: 34 -> 39; matrix products, arithmetic and copies ran while one was open for 15% -> 16% of each run, Pallas kernels for 24% -> 24%
where the time goes in v6:
time: 770 us; the launch traced here: 759 us
  waiting for transfers between devices  244 us (32%)
  Pallas kernels  196 us (25%)
  starting transfers between devices  156 us (20%)
  other arithmetic  80.8 us (10%)
  local copies, waits for them, and re-layouts  61.3 us (8%)
  matrix products  16 us (2%)
    ppermute x88, waiting for transfers between devices, send(): self.last = [lax.ppermute(v, 'dp', m) for v, (_, m) in zip(values, sends)]  212 us
    ppermute x88, starting transfers between devices, send(): self.last = [lax.ppermute(v, 'dp', m) for v, (_, m) in zip(values, sends)]  145 us
    pallas_call x10, Pallas kernels, place(): pl.pallas_call(functools.partial(place_kernel, high), in_specs=[pl.BlockS...  62.8 us
    pallas_call x10, Pallas kernels, rows_product(): pl.pallas_call(functools.partial(product_kernel, len(lefts), turned), gri...  41 us
    pallas_call x4, Pallas kernels, times_back(): pl.pallas_call(functools.partial(back_kernel, turned), grid_spec=pltpu.Pr...  26.3 us
    unnamed x181, local copies, waits for them, and re-layouts  26.1 us
    pallas_call x4, Pallas kernels, times_columns(): pl.pallas_call(columns_kernel, grid_spec=pltpu.PrefetchScalarGridSpec(num...  25.1 us
    ppermute x6, waiting for transfers between devices, from_chip(): return lax.ppermute(value, 'dp', moves)  25.1 us
  transfers between devices with their start and end apart: 110, of which 39 were waited for; matrix products, arithmetic and copies ran while one was open for 16% of the time, Pallas kernels for 24%

profile of v6, /device:TPU:0, one launch (start us, length us, event | category | flops | bytes accessed | tf_op | source)
XLA Modules:
  0.0 759.0 jit_solution(2695433408957902317)
XLA Ops:
  14.0 21.3 %conditional.7 = (bf16[256,1024]{1,0:T(8,128)(2,1)}, bf16[256,1024]{1,0:T(8,128)(2,1)}, bf16[256,1024]{1,0:T(8,128)(2,1)}, bf16[256,1024]{1,0:T(8,128)(2,1)}, bf...) conditional(s32[]{:T(128)} %convert_element_type.31, () %tuple.144, (bf16[128,1024]{1,0:T(8,128)(2,1)S(1)}, ...), branch_computations={%region_0.1_spmd, %region_1.2_spmd} | conditional | flops 874512384 | bytes 19710170 | solution.py:633
  41.7 37.8 %conditional.8 = (f32[128,2048]{1,0:T(8,128)}, bf16[256,1024]{1,0:T(8,128)(2,1)}, bf16[256,4096]{1,0:T(8,128)(2,1)}, bf16[256,4096]{1,0:T(8,128)(2,1)}, f32[4096...) conditional(s32[]{:T(128)} %convert_element_type.31, () %tuple.143, (bf16[256,1024]{1,0:T(8,128)(2,1)}, ...), branch_computations={%region_2.3_spmd, %region_3.4_spmd} | conditional | flops 3222536192 | bytes 42932700 | solution.py:633
  65.4 13.4 %branch_1_fun.25 = (bf16[256,4096]{1,0:T(8,128)(2,1)}, bf16[256,4096]{1,0:T(8,128)(2,1)}, f32[1,4096]{1,0:T(1,128)}) custom-call(bf16[256,2048]{1,0:T(8,128)(2,1)S(1)} %copy-done.64, bf16[4096,2048]{1,0:T(8,128)(2,1)} %get-tuple-element.204.refs_0_, f32[256,4096]{1,0:T(8,128)S(1)} %branch_1_fun.23.refs_1_, ...), custom_call_target="tpu_custom_call" | custom-call | flops 1073741824 | bytes 7602176 | tf_op jit(solution)/shard_map/cond/branch_1_fun/pallas_call | solution.py:312
  91.3 22.7 %conditional.9 = (f32[128,2048]{1,0:T(8,128)}, bf16[128,2048]{1,0:T(8,128)(2,1)}, bf16[384,2048]{1,0:T(8,128)(2,1)}, bf16[256,1024]{1,0:T(8,128)(2,1)}, bf16[256...) conditional(s32[]{:T(128)} %convert_element_type.31, () %tuple.154, ...), branch_computations={%region_4.5_spmd, %region_5.6_spmd} | conditional | flops 1079771136 | bytes 34343496 | solution.py:633
  124.5 25.5 %conditional.10 = (bf16[3,256,1024]{2,1,0:T(8,128)(2,1)}, bf16[256,3072]{1,0:T(8,128)(2,1)}, bf16[256,3072]{1,0:T(8,128)(2,1)}, bf16[4,256,256]{2,1,0:T(8,128)(2...) conditional(s32[]{:T(128)} %convert_element_type.31, () %tuple.152, ...), branch_computations={%region_6.7_spmd, %region_7.8_spmd} | conditional | flops 1250689024 | bytes 30802540 | solution.py:633
  130.3 10.8 %branch_1_fun.29 = bf16[3,256,1024]{2,1,0:T(8,128)(2,1)} custom-call(s32[1]{0:T(128)} %get-tuple-element.232.first_ref, bf16[256,1024]{1,0:T(8,128)(2,1)} %get-tuple-element.233.q_ref, bf16[256,1024]{1,0:T(8,128)(2,1)} %get-tuple-element.234.k_ref, bf16[256,1024]{1,0:T(8,128)(2,1)} %get-tuple-element.235.v_ref, ...), custom_call_target="tpu_custom_call" | custom-call | flops 167772160 | bytes 917504 | tf_op jit(solution)/shard_map/cond/branch_1_fun/pallas_call | solution.py:425
  168.1 14.3 %conditional.11 = (f32[256,1024]{1,0:T(8,128)S(1)}) conditional(s32[]{:T(128)} %convert_element_type.31, () %tuple.151, (s32[3]{0:T(128)S(1)}, bf16[256,3072]{1,0:T(8,128)(2,1)}, bf16[1024,6144]{1,0:T(8,128)(2,1)}, s32[3]{0:T(128)S(1)}, bf16[256,3072]{1,0:T(8,128)(2,1)}) %tuple.162), branch_computations={%region_8.9_spmd, %region_9.10_spmd} | conditional | flops 805306368 | bytes 4980744 | solution.py:633
  201.4 8.6 %collective-permute-done.34 = bf16[4,256,256]{2,1,0:T(8,128)(2,1)S(1)} collective-permute-done((bf16[4,256,256]{2,1,0:T(8,128)(2,1)S(1)}, bf16[4,256,256]{2,1,0:T(8,128)(2,1)S(1)}, u32[]{:S(2)}, u32[]{:S(2)}) %collective-permute-start.34) | collective-permute-done | bytes 524320 | tf_op jit(solution)/shard_map/ppermute | solution.py:505
  233.1 15.9 %conditional.12 = (bf16[1024,512]{1,0:T(8,128)(2,1)}, bf16[1024,512]{1,0:T(8,128)(2,1)}, bf16[1024,1024]{1,0:T(8,128)(2,1)}) conditional(s32[]{:T(128)} %convert_element_type.31, () %tuple.181, (bf16[256,1024]{1,0:T(8,128)(2,1)}, bf16[256,1024]{1,0:T(8,128)(2,1)}, bf16[256,1024]{1,0:T(8,128)(2,1)}, bf16[256,1024]{1,0:T(8,128)(2,1)}, ...), branch_computations={%region_10.11_spmd, %region_11.12_spmd} | conditional | flops 1082130432 | bytes 15204416 | solution.py:633
  249.8 12.8 %collective-permute-start.59 = (bf16[1024,512]{1,0:T(8,128)(2,1)}, bf16[1024,512]{1,0:T(8,128)(2,1)S(1)}, u32[]{:S(2)}, u32[]{:S(2)}) collective-permute-start(bf16[1024,512]{1,0:T(8,128)(2,1)} %get-tuple-element.578), channel_id=1, source_target_pairs={{0,4},{1,5},{2,6},{3,7},{12,8},{13,9},{14,10},{15,11},{16,20},{17,... | collective-permute-start | bytes 3145736 | tf_op jit(solution)/shard_map/ppermute | solution.py:505
  266.7 11.1 %collective-permute-done.47.refs_3_ = bf16[512,512]{1,0:T(8,128)(2,1)S(1)} collective-permute-done((bf16[512,512]{1,0:T(8,128)(2,1)S(1)}, bf16[512,512]{1,0:T(8,128)(2,1)S(1)}, u32[]{:S(2)}, u32[]{:S(2)}) %collective-permute-start.47) | collective-permute-done | bytes 524320 | tf_op jit(solution)/shard_map/ppermute | solution.py:505
  292.8 10.8 %collective-permute-done.49.refs_1_ = bf16[1024,512]{1,0:T(8,128)(2,1)S(1)} collective-permute-done((bf16[1024,512]{1,0:T(8,128)(2,1)S(1)}, bf16[1024,512]{1,0:T(8,128)(2,1)S(1)}, u32[]{:S(2)}, u32[]{:S(2)}) %collective-permute-start.49) | collective-permute-done | bytes 1048608 | tf_op jit(solution)/shard_map/ppermute | solution.py:505
  336.2 16.4 %collective-permute-done.53.refs_1_ = bf16[1024,512]{1,0:T(8,128)(2,1)S(1)} collective-permute-done((bf16[1024,512]{1,0:T(8,128)(2,1)S(1)}, bf16[1024,512]{1,0:T(8,128)(2,1)S(1)}, u32[]{:S(2)}, u32[]{:S(2)}) %collective-permute-start.53) | collective-permute-done | bytes 1048608 | tf_op jit(solution)/shard_map/ppermute | solution.py:505
  379.5 9.6 %collective-permute-done.57.refs_1_ = bf16[1024,512]{1,0:T(8,128)(2,1)S(1)} collective-permute-done((bf16[1024,512]{1,0:T(8,128)(2,1)S(1)}, bf16[1024,512]{1,0:T(8,128)(2,1)S(1)}, u32[]{:S(2)}, u32[]{:S(2)}) %collective-permute-start.57) | collective-permute-done | bytes 1048608 | tf_op jit(solution)/shard_map/ppermute | solution.py:505
  432.6 17.0 %conditional.13 = (bf16[1024,768]{1,0:T(8,128)(2,1)}, bf16[1024,768]{1,0:T(8,128)(2,1)}, bf16[1024,512]{1,0:T(8,128)(2,1)}) conditional(s32[]{:T(128)} %convert_element_type.31, () %tuple.171, (bf16[256,2048]{1,0:T(8,128)(2,1)S(1)}, bf16[256,2048]{1,0:T(8,128)(2,1)}, bf16[256,2048]{1,0:T(8,128)(2,1)}, bf16[256,2048]{1,0:T(8,128)(2,1)}, ...), branch_computations={%region_12.13_spmd, %region_13.14_spmd} | conditional | flops 1076887552 | bytes 23593136 | solution.py:633
  468.6 22.0 %collective-permute-done.80.refs_1_ = bf16[1024,512]{1,0:T(8,128)(2,1)S(1)} collective-permute-done((bf16[1024,512]{1,0:T(8,128)(2,1)S(1)}, bf16[1024,512]{1,0:T(8,128)(2,1)S(1)}, u32[]{:S(2)}, u32[]{:S(2)}) %collective-permute-start.80) | collective-permute-done | bytes 1048608 | tf_op jit(solution)/shard_map/ppermute | solution.py:505
  514.4 28.9 %collective-permute-done.63 = bf16[1024,768]{1,0:T(8,128)(2,1)S(1)} collective-permute-done((bf16[1024,768]{1,0:T(8,128)(2,1)S(1)}, bf16[1024,768]{1,0:T(8,128)(2,1)S(1)}, u32[]{:S(2)}, u32[]{:S(2)}) %collective-permute-start.63) | collective-permute-done | bytes 1572896 | tf_op jit(solution)/shard_map/ppermute | solution.py:505
  594.7 18.2 %collective-permute-done.88.refs_1_ = bf16[1024,768]{1,0:T(8,128)(2,1)S(1)} collective-permute-done((bf16[1024,768]{1,0:T(8,128)(2,1)S(1)}, bf16[1024,768]{1,0:T(8,128)(2,1)S(1)}, u32[]{:S(2)}, u32[]{:S(2)}) %collective-permute-start.88) | collective-permute-done | bytes 1572896 | tf_op jit(solution)/shard_map/ppermute | solution.py:505
  623.3 7.5 shard_map.288
  637.4 8.7 %fusion.21 = f32[256,2048]{1,0:T(8,128)S(1)} fusion(bf16[256,4096]{1,0:T(8,128)(2,1)} %get-tuple-element.469, bf16[4096,2048]{1,0:T(8,128)(2,1)} %param.36), kind=kOutput, calls=%fused_computation.122 | convolution fusion | flops 4294967296 | bytes 20971520 | tf_op jit(solution)/shard_map/dot_general | solution.py:45
  651.6 16.1 %collective-permute-done.92.refs_1_ = bf16[1024,768]{1,0:T(8,128)(2,1)S(1)} collective-permute-done((bf16[1024,768]{1,0:T(8,128)(2,1)S(1)}, bf16[1024,768]{1,0:T(8,128)(2,1)S(1)}, u32[]{:S(2)}, u32[]{:S(2)}) %collective-permute-start.92) | collective-permute-done | bytes 1572896 | tf_op jit(solution)/shard_map/ppermute | solution.py:505
  677.0 10.1 %shard_map.290.refs_5_ = f32[1024,6144]{1,0:T(8,128)} custom-call(s32[96]{0:T(128)S(1)} %stack.189.table_ref, bf16[1024,768]{1,0:T(8,128)(2,1)S(1)} %copy-done.1, bf16[1024,768]{1,0:T(8,128)(2,1)S(1)} %copy-done.11, bf16[1024,768]{1,0:T(8,128)(2,1)S(1)} %copy-done.13, ...), custom_call_target="tpu_custom_call", output_to_operand_aliasing={{}: (6, {})} | custom-call | bytes 4718592 | tf_op jit(solution)/shard_map/pallas_call | solution.py:470
  695.2 22.7 %collective-permute-done.105 = f32[192,128]{1,0:T(8,128)} collective-permute-done((f32[192,128]{1,0:T(8,128)}, f32[192,128]{1,0:T(8,128)}, u32[]{:S(2)}, u32[]{:S(2)}) %collective-permute-start.105) | collective-permute-done | bytes 98336 | tf_op jit(solution)/shard_map/ppermute | solution.py:843
  730.1 9.5 %shard_map.291 = f32[1024,6144]{1,0:T(8,128)} custom-call(s32[96]{0:T(128)S(1)} %stack.145.table_ref, bf16[1024,768]{1,0:T(8,128)(2,1)S(1)} %broadcast_select_fusion.2.refs_0_, bf16[1024,768]{1,0:T(8,128)(2,1)S(1)} %copy-done.7, bf16[1024,768]{1,0:T(8,128)(2,1)S(1)} %copy-done.9, bf16[512,768]{1,0:T(8,128)(2,1)S(1)} %copy-done.37, ...), custom_call_target="tpu_custom_call", output_to_operand_aliasing={{}: (6, {})} | custom-call | bytes 4718592 | tf_op jit(solution)/shard_map/pallas_call | solution.py:470
  (548 shorter events, 516.9 us)
Async XLA Ops:
  35.8 43.7 %collective-permute-start.16 = (bf16[256,2048]{1,0:T(8,128)(2,1)S(1)}, bf16[256,2048]{1,0:T(8,128)(2,1)}, u32[]{:S(2)}, u32[]{:S(2)}) collective-permute-start(bf16[256,2048]{1,0:T(8,128)(2,1)S(1)} %get-tuple-element.572), channel_id=1, source_target_pairs={{0,1},{1,0},{2,3},{3,2},{4,5},{5,4},{6,7},{7,6},{8,9},{9,8},{10,11... | collective-permute-start | bytes 3145736 | tf_op jit(solution)/shard_map/ppermute | solution.py:505
  37.5 47.5 %collective-permute-start.17 = (bf16[256,2048]{1,0:T(8,128)(2,1)S(1)}, bf16[256,2048]{1,0:T(8,128)(2,1)}, u32[]{:S(2)}, u32[]{:S(2)}) collective-permute-start(bf16[256,2048]{1,0:T(8,128)(2,1)S(1)} %get-tuple-element.572), channel_id=1, source_target_pairs={{0,2},{1,3},{2,0},{3,1},{4,6},{5,7},{6,4},{7,5},{8,10},{9,11},{10,... | collective-permute-start | bytes 3145736 | tf_op jit(solution)/shard_map/ppermute | solution.py:505
  39.0 46.0 %collective-permute-start.18 = (bf16[256,2048]{1,0:T(8,128)(2,1)S(1)}, bf16[256,2048]{1,0:T(8,128)(2,1)}, u32[]{:S(2)}, u32[]{:S(2)}) collective-permute-start(bf16[256,2048]{1,0:T(8,128)(2,1)S(1)} %get-tuple-element.572), channel_id=1, source_target_pairs={{0,3},{1,2},{2,1},{3,0},{4,7},{5,6},{6,5},{7,4},{8,11},{9,10},{10,... | collective-permute-start | bytes 3145736 | tf_op jit(solution)/shard_map/ppermute | solution.py:505
  116.6 37.0 %collective-permute-start.26 = (bf16[1024,512]{1,0:T(8,128)(2,1)S(1)}, bf16[1024,512]{1,0:T(8,128)(2,1)}, u32[]{:S(2)}, u32[]{:S(2)}) collective-permute-start(bf16[1024,512]{1,0:T(8,128)(2,1)S(1)} %shard_map.275), channel_id=1, source_target_pairs={{0,4},{1,5},{2,6},{3,7},{12,8},{13,9},{14,10},{15,11},{16,20},{17,... | collective-permute-start | bytes 3145736 | tf_op jit(solution)/shard_map/ppermute | solution.py:505
  224.4 38.1 %collective-permute-start.45 = (bf16[1024,512]{1,0:T(8,128)(2,1)S(1)}, bf16[1024,512]{1,0:T(8,128)(2,1)S(1)}, u32[]{:S(2)}, u32[]{:S(2)}) collective-permute-start(bf16[1024,512]{1,0:T(8,128)(2,1)S(1)} %broadcast_select_fusion.9.refs_0_), channel_id=1, source_target_pairs={{0,1},{1,0},{2,3},{3,2},{4,5},{5,4},{6,7},{7,6},{8,9},{9,8},{10,11... | collective-permute-start | bytes 3145736 | tf_op jit(solution)/shard_map/ppermute | solution.py:505
  225.9 36.7 %collective-permute-start.46 = (bf16[1024,512]{1,0:T(8,128)(2,1)S(1)}, bf16[1024,512]{1,0:T(8,128)(2,1)}, u32[]{:S(2)}, u32[]{:S(2)}) collective-permute-start(bf16[1024,512]{1,0:T(8,128)(2,1)S(1)} %broadcast_select_fusion.9.refs_0_), channel_id=1, source_target_pairs={{0,2},{1,3},{2,0},{3,1},{4,6},{5,7},{6,4},{7,5},{8,10},{9,11},{10,... | collective-permute-start | bytes 3145736 | tf_op jit(solution)/shard_map/ppermute | solution.py:505
  229.3 36.1 %collective-permute-start.42 = (bf16[1024,512]{1,0:T(8,128)(2,1)}, bf16[1024,512]{1,0:T(8,128)(2,1)}, u32[]{:S(2)}, u32[]{:S(2)}) collective-permute-start(bf16[1024,512]{1,0:T(8,128)(2,1)} %add.326), channel_id=1, source_target_pairs={{4,0},{5,1},{6,2},{7,3},{8,12},{9,13},{10,14},{11,15},{20,16},{21,... | collective-permute-start | bytes 3145736 | tf_op jit(solution)/shard_map/ppermute | solution.py:505
  249.0 33.3 %collective-permute-start.40 = (bf16[1024,512]{1,0:T(8,128)(2,1)}, bf16[1024,512]{1,0:T(8,128)(2,1)S(1)}, u32[]{:S(2)}, u32[]{:S(2)}) collective-permute-start(bf16[1024,512]{1,0:T(8,128)(2,1)} %add.322), channel_id=1, source_target_pairs={{4,8},{5,9},{6,10},{7,11},{8,4},{9,5},{10,6},{11,7},{20,24},{21,25... | collective-permute-start | bytes 3145736 | tf_op jit(solution)/shard_map/ppermute | solution.py:505
  249.8 35.8 %collective-permute-start.59 = (bf16[1024,512]{1,0:T(8,128)(2,1)}, bf16[1024,512]{1,0:T(8,128)(2,1)S(1)}, u32[]{:S(2)}, u32[]{:S(2)}) collective-permute-start(bf16[1024,512]{1,0:T(8,128)(2,1)} %get-tuple-element.578), channel_id=1, source_target_pairs={{0,4},{1,5},{2,6},{3,7},{12,8},{13,9},{14,10},{15,11},{16,20},{17,... | collective-permute-start | bytes 3145736 | tf_op jit(solution)/shard_map/ppermute | solution.py:505
  291.5 36.1 %collective-permute-start.43 = (bf16[1024,512]{1,0:T(8,128)(2,1)}, bf16[1024,512]{1,0:T(8,128)(2,1)}, u32[]{:S(2)}, u32[]{:S(2)}) collective-permute-start(bf16[1024,512]{1,0:T(8,128)(2,1)} %add.325), channel_id=1, source_target_pairs={{4,0},{5,1},{6,2},{7,3},{8,12},{9,13},{10,14},{11,15},{20,16},{21,... | collective-permute-start | bytes 3145736 | tf_op jit(solution)/shard_map/ppermute | solution.py:505
  313.2 59.8 %collective-permute-start.61 = (bf16[1024,1024]{1,0:T(8,128)(2,1)}, bf16[1024,1024]{1,0:T(8,128)(2,1)}, u32[]{:S(2)}, u32[]{:S(2)}) collective-permute-start(bf16[1024,1024]{1,0:T(8,128)(2,1)} %get-tuple-element.580), channel_id=1, source_target_pairs={{0,4},{1,5},{2,6},{3,7},{12,8},{13,9},{14,10},{15,11},{16,20},{17,... | collective-permute-start | bytes 6291464 | tf_op jit(solution)/shard_map/ppermute | solution.py:505
  334.6 42.9 %collective-permute-start.65 = (bf16[1024,512]{1,0:T(8,128)(2,1)}, bf16[1024,512]{1,0:T(8,128)(2,1)}, u32[]{:S(2)}, u32[]{:S(2)}) collective-permute-start(bf16[1024,512]{1,0:T(8,128)(2,1)} %add.342), channel_id=1, source_target_pairs={{4,8},{5,9},{6,10},{7,11},{8,4},{9,5},{10,6},{11,7},{20,24},{21,25... | collective-permute-start | bytes 3145736 | tf_op jit(solution)/shard_map/ppermute | solution.py:505
  419.0 86.1 %collective-permute-start.71 = (bf16[1024,1024]{1,0:T(8,128)(2,1)}, bf16[1024,1024]{1,0:T(8,128)(2,1)}, u32[]{:S(2)}, u32[]{:S(2)}) collective-permute-start(bf16[1024,1024]{1,0:T(8,128)(2,1)} %add.346), channel_id=1, source_target_pairs={{4,0},{5,1},{6,2},{7,3},{8,12},{9,13},{10,14},{11,15},{20,16},{21,... | collective-permute-start | bytes 6291464 | tf_op jit(solution)/shard_map/ppermute | solution.py:505
  449.5 47.2 %collective-permute-start.62 = (bf16[1024,768]{1,0:T(8,128)(2,1)}, bf16[1024,768]{1,0:T(8,128)(2,1)}, u32[]{:S(2)}, u32[]{:S(2)}) collective-permute-start(bf16[1024,768]{1,0:T(8,128)(2,1)} %get-tuple-element.581), channel_id=1, source_target_pairs={{0,4},{1,5},{2,6},{3,7},{12,8},{13,9},{14,10},{15,11},{16,20},{17,... | collective-permute-start | bytes 4718600 | tf_op jit(solution)/shard_map/ppermute | solution.py:505
  508.3 45.4 %collective-permute-start.84 = (bf16[1024,1024]{1,0:T(8,128)(2,1)S(1)}, bf16[1024,1024]{1,0:T(8,128)(2,1)S(1)}, u32[]{:S(2)}, u32[]{:S(2)}) collective-permute-start(bf16[1024,1024]{1,0:T(8,128)(2,1)S(1)} %broadcast_select_fusion.refs_0_), channel_id=1, source_target_pairs={{0,1},{1,0},{2,3},{3,2},{4,5},{5,4},{6,7},{7,6},{8,9},{9,8},{10,11... | collective-permute-start | bytes 6291464 | tf_op jit(solution)/shard_map/ppermute | solution.py:505
  509.8 45.4 %collective-permute-start.85 = (bf16[1024,1024]{1,0:T(8,128)(2,1)S(1)}, bf16[1024,1024]{1,0:T(8,128)(2,1)S(1)}, u32[]{:S(2)}, u32[]{:S(2)}) collective-permute-start(bf16[1024,1024]{1,0:T(8,128)(2,1)S(1)} %broadcast_select_fusion.refs_0_), channel_id=1, source_target_pairs={{0,2},{1,3},{2,0},{3,1},{4,6},{5,7},{6,4},{7,5},{8,10},{9,11},{10,... | collective-permute-start | bytes 6291464 | tf_op jit(solution)/shard_map/ppermute | solution.py:505
  510.1 33.2 %collective-permute-start.63 = (bf16[1024,768]{1,0:T(8,128)(2,1)S(1)}, bf16[1024,768]{1,0:T(8,128)(2,1)S(1)}, u32[]{:S(2)}, u32[]{:S(2)}) collective-permute-start(bf16[1024,768]{1,0:T(8,128)(2,1)S(1)} %copy-done.52), channel_id=1, source_target_pairs={{0,4},{1,5},{2,6},{3,7},{12,8},{13,9},{14,10},{15,11},{16,20},{17,... | collective-permute-start | bytes 4718600 | tf_op jit(solution)/shard_map/ppermute | solution.py:505
  513.2 58.0 %collective-permute-start.72 = (bf16[1024,768]{1,0:T(8,128)(2,1)}, bf16[1024,768]{1,0:T(8,128)(2,1)}, u32[]{:S(2)}, u32[]{:S(2)}) collective-permute-start(bf16[1024,768]{1,0:T(8,128)(2,1)} %add.345), channel_id=1, source_target_pairs={{4,0},{5,1},{6,2},{7,3},{8,12},{9,13},{10,14},{11,15},{20,16},{21,... | collective-permute-start | bytes 4718600 | tf_op jit(solution)/shard_map/ppermute | solution.py:505
  544.9 38.4 %collective-permute-start.68 = (bf16[1024,768]{1,0:T(8,128)(2,1)}, bf16[1024,768]{1,0:T(8,128)(2,1)}, u32[]{:S(2)}, u32[]{:S(2)}) collective-permute-start(bf16[1024,768]{1,0:T(8,128)(2,1)} %add.339), channel_id=1, source_target_pairs={{4,8},{5,9},{6,10},{7,11},{8,4},{9,5},{10,6},{11,7},{20,24},{21,25... | collective-permute-start | bytes 4718600 | tf_op jit(solution)/shard_map/ppermute | solution.py:505
  586.7 44.0 %collective-permute-start.73 = (bf16[1024,768]{1,0:T(8,128)(2,1)}, bf16[1024,768]{1,0:T(8,128)(2,1)}, u32[]{:S(2)}, u32[]{:S(2)}) collective-permute-start(bf16[1024,768]{1,0:T(8,128)(2,1)} %add.344), channel_id=1, source_target_pairs={{4,0},{5,1},{6,2},{7,3},{8,12},{9,13},{10,14},{11,15},{20,16},{21,... | collective-permute-start | bytes 4718600 | tf_op jit(solution)/shard_map/ppermute | solution.py:505
  634.1 33.7 %collective-permute-start.92 = (bf16[1024,768]{1,0:T(8,128)(2,1)S(1)}, bf16[1024,768]{1,0:T(8,128)(2,1)S(1)}, u32[]{:S(2)}, u32[]{:S(2)}) collective-permute-start(bf16[1024,768]{1,0:T(8,128)(2,1)S(1)} %broadcast_select_fusion.2.refs_0_), channel_id=1, source_target_pairs={{0,1},{1,0},{2,3},{3,2},{4,5},{5,4},{6,7},{7,6},{8,9},{9,8},{10,11... | collective-permute-start | bytes 4718600 | tf_op jit(solution)/shard_map/ppermute | solution.py:505
  647.3 79.3 %collective-permute-start.19 = (f32[128,2048]{1,0:T(8,128)}, f32[128,2048]{1,0:T(8,128)}, u32[]{:S(2)}, u32[]{:S(2)}) collective-permute-start(f32[128,2048]{1,0:T(8,128)} %slice.229), channel_id=1, source_target_pairs={{0,16},{16,0},{1,17},{17,1},{2,18},{18,2},{3,19},{19,3},{4,20},{20... | collective-permute-start | bytes 3145736 | tf_op jit(solution)/shard_map/ppermute | solution.py:543
  688.9 50.7 %collective-permute-start.99 = (bf16[1024,512]{1,0:T(8,128)(2,1)S(1)}, bf16[1024,512]{1,0:T(8,128)(2,1)}, u32[]{:S(2)}, u32[]{:S(2)}) collective-permute-start(bf16[1024,512]{1,0:T(8,128)(2,1)S(1)} %broadcast_select_fusion.3.refs_0_), channel_id=1, source_target_pairs={{0,1},{1,0},{2,3},{3,2},{4,5},{5,4},{6,7},{7,6},{8,9},{9,8},{10,11... | collective-permute-start | bytes 3145736 | tf_op jit(solution)/shard_map/ppermute | solution.py:505
  688.9 51.8 %collective-permute-start.100 = (bf16[1024,512]{1,0:T(8,128)(2,1)S(1)}, bf16[1024,512]{1,0:T(8,128)(2,1)}, u32[]{:S(2)}, u32[]{:S(2)}) collective-permute-start(bf16[1024,512]{1,0:T(8,128)(2,1)S(1)} %broadcast_select_fusion.3.refs_0_), channel_id=1, source_target_pairs={{0,2},{1,3},{2,0},{3,1},{4,6},{5,7},{6,4},{7,5},{8,10},{9,11},{10,... | collective-permute-start | bytes 3145736 | tf_op jit(solution)/shard_map/ppermute | solution.py:505
  (180 other events, 2357.7 us)

commit v7 on v6

--- a/solution.py
+++ b/solution.py
@@ -12,7 +12,6 @@
 LAYER = 12
 LINE = 4
 STREAMS = 1
-LATE = ()
 GROUP = 4
 F32 = jnp.float32
 LOW = jnp.bfloat16
@@ -537,7 +536,7 @@
     half = width // 2
     inner = up_weight.shape[1]
     inner_half = inner // 2
-    across, middle_across, first_hop, middle_hop, last_hop = (Lane() for _ in range(5))
+    across, first_hop, middle_hop, last_hop = (Lane() for _ in range(4))
 
     def swap(value):
         return lax.ppermute(value, "sp", [(0, 1), (1, 0)])
@@ -592,29 +591,13 @@
             distance *= 2
         return value
 
-    def spread(value, after):
+    def spread(value, after, more=()):
         size = value.shape[0] // 2
         first, second = across.send([(value, in_plane(1)), (value, in_plane(2))], after[0])
-        upper, lower = across.send(
-            [(first[:size], in_plane(2)), (second[size:], in_plane(1))], after[1]
+        upper, lower, *more = across.send(
+            [(first[:size], in_plane(2)), (second[size:], in_plane(1)), *more], after[1]
         )
-        return [value, first, second, upper, lower]
-
-    def spread_late(value, after):
-        size = value.shape[0] // 2
-
-        def middle_only(distance):
-            return [(a, b) for a, b in in_plane(distance) if 0 < a // plane < LINE - 1]
-
-        near = middle_across.send(
-            [(value[:size], middle_only(1)), (value[size:], middle_only(2))]
-        )
-        own = line_end(value)
-        first = across.send([(own[:size], in_plane(2)), (own[size:], in_plane(1))], after[0])
-        near_ends = last_hop.send([(v, outward) for v in near])
-        near = [jnp.where(end, e, v) for e, v in zip(near_ends, near)]
-        second = across.send([(near[0], in_plane(2)), (near[1], in_plane(1))], after[1])
-        return [own, near[0], first[1], first[0], near[1], *second]
+        return [value, first, second, upper, lower], more
 
     def table(size, start, count=None):
         return jnp.arange(size if count is None else count, dtype=jnp.int32) + start
@@ -834,35 +817,19 @@
     ).reshape(-1, 128)
     small = small + swap(small)
 
-    def exchange_sum(value, step, count):
-        def from_chip(distance):
-            moves = []
-            for i in range(chips):
-                place = i // step % count
-                moves.append((i, i + ((place ^ distance) - place) * step))
-            return lax.ppermute(value, "dp", moves)
-
-        others = [value] + [from_chip(d) for d in range(1, count)]
-        while len(others) > 1:
-            others = [a + b for a, b in zip(others[::2], others[1::2])]
-        return others[0]
-
-    small = exchange_sum(small, 1, GROUP)
-    distance = GROUP
-    while distance < plane:
-        small = small + lax.ppermute(small, "dp", in_plane(distance))
-        distance *= 2
-    small_sum = exchange_sum(small, plane, LINE)
-    small = small_sum.reshape(-1)
-    small_grads = []
-    first = 0
-    for size in (width, width, width, inner, width, width, width, width, width):
-        small_grads.append(small[first : first + size])
-        first += size
+    small_sends = [(small, in_plane(d)) for d in range(1, GROUP)]
+
+    def pair_sums(values):
+        while len(values) > 1:
+            values = [a + b for a, b in zip(values[::2], values[1::2])]
+        return values[0]
+
+    def line_moves(distance):
+        return [(i, (i // plane ^ distance) * plane + i % plane) for i in range(chips)]
 
     chunks = [("down", value, index) for index, value in enumerate(sums)]
     chunks += [("up", None, 2 * GROUP * core), ("up", None, 2 * GROUP * core + 1)]
-    chunks += [("up", None, GROUP * other)]
+    chunks += [("up", None, 2 * GROUP * other), ("up", None, 2 * GROUP * other + 1)]
     chunks += [("qkv", None, core), ("qkv", None, other), ("out", None, 0)]
     up_width = inner_half // GROUP
     up_block = min(512, up_width)
@@ -875,9 +842,10 @@
         for first in range(inner_half // GROUP // up_block):
             rights = [columns_from(right, length, 0, first, up_block) for right in mine]
             results.append(rows_product(lefts, rights, half, up_block, 1))
-        rights = [columns_from(theirs, length, d, 0, up_block) for d in range(GROUP)]
-        steps = inner_half // GROUP // up_block
-        return [*results, rows_product(lefts, rights, half, up_block, steps, True)]
+        for first in range(inner_half // GROUP // up_block):
+            rights = [columns_from(theirs, length, d, first, up_block) for d in range(GROUP)]
+            results.append(rows_product(lefts, rights, half, up_block, 1, True))
+        return results
 
     rest_block = half // GROUP
 
@@ -914,20 +882,32 @@
     for index, (name, value, where) in enumerate(chunks):
         if value is None:
             value = values.pop(0)
+        more, held = (), [done[-1]]
         if index == 0:
             values = segment(to_up, *hold(up_left, late), *up_right)
-        after = done[-2], {0: values, len(chunks) - 1: done[-1]}.get(index, ())
+            held.append(values)
+        if index == 4:
+            rest = segment(to_rest, *early, *late)
+            held.append(rest)
+        if index == len(chunks) - 2:
+            more = small_sends
+        if index == len(chunks) - 1:
+            small = pair_sums([small, *more_results])
+            distance = GROUP
+            while distance < plane:
+                small = small + lax.ppermute(small, "dp", in_plane(distance))
+                distance *= 2
+            lines = [lax.ppermute(small, "dp", line_moves(d)) for d in range(1, LINE)]
+            held += [done[-1], lines]
+        after = (), held
         if index > 0:
             value = line_middle(value)
-        if plane == GROUP and name in LATE:
-            pieces = spread_late(value, after)
-        else:
-            value = blocks_sum(line_end(value) if index > 0 else value)
-            pieces = spread(value, after)
+            value = line_end(value)
+        pieces, more_results = spread(blocks_sum(value), after, more)
+        value = pieces[0]
         if index == 0:
-            values = [line_start(v) for v in values]
-        if index == 3:
-            rest = segment(to_rest, *hold(early, pieces[1:3]), *late)
+            values = [line_start(v) for v in hold(values, pieces[3:])]
+        if index == 4:
             values += [line_start(v) for v in rest]
         tall, wide = value.shape
         high = min(256, tall)
@@ -950,6 +930,13 @@
         wholes[name] = place(pieces, wholes[name], places, high, broad)
         done.append(wholes[name])
 
+    small = pair_sums([small, *lines]).reshape(-1)
+    small_grads = []
+    first = 0
+    for size in (width, width, width, inner, width, width, width, width, width):
+        small_grads.append(small[first : first + size])
+        first += size
+
     return (
         output.astype(LOW)[None],
         input_grad[None],

time: 770 us -> 766 us (level)
  waiting for transfers between devices: 244 us -> 181 us
  starting transfers between devices: 156 us -> 188 us
  other arithmetic: 80.8 us -> 95.3 us
  Pallas kernels: 196 us -> 205 us
    ppermute x88 -> x98, waiting for transfers between devices: 212 us -> 173 us  [send(): self.last = [lax.ppermute(v, 'dp', m) for v, (_, m) in zip(values, sends)]]
    ppermute x88 -> x98, starting transfers between devices: 145 us -> 172 us  [send(): self.last = [lax.ppermute(v, 'dp', m) for v, (_, m) in zip(values, sends)]]
    ppermute x6 -> x3, waiting for transfers between devices: 25.1 us -> 0.01 us  [per_device(): lines = [lax.ppermute(small, 'dp', line_moves(d)) for d in range(1, LINE)]]
    add x9 -> x10, other arithmetic: 20 us -> 28.6 us  [line_middle(): return value + middle_hop.send([(value, middle_moves)])[0]]
    pallas_call x10 -> x11, Pallas kernels: 62.8 us -> 69.4 us  [place(): pl.pallas_call(functools.partial(place_kernel, high), in_specs=[pl.BlockS...]
    add x7 -> x8, other arithmetic: 14.6 us -> 19.2 us  [line_start(): return value + hold(first_hop.send([(value, inward)])[0], after)]
    unnamed x181 -> x141, local copies, waits for them, and re-layouts: 26.1 us -> 22.5 us
    pallas_call x10 -> x11, Pallas kernels: 41 us -> 42.7 us  [rows_product(): pl.pallas_call(functools.partial(product_kernel, len(lefts), turned), gri...]
  transfers between devices with their start and end apart: 110 -> 117, of which waited for: 39 -> 43; matrix products, arithmetic and copies ran while one was open for 16% -> 19% of each run, Pallas kernels for 24% -> 26%
where the time goes in v7:
time: 766 us; the launch traced here: 753 us
  Pallas kernels  205 us (27%)
  starting transfers between devices  188 us (25%)
  waiting for transfers between devices  181 us (24%)
  other arithmetic  95.3 us (12%)
  local copies, waits for them, and re-layouts  62.9 us (8%)
  matrix products  15.9 us (2%)
    ppermute x98, waiting for transfers between devices, send(): self.last = [lax.ppermute(v, 'dp', m) for v, (_, m) in zip(values, sends)]  173 us
    ppermute x98, starting transfers between devices, send(): self.last = [lax.ppermute(v, 'dp', m) for v, (_, m) in zip(values, sends)]  172 us
    pallas_call x11, Pallas kernels, place(): pl.pallas_call(functools.partial(place_kernel, high), in_specs=[pl.BlockS...  69.4 us
    pallas_call x11, Pallas kernels, rows_product(): pl.pallas_call(functools.partial(product_kernel, len(lefts), turned), gri...  42.7 us
    add x10, other arithmetic, line_middle(): return value + middle_hop.send([(value, middle_moves)])[0]  28.6 us
    pallas_call x4, Pallas kernels, times_back(): pl.pallas_call(functools.partial(back_kernel, turned), grid_spec=pltpu.Pr...  27.2 us
    pallas_call x4, Pallas kernels, times_columns(): pl.pallas_call(columns_kernel, grid_spec=pltpu.PrefetchScalarGridSpec(num...  25.1 us
    unnamed x141, local copies, waits for them, and re-layouts  22.5 us
  transfers between devices with their start and end apart: 117, of which 43 were waited for; matrix products, arithmetic and copies ran while one was open for 19% of the time, Pallas kernels for 26%

profile of v7, /device:TPU:0, one launch (start us, length us, event | category | flops | bytes accessed | tf_op | source)
XLA Modules:
  0.0 753.1 jit_solution(17107215498636560753)
XLA Ops:
  13.4 22.3 %conditional.7 = (bf16[256,1024]{1,0:T(8,128)(2,1)}, bf16[256,1024]{1,0:T(8,128)(2,1)}, bf16[256,1024]{1,0:T(8,128)(2,1)}, bf16[256,1024]{1,0:T(8,128)(2,1)}, bf...) conditional(s32[]{:T(128)} %convert_element_type.31, () %tuple.149, (bf16[128,1024]{1,0:T(8,128)(2,1)S(1)}, ...), branch_computations={%region_0.1_spmd, %region_1.2_spmd} | conditional | flops 874512384 | bytes 19710170 | solution.py:616
  41.4 37.7 %conditional.8 = (f32[128,2048]{1,0:T(8,128)}, bf16[256,1024]{1,0:T(8,128)(2,1)}, bf16[256,4096]{1,0:T(8,128)(2,1)}, bf16[256,4096]{1,0:T(8,128)(2,1)}, f32[4096...) conditional(s32[]{:T(128)} %convert_element_type.31, () %tuple.148, (bf16[256,1024]{1,0:T(8,128)(2,1)}, ...), branch_computations={%region_2.3_spmd, %region_3.4_spmd} | conditional | flops 3222536192 | bytes 42932700 | solution.py:616
  65.1 13.4 %branch_1_fun.26 = (bf16[256,4096]{1,0:T(8,128)(2,1)}, bf16[256,4096]{1,0:T(8,128)(2,1)}, f32[1,4096]{1,0:T(1,128)}) custom-call(bf16[256,2048]{1,0:T(8,128)(2,1)S(1)} %copy-done.51, bf16[4096,2048]{1,0:T(8,128)(2,1)} %get-tuple-element.204.refs_0_, f32[256,4096]{1,0:T(8,128)S(1)} %branch_1_fun.24.refs_1_, ...), custom_call_target="tpu_custom_call" | custom-call | flops 1073741824 | bytes 7602176 | tf_op jit(solution)/shard_map/cond/branch_1_fun/pallas_call | solution.py:311
  91.7 22.5 %conditional.9 = (f32[128,2048]{1,0:T(8,128)}, bf16[128,2048]{1,0:T(8,128)(2,1)}, bf16[384,2048]{1,0:T(8,128)(2,1)}, bf16[256,1024]{1,0:T(8,128)(2,1)}, bf16[256...) conditional(s32[]{:T(128)} %convert_element_type.31, () %tuple.159, ...), branch_computations={%region_4.5_spmd, %region_5.6_spmd} | conditional | flops 1079771136 | bytes 34343496 | solution.py:616
  124.8 25.4 %conditional.10 = (bf16[3,256,1024]{2,1,0:T(8,128)(2,1)}, bf16[256,3072]{1,0:T(8,128)(2,1)}, bf16[256,3072]{1,0:T(8,128)(2,1)}, bf16[4,256,256]{2,1,0:T(8,128)(2...) conditional(s32[]{:T(128)} %convert_element_type.31, () %tuple.157, ...), branch_computations={%region_6.7_spmd, %region_7.8_spmd} | conditional | flops 1250689024 | bytes 30802540 | solution.py:616
  130.5 10.8 %branch_1_fun.30 = bf16[3,256,1024]{2,1,0:T(8,128)(2,1)} custom-call(s32[1]{0:T(128)} %get-tuple-element.232.first_ref, bf16[256,1024]{1,0:T(8,128)(2,1)} %get-tuple-element.233.q_ref, bf16[256,1024]{1,0:T(8,128)(2,1)} %get-tuple-element.234.k_ref, bf16[256,1024]{1,0:T(8,128)(2,1)} %get-tuple-element.235.v_ref, ...), custom_call_target="tpu_custom_call" | custom-call | flops 167772160 | bytes 917504 | tf_op jit(solution)/shard_map/cond/branch_1_fun/pallas_call | solution.py:424
  167.2 15.2 %conditional.11 = (f32[256,1024]{1,0:T(8,128)}) conditional(s32[]{:T(128)} %convert_element_type.31, () %tuple.156, (s32[3]{0:T(128)S(1)}, bf16[256,3072]{1,0:T(8,128)(2,1)}, bf16[1024,6144]{1,0:T(8,128)(2,1)}, s32[3]{0:T(128)S(1)}, bf16[256,3072]{1,0:T(8,128)(2,1)}) %tuple.167), branch_computations={%region_8.9_spmd, %region_9.10_spmd} | conditional | flops 805306368 | bytes 4980744 | solution.py:616
  174.3 8.1 %branch_1_fun.32 = f32[256,1024]{1,0:T(8,128)} custom-call(s32[3]{0:T(128)S(1)} %get-tuple-element.239.table_ref, bf16[256,3072]{1,0:T(8,128)(2,1)} %get-tuple-element.240.left_ref, bf16[1024,6144]{1,0:T(8,128)(2,1)} %get-tuple-element.241.refs_0_, f32[256,1024]{1,0:T(8,128)S(1)} %branch_1_fun.31.refs_1_), custom_call_target="tpu_custom_call" | custom-call | flops 402653184 | bytes 2490368 | tf_op jit(solution)/shard_map/cond/branch_1_fun/pallas_call | solution.py:277
  204.2 8.7 %collective-permute-done.34 = bf16[4,256,256]{2,1,0:T(8,128)(2,1)} collective-permute-done((bf16[4,256,256]{2,1,0:T(8,128)(2,1)S(1)}, bf16[4,256,256]{2,1,0:T(8,128)(2,1)}, u32[]{:S(2)}, u32[]{:S(2)}) %collective-permute-start.34) | collective-permute-done | bytes 524320 | tf_op jit(solution)/shard_map/ppermute | solution.py:504
  214.5 7.4 collective-permute-done.35
  233.6 17.9 %conditional.13 = (bf16[1024,512]{1,0:T(8,128)(2,1)}, bf16[1024,512]{1,0:T(8,128)(2,1)}, bf16[1024,512]{1,0:T(8,128)(2,1)}, bf16[1024,512]{1,0:T(8,128)(2,1)}) conditional(s32[]{:T(128)} %convert_element_type.31, () %tuple.178, (bf16[256,1024]{1,0:T(8,128)(2,1)}, bf16[256,1024]{1,0:T(8,128)(2,1)}, bf16[256,1024]{1,0:T(8,128)(2,1)}, ...), branch_computations={%region_12.13_spmd, %region_13.14_spmd} | conditional | flops 1082130432 | bytes 15728712 | solution.py:616
  258.4 13.5 %collective-permute-start.42 = (bf16[1024,512]{1,0:T(8,128)(2,1)S(1)}, bf16[1024,512]{1,0:T(8,128)(2,1)S(1)}, u32[]{:S(2)}, u32[]{:S(2)}) collective-permute-start(bf16[1024,512]{1,0:T(8,128)(2,1)S(1)} %shard_map.279), channel_id=1, source_target_pairs={{0,4},{1,5},{2,6},{3,7},{12,8},{13,9},{14,10},{15,11},{16,20},{17,... | collective-permute-start | bytes 3145736 | tf_op jit(solution)/shard_map/ppermute | solution.py:504
  280.4 14.0 %collective-permute-done.42 = bf16[1024,512]{1,0:T(8,128)(2,1)S(1)} collective-permute-done((bf16[1024,512]{1,0:T(8,128)(2,1)S(1)}, bf16[1024,512]{1,0:T(8,128)(2,1)S(1)}, u32[]{:S(2)}, u32[]{:S(2)}) %collective-permute-start.42) | collective-permute-done | bytes 1048608 | tf_op jit(solution)/shard_map/ppermute | solution.py:504
  326.2 8.7 %collective-permute-done.43 = bf16[1024,512]{1,0:T(8,128)(2,1)S(1)} collective-permute-done((bf16[1024,512]{1,0:T(8,128)(2,1)S(1)}, bf16[1024,512]{1,0:T(8,128)(2,1)S(1)}, u32[]{:S(2)}, u32[]{:S(2)}) %collective-permute-start.43) | collective-permute-done | bytes 1048608 | tf_op jit(solution)/shard_map/ppermute | solution.py:504
  366.1 8.3 %collective-permute-done.44 = bf16[1024,512]{1,0:T(8,128)(2,1)S(1)} collective-permute-done((bf16[1024,512]{1,0:T(8,128)(2,1)S(1)}, bf16[1024,512]{1,0:T(8,128)(2,1)S(1)}, u32[]{:S(2)}, u32[]{:S(2)}) %collective-permute-start.44) | collective-permute-done | bytes 1048608 | tf_op jit(solution)/shard_map/ppermute | solution.py:504
  413.3 17.8 %conditional.12 = (bf16[1024,768]{1,0:T(8,128)(2,1)}, bf16[1024,768]{1,0:T(8,128)(2,1)}, bf16[1024,512]{1,0:T(8,128)(2,1)}) conditional(s32[]{:T(128)} %convert_element_type.31, () %tuple.176, (bf16[256,2048]{1,0:T(8,128)(2,1)}, bf16[256,2048]{1,0:T(8,128)(2,1)}, bf16[256,2048]{1,0:T(8,128)(2,1)}, bf16[256,2048]{1,0:T(8,128)(2,1)}, ...), branch_computations={%region_10.11_spmd, %region_11.12_spmd} | conditional | flops 1076887552 | bytes 17301596 | solution.py:616
  447.5 8.1 %collective-permute-start.47 = (bf16[1024,768]{1,0:T(8,128)(2,1)}, bf16[1024,768]{1,0:T(8,128)(2,1)}, u32[]{:S(2)}, u32[]{:S(2)}) collective-permute-start(bf16[1024,768]{1,0:T(8,128)(2,1)} %get-tuple-element.576), channel_id=1, source_target_pairs={{0,4},{1,5},{2,6},{3,7},{12,8},{13,9},{14,10},{15,11},{16,20},{17,... | collective-permute-start | bytes 4718600 | tf_op jit(solution)/shard_map/ppermute | solution.py:504
  478.3 7.6 %collective-permute-done.83.refs_1_ = bf16[1024,512]{1,0:T(8,128)(2,1)} collective-permute-done((bf16[1024,512]{1,0:T(8,128)(2,1)S(1)}, bf16[1024,512]{1,0:T(8,128)(2,1)}, u32[]{:S(2)}, u32[]{:S(2)}) %collective-permute-start.83) | collective-permute-done | bytes 1048608 | tf_op jit(solution)/shard_map/ppermute | solution.py:504
  589.1 18.5 %collective-permute-done.95.refs_1_ = bf16[1024,768]{1,0:T(8,128)(2,1)} collective-permute-done((bf16[1024,768]{1,0:T(8,128)(2,1)S(1)}, bf16[1024,768]{1,0:T(8,128)(2,1)}, u32[]{:S(2)}, u32[]{:S(2)}) %collective-permute-start.95) | collective-permute-done | bytes 1572896 | tf_op jit(solution)/shard_map/ppermute | solution.py:504
  648.1 11.2 %shard_map.291.refs_5_ = f32[1024,6144]{1,0:T(8,128)} custom-call(s32[96]{0:T(128)S(1)} %stack.216.table_ref, bf16[1024,768]{1,0:T(8,128)(2,1)S(1)} %broadcast_select_fusion.refs_0_, bf16[1024,768]{1,0:T(8,128)(2,1)} %collective-permute-done.95.refs_1_, bf16[1024,768]{1,0:T(8,128)(2,1)} %collective-permute-done.96.refs_2_, ...), custom_call_target="tpu_custom_call", output_to_operand_aliasing={{}: (6, {})} | custom-call | bytes 4718592 | tf_op jit(solution)/shard_map/pallas_call | solution.py:469
  664.3 8.7 %fusion.21 = f32[256,2048]{1,0:T(8,128)S(1)} fusion(bf16[256,4096]{1,0:T(8,128)(2,1)} %get-tuple-element.480, bf16[4096,2048]{1,0:T(8,128)(2,1)} %param.36), kind=kOutput, calls=%fused_computation.123 | convolution fusion | flops 4294967296 | bytes 20971520 | tf_op jit(solution)/shard_map/dot_general | solution.py:44
  674.9 18.8 %collective-permute-done.106 = bf16[1024,512]{1,0:T(8,128)(2,1)S(1)} collective-permute-done((bf16[1024,512]{1,0:T(8,128)(2,1)S(1)}, bf16[1024,512]{1,0:T(8,128)(2,1)S(1)}, u32[]{:S(2)}, u32[]{:S(2)}) %collective-permute-start.106) | collective-permute-done | bytes 1048608 | tf_op jit(solution)/shard_map/ppermute | solution.py:504
  705.5 12.1 %collective-permute-start.112 = (f32[192,128]{1,0:T(8,128)S(1)}, f32[192,128]{1,0:T(8,128)S(1)}, u32[]{:S(2)}, u32[]{:S(2)}) collective-permute-start(f32[192,128]{1,0:T(8,128)S(1)} %add_add_fusion.1), channel_id=1, source_target_pairs={{0,4},{1,5},{2,6},{3,7},{4,0},{5,1},{6,2},{7,3},{8,12},{9,13},{10,... | collective-permute-start | bytes 294920 | tf_op jit(solution)/shard_map/ppermute | solution.py:900
  722.9 10.8 %shard_map.292 = f32[1024,6144]{1,0:T(8,128)} custom-call(s32[96]{0:T(128)S(1)} %stack.163.table_ref, bf16[1024,768]{1,0:T(8,128)(2,1)S(1)} %broadcast_select_fusion.1.refs_0_, bf16[1024,768]{1,0:T(8,128)(2,1)} %collective-permute-done.99.refs_1_, bf16[1024,768]{1,0:T(8,128)(2,1)} %collective-permute-done.100.refs_2_, ...), custom_call_target="tpu_custom_call", output_to_operand_aliasing={{}: (6, {})} | custom-call | bytes 4718592 | tf_op jit(solution)/shard_map/pallas_call | solution.py:469
  (524 shorter events, 559.2 us)
Async XLA Ops:
  35.7 43.4 %collective-permute-start.16 = (bf16[256,2048]{1,0:T(8,128)(2,1)}, bf16[256,2048]{1,0:T(8,128)(2,1)}, u32[]{:S(2)}, u32[]{:S(2)}) collective-permute-start(bf16[256,2048]{1,0:T(8,128)(2,1)} %get-tuple-element.536), channel_id=1, source_target_pairs={{0,1},{1,0},{2,3},{3,2},{4,5},{5,4},{6,7},{7,6},{8,9},{9,8},{10,11... | collective-permute-start | bytes 3145736 | tf_op jit(solution)/shard_map/ppermute | solution.py:504
  37.8 47.7 %collective-permute-start.17 = (bf16[256,2048]{1,0:T(8,128)(2,1)}, bf16[256,2048]{1,0:T(8,128)(2,1)}, u32[]{:S(2)}, u32[]{:S(2)}) collective-permute-start(bf16[256,2048]{1,0:T(8,128)(2,1)} %get-tuple-element.536), channel_id=1, source_target_pairs={{0,2},{1,3},{2,0},{3,1},{4,6},{5,7},{6,4},{7,5},{8,10},{9,11},{10,... | collective-permute-start | bytes 3145736 | tf_op jit(solution)/shard_map/ppermute | solution.py:504
  39.3 46.2 %collective-permute-start.18 = (bf16[256,2048]{1,0:T(8,128)(2,1)}, bf16[256,2048]{1,0:T(8,128)(2,1)}, u32[]{:S(2)}, u32[]{:S(2)}) collective-permute-start(bf16[256,2048]{1,0:T(8,128)(2,1)} %get-tuple-element.536), channel_id=1, source_target_pairs={{0,3},{1,2},{2,1},{3,0},{4,7},{5,6},{6,5},{7,4},{8,11},{9,10},{10,... | collective-permute-start | bytes 3145736 | tf_op jit(solution)/shard_map/ppermute | solution.py:504
  116.8 37.0 %collective-permute-start.26 = (bf16[1024,512]{1,0:T(8,128)(2,1)S(1)}, bf16[1024,512]{1,0:T(8,128)(2,1)}, u32[]{:S(2)}, u32[]{:S(2)}) collective-permute-start(bf16[1024,512]{1,0:T(8,128)(2,1)S(1)} %shard_map.275), channel_id=1, source_target_pairs={{0,4},{1,5},{2,6},{3,7},{12,8},{13,9},{14,10},{15,11},{16,20},{17,... | collective-permute-start | bytes 3145736 | tf_op jit(solution)/shard_map/ppermute | solution.py:504
  121.3 32.4 %collective-permute-start.23 = (bf16[256,1024]{1,0:T(8,128)(2,1)}, bf16[256,1024]{1,0:T(8,128)(2,1)}, u32[]{:S(2)}, u32[]{:S(2)}) collective-permute-start(bf16[256,1024]{1,0:T(8,128)(2,1)} %get-tuple-element.506), channel_id=1, source_target_pairs={{0,1},{1,0},{2,3},{3,2},{4,5},{5,4},{6,7},{7,6},{8,9},{9,8},{10,11... | collective-permute-start | bytes 1572872 | tf_op jit(solution)/shard_map/ppermute | solution.py:504
  228.2 43.7 %collective-permute-start.58 = (bf16[1024,512]{1,0:T(8,128)(2,1)}, bf16[1024,512]{1,0:T(8,128)(2,1)}, u32[]{:S(2)}, u32[]{:S(2)}) collective-permute-start(bf16[1024,512]{1,0:T(8,128)(2,1)} %add.360), channel_id=1, source_target_pairs={{4,0},{5,1},{6,2},{7,3},{8,12},{9,13},{10,14},{11,15},{20,16},{21,... | collective-permute-start | bytes 3145736 | tf_op jit(solution)/shard_map/ppermute | solution.py:504
  232.0 44.2 %collective-permute-start.50 = (bf16[1024,512]{1,0:T(8,128)(2,1)}, bf16[1024,512]{1,0:T(8,128)(2,1)}, u32[]{:S(2)}, u32[]{:S(2)}) collective-permute-start(bf16[1024,512]{1,0:T(8,128)(2,1)} %add.350), channel_id=1, source_target_pairs={{4,8},{5,9},{6,10},{7,11},{8,4},{9,5},{10,6},{11,7},{20,24},{21,25... | collective-permute-start | bytes 3145736 | tf_op jit(solution)/shard_map/ppermute | solution.py:504
  258.4 35.9 %collective-permute-start.42 = (bf16[1024,512]{1,0:T(8,128)(2,1)S(1)}, bf16[1024,512]{1,0:T(8,128)(2,1)S(1)}, u32[]{:S(2)}, u32[]{:S(2)}) collective-permute-start(bf16[1024,512]{1,0:T(8,128)(2,1)S(1)} %shard_map.279), channel_id=1, source_target_pairs={{0,4},{1,5},{2,6},{3,7},{12,8},{13,9},{14,10},{15,11},{16,20},{17,... | collective-permute-start | bytes 3145736 | tf_op jit(solution)/shard_map/ppermute | solution.py:504
  279.1 35.0 %collective-permute-start.59 = (bf16[1024,512]{1,0:T(8,128)(2,1)}, bf16[1024,512]{1,0:T(8,128)(2,1)}, u32[]{:S(2)}, u32[]{:S(2)}) collective-permute-start(bf16[1024,512]{1,0:T(8,128)(2,1)} %add.359), channel_id=1, source_target_pairs={{4,0},{5,1},{6,2},{7,3},{8,12},{9,13},{10,14},{11,15},{20,16},{21,... | collective-permute-start | bytes 3145736 | tf_op jit(solution)/shard_map/ppermute | solution.py:504
  374.4 32.6 %collective-permute-start.45 = (bf16[1024,512]{1,0:T(8,128)(2,1)}, bf16[1024,512]{1,0:T(8,128)(2,1)}, u32[]{:S(2)}, u32[]{:S(2)}) collective-permute-start(bf16[1024,512]{1,0:T(8,128)(2,1)} %get-tuple-element.574), channel_id=1, source_target_pairs={{0,4},{1,5},{2,6},{3,7},{12,8},{13,9},{14,10},{15,11},{16,20},{17,... | collective-permute-start | bytes 3145736 | tf_op jit(solution)/shard_map/ppermute | solution.py:504
  405.1 39.0 %collective-permute-start.79 = (bf16[1024,512]{1,0:T(8,128)(2,1)S(1)}, bf16[1024,512]{1,0:T(8,128)(2,1)S(1)}, u32[]{:S(2)}, u32[]{:S(2)}) collective-permute-start(bf16[1024,512]{1,0:T(8,128)(2,1)S(1)} %broadcast_select_fusion.6.refs_0_), channel_id=1, source_target_pairs={{0,1},{1,0},{2,3},{3,2},{4,5},{5,4},{6,7},{7,6},{8,9},{9,8},{10,11... | collective-permute-start | bytes 3145736 | tf_op jit(solution)/shard_map/ppermute | solution.py:504
  406.9 37.2 %collective-permute-start.80 = (bf16[1024,512]{1,0:T(8,128)(2,1)S(1)}, bf16[1024,512]{1,0:T(8,128)(2,1)}, u32[]{:S(2)}, u32[]{:S(2)}) collective-permute-start(bf16[1024,512]{1,0:T(8,128)(2,1)S(1)} %broadcast_select_fusion.6.refs_0_), channel_id=1, source_target_pairs={{0,2},{1,3},{2,0},{3,1},{4,6},{5,7},{6,4},{7,5},{8,10},{9,11},{10,... | collective-permute-start | bytes 3145736 | tf_op jit(solution)/shard_map/ppermute | solution.py:504
  406.9 40.6 %collective-permute-start.46 = (bf16[1024,512]{1,0:T(8,128)(2,1)}, bf16[1024,512]{1,0:T(8,128)(2,1)}, u32[]{:S(2)}, u32[]{:S(2)}) collective-permute-start(bf16[1024,512]{1,0:T(8,128)(2,1)} %get-tuple-element.575), channel_id=1, source_target_pairs={{0,4},{1,5},{2,6},{3,7},{12,8},{13,9},{14,10},{15,11},{16,20},{17,... | collective-permute-start | bytes 3145736 | tf_op jit(solution)/shard_map/ppermute | solution.py:504
  412.0 43.6 %collective-permute-start.62 = (bf16[1024,512]{1,0:T(8,128)(2,1)}, bf16[1024,512]{1,0:T(8,128)(2,1)}, u32[]{:S(2)}, u32[]{:S(2)}) collective-permute-start(bf16[1024,512]{1,0:T(8,128)(2,1)} %add.356), channel_id=1, source_target_pairs={{4,0},{5,1},{6,2},{7,3},{8,12},{9,13},{10,14},{11,15},{20,16},{21,... | collective-permute-start | bytes 3145736 | tf_op jit(solution)/shard_map/ppermute | solution.py:504
  447.5 41.9 %collective-permute-start.47 = (bf16[1024,768]{1,0:T(8,128)(2,1)}, bf16[1024,768]{1,0:T(8,128)(2,1)}, u32[]{:S(2)}, u32[]{:S(2)}) collective-permute-start(bf16[1024,768]{1,0:T(8,128)(2,1)} %get-tuple-element.576), channel_id=1, source_target_pairs={{0,4},{1,5},{2,6},{3,7},{12,8},{13,9},{14,10},{15,11},{16,20},{17,... | collective-permute-start | bytes 4718600 | tf_op jit(solution)/shard_map/ppermute | solution.py:504
  492.9 36.1 %collective-permute-start.56 = (bf16[1024,768]{1,0:T(8,128)(2,1)}, bf16[1024,768]{1,0:T(8,128)(2,1)}, u32[]{:S(2)}, u32[]{:S(2)}) collective-permute-start(bf16[1024,768]{1,0:T(8,128)(2,1)} %add.344), channel_id=1, source_target_pairs={{4,8},{5,9},{6,10},{7,11},{8,4},{9,5},{10,6},{11,7},{20,24},{21,25... | collective-permute-start | bytes 4718600 | tf_op jit(solution)/shard_map/ppermute | solution.py:504
  508.9 36.9 %collective-permute-start.48 = (bf16[1024,768]{1,0:T(8,128)(2,1)}, bf16[1024,768]{1,0:T(8,128)(2,1)}, u32[]{:S(2)}, u32[]{:S(2)}) collective-permute-start(bf16[1024,768]{1,0:T(8,128)(2,1)} %get-tuple-element.577), channel_id=1, source_target_pairs={{0,4},{1,5},{2,6},{3,7},{12,8},{13,9},{14,10},{15,11},{16,20},{17,... | collective-permute-start | bytes 4718600 | tf_op jit(solution)/shard_map/ppermute | solution.py:504
  532.4 37.5 %collective-permute-start.65 = (bf16[1024,768]{1,0:T(8,128)(2,1)}, bf16[1024,768]{1,0:T(8,128)(2,1)}, u32[]{:S(2)}, u32[]{:S(2)}) collective-permute-start(bf16[1024,768]{1,0:T(8,128)(2,1)} %add.353), channel_id=1, source_target_pairs={{4,0},{5,1},{6,2},{7,3},{8,12},{9,13},{10,14},{11,15},{20,16},{21,... | collective-permute-start | bytes 4718600 | tf_op jit(solution)/shard_map/ppermute | solution.py:504
  576.7 33.0 %collective-permute-start.96 = (bf16[1024,768]{1,0:T(8,128)(2,1)S(1)}, bf16[1024,768]{1,0:T(8,128)(2,1)}, u32[]{:S(2)}, u32[]{:S(2)}) collective-permute-start(bf16[1024,768]{1,0:T(8,128)(2,1)S(1)} %broadcast_select_fusion.refs_0_), channel_id=1, source_target_pairs={{0,2},{1,3},{2,0},{3,1},{4,6},{5,7},{6,4},{7,5},{8,10},{9,11},{10,... | collective-permute-start | bytes 4718600 | tf_op jit(solution)/shard_map/ppermute | solution.py:504
  581.2 39.7 %collective-permute-start.66 = (bf16[1024,768]{1,0:T(8,128)(2,1)}, bf16[1024,768]{1,0:T(8,128)(2,1)}, u32[]{:S(2)}, u32[]{:S(2)}) collective-permute-start(bf16[1024,768]{1,0:T(8,128)(2,1)} %add.352), channel_id=1, source_target_pairs={{4,0},{5,1},{6,2},{7,3},{8,12},{9,13},{10,14},{11,15},{20,16},{21,... | collective-permute-start | bytes 4718600 | tf_op jit(solution)/shard_map/ppermute | solution.py:504
  646.6 47.1 %collective-permute-start.106 = (bf16[1024,512]{1,0:T(8,128)(2,1)S(1)}, bf16[1024,512]{1,0:T(8,128)(2,1)S(1)}, u32[]{:S(2)}, u32[]{:S(2)}) collective-permute-start(bf16[1024,512]{1,0:T(8,128)(2,1)S(1)} %add.748), channel_id=1, source_target_pairs={{4,0},{5,1},{6,2},{7,3},{8,12},{9,13},{10,14},{11,15},{20,16},{21,... | collective-permute-start | bytes 3145736 | tf_op jit(solution)/shard_map/ppermute | solution.py:504
  661.8 39.8 %collective-permute-start.102 = (bf16[512,768]{1,0:T(8,128)(2,1)S(1)}, bf16[512,768]{1,0:T(8,128)(2,1)S(1)}, u32[]{:S(2)}, u32[]{:S(2)}) collective-permute-start(bf16[512,768]{1,0:T(8,128)(2,1)S(1)} %slice.256), channel_id=1, source_target_pairs={{0,2},{1,3},{2,0},{3,1},{4,6},{5,7},{6,4},{7,5},{8,10},{9,11},{10,... | collective-permute-start | bytes 2359304 | tf_op jit(solution)/shard_map/ppermute | solution.py:504
  663.0 38.5 %collective-permute-start.103 = (bf16[512,768]{1,0:T(8,128)(2,1)S(1)}, bf16[512,768]{1,0:T(8,128)(2,1)S(1)}, u32[]{:S(2)}, u32[]{:S(2)}) collective-permute-start(bf16[512,768]{1,0:T(8,128)(2,1)S(1)} %slice.257), channel_id=1, source_target_pairs={{0,1},{1,0},{2,3},{3,2},{4,5},{5,4},{6,7},{7,6},{8,9},{9,8},{10,11... | collective-permute-start | bytes 2359304 | tf_op jit(solution)/shard_map/ppermute | solution.py:504
  674.1 43.9 %collective-permute-start.19 = (f32[128,2048]{1,0:T(8,128)}, f32[128,2048]{1,0:T(8,128)}, u32[]{:S(2)}, u32[]{:S(2)}) collective-permute-start(f32[128,2048]{1,0:T(8,128)} %slice.237), channel_id=1, source_target_pairs={{0,16},{16,0},{1,17},{17,1},{2,18},{18,2},{3,19},{19,3},{4,20},{20... | collective-permute-start | bytes 3145736 | tf_op jit(solution)/shard_map/ppermute | solution.py:542
  (164 other events, 2381.7 us)

commit v8 on v7

--- a/solution.py
+++ b/solution.py
@@ -877,17 +877,19 @@
         "qkv": blank((half, 3 * width)),
     }
     size = inner_half // GROUP
-    values = []
+    begun, raw = sums, []
     done = [(), ()]
     for index, (name, value, where) in enumerate(chunks):
-        if value is None:
-            value = values.pop(0)
+        value = begun[index]
         more, held = (), [done[-1]]
         if index == 0:
-            values = segment(to_up, *hold(up_left, late), *up_right)
-            held.append(values)
+            held.append(begun[3])
+        if index == 1:
+            raw += segment(to_up, *hold(up_left, late), *up_right)
+            held.append(raw)
         if index == 4:
             rest = segment(to_rest, *early, *late)
+            raw += rest
             held.append(rest)
         if index == len(chunks) - 2:
             more = small_sends
@@ -900,15 +902,13 @@
             lines = [lax.ppermute(small, "dp", line_moves(d)) for d in range(1, LINE)]
             held += [done[-1], lines]
         after = (), held
-        if index > 0:
-            value = line_middle(value)
-            value = line_end(value)
+        if 0 < index < len(chunks) - 1:
+            value = line_end(line_middle(value))
+        if index == len(chunks) - 2:
+            begun[-1] = line_end(line_middle(begun[-1]))
+            held.append(begun[-1])
         pieces, more_results = spread(blocks_sum(value), after, more)
         value = pieces[0]
-        if index == 0:
-            values = [line_start(v) for v in hold(values, pieces[3:])]
-        if index == 4:
-            values += [line_start(v) for v in rest]
         tall, wide = value.shape
         high = min(256, tall)
         broad = wide // 3 if name == "qkv" else wide
@@ -929,6 +929,12 @@
                     places += [row, column]
         wholes[name] = place(pieces, wholes[name], places, high, broad)
         done.append(wholes[name])
+        while len(begun) < len(chunks) and raw:
+            number = len(begun)
+            placed = number - (4 if number < 8 else 5)
+            if placed > index:
+                break
+            begun.append(line_start(hold(raw.pop(0), done[placed + 2])))
 
     small = pair_sums([small, *lines]).reshape(-1)
     small_grads = []

time: 766 us -> 762 us (level)
  starting transfers between devices: 188 us -> 175 us
  waiting for transfers between devices: 181 us -> 189 us
    unnamed x141 -> x149, local copies, waits for them, and re-layouts: 22.5 us -> 33.7 us
    ppermute x3, starting transfers between devices: 14.5 us -> 4.44 us  [per_device(): lines = [lax.ppermute(small, 'dp', line_moves(d)) for d in range(1, LINE)]]
    ppermute x98, waiting for transfers between devices: 173 us -> 181 us  [send(): self.last = [lax.ppermute(v, 'dp', m) for v, (_, m) in zip(values, sends)]]
  transfers between devices with their start and end apart: 117 -> 117, of which waited for: 43 -> 46; matrix products, arithmetic and copies ran while one was open for 19% -> 18% of each run, Pallas kernels for 26% -> 26%
where the time goes in v8:
time: 762 us; the launch traced here: 749 us
  Pallas kernels  203 us (27%)
  waiting for transfers between devices  189 us (25%)
  starting transfers between devices  175 us (23%)
  other arithmetic  90.5 us (12%)
  local copies, waits for them, and re-layouts  70.2 us (9%)
  matrix products  16 us (2%)
    ppermute x98, waiting for transfers between devices, send(): self.last = [lax.ppermute(v, 'dp', m) for v, (_, m) in zip(values, sends)]  181 us
    ppermute x98, starting transfers between devices, send(): self.last = [lax.ppermute(v, 'dp', m) for v, (_, m) in zip(values, sends)]  169 us
    pallas_call x11, Pallas kernels, place(): pl.pallas_call(functools.partial(place_kernel, high), in_specs=[pl.BlockS...  68.1 us
    pallas_call x11, Pallas kernels, rows_product(): pl.pallas_call(functools.partial(product_kernel, len(lefts), turned), gri...  42.4 us
    unnamed x149, local copies, waits for them, and re-layouts  33.7 us
    pallas_call x4, Pallas kernels, times_back(): pl.pallas_call(functools.partial(back_kernel, turned), grid_spec=pltpu.Pr...  27.1 us
    add x10, other arithmetic, line_middle(): return value + middle_hop.send([(value, middle_moves)])[0]  25.5 us
    pallas_call x4, Pallas kernels, times_columns(): pl.pallas_call(columns_kernel, grid_spec=pltpu.PrefetchScalarGridSpec(num...  25.2 us
  transfers between devices with their start and end apart: 117, of which 46 were waited for; matrix products, arithmetic and copies ran while one was open for 18% of the time, Pallas kernels for 26%

profile of v8, /device:TPU:0, one launch (start us, length us, event | category | flops | bytes accessed | tf_op | source)
XLA Modules:
  0.0 749.2 jit_solution(12076118694681505981)
XLA Ops:
  14.0 21.4 %conditional.7 = (bf16[256,1024]{1,0:T(8,128)(2,1)}, bf16[256,1024]{1,0:T(8,128)(2,1)}, bf16[256,1024]{1,0:T(8,128)(2,1)}, bf16[256,1024]{1,0:T(8,128)(2,1)}, bf...) conditional(s32[]{:T(128)} %convert_element_type.31, () %tuple.155, (bf16[128,1024]{1,0:T(8,128)(2,1)S(1)}, ...), branch_computations={%region_0.1_spmd, %region_1.2_spmd} | conditional | flops 874512384 | bytes 19710170 | solution.py:616
  41.7 37.8 %conditional.8 = (f32[128,2048]{1,0:T(8,128)}, bf16[256,1024]{1,0:T(8,128)(2,1)}, bf16[256,4096]{1,0:T(8,128)(2,1)}, bf16[256,4096]{1,0:T(8,128)(2,1)}, f32[4096...) conditional(s32[]{:T(128)} %convert_element_type.31, () %tuple.154, (bf16[256,1024]{1,0:T(8,128)(2,1)}, ...), branch_computations={%region_2.3_spmd, %region_3.4_spmd} | conditional | flops 3222536192 | bytes 42932700 | solution.py:616
  65.3 13.4 %branch_1_fun.26 = (bf16[256,4096]{1,0:T(8,128)(2,1)}, bf16[256,4096]{1,0:T(8,128)(2,1)}, f32[1,4096]{1,0:T(1,128)}) custom-call(bf16[256,2048]{1,0:T(8,128)(2,1)S(1)} %copy-done.58, bf16[4096,2048]{1,0:T(8,128)(2,1)} %get-tuple-element.204.refs_0_, f32[256,4096]{1,0:T(8,128)S(1)} %branch_1_fun.24.refs_1_, ...), custom_call_target="tpu_custom_call" | custom-call | flops 1073741824 | bytes 7602176 | tf_op jit(solution)/shard_map/cond/branch_1_fun/pallas_call | solution.py:311
  91.2 22.9 %conditional.9 = (f32[128,2048]{1,0:T(8,128)}, bf16[128,2048]{1,0:T(8,128)(2,1)}, bf16[384,2048]{1,0:T(8,128)(2,1)}, bf16[256,1024]{1,0:T(8,128)(2,1)}, bf16[256...) conditional(s32[]{:T(128)} %convert_element_type.31, () %tuple.165, ...), branch_computations={%region_4.5_spmd, %region_5.6_spmd} | conditional | flops 1079771136 | bytes 34343496 | solution.py:616
  124.7 24.0 %conditional.10 = (bf16[3,256,1024]{2,1,0:T(8,128)(2,1)}, bf16[256,3072]{1,0:T(8,128)(2,1)}, bf16[256,3072]{1,0:T(8,128)(2,1)}, bf16[4,256,256]{2,1,0:T(8,128)(2...) conditional(s32[]{:T(128)} %convert_element_type.31, () %tuple.163, ...), branch_computations={%region_6.7_spmd, %region_7.8_spmd} | conditional | flops 1250689024 | bytes 43385508 | solution.py:616
  130.4 10.3 %branch_1_fun.30 = bf16[3,256,1024]{2,1,0:T(8,128)(2,1)S(1)} custom-call(s32[1]{0:T(128)} %get-tuple-element.232.first_ref, bf16[256,1024]{1,0:T(8,128)(2,1)} %get-tuple-element.233.q_ref, bf16[256,1024]{1,0:T(8,128)(2,1)} %get-tuple-element.234.k_ref, bf16[256,1024]{1,0:T(8,128)(2,1)} %get-tuple-element.235.v_ref, ...), custom_call_target="tpu_custom_call" | custom-call | flops 167772160 | bytes 917504 | tf_op jit(solution)/shard_map/cond/branch_1_fun/pallas_call | solution.py:424
  164.8 15.2 %conditional.11 = (f32[256,1024]{1,0:T(8,128)}) conditional(s32[]{:T(128)} %convert_element_type.31, () %tuple.162, (s32[3]{0:T(128)S(1)}, bf16[256,3072]{1,0:T(8,128)(2,1)}, bf16[1024,6144]{1,0:T(8,128)(2,1)}, s32[3]{0:T(128)S(1)}, bf16[256,3072]{1,0:T(8,128)(2,1)}) %tuple.173), branch_computations={%region_8.9_spmd, %region_9.10_spmd} | conditional | flops 805306368 | bytes 4980744 | solution.py:616
  171.9 8.1 %branch_1_fun.32 = f32[256,1024]{1,0:T(8,128)} custom-call(s32[3]{0:T(128)S(1)} %get-tuple-element.239.table_ref, bf16[256,3072]{1,0:T(8,128)(2,1)} %get-tuple-element.240.left_ref, bf16[1024,6144]{1,0:T(8,128)(2,1)} %get-tuple-element.241.refs_0_, f32[256,1024]{1,0:T(8,128)S(1)} %branch_1_fun.31.refs_1_), custom_call_target="tpu_custom_call" | custom-call | flops 402653184 | bytes 2490368 | tf_op jit(solution)/shard_map/cond/branch_1_fun/pallas_call | solution.py:277
  202.4 8.7 %collective-permute-done.34 = bf16[4,256,256]{2,1,0:T(8,128)(2,1)} collective-permute-done((bf16[4,256,256]{2,1,0:T(8,128)(2,1)S(1)}, bf16[4,256,256]{2,1,0:T(8,128)(2,1)}, u32[]{:S(2)}, u32[]{:S(2)}) %collective-permute-start.34) | collective-permute-done | bytes 524320 | tf_op jit(solution)/shard_map/ppermute | solution.py:504
  231.1 11.2 %collective-permute-done.40 = bf16[1024,512]{1,0:T(8,128)(2,1)S(1)} collective-permute-done((bf16[1024,512]{1,0:T(8,128)(2,1)S(1)}, bf16[1024,512]{1,0:T(8,128)(2,1)S(1)}, u32[]{:S(2)}, u32[]{:S(2)}) %collective-permute-start.40) | collective-permute-done | bytes 1048608 | tf_op jit(solution)/shard_map/ppermute | solution.py:504
  266.6 17.5 %conditional.13 = (bf16[1024,512]{1,0:T(8,128)(2,1)}, bf16[1024,512]{1,0:T(8,128)(2,1)}, bf16[1024,512]{1,0:T(8,128)(2,1)}, bf16[1024,512]{1,0:T(8,128)(2,1)}) conditional(s32[]{:T(128)} %convert_element_type.31, () %tuple.184, (bf16[256,1024]{1,0:T(8,128)(2,1)}, bf16[256,1024]{1,0:T(8,128)(2,1)}, bf16[256,1024]{1,0:T(8,128)(2,1)}, ...), branch_computations={%region_12.13_spmd, %region_13.14_spmd} | conditional | flops 1082130432 | bytes 15728712 | solution.py:616
  316.6 9.7 %collective-permute-done.43 = bf16[1024,512]{1,0:T(8,128)(2,1)S(1)} collective-permute-done((bf16[1024,512]{1,0:T(8,128)(2,1)S(1)}, bf16[1024,512]{1,0:T(8,128)(2,1)S(1)}, u32[]{:S(2)}, u32[]{:S(2)}) %collective-permute-start.43) | collective-permute-done | bytes 1048608 | tf_op jit(solution)/shard_map/ppermute | solution.py:504
  412.9 17.4 %conditional.12 = (bf16[1024,768]{1,0:T(8,128)(2,1)}, bf16[1024,768]{1,0:T(8,128)(2,1)}, bf16[1024,512]{1,0:T(8,128)(2,1)}) conditional(s32[]{:T(128)} %convert_element_type.31, () %tuple.182, (bf16[256,2048]{1,0:T(8,128)(2,1)S(1)}, bf16[256,2048]{1,0:T(8,128)(2,1)}, bf16[256,2048]{1,0:T(8,128)(2,1)}, bf16[256,2048]{1,0:T(8,128)(2,1)}, ...), branch_computations={%region_10.11_spmd, %region_11.12_spmd} | conditional | flops 1076887552 | bytes 17301596 | solution.py:616
  435.7 9.1 %collective-permute-start.71 = (bf16[1024,768]{1,0:T(8,128)(2,1)}, bf16[1024,768]{1,0:T(8,128)(2,1)}, u32[]{:S(2)}, u32[]{:S(2)}) collective-permute-start(bf16[1024,768]{1,0:T(8,128)(2,1)} %get-tuple-element.608), channel_id=1, source_target_pairs={{0,4},{1,5},{2,6},{3,7},{12,8},{13,9},{14,10},{15,11},{16,20},{17,... | collective-permute-start | bytes 4718600 | tf_op jit(solution)/shard_map/ppermute | solution.py:504
  465.1 8.6 %collective-permute-done.83.refs_1_ = bf16[1024,512]{1,0:T(8,128)(2,1)} collective-permute-done((bf16[1024,512]{1,0:T(8,128)(2,1)S(1)}, bf16[1024,512]{1,0:T(8,128)(2,1)}, u32[]{:S(2)}, u32[]{:S(2)}) %collective-permute-start.83) | collective-permute-done | bytes 1048608 | tf_op jit(solution)/shard_map/ppermute | solution.py:504
  482.9 8.4 %collective-permute-done.79 = bf16[1024,512]{1,0:T(8,128)(2,1)} collective-permute-done((bf16[1024,512]{1,0:T(8,128)(2,1)}, bf16[1024,512]{1,0:T(8,128)(2,1)}, u32[]{:S(2)}, u32[]{:S(2)}) %collective-permute-start.79) | collective-permute-done | bytes 1048608 | tf_op jit(solution)/shard_map/ppermute | solution.py:504
  576.5 11.5 %collective-permute-start.102 = (bf16[1024,512]{1,0:T(8,128)(2,1)}, bf16[1024,512]{1,0:T(8,128)(2,1)S(1)}, u32[]{:S(2)}, u32[]{:S(2)}) collective-permute-start(bf16[1024,512]{1,0:T(8,128)(2,1)} %get-tuple-element.647), channel_id=1, source_target_pairs={{0,4},{1,5},{2,6},{3,7},{12,8},{13,9},{14,10},{15,11},{16,20},{17,... | collective-permute-start | bytes 3145736 | tf_op jit(solution)/shard_map/ppermute | solution.py:504
  588.1 19.0 %collective-permute-done.102 = bf16[1024,512]{1,0:T(8,128)(2,1)S(1)} collective-permute-done((bf16[1024,512]{1,0:T(8,128)(2,1)}, bf16[1024,512]{1,0:T(8,128)(2,1)S(1)}, u32[]{:S(2)}, u32[]{:S(2)}) %collective-permute-start.102) | collective-permute-done | bytes 1048608 | tf_op jit(solution)/shard_map/ppermute | solution.py:504
  627.9 12.1 %collective-permute-done.97.refs_3_ = bf16[512,768]{1,0:T(8,128)(2,1)} collective-permute-done((bf16[512,768]{1,0:T(8,128)(2,1)}, bf16[512,768]{1,0:T(8,128)(2,1)}, u32[]{:S(2)}, u32[]{:S(2)}) %collective-permute-start.97) | collective-permute-done | bytes 786464 | tf_op jit(solution)/shard_map/ppermute | solution.py:504
  652.4 13.5 %collective-permute-done.104 = bf16[1024,512]{1,0:T(8,128)(2,1)} collective-permute-done((bf16[1024,512]{1,0:T(8,128)(2,1)}, bf16[1024,512]{1,0:T(8,128)(2,1)}, u32[]{:S(2)}, u32[]{:S(2)}) %collective-permute-start.104) | collective-permute-done | bytes 1048608 | tf_op jit(solution)/shard_map/ppermute | solution.py:504
  668.2 11.2 %shard_map.291.refs_5_ = f32[1024,6144]{1,0:T(8,128)} custom-call(s32[96]{0:T(128)S(1)} %stack.216.table_ref, bf16[1024,768]{1,0:T(8,128)(2,1)S(1)} %broadcast_select_fusion.refs_0_, bf16[1024,768]{1,0:T(8,128)(2,1)} %collective-permute-done.95.refs_1_, bf16[1024,768]{1,0:T(8,128)(2,1)} %collective-permute-done.96.refs_2_, ...), custom_call_target="tpu_custom_call", output_to_operand_aliasing={{}: (6, {})} | custom-call | bytes 4718592 | tf_op jit(solution)/shard_map/pallas_call | solution.py:469
  683.5 8.7 %fusion.21 = f32[256,2048]{1,0:T(8,128)S(1)} fusion(bf16[256,4096]{1,0:T(8,128)(2,1)} %get-tuple-element.483, bf16[4096,2048]{1,0:T(8,128)(2,1)} %param.36), kind=kOutput, calls=%fused_computation.123 | convolution fusion | flops 4294967296 | bytes 20971520 | tf_op jit(solution)/shard_map/dot_general | solution.py:44
  717.0 10.8 %shard_map.292 = f32[1024,6144]{1,0:T(8,128)} custom-call(s32[96]{0:T(128)S(1)} %stack.163.table_ref, bf16[1024,768]{1,0:T(8,128)(2,1)S(1)} %broadcast_select_fusion.1.refs_0_, bf16[1024,768]{1,0:T(8,128)(2,1)} %collective-permute-done.99.refs_1_, bf16[1024,768]{1,0:T(8,128)(2,1)} %collective-permute-done.100.refs_2_, ...), custom_call_target="tpu_custom_call", output_to_operand_aliasing={{}: (6, {})} | custom-call | bytes 4718592 | tf_op jit(solution)/shard_map/pallas_call | solution.py:469
  734.2 8.3 %collective-permute-done.115.refs_3_ = bf16[512,512]{1,0:T(8,128)(2,1)S(1)} collective-permute-done((bf16[512,512]{1,0:T(8,128)(2,1)S(1)}, bf16[512,512]{1,0:T(8,128)(2,1)S(1)}, u32[]{:S(2)}, u32[]{:S(2)}) %collective-permute-start.115) | collective-permute-done | bytes 524320 | tf_op jit(solution)/shard_map/ppermute | solution.py:504
  (536 shorter events, 561.3 us)
Async XLA Ops:
  35.8 43.6 %collective-permute-start.16 = (bf16[256,2048]{1,0:T(8,128)(2,1)S(1)}, bf16[256,2048]{1,0:T(8,128)(2,1)}, u32[]{:S(2)}, u32[]{:S(2)}) collective-permute-start(bf16[256,2048]{1,0:T(8,128)(2,1)S(1)} %get-tuple-element.539), channel_id=1, source_target_pairs={{0,1},{1,0},{2,3},{3,2},{4,5},{5,4},{6,7},{7,6},{8,9},{9,8},{10,11... | collective-permute-start | bytes 3145736 | tf_op jit(solution)/shard_map/ppermute | solution.py:504
  37.5 47.5 %collective-permute-start.17 = (bf16[256,2048]{1,0:T(8,128)(2,1)S(1)}, bf16[256,2048]{1,0:T(8,128)(2,1)}, u32[]{:S(2)}, u32[]{:S(2)}) collective-permute-start(bf16[256,2048]{1,0:T(8,128)(2,1)S(1)} %get-tuple-element.539), channel_id=1, source_target_pairs={{0,2},{1,3},{2,0},{3,1},{4,6},{5,7},{6,4},{7,5},{8,10},{9,11},{10,... | collective-permute-start | bytes 3145736 | tf_op jit(solution)/shard_map/ppermute | solution.py:504
  39.0 46.0 %collective-permute-start.18 = (bf16[256,2048]{1,0:T(8,128)(2,1)S(1)}, bf16[256,2048]{1,0:T(8,128)(2,1)}, u32[]{:S(2)}, u32[]{:S(2)}) collective-permute-start(bf16[256,2048]{1,0:T(8,128)(2,1)S(1)} %get-tuple-element.539), channel_id=1, source_target_pairs={{0,3},{1,2},{2,1},{3,0},{4,7},{5,6},{6,5},{7,4},{8,11},{9,10},{10,... | collective-permute-start | bytes 3145736 | tf_op jit(solution)/shard_map/ppermute | solution.py:504
  116.7 35.5 %collective-permute-start.26 = (bf16[1024,512]{1,0:T(8,128)(2,1)S(1)}, bf16[1024,512]{1,0:T(8,128)(2,1)}, u32[]{:S(2)}, u32[]{:S(2)}) collective-permute-start(bf16[1024,512]{1,0:T(8,128)(2,1)S(1)} %shard_map.275), channel_id=1, source_target_pairs={{0,4},{1,5},{2,6},{3,7},{12,8},{13,9},{14,10},{15,11},{16,20},{17,... | collective-permute-start | bytes 3145736 | tf_op jit(solution)/shard_map/ppermute | solution.py:504
  152.2 33.2 %collective-permute-start.31 = (bf16[1024,512]{1,0:T(8,128)(2,1)}, bf16[1024,512]{1,0:T(8,128)(2,1)}, u32[]{:S(2)}, u32[]{:S(2)}) collective-permute-start(bf16[1024,512]{1,0:T(8,128)(2,1)} %shard_map.276), channel_id=1, source_target_pairs={{0,4},{1,5},{2,6},{3,7},{12,8},{13,9},{14,10},{15,11},{16,20},{17,... | collective-permute-start | bytes 3145736 | tf_op jit(solution)/shard_map/ppermute | solution.py:504
  259.9 33.2 %collective-permute-start.52 = (bf16[1024,512]{1,0:T(8,128)(2,1)S(1)}, bf16[1024,512]{1,0:T(8,128)(2,1)S(1)}, u32[]{:S(2)}, u32[]{:S(2)}) collective-permute-start(bf16[1024,512]{1,0:T(8,128)(2,1)S(1)} %broadcast_select_fusion.6.refs_0_), channel_id=1, source_target_pairs={{0,1},{1,0},{2,3},{3,2},{4,5},{5,4},{6,7},{7,6},{8,9},{9,8},{10,11... | collective-permute-start | bytes 3145736 | tf_op jit(solution)/shard_map/ppermute | solution.py:504
  263.5 40.4 %collective-permute-start.49 = (bf16[1024,512]{1,0:T(8,128)(2,1)}, bf16[1024,512]{1,0:T(8,128)(2,1)}, u32[]{:S(2)}, u32[]{:S(2)}) collective-permute-start(bf16[1024,512]{1,0:T(8,128)(2,1)} %add.365), channel_id=1, source_target_pairs={{4,0},{5,1},{6,2},{7,3},{8,12},{9,13},{10,14},{11,15},{20,16},{21,... | collective-permute-start | bytes 3145736 | tf_op jit(solution)/shard_map/ppermute | solution.py:504
  264.8 47.5 %collective-permute-start.46 = (bf16[1024,512]{1,0:T(8,128)(2,1)}, bf16[1024,512]{1,0:T(8,128)(2,1)}, u32[]{:S(2)}, u32[]{:S(2)}) collective-permute-start(bf16[1024,512]{1,0:T(8,128)(2,1)} %add.359), channel_id=1, source_target_pairs={{4,8},{5,9},{6,10},{7,11},{8,4},{9,5},{10,6},{11,7},{20,24},{21,25... | collective-permute-start | bytes 3145736 | tf_op jit(solution)/shard_map/ppermute | solution.py:504
  315.2 32.7 %collective-permute-start.50 = (bf16[1024,512]{1,0:T(8,128)(2,1)}, bf16[1024,512]{1,0:T(8,128)(2,1)}, u32[]{:S(2)}, u32[]{:S(2)}) collective-permute-start(bf16[1024,512]{1,0:T(8,128)(2,1)} %add.364), channel_id=1, source_target_pairs={{4,0},{5,1},{6,2},{7,3},{8,12},{9,13},{10,14},{11,15},{20,16},{21,... | collective-permute-start | bytes 3145736 | tf_op jit(solution)/shard_map/ppermute | solution.py:504
  368.0 36.8 %collective-permute-start.69 = (bf16[1024,512]{1,0:T(8,128)(2,1)}, bf16[1024,512]{1,0:T(8,128)(2,1)}, u32[]{:S(2)}, u32[]{:S(2)}) collective-permute-start(bf16[1024,512]{1,0:T(8,128)(2,1)} %get-tuple-element.606), channel_id=1, source_target_pairs={{0,4},{1,5},{2,6},{3,7},{12,8},{13,9},{14,10},{15,11},{16,20},{17,... | collective-permute-start | bytes 3145736 | tf_op jit(solution)/shard_map/ppermute | solution.py:504
  393.6 39.3 %collective-permute-start.64 = (bf16[1024,512]{1,0:T(8,128)(2,1)S(1)}, bf16[1024,512]{1,0:T(8,128)(2,1)S(1)}, u32[]{:S(2)}, u32[]{:S(2)}) collective-permute-start(bf16[1024,512]{1,0:T(8,128)(2,1)S(1)} %broadcast_select_fusion.9.refs_0_), channel_id=1, source_target_pairs={{0,1},{1,0},{2,3},{3,2},{4,5},{5,4},{6,7},{7,6},{8,9},{9,8},{10,11... | collective-permute-start | bytes 3145736 | tf_op jit(solution)/shard_map/ppermute | solution.py:504
  395.1 37.8 %collective-permute-start.65 = (bf16[1024,512]{1,0:T(8,128)(2,1)S(1)}, bf16[1024,512]{1,0:T(8,128)(2,1)}, u32[]{:S(2)}, u32[]{:S(2)}) collective-permute-start(bf16[1024,512]{1,0:T(8,128)(2,1)S(1)} %broadcast_select_fusion.9.refs_0_), channel_id=1, source_target_pairs={{0,2},{1,3},{2,0},{3,1},{4,6},{5,7},{6,4},{7,5},{8,10},{9,11},{10,... | collective-permute-start | bytes 3145736 | tf_op jit(solution)/shard_map/ppermute | solution.py:504
  411.6 33.2 %collective-permute-start.78 = (bf16[1024,512]{1,0:T(8,128)(2,1)}, bf16[1024,512]{1,0:T(8,128)(2,1)}, u32[]{:S(2)}, u32[]{:S(2)}) collective-permute-start(bf16[1024,512]{1,0:T(8,128)(2,1)} %add.719), channel_id=1, source_target_pairs={{4,0},{5,1},{6,2},{7,3},{8,12},{9,13},{10,14},{11,15},{20,16},{21,... | collective-permute-start | bytes 3145736 | tf_op jit(solution)/shard_map/ppermute | solution.py:504
  435.7 41.8 %collective-permute-start.71 = (bf16[1024,768]{1,0:T(8,128)(2,1)}, bf16[1024,768]{1,0:T(8,128)(2,1)}, u32[]{:S(2)}, u32[]{:S(2)}) collective-permute-start(bf16[1024,768]{1,0:T(8,128)(2,1)} %get-tuple-element.608), channel_id=1, source_target_pairs={{0,4},{1,5},{2,6},{3,7},{12,8},{13,9},{14,10},{15,11},{16,20},{17,... | collective-permute-start | bytes 4718600 | tf_op jit(solution)/shard_map/ppermute | solution.py:504
  456.5 34.8 %collective-permute-start.79 = (bf16[1024,512]{1,0:T(8,128)(2,1)}, bf16[1024,512]{1,0:T(8,128)(2,1)}, u32[]{:S(2)}, u32[]{:S(2)}) collective-permute-start(bf16[1024,512]{1,0:T(8,128)(2,1)} %add.718), channel_id=1, source_target_pairs={{4,0},{5,1},{6,2},{7,3},{8,12},{9,13},{10,14},{11,15},{20,16},{21,... | collective-permute-start | bytes 3145736 | tf_op jit(solution)/shard_map/ppermute | solution.py:504
  481.0 41.1 %collective-permute-start.76 = (bf16[1024,768]{1,0:T(8,128)(2,1)}, bf16[1024,768]{1,0:T(8,128)(2,1)}, u32[]{:S(2)}, u32[]{:S(2)}) collective-permute-start(bf16[1024,768]{1,0:T(8,128)(2,1)} %add.368), channel_id=1, source_target_pairs={{4,8},{5,9},{6,10},{7,11},{8,4},{9,5},{10,6},{11,7},{20,24},{21,25... | collective-permute-start | bytes 4718600 | tf_op jit(solution)/shard_map/ppermute | solution.py:504
  500.6 37.7 %collective-permute-start.72 = (bf16[1024,768]{1,0:T(8,128)(2,1)}, bf16[1024,768]{1,0:T(8,128)(2,1)}, u32[]{:S(2)}, u32[]{:S(2)}) collective-permute-start(bf16[1024,768]{1,0:T(8,128)(2,1)} %get-tuple-element.609), channel_id=1, source_target_pairs={{0,4},{1,5},{2,6},{3,7},{12,8},{13,9},{14,10},{15,11},{16,20},{17,... | collective-permute-start | bytes 4718600 | tf_op jit(solution)/shard_map/ppermute | solution.py:504
  525.5 39.6 %collective-permute-start.81 = (bf16[1024,768]{1,0:T(8,128)(2,1)}, bf16[1024,768]{1,0:T(8,128)(2,1)}, u32[]{:S(2)}, u32[]{:S(2)}) collective-permute-start(bf16[1024,768]{1,0:T(8,128)(2,1)} %add.716), channel_id=1, source_target_pairs={{4,0},{5,1},{6,2},{7,3},{8,12},{9,13},{10,14},{11,15},{20,16},{21,... | collective-permute-start | bytes 4718600 | tf_op jit(solution)/shard_map/ppermute | solution.py:504
  569.4 49.4 %collective-permute-start.95 = (bf16[1024,768]{1,0:T(8,128)(2,1)S(1)}, bf16[1024,768]{1,0:T(8,128)(2,1)}, u32[]{:S(2)}, u32[]{:S(2)}) collective-permute-start(bf16[1024,768]{1,0:T(8,128)(2,1)S(1)} %broadcast_select_fusion.refs_0_), channel_id=1, source_target_pairs={{0,1},{1,0},{2,3},{3,2},{4,5},{5,4},{6,7},{7,6},{8,9},{9,8},{10,11... | collective-permute-start | bytes 4718600 | tf_op jit(solution)/shard_map/ppermute | solution.py:504
  570.7 50.2 %collective-permute-start.96 = (bf16[1024,768]{1,0:T(8,128)(2,1)S(1)}, bf16[1024,768]{1,0:T(8,128)(2,1)}, u32[]{:S(2)}, u32[]{:S(2)}) collective-permute-start(bf16[1024,768]{1,0:T(8,128)(2,1)S(1)} %broadcast_select_fusion.refs_0_), channel_id=1, source_target_pairs={{0,2},{1,3},{2,0},{3,1},{4,6},{5,7},{6,4},{7,5},{8,10},{9,11},{10,... | collective-permute-start | bytes 4718600 | tf_op jit(solution)/shard_map/ppermute | solution.py:504
  575.2 51.1 %collective-permute-start.82 = (bf16[1024,768]{1,0:T(8,128)(2,1)}, bf16[1024,768]{1,0:T(8,128)(2,1)}, u32[]{:S(2)}, u32[]{:S(2)}) collective-permute-start(bf16[1024,768]{1,0:T(8,128)(2,1)} %add.715), channel_id=1, source_target_pairs={{4,0},{5,1},{6,2},{7,3},{8,12},{9,13},{10,14},{11,15},{20,16},{21,... | collective-permute-start | bytes 4718600 | tf_op jit(solution)/shard_map/ppermute | solution.py:504
  609.6 34.0 %collective-permute-start.103 = (bf16[1024,512]{1,0:T(8,128)(2,1)}, bf16[1024,512]{1,0:T(8,128)(2,1)}, u32[]{:S(2)}, u32[]{:S(2)}) collective-permute-start(bf16[1024,512]{1,0:T(8,128)(2,1)} %add.747), channel_id=1, source_target_pairs={{4,8},{5,9},{6,10},{7,11},{8,4},{9,5},{10,6},{11,7},{20,24},{21,25... | collective-permute-start | bytes 3145736 | tf_op jit(solution)/shard_map/ppermute | solution.py:504
  642.0 37.4 %collective-permute-start.99 = (bf16[1024,768]{1,0:T(8,128)(2,1)S(1)}, bf16[1024,768]{1,0:T(8,128)(2,1)}, u32[]{:S(2)}, u32[]{:S(2)}) collective-permute-start(bf16[1024,768]{1,0:T(8,128)(2,1)S(1)} %broadcast_select_fusion.1.refs_0_), channel_id=1, source_target_pairs={{0,1},{1,0},{2,3},{3,2},{4,5},{5,4},{6,7},{7,6},{8,9},{9,8},{10,11... | collective-permute-start | bytes 4718600 | tf_op jit(solution)/shard_map/ppermute | solution.py:504
  642.7 38.0 %collective-permute-start.100 = (bf16[1024,768]{1,0:T(8,128)(2,1)S(1)}, bf16[1024,768]{1,0:T(8,128)(2,1)}, u32[]{:S(2)}, u32[]{:S(2)}) collective-permute-start(bf16[1024,768]{1,0:T(8,128)(2,1)S(1)} %broadcast_select_fusion.1.refs_0_), channel_id=1, source_target_pairs={{0,2},{1,3},{2,0},{3,1},{4,6},{5,7},{6,4},{7,5},{8,10},{9,11},{10,... | collective-permute-start | bytes 4718600 | tf_op jit(solution)/shard_map/ppermute | solution.py:504
  (170 other events, 2189.2 us)

commit v9 on v8

--- a/solution.py
+++ b/solution.py
@@ -752,6 +752,8 @@
     sums[0] += come
     (passed,) = middle_hop.send([(sums[0], middle_moves)])
     (come,) = first_hop.send([(sums[1], inward)])
+    up_theirs = swap(jnp.concatenate(up_right))
+    normed_two_half, up_theirs = lax.optimization_barrier((normed_two_half, up_theirs))
     up_left = gather_group(normed_two_half)
 
     def to_input(flat, theirs, qkv_weight, tables):
@@ -771,6 +773,8 @@
     passed, come, late = lax.optimization_barrier(
         (last_hop.send([(sums[0], outward)]), come, late)
     )
+    late_theirs = swap(jnp.concatenate(late))
+    passed, late_theirs = lax.optimization_barrier((passed, late_theirs))
     sums[0] = jnp.where(end, passed[0], sums[0])
     sums.append(value + come[0])
     sums.append(line_start(hold(down_product(3, 1), late)))
@@ -830,45 +834,58 @@
     chunks = [("down", value, index) for index, value in enumerate(sums)]
     chunks += [("up", None, 2 * GROUP * core), ("up", None, 2 * GROUP * core + 1)]
     chunks += [("up", None, 2 * GROUP * other), ("up", None, 2 * GROUP * other + 1)]
-    chunks += [("qkv", None, core), ("qkv", None, other), ("out", None, 0)]
+    chunks.append(("qkv", None, ((0, core), (1, core))))
+    chunks.append(("qkv", None, ((2, core), (0, other))))
+    chunks.append(("qkv", None, ((1, other), (2, other))))
+    chunks.append(("out", None, 0))
     up_width = inner_half // GROUP
     up_block = min(512, up_width)
 
-    def to_up(*operands):
-        lefts = [(left, 0) for left in operands[:GROUP]]
-        mine = operands[GROUP:]
-        theirs = swap(jnp.concatenate(mine))
-        results = []
-        for first in range(inner_half // GROUP // up_block):
-            rights = [columns_from(right, length, 0, first, up_block) for right in mine]
-            results.append(rows_product(lefts, rights, half, up_block, 1))
-        for first in range(inner_half // GROUP // up_block):
-            rights = [columns_from(theirs, length, d, first, up_block) for d in range(GROUP)]
-            results.append(rows_product(lefts, rights, half, up_block, 1, True))
-        return results
+    def up_products(rights, turned):
+        lefts = [(left, 0) for left in up_left]
+        return [
+            rows_product(lefts, [right(first) for right in rights], half, up_block, 1, turned)
+            for first in range(up_width // up_block)
+        ]
+
+    def up_own():
+        def place(right):
+            return lambda first: columns_from(right, length, 0, first, up_block)
+
+        return up_products([place(right) for right in hold(up_right, late)], False)
+
+    def up_other(theirs):
+        def place(d):
+            return lambda first: columns_from(theirs, length, d, first, up_block)
+
+        return up_products([place(d) for d in range(GROUP)], True)
 
     rest_block = half // GROUP
 
-    def to_rest(*operands):
-        early, mine = operands[:GROUP], operands[GROUP:]
-        theirs = swap(jnp.concatenate(mine))
-
-        def part(value, d):
-            return value, (1, length, rest_block), lambda j: (4 * d + j, 0, 0)
-
+    def rest_product(rights, first, steps, turned):
+        lefts = [(left, 0) for left in early]
+        shape = (1, length, rest_block)
+        rights = [
+            (value, shape, functools.partial(lambda b, j: (b + j, 0, 0), 4 * d + first))
+            for value, d in rights
+        ]
+        return rows_product(lefts, rights, half, rest_block, steps, turned)
+
+    def rest_own(mine):
+        rights = [(right, 0) for right in mine]
+        return [rest_product(rights, 0, 2, False), rest_product(rights, 2, 1, False)]
+
+    def rest_other(mine, theirs):
         def out_part(value, d):
             return value, (1, rows, rest_block), lambda j: (4 * d + 3, j, 0)
 
-        lefts = [(left, 0) for left in early]
-        rights = [part(right, 0) for right in mine]
-        own = rows_product(lefts, rights, half, rest_block, 3)
-        rights = [part(theirs, d) for d in range(GROUP)]
-        other_half = rows_product(lefts, rights, half, rest_block, 3, True)
+        rights = [(theirs, d) for d in range(GROUP)]
+        results = [rest_product(rights, 0, 1, True), rest_product(rights, 1, 2, True)]
         lefts = [(left, 1) for left in early]
         rights = []
         for d, right in enumerate(mine):
             rights += [out_part(right, 0), out_part(theirs, d)]
-        return [own, other_half, rows_product(lefts, rights, half, rest_block, 2)]
+        return [*results, rows_product(lefts, rights, half, rest_block, 2)]
 
     wholes = {
         "down": blank((inner_half, width)),
@@ -878,19 +895,35 @@
     }
     size = inner_half // GROUP
     begun, raw = sums, []
+    middle, ended = [None, line_middle(begun[1])], [begun[0]]
     done = [(), ()]
-    for index, (name, value, where) in enumerate(chunks):
-        value = begun[index]
+    for index, (name, _, where) in enumerate(chunks):
         more, held = (), [done[-1]]
         if index == 0:
             held.append(begun[3])
+        fresh = []
+        if index == 0:
+            fresh = up_own()
         if index == 1:
-            raw += segment(to_up, *hold(up_left, late), *up_right)
-            held.append(raw)
+            fresh = up_other(hold(up_theirs, done[-1]))
+        if index == 3:
+            first_part, cut = rest_own(hold(late, done[-1]))
+            fresh = [first_part]
         if index == 4:
-            rest = segment(to_rest, *early, *late)
-            raw += rest
-            held.append(rest)
+            other_cut, *fresh = rest_other(*hold((late, late_theirs), done[-1]))
+            fresh = [jnp.concatenate([cut, other_cut], 1), *fresh]
+        raw += fresh
+        held.append(fresh)
+        if index + 1 < len(chunks):
+            ended.append(line_end(middle[index + 1]))
+        if index + 2 < len(chunks):
+            middle.append(line_middle(begun[index + 2]))
+        if index > 0:
+            if index + 3 < len(chunks):
+                begun.append(line_start(raw.pop(0)))
+            held += [ended[index + 1 :], middle[index + 2 :], begun[index + 3 :]]
+        else:
+            held.append(begun[3])
         if index == len(chunks) - 2:
             more = small_sends
         if index == len(chunks) - 1:
@@ -902,16 +935,12 @@
             lines = [lax.ppermute(small, "dp", line_moves(d)) for d in range(1, LINE)]
             held += [done[-1], lines]
         after = (), held
-        if 0 < index < len(chunks) - 1:
-            value = line_end(line_middle(value))
-        if index == len(chunks) - 2:
-            begun[-1] = line_end(line_middle(begun[-1]))
-            held.append(begun[-1])
+        value = ended[index]
         pieces, more_results = spread(blocks_sum(value), after, more)
         value = pieces[0]
         tall, wide = value.shape
         high = min(256, tall)
-        broad = wide // 3 if name == "qkv" else wide
+        broad = wide // 2 if name == "qkv" else wide
         places = []
         for d in range(GROUP):
             owner = spot ^ d
@@ -924,17 +953,11 @@
                 elif name == "out":
                     columns = [owner]
                 else:
-                    columns = [(2 * p + where) * GROUP + owner for p in range(3)]
+                    columns = [(2 * p + c) * GROUP + owner for p, c in where]
                 for column in columns:
                     places += [row, column]
         wholes[name] = place(pieces, wholes[name], places, high, broad)
         done.append(wholes[name])
-        while len(begun) < len(chunks) and raw:
-            number = len(begun)
-            placed = number - (4 if number < 8 else 5)
-            if placed > index:
-                break
-            begun.append(line_start(hold(raw.pop(0), done[placed + 2])))
 
     small = pair_sums([small, *lines]).reshape(-1)
     small_grads = []

time: 762 us -> 785 us (1.030)
  starting transfers between devices: 175 us -> 198 us
  other arithmetic: 90.5 us -> 102 us
    ppermute x98 -> x105, starting transfers between devices: 169 us -> 191 us  [send(): self.last = [lax.ppermute(v, 'dp', m) for v, (_, m) in zip(values, sends)]]
    unnamed x149 -> x249, local copies, waits for them, and re-layouts: 33.7 us -> 23.1 us
    select_n x10 -> x11, other arithmetic: 13.6 us -> 19 us  [line_end(): return jnp.where(end, last_hop.send([(value, outward)])[0], value)]
    add x8 -> x9, other arithmetic: 19.5 us -> 23.4 us  [line_start(): return value + hold(first_hop.send([(value, inward)])[0], after)]
    add x10 -> x11, other arithmetic: 25.5 us -> 27.9 us  [line_middle(): return value + middle_hop.send([(value, middle_moves)])[0]]
    pallas_call x11 -> x12, Pallas kernels: 68.1 us -> 70.4 us  [place(): pl.pallas_call(functools.partial(place_kernel, high), in_specs=[pl.BlockS...]
    ppermute x98 -> x105, waiting for transfers between devices: 181 us -> 179 us  [send(): self.last = [lax.ppermute(v, 'dp', m) for v, (_, m) in zip(values, sends)]]
    pallas_call x11 -> x13, Pallas kernels: 42.4 us -> 43.5 us  [rows_product(): pl.pallas_call(functools.partial(product_kernel, len(lefts), turned), gri...]
  transfers between devices with their start and end apart: 117 -> 124, of which waited for: 46 -> 42; matrix products, arithmetic and copies ran while one was open for 18% -> 17% of each run, Pallas kernels for 26% -> 25%
where the time goes in v9:
time: 785 us; the launch traced here: 773 us
  Pallas kernels  206 us (26%)
  starting transfers between devices  198 us (25%)
  waiting for transfers between devices  186 us (24%)
  other arithmetic  102 us (13%)
  local copies, waits for them, and re-layouts  63.5 us (8%)
  matrix products  11.8 us (2%)
    ppermute x105, starting transfers between devices, send(): self.last = [lax.ppermute(v, 'dp', m) for v, (_, m) in zip(values, sends)]  191 us
    ppermute x105, waiting for transfers between devices, send(): self.last = [lax.ppermute(v, 'dp', m) for v, (_, m) in zip(values, sends)]  179 us
    pallas_call x12, Pallas kernels, place(): pl.pallas_call(functools.partial(place_kernel, high), in_specs=[pl.BlockS...  70.4 us
    pallas_call x13, Pallas kernels, rows_product(): pl.pallas_call(functools.partial(product_kernel, len(lefts), turned), gri...  43.5 us
    add x11, other arithmetic, line_middle(): return value + middle_hop.send([(value, middle_moves)])[0]  27.9 us
    pallas_call x4, Pallas kernels, times_back(): pl.pallas_call(functools.partial(back_kernel, turned), grid_spec=pltpu.Pr...  26.5 us
    pallas_call x4, Pallas kernels, times_columns(): pl.pallas_call(columns_kernel, grid_spec=pltpu.PrefetchScalarGridSpec(num...  25.2 us
    add x9, other arithmetic, line_start(): return value + hold(first_hop.send([(value, inward)])[0], after)  23.4 us
  transfers between devices with their start and end apart: 124, of which 42 were waited for; matrix products, arithmetic and copies ran while one was open for 17% of the time, Pallas kernels for 25%

profile of v9, /device:TPU:0, one launch (start us, length us, event | category | flops | bytes accessed | tf_op | source)
XLA Modules:
  0.0 773.0 jit_solution(8473450844212751119)
XLA Ops:
  14.0 22.4 %conditional.5 = (bf16[256,1024]{1,0:T(8,128)(2,1)}, bf16[256,1024]{1,0:T(8,128)(2,1)}, bf16[256,1024]{1,0:T(8,128)(2,1)}, bf16[256,1024]{1,0:T(8,128)(2,1)}, bf...) conditional(s32[]{:T(128)} %convert_element_type.29, () %tuple.142, (bf16[128,1024]{1,0:T(8,128)(2,1)S(1)}, ...), branch_computations={%region_0.1_spmd, %region_1.2_spmd} | conditional | flops 874512384 | bytes 19710170 | solution.py:616
  43.0 37.9 %conditional.6 = (f32[128,2048]{1,0:T(8,128)}, bf16[256,1024]{1,0:T(8,128)(2,1)}, bf16[256,4096]{1,0:T(8,128)(2,1)}, bf16[256,4096]{1,0:T(8,128)(2,1)}, f32[4096...) conditional(s32[]{:T(128)} %convert_element_type.29, () %tuple.141, (bf16[256,1024]{1,0:T(8,128)(2,1)}, ...), branch_computations={%region_2.3_spmd, %region_3.4_spmd} | conditional | flops 3222536192 | bytes 45029880 | solution.py:616
  66.8 13.5 %branch_1_fun.19 = (bf16[256,4096]{1,0:T(8,128)(2,1)}, bf16[256,4096]{1,0:T(8,128)(2,1)}, f32[1,4096]{1,0:T(1,128)}) custom-call(bf16[256,2048]{1,0:T(8,128)(2,1)S(1)} %copy-done.103, bf16[4096,2048]{1,0:T(8,128)(2,1)} %get-tuple-element.172.refs_0_, f32[256,4096]{1,0:T(8,128)S(1)} %branch_1_fun.17.refs_1_, ...), custom_call_target="tpu_custom_call" | custom-call | flops 1073741824 | bytes 7602176 | tf_op jit(solution)/shard_map/cond/branch_1_fun/pallas_call | solution.py:311
  93.4 22.9 %conditional.7 = (f32[128,2048]{1,0:T(8,128)}, bf16[128,2048]{1,0:T(8,128)(2,1)}, bf16[384,2048]{1,0:T(8,128)(2,1)}, bf16[256,1024]{1,0:T(8,128)(2,1)}, bf16[256...) conditional(s32[]{:T(128)} %convert_element_type.29, () %tuple.152, ...), branch_computations={%region_4.5_spmd, %region_5.6_spmd} | conditional | flops 1079771136 | bytes 55315128 | solution.py:616
  128.5 24.1 %conditional.8 = (bf16[3,256,1024]{2,1,0:T(8,128)(2,1)}, bf16[256,3072]{1,0:T(8,128)(2,1)}, bf16[256,3072]{1,0:T(8,128)(2,1)}, bf16[4,256,256]{2,1,0:T(8,128)(2,...) conditional(s32[]{:T(128)} %convert_element_type.29, () %tuple.150, ...), branch_computations={%region_6.7_spmd, %region_7.8_spmd} | conditional | flops 1250689024 | bytes 43385508 | solution.py:616
  134.2 10.3 %branch_1_fun.23 = bf16[3,256,1024]{2,1,0:T(8,128)(2,1)S(1)} custom-call(s32[1]{0:T(128)} %get-tuple-element.200.first_ref, bf16[256,1024]{1,0:T(8,128)(2,1)} %get-tuple-element.201.q_ref, bf16[256,1024]{1,0:T(8,128)(2,1)} %get-tuple-element.202.k_ref, bf16[256,1024]{1,0:T(8,128)(2,1)} %get-tuple-element.203.v_ref, ...), custom_call_target="tpu_custom_call" | custom-call | flops 167772160 | bytes 917504 | tf_op jit(solution)/shard_map/cond/branch_1_fun/pallas_call | solution.py:424
  174.2 15.2 %conditional.9 = (f32[256,1024]{1,0:T(8,128)}) conditional(s32[]{:T(128)} %convert_element_type.29, () %tuple.149, (s32[3]{0:T(128)S(1)}, bf16[256,3072]{1,0:T(8,128)(2,1)}, bf16[1024,6144]{1,0:T(8,128)(2,1)}, s32[3]{0:T(128)S(1)}, bf16[256,3072]{1,0:T(8,128)(2,1)}) %tuple.160), branch_computations={%region_8.9_spmd, %region_9.10_spmd} | conditional | flops 805306368 | bytes 4980744 | solution.py:616
  181.3 8.1 %branch_1_fun.25 = f32[256,1024]{1,0:T(8,128)} custom-call(s32[3]{0:T(128)S(1)} %get-tuple-element.207.table_ref, bf16[256,3072]{1,0:T(8,128)(2,1)} %get-tuple-element.208.left_ref, bf16[1024,6144]{1,0:T(8,128)(2,1)} %get-tuple-element.209.refs_0_, f32[256,1024]{1,0:T(8,128)S(1)} %branch_1_fun.24.refs_1_), custom_call_target="tpu_custom_call" | custom-call | flops 402653184 | bytes 2490368 | tf_op jit(solution)/shard_map/cond/branch_1_fun/pallas_call | solution.py:277
  204.5 11.4 %collective-permute-done.33.refs_5_.refs_6_ = bf16[4,256,256]{2,1,0:T(8,128)(2,1)S(1)} collective-permute-done((bf16[4,256,256]{2,1,0:T(8,128)(2,1)S(1)}, bf16[4,256,256]{2,1,0:T(8,128)(2,1)S(1)}, u32[]{:S(2)}, u32[]{:S(2)}) %collective-permute-start.33) | collective-permute-done | bytes 524320 | tf_op jit(solution)/shard_map/ppermute | solution.py:504
  215.8 9.0 %collective-permute-done.34.refs_6_.refs_8_ = bf16[4,256,256]{2,1,0:T(8,128)(2,1)S(1)} collective-permute-done((bf16[4,256,256]{2,1,0:T(8,128)(2,1)S(1)}, bf16[4,256,256]{2,1,0:T(8,128)(2,1)S(1)}, u32[]{:S(2)}, u32[]{:S(2)}) %collective-permute-start.34) | collective-permute-done | bytes 524320 | tf_op jit(solution)/shard_map/ppermute | solution.py:504
  258.6 8.0 %collective-permute-done.38 = bf16[1024,512]{1,0:T(8,128)(2,1)S(1)} collective-permute-done((bf16[1024,512]{1,0:T(8,128)(2,1)S(1)}, bf16[1024,512]{1,0:T(8,128)(2,1)S(1)}, u32[]{:S(2)}, u32[]{:S(2)}) %collective-permute-start.38) | collective-permute-done | bytes 1048608 | tf_op jit(solution)/shard_map/ppermute | solution.py:504
  273.7 18.4 %collective-permute-start.51 = (bf16[1024,512]{1,0:T(8,128)(2,1)}, bf16[1024,512]{1,0:T(8,128)(2,1)}, u32[]{:S(2)}, u32[]{:S(2)}) collective-permute-start(bf16[1024,512]{1,0:T(8,128)(2,1)} %shard_map.280), channel_id=1, source_target_pairs={{0,4},{1,5},{2,6},{3,7},{12,8},{13,9},{14,10},{15,11},{16,20},{17,... | collective-permute-start | bytes 3145736 | tf_op jit(solution)/shard_map/ppermute | solution.py:504
  299.2 13.4 %collective-permute-done.51 = bf16[1024,512]{1,0:T(8,128)(2,1)} collective-permute-done((bf16[1024,512]{1,0:T(8,128)(2,1)}, bf16[1024,512]{1,0:T(8,128)(2,1)}, u32[]{:S(2)}, u32[]{:S(2)}) %collective-permute-start.51) | collective-permute-done | bytes 1048608 | tf_op jit(solution)/shard_map/ppermute | solution.py:504
  350.8 10.3 %collective-permute-done.57 = bf16[1024,512]{1,0:T(8,128)(2,1)} collective-permute-done((bf16[1024,512]{1,0:T(8,128)(2,1)}, bf16[1024,512]{1,0:T(8,128)(2,1)}, u32[]{:S(2)}, u32[]{:S(2)}) %collective-permute-start.57) | collective-permute-done | bytes 1048608 | tf_op jit(solution)/shard_map/ppermute | solution.py:504
  396.5 8.4 %collective-permute-done.62 = bf16[1024,512]{1,0:T(8,128)(2,1)} collective-permute-done((bf16[1024,512]{1,0:T(8,128)(2,1)}, bf16[1024,512]{1,0:T(8,128)(2,1)}, u32[]{:S(2)}, u32[]{:S(2)}) %collective-permute-start.62) | collective-permute-done | bytes 1048608 | tf_op jit(solution)/shard_map/ppermute | solution.py:504
  438.0 8.0 %collective-permute-done.76 = bf16[1024,512]{1,0:T(8,128)(2,1)} collective-permute-done((bf16[1024,512]{1,0:T(8,128)(2,1)}, bf16[1024,512]{1,0:T(8,128)(2,1)}, u32[]{:S(2)}, u32[]{:S(2)}) %collective-permute-start.76) | collective-permute-done | bytes 1048608 | tf_op jit(solution)/shard_map/ppermute | solution.py:504
  480.8 7.5 collective-permute-start.68
  494.5 8.8 %collective-permute-done.77 = bf16[1024,512]{1,0:T(8,128)(2,1)} collective-permute-done((bf16[1024,512]{1,0:T(8,128)(2,1)}, bf16[1024,512]{1,0:T(8,128)(2,1)}, u32[]{:S(2)}, u32[]{:S(2)}) %collective-permute-start.77) | collective-permute-done | bytes 1048608 | tf_op jit(solution)/shard_map/ppermute | solution.py:504
  518.8 8.6 %collective-permute-start.69 = (bf16[1024,512]{1,0:T(8,128)(2,1)}, bf16[1024,512]{1,0:T(8,128)(2,1)}, u32[]{:S(2)}, u32[]{:S(2)}) collective-permute-start(bf16[1024,512]{1,0:T(8,128)(2,1)} %pad_maximum_fusion.10), channel_id=1, source_target_pairs={{0,4},{1,5},{2,6},{3,7},{12,8},{13,9},{14,10},{15,11},{16,20},{17,... | collective-permute-start | bytes 3145736 | tf_op jit(solution)/shard_map/ppermute | solution.py:504
  558.2 7.5 collective-permute-start.70
  596.2 7.7 collective-permute-start.100
  660.6 8.0 %shard_map.300.refs_5_ = f32[1024,6144]{1,0:T(8,128)} custom-call(s32[64]{0:T(128)S(1)} %stack.210.table_ref, bf16[1024,512]{1,0:T(8,128)(2,1)S(1)} %broadcast_select_fusion.4.refs_0_, bf16[1024,512]{1,0:T(8,128)(2,1)} %collective-permute-done.98.refs_1_, bf16[1024,512]{1,0:T(8,128)(2,1)} %collective-permute-done.99.refs_2_, ...), custom_call_target="tpu_custom_call", output_to_operand_aliasing={{}: (6, {})} | custom-call | bytes 3145728 | tf_op jit(solution)/shard_map/pallas_call | solution.py:469
  689.4 11.2 %collective-permute-done.111 = bf16[1024,512]{1,0:T(8,128)(2,1)} collective-permute-done((bf16[1024,512]{1,0:T(8,128)(2,1)S(1)}, bf16[1024,512]{1,0:T(8,128)(2,1)}, u32[]{:S(2)}, u32[]{:S(2)}) %collective-permute-start.111) | collective-permute-done | bytes 1048608 | tf_op jit(solution)/shard_map/ppermute | solution.py:504
  712.9 13.1 %collective-permute-done.114 = f32[192,128]{1,0:T(8,128)S(1)} collective-permute-done((f32[192,128]{1,0:T(8,128)S(1)}, f32[192,128]{1,0:T(8,128)S(1)}, u32[]{:S(2)}, u32[]{:S(2)}) %collective-permute-start.114) | collective-permute-done | bytes 98336 | tf_op jit(solution)/shard_map/ppermute | solution.py:504
  (667 shorter events, 576.5 us)
Async XLA Ops:
  8.0 28.5 %collective-permute-start.11 = (bf16[128,2048]{1,0:T(8,128)(2,1)}, bf16[128,2048]{1,0:T(8,128)(2,1)S(1)}, u32[]{:S(2)}, u32[]{:S(2)}) collective-permute-start(bf16[128,2048]{1,0:T(8,128)(2,1)} %get-tuple-element.456.refs_4_), channel_id=1, source_target_pairs={{0,1},{1,0},{2,3},{3,2},{4,5},{5,4},{6,7},{7,6},{8,9},{9,8},{10,11... | collective-permute-start | bytes 1572872 | tf_op jit(solution)/shard_map/ppermute | solution.py:504
  36.5 44.4 %collective-permute-start.14 = (bf16[256,2048]{1,0:T(8,128)(2,1)}, bf16[256,2048]{1,0:T(8,128)(2,1)S(1)}, u32[]{:S(2)}, u32[]{:S(2)}) collective-permute-start(bf16[256,2048]{1,0:T(8,128)(2,1)} %get-tuple-element.508.refs_0_), channel_id=1, source_target_pairs={{0,1},{1,0},{2,3},{3,2},{4,5},{5,4},{6,7},{7,6},{8,9},{9,8},{10,11... | collective-permute-start | bytes 3145736 | tf_op jit(solution)/shard_map/ppermute | solution.py:504
  38.6 47.6 %collective-permute-start.15 = (bf16[256,2048]{1,0:T(8,128)(2,1)}, bf16[256,2048]{1,0:T(8,128)(2,1)S(1)}, u32[]{:S(2)}, u32[]{:S(2)}) collective-permute-start(bf16[256,2048]{1,0:T(8,128)(2,1)} %get-tuple-element.508.refs_0_), channel_id=1, source_target_pairs={{0,2},{1,3},{2,0},{3,1},{4,6},{5,7},{6,4},{7,5},{8,10},{9,11},{10,... | collective-permute-start | bytes 3145736 | tf_op jit(solution)/shard_map/ppermute | solution.py:504
  40.1 46.1 %collective-permute-start.16 = (bf16[256,2048]{1,0:T(8,128)(2,1)}, bf16[256,2048]{1,0:T(8,128)(2,1)S(1)}, u32[]{:S(2)}, u32[]{:S(2)}) collective-permute-start(bf16[256,2048]{1,0:T(8,128)(2,1)} %get-tuple-element.508.refs_0_), channel_id=1, source_target_pairs={{0,3},{1,2},{2,1},{3,0},{4,7},{5,6},{6,5},{7,4},{8,11},{9,10},{10,... | collective-permute-start | bytes 3145736 | tf_op jit(solution)/shard_map/ppermute | solution.py:504
  120.5 35.7 %collective-permute-start.24 = (bf16[1024,512]{1,0:T(8,128)(2,1)}, bf16[1024,512]{1,0:T(8,128)(2,1)}, u32[]{:S(2)}, u32[]{:S(2)}) collective-permute-start(bf16[1024,512]{1,0:T(8,128)(2,1)} %shard_map.275), channel_id=1, source_target_pairs={{0,4},{1,5},{2,6},{3,7},{12,8},{13,9},{14,10},{15,11},{16,20},{17,... | collective-permute-start | bytes 3145736 | tf_op jit(solution)/shard_map/ppermute | solution.py:504
  125.0 31.2 %collective-permute-start.21 = (bf16[256,1024]{1,0:T(8,128)(2,1)}, bf16[256,1024]{1,0:T(8,128)(2,1)}, u32[]{:S(2)}, u32[]{:S(2)}) collective-permute-start(bf16[256,1024]{1,0:T(8,128)(2,1)} %get-tuple-element.468), channel_id=1, source_target_pairs={{0,1},{1,0},{2,3},{3,2},{4,5},{5,4},{6,7},{7,6},{8,9},{9,8},{10,11... | collective-permute-start | bytes 1572872 | tf_op jit(solution)/shard_map/ppermute | solution.py:504
  125.8 30.3 %collective-permute-start.22 = (bf16[256,1024]{1,0:T(8,128)(2,1)}, bf16[256,1024]{1,0:T(8,128)(2,1)}, u32[]{:S(2)}, u32[]{:S(2)}) collective-permute-start(bf16[256,1024]{1,0:T(8,128)(2,1)} %get-tuple-element.469), channel_id=1, source_target_pairs={{0,2},{1,3},{2,0},{3,1},{4,6},{5,7},{6,4},{7,5},{8,10},{9,11},{10,... | collective-permute-start | bytes 1572872 | tf_op jit(solution)/shard_map/ppermute | solution.py:504
  127.5 28.7 %collective-permute-start.23 = (bf16[256,1024]{1,0:T(8,128)(2,1)}, bf16[256,1024]{1,0:T(8,128)(2,1)}, u32[]{:S(2)}, u32[]{:S(2)}) collective-permute-start(bf16[256,1024]{1,0:T(8,128)(2,1)} %get-tuple-element.470), channel_id=1, source_target_pairs={{0,3},{1,2},{2,1},{3,0},{4,7},{5,6},{6,5},{7,4},{8,11},{9,10},{10,... | collective-permute-start | bytes 1572872 | tf_op jit(solution)/shard_map/ppermute | solution.py:504
  161.0 28.4 %collective-permute-start.29 = (bf16[1024,512]{1,0:T(8,128)(2,1)}, bf16[1024,512]{1,0:T(8,128)(2,1)}, u32[]{:S(2)}, u32[]{:S(2)}) collective-permute-start(bf16[1024,512]{1,0:T(8,128)(2,1)} %add.333), channel_id=1, source_target_pairs={{4,8},{5,9},{6,10},{7,11},{8,4},{9,5},{10,6},{11,7},{20,24},{21,25... | collective-permute-start | bytes 3145736 | tf_op jit(solution)/shard_map/ppermute | solution.py:504
  194.9 30.0 %collective-permute-start.31 = (bf16[1024,512]{1,0:T(8,128)(2,1)S(1)}, bf16[1024,512]{1,0:T(8,128)(2,1)S(1)}, u32[]{:S(2)}, u32[]{:S(2)}) collective-permute-start(bf16[1024,512]{1,0:T(8,128)(2,1)S(1)} %add.334), channel_id=1, source_target_pairs={{4,0},{5,1},{6,2},{7,3},{8,12},{9,13},{10,14},{11,15},{20,16},{21,... | collective-permute-start | bytes 3145736 | tf_op jit(solution)/shard_map/ppermute | solution.py:504
  196.2 28.7 %collective-permute-start.32 = (bf16[1024,512]{1,0:T(8,128)(2,1)S(1)}, bf16[1024,512]{1,0:T(8,128)(2,1)S(1)}, u32[]{:S(2)}, u32[]{:S(2)}) collective-permute-start(bf16[1024,512]{1,0:T(8,128)(2,1)S(1)} %copy-done.36), channel_id=1, source_target_pairs={{0,4},{1,5},{2,6},{3,7},{12,8},{13,9},{14,10},{15,11},{16,20},{17,... | collective-permute-start | bytes 3145736 | tf_op jit(solution)/shard_map/ppermute | solution.py:504
  249.3 44.1 %collective-permute-start.42 = (bf16[1024,512]{1,0:T(8,128)(2,1)S(1)}, bf16[1024,512]{1,0:T(8,128)(2,1)S(1)}, u32[]{:S(2)}, u32[]{:S(2)}) collective-permute-start(bf16[1024,512]{1,0:T(8,128)(2,1)S(1)} %add.360), channel_id=1, source_target_pairs={{4,0},{5,1},{6,2},{7,3},{8,12},{9,13},{10,14},{11,15},{20,16},{21,... | collective-permute-start | bytes 3145736 | tf_op jit(solution)/shard_map/ppermute | solution.py:504
  272.1 43.3 %collective-permute-start.41 = (bf16[1024,512]{1,0:T(8,128)(2,1)}, bf16[1024,512]{1,0:T(8,128)(2,1)}, u32[]{:S(2)}, u32[]{:S(2)}) collective-permute-start(bf16[1024,512]{1,0:T(8,128)(2,1)} %add.355), channel_id=1, source_target_pairs={{4,8},{5,9},{6,10},{7,11},{8,4},{9,5},{10,6},{11,7},{20,24},{21,25... | collective-permute-start | bytes 3145736 | tf_op jit(solution)/shard_map/ppermute | solution.py:504
  273.7 38.9 %collective-permute-start.51 = (bf16[1024,512]{1,0:T(8,128)(2,1)}, bf16[1024,512]{1,0:T(8,128)(2,1)}, u32[]{:S(2)}, u32[]{:S(2)}) collective-permute-start(bf16[1024,512]{1,0:T(8,128)(2,1)} %shard_map.280), channel_id=1, source_target_pairs={{0,4},{1,5},{2,6},{3,7},{12,8},{13,9},{14,10},{15,11},{16,20},{17,... | collective-permute-start | bytes 3145736 | tf_op jit(solution)/shard_map/ppermute | solution.py:504
  297.4 36.2 %collective-permute-start.49 = (bf16[1024,512]{1,0:T(8,128)(2,1)}, bf16[1024,512]{1,0:T(8,128)(2,1)}, u32[]{:S(2)}, u32[]{:S(2)}) collective-permute-start(bf16[1024,512]{1,0:T(8,128)(2,1)} %broadcast_select_fusion.8.refs_0_), channel_id=1, source_target_pairs={{0,1},{1,0},{2,3},{3,2},{4,5},{5,4},{6,7},{7,6},{8,9},{9,8},{10,11... | collective-permute-start | bytes 3145736 | tf_op jit(solution)/shard_map/ppermute | solution.py:504
  298.4 36.2 %collective-permute-start.50 = (bf16[1024,512]{1,0:T(8,128)(2,1)}, bf16[1024,512]{1,0:T(8,128)(2,1)}, u32[]{:S(2)}, u32[]{:S(2)}) collective-permute-start(bf16[1024,512]{1,0:T(8,128)(2,1)} %broadcast_select_fusion.8.refs_0_), channel_id=1, source_target_pairs={{0,2},{1,3},{2,0},{3,1},{4,6},{5,7},{6,4},{7,5},{8,10},{9,11},{10,... | collective-permute-start | bytes 3145736 | tf_op jit(solution)/shard_map/ppermute | solution.py:504
  391.9 28.5 %collective-permute-start.60 = (bf16[1024,512]{1,0:T(8,128)(2,1)}, bf16[1024,512]{1,0:T(8,128)(2,1)}, u32[]{:S(2)}, u32[]{:S(2)}) collective-permute-start(bf16[1024,512]{1,0:T(8,128)(2,1)} %broadcast_select_fusion.10.refs_0_), channel_id=1, source_target_pairs={{0,1},{1,0},{2,3},{3,2},{4,5},{5,4},{6,7},{7,6},{8,9},{9,8},{10,11... | collective-permute-start | bytes 3145736 | tf_op jit(solution)/shard_map/ppermute | solution.py:504
  392.9 28.6 %collective-permute-start.61 = (bf16[1024,512]{1,0:T(8,128)(2,1)}, bf16[1024,512]{1,0:T(8,128)(2,1)}, u32[]{:S(2)}, u32[]{:S(2)}) collective-permute-start(bf16[1024,512]{1,0:T(8,128)(2,1)} %broadcast_select_fusion.10.refs_0_), channel_id=1, source_target_pairs={{0,2},{1,3},{2,0},{3,1},{4,6},{5,7},{6,4},{7,5},{8,10},{9,11},{10,... | collective-permute-start | bytes 3145736 | tf_op jit(solution)/shard_map/ppermute | solution.py:504
  435.6 37.7 %collective-permute-start.82 = (bf16[1024,512]{1,0:T(8,128)(2,1)}, bf16[1024,512]{1,0:T(8,128)(2,1)}, u32[]{:S(2)}, u32[]{:S(2)}) collective-permute-start(bf16[1024,512]{1,0:T(8,128)(2,1)} %broadcast_select_fusion.7.refs_0_), channel_id=1, source_target_pairs={{0,1},{1,0},{2,3},{3,2},{4,5},{5,4},{6,7},{7,6},{8,9},{9,8},{10,11... | collective-permute-start | bytes 3145736 | tf_op jit(solution)/shard_map/ppermute | solution.py:504
  436.6 37.8 %collective-permute-start.83 = (bf16[1024,512]{1,0:T(8,128)(2,1)}, bf16[1024,512]{1,0:T(8,128)(2,1)}, u32[]{:S(2)}, u32[]{:S(2)}) collective-permute-start(bf16[1024,512]{1,0:T(8,128)(2,1)} %broadcast_select_fusion.7.refs_0_), channel_id=1, source_target_pairs={{0,2},{1,3},{2,0},{3,1},{4,6},{5,7},{6,4},{7,5},{8,10},{9,11},{10,... | collective-permute-start | bytes 3145736 | tf_op jit(solution)/shard_map/ppermute | solution.py:504
  503.4 30.8 %collective-permute-start.78 = (bf16[1024,512]{1,0:T(8,128)(2,1)}, bf16[1024,512]{1,0:T(8,128)(2,1)}, u32[]{:S(2)}, u32[]{:S(2)}) collective-permute-start(bf16[1024,512]{1,0:T(8,128)(2,1)} %add.718), channel_id=1, source_target_pairs={{4,0},{5,1},{6,2},{7,3},{8,12},{9,13},{10,14},{11,15},{20,16},{21,... | collective-permute-start | bytes 3145736 | tf_op jit(solution)/shard_map/ppermute | solution.py:504
  673.1 27.5 %collective-permute-start.111 = (bf16[1024,512]{1,0:T(8,128)(2,1)S(1)}, bf16[1024,512]{1,0:T(8,128)(2,1)}, u32[]{:S(2)}, u32[]{:S(2)}) collective-permute-start(bf16[1024,512]{1,0:T(8,128)(2,1)S(1)} %add.747), channel_id=1, source_target_pairs={{4,0},{5,1},{6,2},{7,3},{8,12},{9,13},{10,14},{11,15},{20,16},{21,... | collective-permute-start | bytes 3145736 | tf_op jit(solution)/shard_map/ppermute | solution.py:504
  681.0 27.7 %collective-permute-start.108 = (bf16[1024,512]{1,0:T(8,128)(2,1)S(1)}, bf16[1024,512]{1,0:T(8,128)(2,1)S(1)}, u32[]{:S(2)}, u32[]{:S(2)}) collective-permute-start(bf16[1024,512]{1,0:T(8,128)(2,1)S(1)} %broadcast_select_fusion.6.refs_0_), channel_id=1, source_target_pairs={{0,1},{1,0},{2,3},{3,2},{4,5},{5,4},{6,7},{7,6},{8,9},{9,8},{10,11... | collective-permute-start | bytes 3145736 | tf_op jit(solution)/shard_map/ppermute | solution.py:504
  688.9 49.3 %collective-permute-start.17 = (f32[128,2048]{1,0:T(8,128)}, f32[128,2048]{1,0:T(8,128)}, u32[]{:S(2)}, u32[]{:S(2)}) collective-permute-start(f32[128,2048]{1,0:T(8,128)} %slice.245), channel_id=1, source_target_pairs={{0,16},{16,0},{1,17},{17,1},{2,18},{18,2},{3,19},{19,3},{4,20},{20... | collective-permute-start | bytes 3145736 | tf_op jit(solution)/shard_map/ppermute | solution.py:542
  (231 other events, 2715.5 us)

commit v10 on v8

--- a/solution.py
+++ b/solution.py
@@ -905,8 +905,9 @@
         if 0 < index < len(chunks) - 1:
             value = line_end(line_middle(value))
         if index == len(chunks) - 2:
-            begun[-1] = line_end(line_middle(begun[-1]))
-            held.append(begun[-1])
+            last = line_middle(begun[-1])
+            held.append(last)
+            begun[-1] = line_end(last)
         pieces, more_results = spread(blocks_sum(value), after, more)
         value = pieces[0]
         tall, wide = value.shape

time: 762 us -> 757 us (level)
    ppermute x3, starting transfers between devices: 4.44 us -> 13.6 us  [per_device(): lines = [lax.ppermute(small, 'dp', line_moves(d)) for d in range(1, LINE)]]
    unnamed x149 -> x141, local copies, waits for them, and re-layouts: 33.7 us -> 29.7 us
  transfers between devices with their start and end apart: 117 -> 117, of which waited for: 46 -> 48; matrix products, arithmetic and copies ran while one was open for 18% -> 17% of each run, Pallas kernels for 26% -> 26%
where the time goes in v10:
time: 757 us; the launch traced here: 744 us
  Pallas kernels  204 us (27%)
  waiting for transfers between devices  183 us (24%)
  starting transfers between devices  181 us (24%)
  other arithmetic  87.8 us (12%)
  local copies, waits for them, and re-layouts  67.2 us (9%)
  matrix products  16 us (2%)
    ppermute x98, waiting for transfers between devices, send(): self.last = [lax.ppermute(v, 'dp', m) for v, (_, m) in zip(values, sends)]  175 us
    ppermute x98, starting transfers between devices, send(): self.last = [lax.ppermute(v, 'dp', m) for v, (_, m) in zip(values, sends)]  166 us
    pallas_call x11, Pallas kernels, place(): pl.pallas_call(functools.partial(place_kernel, high), in_specs=[pl.BlockS...  68.4 us
    pallas_call x11, Pallas kernels, rows_product(): pl.pallas_call(functools.partial(product_kernel, len(lefts), turned), gri...  42.5 us
    unnamed x141, local copies, waits for them, and re-layouts  29.7 us
    pallas_call x4, Pallas kernels, times_back(): pl.pallas_call(functools.partial(back_kernel, turned), grid_spec=pltpu.Pr...  27.2 us
    pallas_call x4, Pallas kernels, times_columns(): pl.pallas_call(columns_kernel, grid_spec=pltpu.PrefetchScalarGridSpec(num...  25.2 us
    add x10, other arithmetic, line_middle(): return value + middle_hop.send([(value, middle_moves)])[0]  24.5 us
  transfers between devices with their start and end apart: 117, of which 48 were waited for; matrix products, arithmetic and copies ran while one was open for 17% of the time, Pallas kernels for 26%

profile of v10, /device:TPU:0, one launch (start us, length us, event | category | flops | bytes accessed | tf_op | source)
XLA Modules:
  0.0 744.5 jit_solution(17091520223556310381)
XLA Ops:
  14.0 21.3 %conditional.7 = (bf16[256,1024]{1,0:T(8,128)(2,1)}, bf16[256,1024]{1,0:T(8,128)(2,1)}, bf16[256,1024]{1,0:T(8,128)(2,1)}, bf16[256,1024]{1,0:T(8,128)(2,1)}, bf...) conditional(s32[]{:T(128)} %convert_element_type.31, () %tuple.155, (bf16[128,1024]{1,0:T(8,128)(2,1)S(1)}, ...), branch_computations={%region_0.1_spmd, %region_1.2_spmd} | conditional | flops 874512384 | bytes 19710170 | solution.py:616
  41.7 37.8 %conditional.8 = (f32[128,2048]{1,0:T(8,128)}, bf16[256,1024]{1,0:T(8,128)(2,1)}, bf16[256,4096]{1,0:T(8,128)(2,1)}, bf16[256,4096]{1,0:T(8,128)(2,1)}, f32[4096...) conditional(s32[]{:T(128)} %convert_element_type.31, () %tuple.154, (bf16[256,1024]{1,0:T(8,128)(2,1)}, ...), branch_computations={%region_2.3_spmd, %region_3.4_spmd} | conditional | flops 3222536192 | bytes 42932700 | solution.py:616
  51.6 7.2 branch_1_fun.25
  65.3 13.4 %branch_1_fun.26 = (bf16[256,4096]{1,0:T(8,128)(2,1)}, bf16[256,4096]{1,0:T(8,128)(2,1)}, f32[1,4096]{1,0:T(1,128)}) custom-call(bf16[256,2048]{1,0:T(8,128)(2,1)S(1)} %copy-done.54, bf16[4096,2048]{1,0:T(8,128)(2,1)} %get-tuple-element.204.refs_0_, f32[256,4096]{1,0:T(8,128)S(1)} %branch_1_fun.24.refs_1_, ...), custom_call_target="tpu_custom_call" | custom-call | flops 1073741824 | bytes 7602176 | tf_op jit(solution)/shard_map/cond/branch_1_fun/pallas_call | solution.py:311
  91.2 23.0 %conditional.9 = (f32[128,2048]{1,0:T(8,128)}, bf16[128,2048]{1,0:T(8,128)(2,1)}, bf16[384,2048]{1,0:T(8,128)(2,1)}, bf16[256,1024]{1,0:T(8,128)(2,1)}, bf16[256...) conditional(s32[]{:T(128)} %convert_element_type.31, () %tuple.165, ...), branch_computations={%region_4.5_spmd, %region_5.6_spmd} | conditional | flops 1079771136 | bytes 34343496 | solution.py:616
  124.8 24.0 %conditional.10 = (bf16[3,256,1024]{2,1,0:T(8,128)(2,1)}, bf16[256,3072]{1,0:T(8,128)(2,1)}, bf16[256,3072]{1,0:T(8,128)(2,1)}, bf16[4,256,256]{2,1,0:T(8,128)(2...) conditional(s32[]{:T(128)} %convert_element_type.31, () %tuple.163, ...), branch_computations={%region_6.7_spmd, %region_7.8_spmd} | conditional | flops 1250689024 | bytes 43385508 | solution.py:616
  130.6 10.3 %branch_1_fun.30 = bf16[3,256,1024]{2,1,0:T(8,128)(2,1)S(1)} custom-call(s32[1]{0:T(128)} %get-tuple-element.232.first_ref, bf16[256,1024]{1,0:T(8,128)(2,1)} %get-tuple-element.233.q_ref, bf16[256,1024]{1,0:T(8,128)(2,1)} %get-tuple-element.234.k_ref, bf16[256,1024]{1,0:T(8,128)(2,1)} %get-tuple-element.235.v_ref, ...), custom_call_target="tpu_custom_call" | custom-call | flops 167772160 | bytes 917504 | tf_op jit(solution)/shard_map/cond/branch_1_fun/pallas_call | solution.py:424
  166.0 15.2 %conditional.11 = (f32[256,1024]{1,0:T(8,128)}) conditional(s32[]{:T(128)} %convert_element_type.31, () %tuple.162, (s32[3]{0:T(128)S(1)}, bf16[256,3072]{1,0:T(8,128)(2,1)}, bf16[1024,6144]{1,0:T(8,128)(2,1)}, s32[3]{0:T(128)S(1)}, bf16[256,3072]{1,0:T(8,128)(2,1)}) %tuple.173), branch_computations={%region_8.9_spmd, %region_9.10_spmd} | conditional | flops 805306368 | bytes 4980744 | solution.py:616
  173.1 8.1 %branch_1_fun.32 = f32[256,1024]{1,0:T(8,128)} custom-call(s32[3]{0:T(128)S(1)} %get-tuple-element.239.table_ref, bf16[256,3072]{1,0:T(8,128)(2,1)} %get-tuple-element.240.left_ref, bf16[1024,6144]{1,0:T(8,128)(2,1)} %get-tuple-element.241.refs_0_, f32[256,1024]{1,0:T(8,128)S(1)} %branch_1_fun.31.refs_1_), custom_call_target="tpu_custom_call" | custom-call | flops 402653184 | bytes 2490368 | tf_op jit(solution)/shard_map/cond/branch_1_fun/pallas_call | solution.py:277
  203.1 8.7 %collective-permute-done.34 = bf16[4,256,256]{2,1,0:T(8,128)(2,1)} collective-permute-done((bf16[4,256,256]{2,1,0:T(8,128)(2,1)S(1)}, bf16[4,256,256]{2,1,0:T(8,128)(2,1)}, u32[]{:S(2)}, u32[]{:S(2)}) %collective-permute-start.34) | collective-permute-done | bytes 524320 | tf_op jit(solution)/shard_map/ppermute | solution.py:504
  231.2 10.5 %collective-permute-done.40 = bf16[1024,512]{1,0:T(8,128)(2,1)S(1)} collective-permute-done((bf16[1024,512]{1,0:T(8,128)(2,1)S(1)}, bf16[1024,512]{1,0:T(8,128)(2,1)S(1)}, u32[]{:S(2)}, u32[]{:S(2)}) %collective-permute-start.40) | collective-permute-done | bytes 1048608 | tf_op jit(solution)/shard_map/ppermute | solution.py:504
  266.3 17.5 %conditional.13 = (bf16[1024,512]{1,0:T(8,128)(2,1)}, bf16[1024,512]{1,0:T(8,128)(2,1)}, bf16[1024,512]{1,0:T(8,128)(2,1)}, bf16[1024,512]{1,0:T(8,128)(2,1)}) conditional(s32[]{:T(128)} %convert_element_type.31, () %tuple.184, (bf16[256,1024]{1,0:T(8,128)(2,1)}, bf16[256,1024]{1,0:T(8,128)(2,1)}, bf16[256,1024]{1,0:T(8,128)(2,1)}, ...), branch_computations={%region_12.13_spmd, %region_13.14_spmd} | conditional | flops 1082130432 | bytes 15728712 | solution.py:616
  296.2 8.1 %collective-permute-start.43 = (bf16[1024,512]{1,0:T(8,128)(2,1)S(1)}, bf16[1024,512]{1,0:T(8,128)(2,1)S(1)}, u32[]{:S(2)}, u32[]{:S(2)}) collective-permute-start(bf16[1024,512]{1,0:T(8,128)(2,1)S(1)} %copy-done.55), channel_id=1, source_target_pairs={{0,4},{1,5},{2,6},{3,7},{12,8},{13,9},{14,10},{15,11},{16,20},{17,... | collective-permute-start | bytes 3145736 | tf_op jit(solution)/shard_map/ppermute | solution.py:504
  316.4 10.4 %collective-permute-done.43 = bf16[1024,512]{1,0:T(8,128)(2,1)S(1)} collective-permute-done((bf16[1024,512]{1,0:T(8,128)(2,1)S(1)}, bf16[1024,512]{1,0:T(8,128)(2,1)S(1)}, u32[]{:S(2)}, u32[]{:S(2)}) %collective-permute-start.43) | collective-permute-done | bytes 1048608 | tf_op jit(solution)/shard_map/ppermute | solution.py:504
  413.3 17.4 %conditional.12 = (bf16[1024,768]{1,0:T(8,128)(2,1)}, bf16[1024,768]{1,0:T(8,128)(2,1)}, bf16[1024,512]{1,0:T(8,128)(2,1)}) conditional(s32[]{:T(128)} %convert_element_type.31, () %tuple.182, (bf16[256,2048]{1,0:T(8,128)(2,1)S(1)}, bf16[256,2048]{1,0:T(8,128)(2,1)}, bf16[256,2048]{1,0:T(8,128)(2,1)}, bf16[256,2048]{1,0:T(8,128)(2,1)}, ...), branch_computations={%region_10.11_spmd, %region_11.12_spmd} | conditional | flops 1076887552 | bytes 17301596 | solution.py:616
  436.3 8.9 %collective-permute-start.71 = (bf16[1024,768]{1,0:T(8,128)(2,1)}, bf16[1024,768]{1,0:T(8,128)(2,1)}, u32[]{:S(2)}, u32[]{:S(2)}) collective-permute-start(bf16[1024,768]{1,0:T(8,128)(2,1)} %get-tuple-element.608), channel_id=1, source_target_pairs={{0,4},{1,5},{2,6},{3,7},{12,8},{13,9},{14,10},{15,11},{16,20},{17,... | collective-permute-start | bytes 4718600 | tf_op jit(solution)/shard_map/ppermute | solution.py:504
  465.7 8.6 %collective-permute-done.83.refs_1_ = bf16[1024,512]{1,0:T(8,128)(2,1)} collective-permute-done((bf16[1024,512]{1,0:T(8,128)(2,1)S(1)}, bf16[1024,512]{1,0:T(8,128)(2,1)}, u32[]{:S(2)}, u32[]{:S(2)}) %collective-permute-start.83) | collective-permute-done | bytes 1048608 | tf_op jit(solution)/shard_map/ppermute | solution.py:504
  483.3 8.8 %collective-permute-done.79 = bf16[1024,512]{1,0:T(8,128)(2,1)} collective-permute-done((bf16[1024,512]{1,0:T(8,128)(2,1)}, bf16[1024,512]{1,0:T(8,128)(2,1)}, u32[]{:S(2)}, u32[]{:S(2)}) %collective-permute-start.79) | collective-permute-done | bytes 1048608 | tf_op jit(solution)/shard_map/ppermute | solution.py:504
  582.4 20.1 %collective-permute-done.95.refs_1_ = bf16[1024,768]{1,0:T(8,128)(2,1)} collective-permute-done((bf16[1024,768]{1,0:T(8,128)(2,1)S(1)}, bf16[1024,768]{1,0:T(8,128)(2,1)}, u32[]{:S(2)}, u32[]{:S(2)}) %collective-permute-start.95) | collective-permute-done | bytes 1572896 | tf_op jit(solution)/shard_map/ppermute | solution.py:504
  644.0 11.2 %shard_map.291.refs_5_ = f32[1024,6144]{1,0:T(8,128)} custom-call(s32[96]{0:T(128)S(1)} %stack.216.table_ref, bf16[1024,768]{1,0:T(8,128)(2,1)S(1)} %broadcast_select_fusion.refs_0_, bf16[1024,768]{1,0:T(8,128)(2,1)} %collective-permute-done.95.refs_1_, bf16[1024,768]{1,0:T(8,128)(2,1)} %collective-permute-done.96.refs_2_, ...), custom_call_target="tpu_custom_call", output_to_operand_aliasing={{}: (6, {})} | custom-call | bytes 4718592 | tf_op jit(solution)/shard_map/pallas_call | solution.py:469
  660.3 8.7 %fusion.21 = f32[256,2048]{1,0:T(8,128)S(1)} fusion(bf16[256,4096]{1,0:T(8,128)(2,1)} %get-tuple-element.483, bf16[4096,2048]{1,0:T(8,128)(2,1)} %param.36), kind=kOutput, calls=%fused_computation.123 | convolution fusion | flops 4294967296 | bytes 20971520 | tf_op jit(solution)/shard_map/dot_general | solution.py:44
  671.4 14.7 %collective-permute-done.106 = bf16[1024,512]{1,0:T(8,128)(2,1)S(1)} collective-permute-done((bf16[1024,512]{1,0:T(8,128)(2,1)S(1)}, bf16[1024,512]{1,0:T(8,128)(2,1)S(1)}, u32[]{:S(2)}, u32[]{:S(2)}) %collective-permute-start.106) | collective-permute-done | bytes 1048608 | tf_op jit(solution)/shard_map/ppermute | solution.py:504
  699.5 11.2 %collective-permute-start.112 = (f32[192,128]{1,0:T(8,128)S(1)}, f32[192,128]{1,0:T(8,128)S(1)}, u32[]{:S(2)}, u32[]{:S(2)}) collective-permute-start(f32[192,128]{1,0:T(8,128)S(1)} %add_add_fusion.1), channel_id=1, source_target_pairs={{0,4},{1,5},{2,6},{3,7},{4,0},{5,1},{6,2},{7,3},{8,12},{9,13},{10,... | collective-permute-start | bytes 294920 | tf_op jit(solution)/shard_map/ppermute | solution.py:902
  716.0 10.8 %shard_map.292 = f32[1024,6144]{1,0:T(8,128)} custom-call(s32[96]{0:T(128)S(1)} %stack.163.table_ref, bf16[1024,768]{1,0:T(8,128)(2,1)S(1)} %broadcast_select_fusion.1.refs_0_, bf16[1024,768]{1,0:T(8,128)(2,1)} %collective-permute-done.99.refs_1_, bf16[1024,768]{1,0:T(8,128)(2,1)} %collective-permute-done.100.refs_2_, ...), custom_call_target="tpu_custom_call", output_to_operand_aliasing={{}: (6, {})} | custom-call | bytes 4718592 | tf_op jit(solution)/shard_map/pallas_call | solution.py:469
  (528 shorter events, 559.3 us)
Async XLA Ops:
  35.8 43.6 %collective-permute-start.16 = (bf16[256,2048]{1,0:T(8,128)(2,1)S(1)}, bf16[256,2048]{1,0:T(8,128)(2,1)}, u32[]{:S(2)}, u32[]{:S(2)}) collective-permute-start(bf16[256,2048]{1,0:T(8,128)(2,1)S(1)} %get-tuple-element.539), channel_id=1, source_target_pairs={{0,1},{1,0},{2,3},{3,2},{4,5},{5,4},{6,7},{7,6},{8,9},{9,8},{10,11... | collective-permute-start | bytes 3145736 | tf_op jit(solution)/shard_map/ppermute | solution.py:504
  37.5 47.5 %collective-permute-start.17 = (bf16[256,2048]{1,0:T(8,128)(2,1)S(1)}, bf16[256,2048]{1,0:T(8,128)(2,1)}, u32[]{:S(2)}, u32[]{:S(2)}) collective-permute-start(bf16[256,2048]{1,0:T(8,128)(2,1)S(1)} %get-tuple-element.539), channel_id=1, source_target_pairs={{0,2},{1,3},{2,0},{3,1},{4,6},{5,7},{6,4},{7,5},{8,10},{9,11},{10,... | collective-permute-start | bytes 3145736 | tf_op jit(solution)/shard_map/ppermute | solution.py:504
  39.0 46.0 %collective-permute-start.18 = (bf16[256,2048]{1,0:T(8,128)(2,1)S(1)}, bf16[256,2048]{1,0:T(8,128)(2,1)}, u32[]{:S(2)}, u32[]{:S(2)}) collective-permute-start(bf16[256,2048]{1,0:T(8,128)(2,1)S(1)} %get-tuple-element.539), channel_id=1, source_target_pairs={{0,3},{1,2},{2,1},{3,0},{4,7},{5,6},{6,5},{7,4},{8,11},{9,10},{10,... | collective-permute-start | bytes 3145736 | tf_op jit(solution)/shard_map/ppermute | solution.py:504
  116.9 35.6 %collective-permute-start.26 = (bf16[1024,512]{1,0:T(8,128)(2,1)S(1)}, bf16[1024,512]{1,0:T(8,128)(2,1)}, u32[]{:S(2)}, u32[]{:S(2)}) collective-permute-start(bf16[1024,512]{1,0:T(8,128)(2,1)S(1)} %shard_map.275), channel_id=1, source_target_pairs={{0,4},{1,5},{2,6},{3,7},{12,8},{13,9},{14,10},{15,11},{16,20},{17,... | collective-permute-start | bytes 3145736 | tf_op jit(solution)/shard_map/ppermute | solution.py:504
  259.3 33.5 %collective-permute-start.52 = (bf16[1024,512]{1,0:T(8,128)(2,1)S(1)}, bf16[1024,512]{1,0:T(8,128)(2,1)S(1)}, u32[]{:S(2)}, u32[]{:S(2)}) collective-permute-start(bf16[1024,512]{1,0:T(8,128)(2,1)S(1)} %broadcast_select_fusion.6.refs_0_), channel_id=1, source_target_pairs={{0,1},{1,0},{2,3},{3,2},{4,5},{5,4},{6,7},{7,6},{8,9},{9,8},{10,11... | collective-permute-start | bytes 3145736 | tf_op jit(solution)/shard_map/ppermute | solution.py:504
  263.2 41.2 %collective-permute-start.49 = (bf16[1024,512]{1,0:T(8,128)(2,1)}, bf16[1024,512]{1,0:T(8,128)(2,1)}, u32[]{:S(2)}, u32[]{:S(2)}) collective-permute-start(bf16[1024,512]{1,0:T(8,128)(2,1)} %add.365), channel_id=1, source_target_pairs={{4,0},{5,1},{6,2},{7,3},{8,12},{9,13},{10,14},{11,15},{20,16},{21,... | collective-permute-start | bytes 3145736 | tf_op jit(solution)/shard_map/ppermute | solution.py:504
  264.5 47.6 %collective-permute-start.46 = (bf16[1024,512]{1,0:T(8,128)(2,1)}, bf16[1024,512]{1,0:T(8,128)(2,1)}, u32[]{:S(2)}, u32[]{:S(2)}) collective-permute-start(bf16[1024,512]{1,0:T(8,128)(2,1)} %add.359), channel_id=1, source_target_pairs={{4,8},{5,9},{6,10},{7,11},{8,4},{9,5},{10,6},{11,7},{20,24},{21,25... | collective-permute-start | bytes 3145736 | tf_op jit(solution)/shard_map/ppermute | solution.py:504
  315.0 33.4 %collective-permute-start.50 = (bf16[1024,512]{1,0:T(8,128)(2,1)}, bf16[1024,512]{1,0:T(8,128)(2,1)}, u32[]{:S(2)}, u32[]{:S(2)}) collective-permute-start(bf16[1024,512]{1,0:T(8,128)(2,1)} %add.364), channel_id=1, source_target_pairs={{4,0},{5,1},{6,2},{7,3},{8,12},{9,13},{10,14},{11,15},{20,16},{21,... | collective-permute-start | bytes 3145736 | tf_op jit(solution)/shard_map/ppermute | solution.py:504
  368.5 36.8 %collective-permute-start.69 = (bf16[1024,512]{1,0:T(8,128)(2,1)}, bf16[1024,512]{1,0:T(8,128)(2,1)}, u32[]{:S(2)}, u32[]{:S(2)}) collective-permute-start(bf16[1024,512]{1,0:T(8,128)(2,1)} %get-tuple-element.606), channel_id=1, source_target_pairs={{0,4},{1,5},{2,6},{3,7},{12,8},{13,9},{14,10},{15,11},{16,20},{17,... | collective-permute-start | bytes 3145736 | tf_op jit(solution)/shard_map/ppermute | solution.py:504
  394.1 39.2 %collective-permute-start.64 = (bf16[1024,512]{1,0:T(8,128)(2,1)S(1)}, bf16[1024,512]{1,0:T(8,128)(2,1)S(1)}, u32[]{:S(2)}, u32[]{:S(2)}) collective-permute-start(bf16[1024,512]{1,0:T(8,128)(2,1)S(1)} %broadcast_select_fusion.9.refs_0_), channel_id=1, source_target_pairs={{0,1},{1,0},{2,3},{3,2},{4,5},{5,4},{6,7},{7,6},{8,9},{9,8},{10,11... | collective-permute-start | bytes 3145736 | tf_op jit(solution)/shard_map/ppermute | solution.py:504
  395.5 37.8 %collective-permute-start.65 = (bf16[1024,512]{1,0:T(8,128)(2,1)S(1)}, bf16[1024,512]{1,0:T(8,128)(2,1)}, u32[]{:S(2)}, u32[]{:S(2)}) collective-permute-start(bf16[1024,512]{1,0:T(8,128)(2,1)S(1)} %broadcast_select_fusion.9.refs_0_), channel_id=1, source_target_pairs={{0,2},{1,3},{2,0},{3,1},{4,6},{5,7},{6,4},{7,5},{8,10},{9,11},{10,... | collective-permute-start | bytes 3145736 | tf_op jit(solution)/shard_map/ppermute | solution.py:504
  412.0 33.2 %collective-permute-start.78 = (bf16[1024,512]{1,0:T(8,128)(2,1)}, bf16[1024,512]{1,0:T(8,128)(2,1)}, u32[]{:S(2)}, u32[]{:S(2)}) collective-permute-start(bf16[1024,512]{1,0:T(8,128)(2,1)} %add.719), channel_id=1, source_target_pairs={{4,0},{5,1},{6,2},{7,3},{8,12},{9,13},{10,14},{11,15},{20,16},{21,... | collective-permute-start | bytes 3145736 | tf_op jit(solution)/shard_map/ppermute | solution.py:504
  436.3 41.7 %collective-permute-start.71 = (bf16[1024,768]{1,0:T(8,128)(2,1)}, bf16[1024,768]{1,0:T(8,128)(2,1)}, u32[]{:S(2)}, u32[]{:S(2)}) collective-permute-start(bf16[1024,768]{1,0:T(8,128)(2,1)} %get-tuple-element.608), channel_id=1, source_target_pairs={{0,4},{1,5},{2,6},{3,7},{12,8},{13,9},{14,10},{15,11},{16,20},{17,... | collective-permute-start | bytes 4718600 | tf_op jit(solution)/shard_map/ppermute | solution.py:504
  457.1 35.1 %collective-permute-start.79 = (bf16[1024,512]{1,0:T(8,128)(2,1)}, bf16[1024,512]{1,0:T(8,128)(2,1)}, u32[]{:S(2)}, u32[]{:S(2)}) collective-permute-start(bf16[1024,512]{1,0:T(8,128)(2,1)} %add.718), channel_id=1, source_target_pairs={{4,0},{5,1},{6,2},{7,3},{8,12},{9,13},{10,14},{11,15},{20,16},{21,... | collective-permute-start | bytes 3145736 | tf_op jit(solution)/shard_map/ppermute | solution.py:504
  481.5 41.3 %collective-permute-start.76 = (bf16[1024,768]{1,0:T(8,128)(2,1)}, bf16[1024,768]{1,0:T(8,128)(2,1)}, u32[]{:S(2)}, u32[]{:S(2)}) collective-permute-start(bf16[1024,768]{1,0:T(8,128)(2,1)} %add.368), channel_id=1, source_target_pairs={{4,8},{5,9},{6,10},{7,11},{8,4},{9,5},{10,6},{11,7},{20,24},{21,25... | collective-permute-start | bytes 4718600 | tf_op jit(solution)/shard_map/ppermute | solution.py:504
  501.2 37.7 %collective-permute-start.72 = (bf16[1024,768]{1,0:T(8,128)(2,1)}, bf16[1024,768]{1,0:T(8,128)(2,1)}, u32[]{:S(2)}, u32[]{:S(2)}) collective-permute-start(bf16[1024,768]{1,0:T(8,128)(2,1)} %get-tuple-element.609), channel_id=1, source_target_pairs={{0,4},{1,5},{2,6},{3,7},{12,8},{13,9},{14,10},{15,11},{16,20},{17,... | collective-permute-start | bytes 4718600 | tf_op jit(solution)/shard_map/ppermute | solution.py:504
  526.3 39.4 %collective-permute-start.81 = (bf16[1024,768]{1,0:T(8,128)(2,1)}, bf16[1024,768]{1,0:T(8,128)(2,1)}, u32[]{:S(2)}, u32[]{:S(2)}) collective-permute-start(bf16[1024,768]{1,0:T(8,128)(2,1)} %add.716), channel_id=1, source_target_pairs={{4,0},{5,1},{6,2},{7,3},{8,12},{9,13},{10,14},{11,15},{20,16},{21,... | collective-permute-start | bytes 4718600 | tf_op jit(solution)/shard_map/ppermute | solution.py:504
  570.6 33.9 %collective-permute-start.96 = (bf16[1024,768]{1,0:T(8,128)(2,1)S(1)}, bf16[1024,768]{1,0:T(8,128)(2,1)}, u32[]{:S(2)}, u32[]{:S(2)}) collective-permute-start(bf16[1024,768]{1,0:T(8,128)(2,1)S(1)} %broadcast_select_fusion.refs_0_), channel_id=1, source_target_pairs={{0,2},{1,3},{2,0},{3,1},{4,6},{5,7},{6,4},{7,5},{8,10},{9,11},{10,... | collective-permute-start | bytes 4718600 | tf_op jit(solution)/shard_map/ppermute | solution.py:504
  574.5 41.8 %collective-permute-start.82 = (bf16[1024,768]{1,0:T(8,128)(2,1)}, bf16[1024,768]{1,0:T(8,128)(2,1)}, u32[]{:S(2)}, u32[]{:S(2)}) collective-permute-start(bf16[1024,768]{1,0:T(8,128)(2,1)} %add.715), channel_id=1, source_target_pairs={{4,0},{5,1},{6,2},{7,3},{8,12},{9,13},{10,14},{11,15},{20,16},{21,... | collective-permute-start | bytes 4718600 | tf_op jit(solution)/shard_map/ppermute | solution.py:504
  642.4 43.8 %collective-permute-start.106 = (bf16[1024,512]{1,0:T(8,128)(2,1)S(1)}, bf16[1024,512]{1,0:T(8,128)(2,1)S(1)}, u32[]{:S(2)}, u32[]{:S(2)}) collective-permute-start(bf16[1024,512]{1,0:T(8,128)(2,1)S(1)} %add.748), channel_id=1, source_target_pairs={{4,0},{5,1},{6,2},{7,3},{8,12},{9,13},{10,14},{11,15},{20,16},{21,... | collective-permute-start | bytes 3145736 | tf_op jit(solution)/shard_map/ppermute | solution.py:504
  658.7 34.3 %collective-permute-start.104 = (bf16[512,768]{1,0:T(8,128)(2,1)S(1)}, bf16[512,768]{1,0:T(8,128)(2,1)S(1)}, u32[]{:S(2)}, u32[]{:S(2)}) collective-permute-start(bf16[512,768]{1,0:T(8,128)(2,1)S(1)} %slice.256), channel_id=1, source_target_pairs={{0,2},{1,3},{2,0},{3,1},{4,6},{5,7},{6,4},{7,5},{8,10},{9,11},{10,... | collective-permute-start | bytes 2359304 | tf_op jit(solution)/shard_map/ppermute | solution.py:504
  659.5 33.5 %collective-permute-start.105 = (bf16[512,768]{1,0:T(8,128)(2,1)S(1)}, bf16[512,768]{1,0:T(8,128)(2,1)S(1)}, u32[]{:S(2)}, u32[]{:S(2)}) collective-permute-start(bf16[512,768]{1,0:T(8,128)(2,1)S(1)} %slice.257), channel_id=1, source_target_pairs={{0,1},{1,0},{2,3},{3,2},{4,5},{5,4},{6,7},{7,6},{8,9},{9,8},{10,11... | collective-permute-start | bytes 2359304 | tf_op jit(solution)/shard_map/ppermute | solution.py:504
  670.2 40.5 %collective-permute-start.19 = (f32[128,2048]{1,0:T(8,128)}, f32[128,2048]{1,0:T(8,128)}, u32[]{:S(2)}, u32[]{:S(2)}) collective-permute-start(f32[128,2048]{1,0:T(8,128)} %slice.237), channel_id=1, source_target_pairs={{0,16},{16,0},{1,17},{17,1},{2,18},{18,2},{3,19},{19,3},{4,20},{20... | collective-permute-start | bytes 3145736 | tf_op jit(solution)/shard_map/ppermute | solution.py:542
  694.6 33.4 %collective-permute-start.111 = (bf16[1024,512]{1,0:T(8,128)(2,1)S(1)}, bf16[1024,512]{1,0:T(8,128)(2,1)}, u32[]{:S(2)}, u32[]{:S(2)}) collective-permute-start(bf16[1024,512]{1,0:T(8,128)(2,1)S(1)} %broadcast_select_fusion.2.refs_0_), channel_id=1, source_target_pairs={{0,2},{1,3},{2,0},{3,1},{4,6},{5,7},{6,4},{7,5},{8,10},{9,11},{10,... | collective-permute-start | bytes 3145736 | tf_op jit(solution)/shard_map/ppermute | solution.py:504
  (166 other events, 2160.0 us)

commit v11 on v10

--- a/solution.py
+++ b/solution.py
@@ -834,41 +834,51 @@
     up_width = inner_half // GROUP
     up_block = min(512, up_width)
 
-    def to_up(*operands):
-        lefts = [(left, 0) for left in operands[:GROUP]]
-        mine = operands[GROUP:]
+    def up_products(rights, turned):
+        lefts = [(left, 0) for left in up_left]
+        return [
+            rows_product(lefts, [right(first) for right in rights], half, up_block, 1, turned)
+            for first in range(up_width // up_block)
+        ]
+
+    def up_own():
+        def place(right):
+            return lambda first: columns_from(right, length, 0, first, up_block)
+
+        return up_products([place(right) for right in hold(up_right, late)], False)
+
+    def up_other(*mine):
         theirs = swap(jnp.concatenate(mine))
-        results = []
-        for first in range(inner_half // GROUP // up_block):
-            rights = [columns_from(right, length, 0, first, up_block) for right in mine]
-            results.append(rows_product(lefts, rights, half, up_block, 1))
-        for first in range(inner_half // GROUP // up_block):
-            rights = [columns_from(theirs, length, d, first, up_block) for d in range(GROUP)]
-            results.append(rows_product(lefts, rights, half, up_block, 1, True))
-        return results
+
+        def place(d):
+            return lambda first: columns_from(theirs, length, d, first, up_block)
+
+        return up_products([place(d) for d in range(GROUP)], True)
 
     rest_block = half // GROUP
 
-    def to_rest(*operands):
-        early, mine = operands[:GROUP], operands[GROUP:]
+    def rest_part(value, d):
+        return value, (1, length, rest_block), lambda j: (4 * d + j, 0, 0)
+
+    def rest_own(mine):
+        lefts = [(left, 0) for left in early]
+        rights = [rest_part(right, 0) for right in mine]
+        return [rows_product(lefts, rights, half, rest_block, 3)]
+
+    def rest_other(*mine):
         theirs = swap(jnp.concatenate(mine))
-
-        def part(value, d):
-            return value, (1, length, rest_block), lambda j: (4 * d + j, 0, 0)
 
         def out_part(value, d):
             return value, (1, rows, rest_block), lambda j: (4 * d + 3, j, 0)
 
         lefts = [(left, 0) for left in early]
-        rights = [part(right, 0) for right in mine]
-        own = rows_product(lefts, rights, half, rest_block, 3)
-        rights = [part(theirs, d) for d in range(GROUP)]
+        rights = [rest_part(theirs, d) for d in range(GROUP)]
         other_half = rows_product(lefts, rights, half, rest_block, 3, True)
         lefts = [(left, 1) for left in early]
         rights = []
         for d, right in enumerate(mine):
             rights += [out_part(right, 0), out_part(theirs, d)]
-        return [own, other_half, rows_product(lefts, rights, half, rest_block, 2)]
+        return [other_half, rows_product(lefts, rights, half, rest_block, 2)]
 
     wholes = {
         "down": blank((inner_half, width)),
@@ -884,13 +894,17 @@
         more, held = (), [done[-1]]
         if index == 0:
             held.append(begun[3])
+        fresh = []
+        if index == 0:
+            fresh = up_own()
         if index == 1:
-            raw += segment(to_up, *hold(up_left, late), *up_right)
-            held.append(raw)
+            fresh = segment(up_other, *hold(up_right, done[-1]))
+        if index == 3:
+            fresh = rest_own(hold(late, done[-1]))
         if index == 4:
-            rest = segment(to_rest, *early, *late)
-            raw += rest
-            held.append(rest)
+            fresh = segment(rest_other, *hold(late, done[-1]))
+        raw += fresh
+        held.append(fresh)
         if index == len(chunks) - 2:
             more = small_sends
         if index == len(chunks) - 1:

time: 757 us -> 759 us (level)
    ppermute x16, waiting for transfers between devices: 8.05 us -> 16.3 us  [swap(): return lax.ppermute(value, 'sp', [(0, 1), (1, 0)])]
    unnamed x141 -> x135, local copies, waits for them, and re-layouts: 29.7 us -> 22.8 us
  transfers between devices with their start and end apart: 117 -> 117, of which waited for: 48 -> 50; matrix products, arithmetic and copies ran while one was open for 17% -> 18% of each run, Pallas kernels for 26% -> 26%
where the time goes in v11:
time: 759 us; the launch traced here: 746 us
  Pallas kernels  202 us (27%)
  waiting for transfers between devices  187 us (25%)
  starting transfers between devices  183 us (24%)
  other arithmetic  90.9 us (12%)
  local copies, waits for them, and re-layouts  62.6 us (8%)
  matrix products  16 us (2%)
    ppermute x98, waiting for transfers between devices, send(): self.last = [lax.ppermute(v, 'dp', m) for v, (_, m) in zip(values, sends)]  170 us
    ppermute x98, starting transfers between devices, send(): self.last = [lax.ppermute(v, 'dp', m) for v, (_, m) in zip(values, sends)]  166 us
    pallas_call x11, Pallas kernels, place(): pl.pallas_call(functools.partial(place_kernel, high), in_specs=[pl.BlockS...  69 us
    pallas_call x11, Pallas kernels, rows_product(): pl.pallas_call(functools.partial(product_kernel, len(lefts), turned), gri...  40.9 us
    pallas_call x4, Pallas kernels, times_back(): pl.pallas_call(functools.partial(back_kernel, turned), grid_spec=pltpu.Pr...  27.1 us
    pallas_call x4, Pallas kernels, times_columns(): pl.pallas_call(columns_kernel, grid_spec=pltpu.PrefetchScalarGridSpec(num...  25.2 us
    add x10, other arithmetic, line_middle(): return value + middle_hop.send([(value, middle_moves)])[0]  24.5 us
    unnamed x135, local copies, waits for them, and re-layouts  22.8 us
  transfers between devices with their start and end apart: 117, of which 50 were waited for; matrix products, arithmetic and copies ran while one was open for 18% of the time, Pallas kernels for 26%

profile of v11, /device:TPU:0, one launch (start us, length us, event | category | flops | bytes accessed | tf_op | source)
XLA Modules:
  0.0 746.0 jit_solution(5130988114375940733)
XLA Ops:
  13.4 22.3 %conditional.7 = (bf16[256,1024]{1,0:T(8,128)(2,1)}, bf16[256,1024]{1,0:T(8,128)(2,1)}, bf16[256,1024]{1,0:T(8,128)(2,1)}, bf16[256,1024]{1,0:T(8,128)(2,1)}, bf...) conditional(s32[]{:T(128)} %convert_element_type.31, () %tuple.158, (bf16[128,1024]{1,0:T(8,128)(2,1)S(1)}, ...), branch_computations={%region_0.1_spmd, %region_1.2_spmd} | conditional | flops 874512384 | bytes 19710170 | solution.py:616
  41.5 37.8 %conditional.8 = (f32[128,2048]{1,0:T(8,128)}, bf16[256,1024]{1,0:T(8,128)(2,1)}, bf16[256,4096]{1,0:T(8,128)(2,1)}, bf16[256,4096]{1,0:T(8,128)(2,1)}, f32[4096...) conditional(s32[]{:T(128)} %convert_element_type.31, () %tuple.157, (bf16[256,1024]{1,0:T(8,128)(2,1)}, ...), branch_computations={%region_2.3_spmd, %region_3.4_spmd} | conditional | flops 3222536192 | bytes 42932700 | solution.py:616
  51.4 7.2 branch_1_fun.22
  65.1 13.4 %branch_1_fun.23 = (bf16[256,4096]{1,0:T(8,128)(2,1)}, bf16[256,4096]{1,0:T(8,128)(2,1)}, f32[1,4096]{1,0:T(1,128)}) custom-call(bf16[256,2048]{1,0:T(8,128)(2,1)S(1)} %copy-done.49, bf16[4096,2048]{1,0:T(8,128)(2,1)} %get-tuple-element.204.refs_0_, f32[256,4096]{1,0:T(8,128)S(1)} %branch_1_fun.21.refs_1_, ...), custom_call_target="tpu_custom_call" | custom-call | flops 1073741824 | bytes 7602176 | tf_op jit(solution)/shard_map/cond/branch_1_fun/pallas_call | solution.py:311
  91.7 22.8 %conditional.9 = (f32[128,2048]{1,0:T(8,128)}, bf16[128,2048]{1,0:T(8,128)(2,1)}, bf16[384,2048]{1,0:T(8,128)(2,1)}, bf16[256,1024]{1,0:T(8,128)(2,1)}, bf16[256...) conditional(s32[]{:T(128)} %convert_element_type.31, () %tuple.168, ...), branch_computations={%region_4.5_spmd, %region_5.6_spmd} | conditional | flops 1079771136 | bytes 34343496 | solution.py:616
  125.0 25.4 %conditional.10 = (bf16[3,256,1024]{2,1,0:T(8,128)(2,1)}, bf16[256,3072]{1,0:T(8,128)(2,1)}, bf16[256,3072]{1,0:T(8,128)(2,1)}, bf16[4,256,256]{2,1,0:T(8,128)(2...) conditional(s32[]{:T(128)} %convert_element_type.31, () %tuple.166, ...), branch_computations={%region_6.7_spmd, %region_7.8_spmd} | conditional | flops 1250689024 | bytes 30802540 | solution.py:616
  130.8 10.8 %branch_1_fun.27 = bf16[3,256,1024]{2,1,0:T(8,128)(2,1)} custom-call(s32[1]{0:T(128)} %get-tuple-element.232.first_ref, bf16[256,1024]{1,0:T(8,128)(2,1)} %get-tuple-element.233.q_ref, bf16[256,1024]{1,0:T(8,128)(2,1)} %get-tuple-element.234.k_ref, bf16[256,1024]{1,0:T(8,128)(2,1)} %get-tuple-element.235.v_ref, ...), custom_call_target="tpu_custom_call" | custom-call | flops 167772160 | bytes 917504 | tf_op jit(solution)/shard_map/cond/branch_1_fun/pallas_call | solution.py:424
  167.6 15.2 %conditional.11 = (f32[256,1024]{1,0:T(8,128)}) conditional(s32[]{:T(128)} %convert_element_type.31, () %tuple.165, (s32[3]{0:T(128)S(1)}, bf16[256,3072]{1,0:T(8,128)(2,1)}, bf16[1024,6144]{1,0:T(8,128)(2,1)}, s32[3]{0:T(128)S(1)}, bf16[256,3072]{1,0:T(8,128)(2,1)}) %tuple.176), branch_computations={%region_8.9_spmd, %region_9.10_spmd} | conditional | flops 805306368 | bytes 4980744 | solution.py:616
  174.8 8.1 %branch_1_fun.29 = f32[256,1024]{1,0:T(8,128)} custom-call(s32[3]{0:T(128)S(1)} %get-tuple-element.239.table_ref, bf16[256,3072]{1,0:T(8,128)(2,1)} %get-tuple-element.240.left_ref, bf16[1024,6144]{1,0:T(8,128)(2,1)} %get-tuple-element.241.refs_0_, f32[256,1024]{1,0:T(8,128)S(1)} %branch_1_fun.28.refs_1_), custom_call_target="tpu_custom_call" | custom-call | flops 402653184 | bytes 2490368 | tf_op jit(solution)/shard_map/cond/branch_1_fun/pallas_call | solution.py:277
  204.7 8.7 %collective-permute-done.34.refs_5_ = bf16[4,256,256]{2,1,0:T(8,128)(2,1)} collective-permute-done((bf16[4,256,256]{2,1,0:T(8,128)(2,1)S(1)}, bf16[4,256,256]{2,1,0:T(8,128)(2,1)}, u32[]{:S(2)}, u32[]{:S(2)}) %collective-permute-start.34) | collective-permute-done | bytes 524320 | tf_op jit(solution)/shard_map/ppermute | solution.py:504
  276.9 13.5 %conditional.12 = (bf16[1024,512]{1,0:T(8,128)(2,1)}, bf16[1024,512]{1,0:T(8,128)(2,1)}) conditional(s32[]{:T(128)} %convert_element_type.31, () %tuple.198, (bf16[256,1024]{1,0:T(8,128)(2,1)}, bf16[256,1024]{1,0:T(8,128)(2,1)}, bf16[256,1024]{1,0:T(8,128)(2,1)}, bf16[256,1024]{1,0:T(8,128)(2,1)}, bf16[256,1024]{1,0:T(8,128)(2,1)}, ...), branch_computations={%region_10.11_spmd, %region_11.12_spmd} | conditional | flops 545259520 | bytes 14155832 | solution.py:616
  294.5 8.0 %collective-permute-start.61 = (bf16[1024,512]{1,0:T(8,128)(2,1)S(1)}, bf16[1024,512]{1,0:T(8,128)(2,1)S(1)}, u32[]{:S(2)}, u32[]{:S(2)}) collective-permute-start(bf16[1024,512]{1,0:T(8,128)(2,1)S(1)} %shard_map.280), channel_id=1, source_target_pairs={{0,4},{1,5},{2,6},{3,7},{12,8},{13,9},{14,10},{15,11},{16,20},{17,... | collective-permute-start | bytes 3145736 | tf_op jit(solution)/shard_map/ppermute | solution.py:504
  313.1 11.5 %collective-permute-done.61 = bf16[1024,512]{1,0:T(8,128)(2,1)S(1)} collective-permute-done((bf16[1024,512]{1,0:T(8,128)(2,1)S(1)}, bf16[1024,512]{1,0:T(8,128)(2,1)S(1)}, u32[]{:S(2)}, u32[]{:S(2)}) %collective-permute-start.61) | collective-permute-done | bytes 1048608 | tf_op jit(solution)/shard_map/ppermute | solution.py:504
  415.9 15.7 %conditional.13 = (bf16[1024,768]{1,0:T(8,128)(2,1)}, bf16[1024,512]{1,0:T(8,128)(2,1)}) conditional(s32[]{:T(128)} %convert_element_type.31, () %tuple.185, (bf16[4,256,256]{2,1,0:T(8,128)(2,1)S(1)}, bf16[4,256,256]{2,1,0:T(8,128)(2,1)}, bf16[4,256,256]{2,1,0:T(8,128)(2,1)}, bf16[4,256,256]{2,1,0:T(8,128)(2,1)}, bf16[256,2048]{1,0:T(8,128)(2,1)}, ...), branch_computations={%region_12.13_spmd, %region_13.14_spmd} | conditional | flops 674234368 | bytes 14286904 | solution.py:616
  436.7 8.7 %collective-permute-start.71 = (bf16[1024,768]{1,0:T(8,128)(2,1)S(1)}, bf16[1024,768]{1,0:T(8,128)(2,1)}, u32[]{:S(2)}, u32[]{:S(2)}) collective-permute-start(bf16[1024,768]{1,0:T(8,128)(2,1)S(1)} %shard_map.286), channel_id=1, source_target_pairs={{0,4},{1,5},{2,6},{3,7},{12,8},{13,9},{14,10},{15,11},{16,20},{17,... | collective-permute-start | bytes 4718600 | tf_op jit(solution)/shard_map/ppermute | solution.py:504
  465.0 8.3 %collective-permute-done.83.refs_1_ = bf16[1024,512]{1,0:T(8,128)(2,1)} collective-permute-done((bf16[1024,512]{1,0:T(8,128)(2,1)}, bf16[1024,512]{1,0:T(8,128)(2,1)}, u32[]{:S(2)}, u32[]{:S(2)}) %collective-permute-start.83) | collective-permute-done | bytes 1048608 | tf_op jit(solution)/shard_map/ppermute | solution.py:504
  482.8 8.2 %collective-permute-done.79 = bf16[1024,512]{1,0:T(8,128)(2,1)} collective-permute-done((bf16[1024,512]{1,0:T(8,128)(2,1)}, bf16[1024,512]{1,0:T(8,128)(2,1)}, u32[]{:S(2)}, u32[]{:S(2)}) %collective-permute-start.79) | collective-permute-done | bytes 1048608 | tf_op jit(solution)/shard_map/ppermute | solution.py:504
  578.6 20.2 %collective-permute-done.95.refs_1_ = bf16[1024,768]{1,0:T(8,128)(2,1)} collective-permute-done((bf16[1024,768]{1,0:T(8,128)(2,1)S(1)}, bf16[1024,768]{1,0:T(8,128)(2,1)}, u32[]{:S(2)}, u32[]{:S(2)}) %collective-permute-start.95) | collective-permute-done | bytes 1572896 | tf_op jit(solution)/shard_map/ppermute | solution.py:504
  605.0 7.8 %collective-permute-start.102 = (bf16[1024,512]{1,0:T(8,128)(2,1)}, bf16[1024,512]{1,0:T(8,128)(2,1)}, u32[]{:S(2)}, u32[]{:S(2)}) collective-permute-start(bf16[1024,512]{1,0:T(8,128)(2,1)} %get-tuple-element.665), channel_id=1, source_target_pairs={{0,4},{1,5},{2,6},{3,7},{12,8},{13,9},{14,10},{15,11},{16,20},{17,... | collective-permute-start | bytes 3145736 | tf_op jit(solution)/shard_map/ppermute | solution.py:504
  641.3 11.2 %shard_map.294.refs_5_ = f32[1024,6144]{1,0:T(8,128)} custom-call(s32[96]{0:T(128)S(1)} %stack.216.table_ref, bf16[1024,768]{1,0:T(8,128)(2,1)S(1)} %broadcast_select_fusion.refs_0_, bf16[1024,768]{1,0:T(8,128)(2,1)} %collective-permute-done.95.refs_1_, bf16[1024,768]{1,0:T(8,128)(2,1)} %collective-permute-done.96.refs_2_, ...), custom_call_target="tpu_custom_call", output_to_operand_aliasing={{}: (6, {})} | custom-call | bytes 4718592 | tf_op jit(solution)/shard_map/pallas_call | solution.py:469
  657.8 8.7 %fusion.21 = f32[256,2048]{1,0:T(8,128)S(1)} fusion(bf16[256,4096]{1,0:T(8,128)(2,1)} %get-tuple-element.492, bf16[4096,2048]{1,0:T(8,128)(2,1)} %param.36), kind=kOutput, calls=%fused_computation.123 | convolution fusion | flops 4294967296 | bytes 20971520 | tf_op jit(solution)/shard_map/dot_general | solution.py:44
  668.7 18.4 %collective-permute-done.106 = bf16[1024,512]{1,0:T(8,128)(2,1)S(1)} collective-permute-done((bf16[1024,512]{1,0:T(8,128)(2,1)S(1)}, bf16[1024,512]{1,0:T(8,128)(2,1)S(1)}, u32[]{:S(2)}, u32[]{:S(2)}) %collective-permute-start.106) | collective-permute-done | bytes 1048608 | tf_op jit(solution)/shard_map/ppermute | solution.py:504
  698.1 12.3 %collective-permute-start.112 = (f32[192,128]{1,0:T(8,128)S(1)}, f32[192,128]{1,0:T(8,128)S(1)}, u32[]{:S(2)}, u32[]{:S(2)}) collective-permute-start(f32[192,128]{1,0:T(8,128)S(1)} %add_add_fusion.1), channel_id=1, source_target_pairs={{0,4},{1,5},{2,6},{3,7},{4,0},{5,1},{6,2},{7,3},{8,12},{9,13},{10,... | collective-permute-start | bytes 294920 | tf_op jit(solution)/shard_map/ppermute | solution.py:916
  715.7 10.8 %shard_map.295 = f32[1024,6144]{1,0:T(8,128)} custom-call(s32[96]{0:T(128)S(1)} %stack.163.table_ref, bf16[1024,768]{1,0:T(8,128)(2,1)S(1)} %broadcast_select_fusion.1.refs_0_, bf16[1024,768]{1,0:T(8,128)(2,1)} %collective-permute-done.99.refs_1_, bf16[1024,768]{1,0:T(8,128)(2,1)} %collective-permute-done.100.refs_2_, ...), custom_call_target="tpu_custom_call", output_to_operand_aliasing={{}: (6, {})} | custom-call | bytes 4718592 | tf_op jit(solution)/shard_map/pallas_call | solution.py:469
  (516 shorter events, 558.4 us)
Async XLA Ops:
  35.8 43.5 %collective-permute-start.16 = (bf16[256,2048]{1,0:T(8,128)(2,1)}, bf16[256,2048]{1,0:T(8,128)(2,1)}, u32[]{:S(2)}, u32[]{:S(2)}) collective-permute-start(bf16[256,2048]{1,0:T(8,128)(2,1)} %get-tuple-element.594.refs_0_), channel_id=1, source_target_pairs={{0,1},{1,0},{2,3},{3,2},{4,5},{5,4},{6,7},{7,6},{8,9},{9,8},{10,11... | collective-permute-start | bytes 3145736 | tf_op jit(solution)/shard_map/ppermute | solution.py:504
  37.8 47.7 %collective-permute-start.17 = (bf16[256,2048]{1,0:T(8,128)(2,1)}, bf16[256,2048]{1,0:T(8,128)(2,1)}, u32[]{:S(2)}, u32[]{:S(2)}) collective-permute-start(bf16[256,2048]{1,0:T(8,128)(2,1)} %get-tuple-element.594.refs_0_), channel_id=1, source_target_pairs={{0,2},{1,3},{2,0},{3,1},{4,6},{5,7},{6,4},{7,5},{8,10},{9,11},{10,... | collective-permute-start | bytes 3145736 | tf_op jit(solution)/shard_map/ppermute | solution.py:504
  39.3 46.2 %collective-permute-start.18 = (bf16[256,2048]{1,0:T(8,128)(2,1)}, bf16[256,2048]{1,0:T(8,128)(2,1)}, u32[]{:S(2)}, u32[]{:S(2)}) collective-permute-start(bf16[256,2048]{1,0:T(8,128)(2,1)} %get-tuple-element.594.refs_0_), channel_id=1, source_target_pairs={{0,3},{1,2},{2,1},{3,0},{4,7},{5,6},{6,5},{7,4},{8,11},{9,10},{10,... | collective-permute-start | bytes 3145736 | tf_op jit(solution)/shard_map/ppermute | solution.py:504
  117.1 37.1 %collective-permute-start.26 = (bf16[1024,512]{1,0:T(8,128)(2,1)S(1)}, bf16[1024,512]{1,0:T(8,128)(2,1)}, u32[]{:S(2)}, u32[]{:S(2)}) collective-permute-start(bf16[1024,512]{1,0:T(8,128)(2,1)S(1)} %shard_map.275), channel_id=1, source_target_pairs={{0,4},{1,5},{2,6},{3,7},{12,8},{13,9},{14,10},{15,11},{16,20},{17,... | collective-permute-start | bytes 3145736 | tf_op jit(solution)/shard_map/ppermute | solution.py:504
  264.9 37.6 %collective-permute-start.43 = (bf16[1024,512]{1,0:T(8,128)(2,1)}, bf16[1024,512]{1,0:T(8,128)(2,1)}, u32[]{:S(2)}, u32[]{:S(2)}) collective-permute-start(bf16[1024,512]{1,0:T(8,128)(2,1)} %add.359), channel_id=1, source_target_pairs={{4,0},{5,1},{6,2},{7,3},{8,12},{9,13},{10,14},{11,15},{20,16},{21,... | collective-permute-start | bytes 3145736 | tf_op jit(solution)/shard_map/ppermute | solution.py:504
  266.2 42.8 %collective-permute-start.41 = (bf16[1024,512]{1,0:T(8,128)(2,1)}, bf16[1024,512]{1,0:T(8,128)(2,1)}, u32[]{:S(2)}, u32[]{:S(2)}) collective-permute-start(bf16[1024,512]{1,0:T(8,128)(2,1)} %add.355), channel_id=1, source_target_pairs={{4,8},{5,9},{6,10},{7,11},{8,4},{9,5},{10,6},{11,7},{20,24},{21,25... | collective-permute-start | bytes 3145736 | tf_op jit(solution)/shard_map/ppermute | solution.py:504
  311.8 34.2 %collective-permute-start.44 = (bf16[1024,512]{1,0:T(8,128)(2,1)}, bf16[1024,512]{1,0:T(8,128)(2,1)}, u32[]{:S(2)}, u32[]{:S(2)}) collective-permute-start(bf16[1024,512]{1,0:T(8,128)(2,1)} %add.358), channel_id=1, source_target_pairs={{4,0},{5,1},{6,2},{7,3},{8,12},{9,13},{10,14},{11,15},{20,16},{21,... | collective-permute-start | bytes 3145736 | tf_op jit(solution)/shard_map/ppermute | solution.py:504
  365.8 40.8 %collective-permute-start.69 = (bf16[1024,512]{1,0:T(8,128)(2,1)}, bf16[1024,512]{1,0:T(8,128)(2,1)}, u32[]{:S(2)}, u32[]{:S(2)}) collective-permute-start(bf16[1024,512]{1,0:T(8,128)(2,1)} %get-tuple-element.624), channel_id=1, source_target_pairs={{0,4},{1,5},{2,6},{3,7},{12,8},{13,9},{14,10},{15,11},{16,20},{17,... | collective-permute-start | bytes 3145736 | tf_op jit(solution)/shard_map/ppermute | solution.py:504
  374.0 34.8 %collective-permute-start.73 = (bf16[1024,512]{1,0:T(8,128)(2,1)}, bf16[1024,512]{1,0:T(8,128)(2,1)}, u32[]{:S(2)}, u32[]{:S(2)}) collective-permute-start(bf16[1024,512]{1,0:T(8,128)(2,1)} %add.714), channel_id=1, source_target_pairs={{4,8},{5,9},{6,10},{7,11},{8,4},{9,5},{10,6},{11,7},{20,24},{21,25... | collective-permute-start | bytes 3145736 | tf_op jit(solution)/shard_map/ppermute | solution.py:504
  396.1 36.3 %collective-permute-start.64 = (bf16[1024,512]{1,0:T(8,128)(2,1)S(1)}, bf16[1024,512]{1,0:T(8,128)(2,1)}, u32[]{:S(2)}, u32[]{:S(2)}) collective-permute-start(bf16[1024,512]{1,0:T(8,128)(2,1)S(1)} %broadcast_select_fusion.6.refs_0_), channel_id=1, source_target_pairs={{0,1},{1,0},{2,3},{3,2},{4,5},{5,4},{6,7},{7,6},{8,9},{9,8},{10,11... | collective-permute-start | bytes 3145736 | tf_op jit(solution)/shard_map/ppermute | solution.py:504
  397.5 36.0 %collective-permute-start.65 = (bf16[1024,512]{1,0:T(8,128)(2,1)S(1)}, bf16[1024,512]{1,0:T(8,128)(2,1)}, u32[]{:S(2)}, u32[]{:S(2)}) collective-permute-start(bf16[1024,512]{1,0:T(8,128)(2,1)S(1)} %broadcast_select_fusion.6.refs_0_), channel_id=1, source_target_pairs={{0,2},{1,3},{2,0},{3,1},{4,6},{5,7},{6,4},{7,5},{8,10},{9,11},{10,... | collective-permute-start | bytes 3145736 | tf_op jit(solution)/shard_map/ppermute | solution.py:504
  411.7 33.7 %collective-permute-start.78 = (bf16[1024,512]{1,0:T(8,128)(2,1)}, bf16[1024,512]{1,0:T(8,128)(2,1)}, u32[]{:S(2)}, u32[]{:S(2)}) collective-permute-start(bf16[1024,512]{1,0:T(8,128)(2,1)} %add.719), channel_id=1, source_target_pairs={{4,0},{5,1},{6,2},{7,3},{8,12},{9,13},{10,14},{11,15},{20,16},{21,... | collective-permute-start | bytes 3145736 | tf_op jit(solution)/shard_map/ppermute | solution.py:504
  436.7 41.3 %collective-permute-start.71 = (bf16[1024,768]{1,0:T(8,128)(2,1)S(1)}, bf16[1024,768]{1,0:T(8,128)(2,1)}, u32[]{:S(2)}, u32[]{:S(2)}) collective-permute-start(bf16[1024,768]{1,0:T(8,128)(2,1)S(1)} %shard_map.286), channel_id=1, source_target_pairs={{0,4},{1,5},{2,6},{3,7},{12,8},{13,9},{14,10},{15,11},{16,20},{17,... | collective-permute-start | bytes 4718600 | tf_op jit(solution)/shard_map/ppermute | solution.py:504
  457.1 33.9 %collective-permute-start.79 = (bf16[1024,512]{1,0:T(8,128)(2,1)}, bf16[1024,512]{1,0:T(8,128)(2,1)}, u32[]{:S(2)}, u32[]{:S(2)}) collective-permute-start(bf16[1024,512]{1,0:T(8,128)(2,1)} %add.718), channel_id=1, source_target_pairs={{4,0},{5,1},{6,2},{7,3},{8,12},{9,13},{10,14},{11,15},{20,16},{21,... | collective-permute-start | bytes 3145736 | tf_op jit(solution)/shard_map/ppermute | solution.py:504
  480.9 39.1 %collective-permute-start.76 = (bf16[1024,768]{1,0:T(8,128)(2,1)}, bf16[1024,768]{1,0:T(8,128)(2,1)}, u32[]{:S(2)}, u32[]{:S(2)}) collective-permute-start(bf16[1024,768]{1,0:T(8,128)(2,1)} %add.368), channel_id=1, source_target_pairs={{4,8},{5,9},{6,10},{7,11},{8,4},{9,5},{10,6},{11,7},{20,24},{21,25... | collective-permute-start | bytes 4718600 | tf_op jit(solution)/shard_map/ppermute | solution.py:504
  499.7 37.3 %collective-permute-start.72 = (bf16[1024,768]{1,0:T(8,128)(2,1)}, bf16[1024,768]{1,0:T(8,128)(2,1)}, u32[]{:S(2)}, u32[]{:S(2)}) collective-permute-start(bf16[1024,768]{1,0:T(8,128)(2,1)} %get-tuple-element.627), channel_id=1, source_target_pairs={{0,4},{1,5},{2,6},{3,7},{12,8},{13,9},{14,10},{15,11},{16,20},{17,... | collective-permute-start | bytes 4718600 | tf_op jit(solution)/shard_map/ppermute | solution.py:504
  523.6 39.7 %collective-permute-start.81 = (bf16[1024,768]{1,0:T(8,128)(2,1)}, bf16[1024,768]{1,0:T(8,128)(2,1)}, u32[]{:S(2)}, u32[]{:S(2)}) collective-permute-start(bf16[1024,768]{1,0:T(8,128)(2,1)} %add.716), channel_id=1, source_target_pairs={{4,0},{5,1},{6,2},{7,3},{8,12},{9,13},{10,14},{11,15},{20,16},{21,... | collective-permute-start | bytes 4718600 | tf_op jit(solution)/shard_map/ppermute | solution.py:504
  565.3 33.5 %collective-permute-start.95 = (bf16[1024,768]{1,0:T(8,128)(2,1)S(1)}, bf16[1024,768]{1,0:T(8,128)(2,1)}, u32[]{:S(2)}, u32[]{:S(2)}) collective-permute-start(bf16[1024,768]{1,0:T(8,128)(2,1)S(1)} %broadcast_select_fusion.refs_0_), channel_id=1, source_target_pairs={{0,1},{1,0},{2,3},{3,2},{4,5},{5,4},{6,7},{7,6},{8,9},{9,8},{10,11... | collective-permute-start | bytes 4718600 | tf_op jit(solution)/shard_map/ppermute | solution.py:504
  567.0 33.9 %collective-permute-start.96 = (bf16[1024,768]{1,0:T(8,128)(2,1)S(1)}, bf16[1024,768]{1,0:T(8,128)(2,1)}, u32[]{:S(2)}, u32[]{:S(2)}) collective-permute-start(bf16[1024,768]{1,0:T(8,128)(2,1)S(1)} %broadcast_select_fusion.refs_0_), channel_id=1, source_target_pairs={{0,2},{1,3},{2,0},{3,1},{4,6},{5,7},{6,4},{7,5},{8,10},{9,11},{10,... | collective-permute-start | bytes 4718600 | tf_op jit(solution)/shard_map/ppermute | solution.py:504
  570.7 43.0 %collective-permute-start.82 = (bf16[1024,768]{1,0:T(8,128)(2,1)}, bf16[1024,768]{1,0:T(8,128)(2,1)}, u32[]{:S(2)}, u32[]{:S(2)}) collective-permute-start(bf16[1024,768]{1,0:T(8,128)(2,1)} %add.715), channel_id=1, source_target_pairs={{4,0},{5,1},{6,2},{7,3},{8,12},{9,13},{10,14},{11,15},{20,16},{21,... | collective-permute-start | bytes 4718600 | tf_op jit(solution)/shard_map/ppermute | solution.py:504
  639.7 47.3 %collective-permute-start.106 = (bf16[1024,512]{1,0:T(8,128)(2,1)S(1)}, bf16[1024,512]{1,0:T(8,128)(2,1)S(1)}, u32[]{:S(2)}, u32[]{:S(2)}) collective-permute-start(bf16[1024,512]{1,0:T(8,128)(2,1)S(1)} %add.748), channel_id=1, source_target_pairs={{4,0},{5,1},{6,2},{7,3},{8,12},{9,13},{10,14},{11,15},{20,16},{21,... | collective-permute-start | bytes 3145736 | tf_op jit(solution)/shard_map/ppermute | solution.py:504
  655.4 38.1 %collective-permute-start.104 = (bf16[512,768]{1,0:T(8,128)(2,1)S(1)}, bf16[512,768]{1,0:T(8,128)(2,1)S(1)}, u32[]{:S(2)}, u32[]{:S(2)}) collective-permute-start(bf16[512,768]{1,0:T(8,128)(2,1)S(1)} %slice.256), channel_id=1, source_target_pairs={{0,2},{1,3},{2,0},{3,1},{4,6},{5,7},{6,4},{7,5},{8,10},{9,11},{10,... | collective-permute-start | bytes 2359304 | tf_op jit(solution)/shard_map/ppermute | solution.py:504
  656.7 36.7 %collective-permute-start.105 = (bf16[512,768]{1,0:T(8,128)(2,1)S(1)}, bf16[512,768]{1,0:T(8,128)(2,1)S(1)}, u32[]{:S(2)}, u32[]{:S(2)}) collective-permute-start(bf16[512,768]{1,0:T(8,128)(2,1)S(1)} %slice.257), channel_id=1, source_target_pairs={{0,1},{1,0},{2,3},{3,2},{4,5},{5,4},{6,7},{7,6},{8,9},{9,8},{10,11... | collective-permute-start | bytes 2359304 | tf_op jit(solution)/shard_map/ppermute | solution.py:504
  667.7 43.5 %collective-permute-start.19 = (f32[128,2048]{1,0:T(8,128)}, f32[128,2048]{1,0:T(8,128)}, u32[]{:S(2)}, u32[]{:S(2)}) collective-permute-start(f32[128,2048]{1,0:T(8,128)} %slice.237), channel_id=1, source_target_pairs={{0,16},{16,0},{1,17},{17,1},{2,18},{18,2},{3,19},{19,3},{4,20},{20... | collective-permute-start | bytes 3145736 | tf_op jit(solution)/shard_map/ppermute | solution.py:542
  (160 other events, 2309.8 us)

commit v12 on v11

--- a/solution.py
+++ b/solution.py
@@ -901,7 +901,7 @@
             fresh = segment(up_other, *hold(up_right, done[-1]))
         if index == 3:
             fresh = rest_own(hold(late, done[-1]))
-        if index == 4:
+        if index == 5:
             fresh = segment(rest_other, *hold(late, done[-1]))
         raw += fresh
         held.append(fresh)

time: 759 us -> 756 us (level)
  waiting for transfers between devices: 187 us -> 200 us
  starting transfers between devices: 183 us -> 174 us
    ppermute x98, waiting for transfers between devices: 170 us -> 183 us  [send(): self.last = [lax.ppermute(v, 'dp', m) for v, (_, m) in zip(values, sends)]]
    ppermute x98, starting transfers between devices: 166 us -> 157 us  [send(): self.last = [lax.ppermute(v, 'dp', m) for v, (_, m) in zip(values, sends)]]
    unnamed x135 -> x141, local copies, waits for them, and re-layouts: 22.8 us -> 20.7 us
  transfers between devices with their start and end apart: 117 -> 117, of which waited for: 50 -> 49; matrix products, arithmetic and copies ran while one was open for 18% -> 18% of each run, Pallas kernels for 26% -> 26%
where the time goes in v12:
time: 756 us; the launch traced here: 744 us
  Pallas kernels  202 us (27%)
  waiting for transfers between devices  200 us (26%)
  starting transfers between devices  174 us (23%)
  other arithmetic  85.9 us (11%)
  local copies, waits for them, and re-layouts  62.2 us (8%)
  matrix products  15.9 us (2%)
    ppermute x98, waiting for transfers between devices, send(): self.last = [lax.ppermute(v, 'dp', m) for v, (_, m) in zip(values, sends)]  183 us
    ppermute x98, starting transfers between devices, send(): self.last = [lax.ppermute(v, 'dp', m) for v, (_, m) in zip(values, sends)]  157 us
    pallas_call x11, Pallas kernels, place(): pl.pallas_call(functools.partial(place_kernel, high), in_specs=[pl.BlockS...  69.5 us
    pallas_call x11, Pallas kernels, rows_product(): pl.pallas_call(functools.partial(product_kernel, len(lefts), turned), gri...  39.9 us
    pallas_call x4, Pallas kernels, times_back(): pl.pallas_call(functools.partial(back_kernel, turned), grid_spec=pltpu.Pr...  27.1 us
    add x10, other arithmetic, line_middle(): return value + middle_hop.send([(value, middle_moves)])[0]  25.2 us
    pallas_call x4, Pallas kernels, times_columns(): pl.pallas_call(columns_kernel, grid_spec=pltpu.PrefetchScalarGridSpec(num...  25.2 us
    unnamed x141, local copies, waits for them, and re-layouts  20.7 us
  transfers between devices with their start and end apart: 117, of which 49 were waited for; matrix products, arithmetic and copies ran while one was open for 18% of the time, Pallas kernels for 26%

profile of v12, /device:TPU:0, one launch (start us, length us, event | category | flops | bytes accessed | tf_op | source)
XLA Modules:
  0.0 743.7 jit_solution(6951783816353899226)
XLA Ops:
  13.4 22.3 %conditional.7 = (bf16[256,1024]{1,0:T(8,128)(2,1)}, bf16[256,1024]{1,0:T(8,128)(2,1)}, bf16[256,1024]{1,0:T(8,128)(2,1)}, bf16[256,1024]{1,0:T(8,128)(2,1)}, bf...) conditional(s32[]{:T(128)} %convert_element_type.31, () %tuple.158, (bf16[128,1024]{1,0:T(8,128)(2,1)S(1)}, ...), branch_computations={%region_0.1_spmd, %region_1.2_spmd} | conditional | flops 874512384 | bytes 19710170 | solution.py:616
  41.5 37.7 %conditional.8 = (f32[128,2048]{1,0:T(8,128)}, bf16[256,1024]{1,0:T(8,128)(2,1)}, bf16[256,4096]{1,0:T(8,128)(2,1)}, bf16[256,4096]{1,0:T(8,128)(2,1)}, f32[4096...) conditional(s32[]{:T(128)} %convert_element_type.31, () %tuple.157, (bf16[256,1024]{1,0:T(8,128)(2,1)}, ...), branch_computations={%region_2.3_spmd, %region_3.4_spmd} | conditional | flops 3222536192 | bytes 42932700 | solution.py:616
  51.4 7.2 branch_1_fun.22
  65.1 13.4 %branch_1_fun.23 = (bf16[256,4096]{1,0:T(8,128)(2,1)}, bf16[256,4096]{1,0:T(8,128)(2,1)}, f32[1,4096]{1,0:T(1,128)}) custom-call(bf16[256,2048]{1,0:T(8,128)(2,1)S(1)} %copy-done.49, bf16[4096,2048]{1,0:T(8,128)(2,1)} %get-tuple-element.204.refs_0_, f32[256,4096]{1,0:T(8,128)S(1)} %branch_1_fun.21.refs_1_, ...), custom_call_target="tpu_custom_call" | custom-call | flops 1073741824 | bytes 7602176 | tf_op jit(solution)/shard_map/cond/branch_1_fun/pallas_call | solution.py:311
  91.7 22.4 %conditional.9 = (f32[128,2048]{1,0:T(8,128)}, bf16[128,2048]{1,0:T(8,128)(2,1)}, bf16[384,2048]{1,0:T(8,128)(2,1)}, bf16[256,1024]{1,0:T(8,128)(2,1)}, bf16[256...) conditional(s32[]{:T(128)} %convert_element_type.31, () %tuple.168, ...), branch_computations={%region_4.5_spmd, %region_5.6_spmd} | conditional | flops 1079771136 | bytes 34343496 | solution.py:616
  124.7 25.5 %conditional.10 = (bf16[3,256,1024]{2,1,0:T(8,128)(2,1)}, bf16[256,3072]{1,0:T(8,128)(2,1)}, bf16[256,3072]{1,0:T(8,128)(2,1)}, bf16[4,256,256]{2,1,0:T(8,128)(2...) conditional(s32[]{:T(128)} %convert_element_type.31, () %tuple.166, ...), branch_computations={%region_6.7_spmd, %region_7.8_spmd} | conditional | flops 1250689024 | bytes 30802540 | solution.py:616
  130.4 10.8 %branch_1_fun.27 = bf16[3,256,1024]{2,1,0:T(8,128)(2,1)} custom-call(s32[1]{0:T(128)} %get-tuple-element.232.first_ref, bf16[256,1024]{1,0:T(8,128)(2,1)} %get-tuple-element.233.q_ref, bf16[256,1024]{1,0:T(8,128)(2,1)} %get-tuple-element.234.k_ref, bf16[256,1024]{1,0:T(8,128)(2,1)} %get-tuple-element.235.v_ref, ...), custom_call_target="tpu_custom_call" | custom-call | flops 167772160 | bytes 917504 | tf_op jit(solution)/shard_map/cond/branch_1_fun/pallas_call | solution.py:424
  167.1 15.2 %conditional.11 = (f32[256,1024]{1,0:T(8,128)}) conditional(s32[]{:T(128)} %convert_element_type.31, () %tuple.165, (s32[3]{0:T(128)S(1)}, bf16[256,3072]{1,0:T(8,128)(2,1)}, bf16[1024,6144]{1,0:T(8,128)(2,1)}, s32[3]{0:T(128)S(1)}, bf16[256,3072]{1,0:T(8,128)(2,1)}) %tuple.176), branch_computations={%region_8.9_spmd, %region_9.10_spmd} | conditional | flops 805306368 | bytes 4980744 | solution.py:616
  167.2 7.1 branch_1_fun.28.refs_1_
  174.3 8.1 %branch_1_fun.29 = f32[256,1024]{1,0:T(8,128)} custom-call(s32[3]{0:T(128)S(1)} %get-tuple-element.239.table_ref, bf16[256,3072]{1,0:T(8,128)(2,1)} %get-tuple-element.240.left_ref, bf16[1024,6144]{1,0:T(8,128)(2,1)} %get-tuple-element.241.refs_0_, f32[256,1024]{1,0:T(8,128)S(1)} %branch_1_fun.28.refs_1_), custom_call_target="tpu_custom_call" | custom-call | flops 402653184 | bytes 2490368 | tf_op jit(solution)/shard_map/cond/branch_1_fun/pallas_call | solution.py:277
  204.3 8.7 %collective-permute-done.34.refs_5_ = bf16[4,256,256]{2,1,0:T(8,128)(2,1)} collective-permute-done((bf16[4,256,256]{2,1,0:T(8,128)(2,1)S(1)}, bf16[4,256,256]{2,1,0:T(8,128)(2,1)}, u32[]{:S(2)}, u32[]{:S(2)}) %collective-permute-start.34) | collective-permute-done | bytes 524320 | tf_op jit(solution)/shard_map/ppermute | solution.py:504
  276.4 12.5 %conditional.12 = (bf16[1024,512]{1,0:T(8,128)(2,1)}, bf16[1024,512]{1,0:T(8,128)(2,1)S(1)}) conditional(s32[]{:T(128)} %convert_element_type.31, () %tuple.202, (bf16[256,1024]{1,0:T(8,128)(2,1)}, bf16[256,1024]{1,0:T(8,128)(2,1)}, bf16[256,1024]{1,0:T(8,128)(2,1)}, bf16[256,1024]{1,0:T(8,128)(2,1)}, bf16[256,1024]{1,0:T(8,128)(2,1)}, ...), branch_computations={%region_10.11_spmd, %region_11.12_spmd} | conditional | flops 545259520 | bytes 14155832 | solution.py:616
  293.5 8.0 %collective-permute-start.43 = (bf16[1024,512]{1,0:T(8,128)(2,1)S(1)}, bf16[1024,512]{1,0:T(8,128)(2,1)S(1)}, u32[]{:S(2)}, u32[]{:S(2)}) collective-permute-start(bf16[1024,512]{1,0:T(8,128)(2,1)S(1)} %shard_map.279), channel_id=1, source_target_pairs={{0,4},{1,5},{2,6},{3,7},{12,8},{13,9},{14,10},{15,11},{16,20},{17,... | collective-permute-start | bytes 3145736 | tf_op jit(solution)/shard_map/ppermute | solution.py:504
  312.2 11.3 %collective-permute-done.43 = bf16[1024,512]{1,0:T(8,128)(2,1)S(1)} collective-permute-done((bf16[1024,512]{1,0:T(8,128)(2,1)S(1)}, bf16[1024,512]{1,0:T(8,128)(2,1)S(1)}, u32[]{:S(2)}, u32[]{:S(2)}) %collective-permute-start.43) | collective-permute-done | bytes 1048608 | tf_op jit(solution)/shard_map/ppermute | solution.py:504
  386.1 7.0 collective-permute-done.62.refs_3_
  447.3 16.0 %conditional.13 = (bf16[1024,768]{1,0:T(8,128)(2,1)}, bf16[1024,512]{1,0:T(8,128)(2,1)}) conditional(s32[]{:T(128)} %convert_element_type.31, () %tuple.185, (bf16[4,256,256]{2,1,0:T(8,128)(2,1)}, bf16[4,256,256]{2,1,0:T(8,128)(2,1)}, bf16[4,256,256]{2,1,0:T(8,128)(2,1)}, bf16[4,256,256]{2,1,0:T(8,128)(2,1)}, bf16[256,2048]{1,0:T(8,128)(2,1)}, ...), branch_computations={%region_12.13_spmd, %region_13.14_spmd} | conditional | flops 674234368 | bytes 16384084 | solution.py:616
  473.8 17.9 %collective-permute-done.79 = bf16[1024,512]{1,0:T(8,128)(2,1)S(1)} collective-permute-done((bf16[1024,512]{1,0:T(8,128)(2,1)}, bf16[1024,512]{1,0:T(8,128)(2,1)S(1)}, u32[]{:S(2)}, u32[]{:S(2)}) %collective-permute-start.79) | collective-permute-done | bytes 1048608 | tf_op jit(solution)/shard_map/ppermute | solution.py:504
  585.5 17.4 %collective-permute-done.95.refs_1_ = bf16[1024,768]{1,0:T(8,128)(2,1)} collective-permute-done((bf16[1024,768]{1,0:T(8,128)(2,1)S(1)}, bf16[1024,768]{1,0:T(8,128)(2,1)}, u32[]{:S(2)}, u32[]{:S(2)}) %collective-permute-start.95) | collective-permute-done | bytes 1572896 | tf_op jit(solution)/shard_map/ppermute | solution.py:504
  617.9 7.1 collective-permute-done.97.refs_3_
  642.6 11.2 %shard_map.294.refs_5_ = f32[1024,6144]{1,0:T(8,128)} custom-call(s32[96]{0:T(128)S(1)} %stack.216.table_ref, bf16[1024,768]{1,0:T(8,128)(2,1)S(1)} %broadcast_select_fusion.refs_0_, bf16[1024,768]{1,0:T(8,128)(2,1)} %collective-permute-done.95.refs_1_, bf16[1024,768]{1,0:T(8,128)(2,1)} %collective-permute-done.96.refs_2_, ...), custom_call_target="tpu_custom_call", output_to_operand_aliasing={{}: (6, {})} | custom-call | bytes 4718592 | tf_op jit(solution)/shard_map/pallas_call | solution.py:469
  660.5 8.7 %fusion.21 = f32[256,2048]{1,0:T(8,128)S(1)} fusion(bf16[256,4096]{1,0:T(8,128)(2,1)} %get-tuple-element.492, bf16[4096,2048]{1,0:T(8,128)(2,1)} %param.36), kind=kOutput, calls=%fused_computation.123 | convolution fusion | flops 4294967296 | bytes 20971520 | tf_op jit(solution)/shard_map/dot_general | solution.py:44
  671.7 14.2 %collective-permute-done.106 = bf16[1024,512]{1,0:T(8,128)(2,1)S(1)} collective-permute-done((bf16[1024,512]{1,0:T(8,128)(2,1)S(1)}, bf16[1024,512]{1,0:T(8,128)(2,1)S(1)}, u32[]{:S(2)}, u32[]{:S(2)}) %collective-permute-start.106) | collective-permute-done | bytes 1048608 | tf_op jit(solution)/shard_map/ppermute | solution.py:504
  697.1 12.0 %collective-permute-start.112 = (f32[192,128]{1,0:T(8,128)S(1)}, f32[192,128]{1,0:T(8,128)S(1)}, u32[]{:S(2)}, u32[]{:S(2)}) collective-permute-start(f32[192,128]{1,0:T(8,128)S(1)} %add_add_fusion.1), channel_id=1, source_target_pairs={{0,4},{1,5},{2,6},{3,7},{4,0},{5,1},{6,2},{7,3},{8,12},{9,13},{10,... | collective-permute-start | bytes 294920 | tf_op jit(solution)/shard_map/ppermute | solution.py:916
  714.4 10.8 %shard_map.295 = f32[1024,6144]{1,0:T(8,128)} custom-call(s32[96]{0:T(128)S(1)} %stack.163.table_ref, bf16[1024,768]{1,0:T(8,128)(2,1)S(1)} %broadcast_select_fusion.1.refs_0_, bf16[1024,768]{1,0:T(8,128)(2,1)} %collective-permute-done.99.refs_1_, bf16[1024,768]{1,0:T(8,128)(2,1)} %collective-permute-done.100.refs_2_, ...), custom_call_target="tpu_custom_call", output_to_operand_aliasing={{}: (6, {})} | custom-call | bytes 4718592 | tf_op jit(solution)/shard_map/pallas_call | solution.py:469
  (524 shorter events, 557.9 us)
Async XLA Ops:
  35.8 43.4 %collective-permute-start.16 = (bf16[256,2048]{1,0:T(8,128)(2,1)}, bf16[256,2048]{1,0:T(8,128)(2,1)}, u32[]{:S(2)}, u32[]{:S(2)}) collective-permute-start(bf16[256,2048]{1,0:T(8,128)(2,1)} %get-tuple-element.598.refs_0_), channel_id=1, source_target_pairs={{0,1},{1,0},{2,3},{3,2},{4,5},{5,4},{6,7},{7,6},{8,9},{9,8},{10,11... | collective-permute-start | bytes 3145736 | tf_op jit(solution)/shard_map/ppermute | solution.py:504
  37.8 47.7 %collective-permute-start.17 = (bf16[256,2048]{1,0:T(8,128)(2,1)}, bf16[256,2048]{1,0:T(8,128)(2,1)}, u32[]{:S(2)}, u32[]{:S(2)}) collective-permute-start(bf16[256,2048]{1,0:T(8,128)(2,1)} %get-tuple-element.598.refs_0_), channel_id=1, source_target_pairs={{0,2},{1,3},{2,0},{3,1},{4,6},{5,7},{6,4},{7,5},{8,10},{9,11},{10,... | collective-permute-start | bytes 3145736 | tf_op jit(solution)/shard_map/ppermute | solution.py:504
  39.3 46.2 %collective-permute-start.18 = (bf16[256,2048]{1,0:T(8,128)(2,1)}, bf16[256,2048]{1,0:T(8,128)(2,1)}, u32[]{:S(2)}, u32[]{:S(2)}) collective-permute-start(bf16[256,2048]{1,0:T(8,128)(2,1)} %get-tuple-element.598.refs_0_), channel_id=1, source_target_pairs={{0,3},{1,2},{2,1},{3,0},{4,7},{5,6},{6,5},{7,4},{8,11},{9,10},{10,... | collective-permute-start | bytes 3145736 | tf_op jit(solution)/shard_map/ppermute | solution.py:504
  116.7 37.0 %collective-permute-start.26 = (bf16[1024,512]{1,0:T(8,128)(2,1)S(1)}, bf16[1024,512]{1,0:T(8,128)(2,1)}, u32[]{:S(2)}, u32[]{:S(2)}) collective-permute-start(bf16[1024,512]{1,0:T(8,128)(2,1)S(1)} %shard_map.275), channel_id=1, source_target_pairs={{0,4},{1,5},{2,6},{3,7},{12,8},{13,9},{14,10},{15,11},{16,20},{17,... | collective-permute-start | bytes 3145736 | tf_op jit(solution)/shard_map/ppermute | solution.py:504
  121.2 32.5 %collective-permute-start.23 = (bf16[256,1024]{1,0:T(8,128)(2,1)}, bf16[256,1024]{1,0:T(8,128)(2,1)}, u32[]{:S(2)}, u32[]{:S(2)}) collective-permute-start(bf16[256,1024]{1,0:T(8,128)(2,1)} %get-tuple-element.518), channel_id=1, source_target_pairs={{0,1},{1,0},{2,3},{3,2},{4,5},{5,4},{6,7},{7,6},{8,9},{9,8},{10,11... | collective-permute-start | bytes 1572872 | tf_op jit(solution)/shard_map/ppermute | solution.py:504
  264.5 37.1 %collective-permute-start.49 = (bf16[1024,512]{1,0:T(8,128)(2,1)}, bf16[1024,512]{1,0:T(8,128)(2,1)}, u32[]{:S(2)}, u32[]{:S(2)}) collective-permute-start(bf16[1024,512]{1,0:T(8,128)(2,1)} %add.365), channel_id=1, source_target_pairs={{4,0},{5,1},{6,2},{7,3},{8,12},{9,13},{10,14},{11,15},{20,16},{21,... | collective-permute-start | bytes 3145736 | tf_op jit(solution)/shard_map/ppermute | solution.py:504
  265.8 42.3 %collective-permute-start.46 = (bf16[1024,512]{1,0:T(8,128)(2,1)}, bf16[1024,512]{1,0:T(8,128)(2,1)}, u32[]{:S(2)}, u32[]{:S(2)}) collective-permute-start(bf16[1024,512]{1,0:T(8,128)(2,1)} %add.359), channel_id=1, source_target_pairs={{4,8},{5,9},{6,10},{7,11},{8,4},{9,5},{10,6},{11,7},{20,24},{21,25... | collective-permute-start | bytes 3145736 | tf_op jit(solution)/shard_map/ppermute | solution.py:504
  310.9 34.4 %collective-permute-start.50 = (bf16[1024,512]{1,0:T(8,128)(2,1)}, bf16[1024,512]{1,0:T(8,128)(2,1)}, u32[]{:S(2)}, u32[]{:S(2)}) collective-permute-start(bf16[1024,512]{1,0:T(8,128)(2,1)} %add.364), channel_id=1, source_target_pairs={{4,0},{5,1},{6,2},{7,3},{8,12},{9,13},{10,14},{11,15},{20,16},{21,... | collective-permute-start | bytes 3145736 | tf_op jit(solution)/shard_map/ppermute | solution.py:504
  365.1 41.0 %collective-permute-start.69 = (bf16[1024,512]{1,0:T(8,128)(2,1)}, bf16[1024,512]{1,0:T(8,128)(2,1)}, u32[]{:S(2)}, u32[]{:S(2)}) collective-permute-start(bf16[1024,512]{1,0:T(8,128)(2,1)} %get-tuple-element.623), channel_id=1, source_target_pairs={{0,4},{1,5},{2,6},{3,7},{12,8},{13,9},{14,10},{15,11},{16,20},{17,... | collective-permute-start | bytes 3145736 | tf_op jit(solution)/shard_map/ppermute | solution.py:504
  373.3 34.2 %collective-permute-start.73 = (bf16[1024,512]{1,0:T(8,128)(2,1)}, bf16[1024,512]{1,0:T(8,128)(2,1)}, u32[]{:S(2)}, u32[]{:S(2)}) collective-permute-start(bf16[1024,512]{1,0:T(8,128)(2,1)} %add.714), channel_id=1, source_target_pairs={{4,8},{5,9},{6,10},{7,11},{8,4},{9,5},{10,6},{11,7},{20,24},{21,25... | collective-permute-start | bytes 3145736 | tf_op jit(solution)/shard_map/ppermute | solution.py:504
  426.4 42.6 %collective-permute-start.71 = (bf16[1024,768]{1,0:T(8,128)(2,1)S(1)}, bf16[1024,768]{1,0:T(8,128)(2,1)}, u32[]{:S(2)}, u32[]{:S(2)}) collective-permute-start(bf16[1024,768]{1,0:T(8,128)(2,1)S(1)} %shard_map.286), channel_id=1, source_target_pairs={{0,4},{1,5},{2,6},{3,7},{12,8},{13,9},{14,10},{15,11},{16,20},{17,... | collective-permute-start | bytes 4718600 | tf_op jit(solution)/shard_map/ppermute | solution.py:504
  437.2 34.7 %collective-permute-start.75 = (bf16[1024,512]{1,0:T(8,128)(2,1)}, bf16[1024,512]{1,0:T(8,128)(2,1)}, u32[]{:S(2)}, u32[]{:S(2)}) collective-permute-start(bf16[1024,512]{1,0:T(8,128)(2,1)} %add.712), channel_id=1, source_target_pairs={{4,8},{5,9},{6,10},{7,11},{8,4},{9,5},{10,6},{11,7},{20,24},{21,25... | collective-permute-start | bytes 3145736 | tf_op jit(solution)/shard_map/ppermute | solution.py:504
  472.0 50.0 %collective-permute-start.76 = (bf16[1024,768]{1,0:T(8,128)(2,1)}, bf16[1024,768]{1,0:T(8,128)(2,1)}, u32[]{:S(2)}, u32[]{:S(2)}) collective-permute-start(bf16[1024,768]{1,0:T(8,128)(2,1)} %add.368), channel_id=1, source_target_pairs={{4,8},{5,9},{6,10},{7,11},{8,4},{9,5},{10,6},{11,7},{20,24},{21,25... | collective-permute-start | bytes 4718600 | tf_op jit(solution)/shard_map/ppermute | solution.py:504
  498.6 38.6 %collective-permute-start.72 = (bf16[1024,768]{1,0:T(8,128)(2,1)}, bf16[1024,768]{1,0:T(8,128)(2,1)}, u32[]{:S(2)}, u32[]{:S(2)}) collective-permute-start(bf16[1024,768]{1,0:T(8,128)(2,1)} %get-tuple-element.626), channel_id=1, source_target_pairs={{0,4},{1,5},{2,6},{3,7},{12,8},{13,9},{14,10},{15,11},{16,20},{17,... | collective-permute-start | bytes 4718600 | tf_op jit(solution)/shard_map/ppermute | solution.py:504
  525.4 36.5 %collective-permute-start.81 = (bf16[1024,768]{1,0:T(8,128)(2,1)}, bf16[1024,768]{1,0:T(8,128)(2,1)}, u32[]{:S(2)}, u32[]{:S(2)}) collective-permute-start(bf16[1024,768]{1,0:T(8,128)(2,1)} %add.716), channel_id=1, source_target_pairs={{4,0},{5,1},{6,2},{7,3},{8,12},{9,13},{10,14},{11,15},{20,16},{21,... | collective-permute-start | bytes 4718600 | tf_op jit(solution)/shard_map/ppermute | solution.py:504
  540.6 32.7 %collective-permute-start.77 = (bf16[1024,768]{1,0:T(8,128)(2,1)}, bf16[1024,768]{1,0:T(8,128)(2,1)}, u32[]{:S(2)}, u32[]{:S(2)}) collective-permute-start(bf16[1024,768]{1,0:T(8,128)(2,1)} %add.367), channel_id=1, source_target_pairs={{4,8},{5,9},{6,10},{7,11},{8,4},{9,5},{10,6},{11,7},{20,24},{21,25... | collective-permute-start | bytes 4718600 | tf_op jit(solution)/shard_map/ppermute | solution.py:504
  570.6 32.4 %collective-permute-start.95 = (bf16[1024,768]{1,0:T(8,128)(2,1)S(1)}, bf16[1024,768]{1,0:T(8,128)(2,1)}, u32[]{:S(2)}, u32[]{:S(2)}) collective-permute-start(bf16[1024,768]{1,0:T(8,128)(2,1)S(1)} %broadcast_select_fusion.refs_0_), channel_id=1, source_target_pairs={{0,1},{1,0},{2,3},{3,2},{4,5},{5,4},{6,7},{7,6},{8,9},{9,8},{10,11... | collective-permute-start | bytes 4718600 | tf_op jit(solution)/shard_map/ppermute | solution.py:504
  572.0 33.0 %collective-permute-start.96 = (bf16[1024,768]{1,0:T(8,128)(2,1)S(1)}, bf16[1024,768]{1,0:T(8,128)(2,1)}, u32[]{:S(2)}, u32[]{:S(2)}) collective-permute-start(bf16[1024,768]{1,0:T(8,128)(2,1)S(1)} %broadcast_select_fusion.refs_0_), channel_id=1, source_target_pairs={{0,2},{1,3},{2,0},{3,1},{4,6},{5,7},{6,4},{7,5},{8,10},{9,11},{10,... | collective-permute-start | bytes 4718600 | tf_op jit(solution)/shard_map/ppermute | solution.py:504
  576.7 39.6 %collective-permute-start.82 = (bf16[1024,768]{1,0:T(8,128)(2,1)}, bf16[1024,768]{1,0:T(8,128)(2,1)}, u32[]{:S(2)}, u32[]{:S(2)}) collective-permute-start(bf16[1024,768]{1,0:T(8,128)(2,1)} %add.715), channel_id=1, source_target_pairs={{4,0},{5,1},{6,2},{7,3},{8,12},{9,13},{10,14},{11,15},{20,16},{21,... | collective-permute-start | bytes 4718600 | tf_op jit(solution)/shard_map/ppermute | solution.py:504
  641.1 44.9 %collective-permute-start.106 = (bf16[1024,512]{1,0:T(8,128)(2,1)S(1)}, bf16[1024,512]{1,0:T(8,128)(2,1)S(1)}, u32[]{:S(2)}, u32[]{:S(2)}) collective-permute-start(bf16[1024,512]{1,0:T(8,128)(2,1)S(1)} %add.748), channel_id=1, source_target_pairs={{4,0},{5,1},{6,2},{7,3},{8,12},{9,13},{10,14},{11,15},{20,16},{21,... | collective-permute-start | bytes 3145736 | tf_op jit(solution)/shard_map/ppermute | solution.py:504
  658.3 34.3 %collective-permute-start.104 = (bf16[512,768]{1,0:T(8,128)(2,1)S(1)}, bf16[512,768]{1,0:T(8,128)(2,1)S(1)}, u32[]{:S(2)}, u32[]{:S(2)}) collective-permute-start(bf16[512,768]{1,0:T(8,128)(2,1)S(1)} %slice.256), channel_id=1, source_target_pairs={{0,2},{1,3},{2,0},{3,1},{4,6},{5,7},{6,4},{7,5},{8,10},{9,11},{10,... | collective-permute-start | bytes 2359304 | tf_op jit(solution)/shard_map/ppermute | solution.py:504
  659.8 32.8 %collective-permute-start.105 = (bf16[512,768]{1,0:T(8,128)(2,1)S(1)}, bf16[512,768]{1,0:T(8,128)(2,1)S(1)}, u32[]{:S(2)}, u32[]{:S(2)}) collective-permute-start(bf16[512,768]{1,0:T(8,128)(2,1)S(1)} %slice.257), channel_id=1, source_target_pairs={{0,1},{1,0},{2,3},{3,2},{4,5},{5,4},{6,7},{7,6},{8,9},{9,8},{10,11... | collective-permute-start | bytes 2359304 | tf_op jit(solution)/shard_map/ppermute | solution.py:504
  670.4 39.1 %collective-permute-start.19 = (f32[128,2048]{1,0:T(8,128)}, f32[128,2048]{1,0:T(8,128)}, u32[]{:S(2)}, u32[]{:S(2)}) collective-permute-start(f32[128,2048]{1,0:T(8,128)} %slice.237), channel_id=1, source_target_pairs={{0,16},{16,0},{1,17},{17,1},{2,18},{18,2},{3,19},{19,3},{4,20},{20... | collective-permute-start | bytes 3145736 | tf_op jit(solution)/shard_map/ppermute | solution.py:542
  694.1 32.3 %collective-permute-start.111 = (bf16[1024,512]{1,0:T(8,128)(2,1)S(1)}, bf16[1024,512]{1,0:T(8,128)(2,1)}, u32[]{:S(2)}, u32[]{:S(2)}) collective-permute-start(bf16[1024,512]{1,0:T(8,128)(2,1)S(1)} %broadcast_select_fusion.2.refs_0_), channel_id=1, source_target_pairs={{0,2},{1,3},{2,0},{3,1},{4,6},{5,7},{6,4},{7,5},{8,10},{9,11},{10,... | collective-permute-start | bytes 3145736 | tf_op jit(solution)/shard_map/ppermute | solution.py:504
  (164 other events, 2376.3 us)
